TPU v7x, 32 devices: a whole 2x2x4 slice. The times are simulated.
32 devices in a mesh: tm: 2 (over y), net: 4 (over z), cols: 4 (over x, core).
Axes of the slice: x: 2, y: 2, z: 4, core: 2. Of those that a mesh axis runs over, the one named last changes fastest.
Arguments:
- jac: bfloat16 [4, 16, 3, 128, 128], P('tm', 'net'), may hold values from -0.5 to 1.5
- block_cols: int32 [16, 2], P('net'), may hold values from 0 to 3
- iface_jac: bfloat16 [4, 4, 4, 128, 128], P('tm', 'net'), may hold values from -0.1796875 to 0.1796875
- iface_send: int32 [4, 4], P('net'), may hold values from 0 to 3
- iface_recv: int32 [4, 4], P('net'), may hold values from 0 to 3
- iface_live: int32 [4, 4], P('net'), may hold values from 0 to 128
- ctrl_node: int32 [768], P('cols'), may hold values from 0 to 2047
- ctrl_gain: float32 [4, 768], P('tm', 'cols'), may hold values from -6 to 6
Outputs:
- sens: bfloat16 [4, 768, 2048], P('tm', 'cols', 'net')
All inputs are finite; a program needn't handle non-finite values.
Results may differ from a plain program's by a relative error of at most 0.013.
Values may be sent and summed in bfloat16 or wider, within the bound.
No kernel may reach another device: no remote copies, remote signals or barrier semaphores. Data moves between devices by JAX's collectives and lax.ppermute only.
A program may use at most 64 MiB of HBM per device.

v0:
```python
import jax
import jax.numpy as jnp
from jax import lax
from jax.sharding import PartitionSpec as P


def from_behind(value, axis, by):
    size = lax.axis_size(axis)
    pairs = [(i, i + by) for i in range(size) if 0 <= i + by < size]
    return lax.ppermute(value, axis, pairs)


def local(jac, block_cols, iface_jac, iface_send, iface_recv, iface_live, ctrl_node, ctrl_gain):
    step_count = jac.shape[0]
    block_count = jac.shape[1]
    block_size = jac.shape[3]
    col_count = ctrl_node.shape[0]
    tm_size = lax.axis_size("tm")
    section_index = lax.axis_index("tm")
    partition = lax.axis_index("net")
    state_count = block_count * block_size
    global_rows = partition * state_count + jnp.arange(state_count, dtype=jnp.int32)
    receive_map = (
        iface_recv[0][:, None] == jnp.arange(block_count, dtype=jnp.int32)[None, :]
    ).astype(jnp.float32)
    live_mask = (jnp.arange(block_size, dtype=jnp.int32)[None, :] < iface_live[0][:, None]).astype(
        jnp.float32
    )
    send_rows = iface_send[0]
    highest = lax.Precision.HIGHEST

    def advance(state, step_jac, step_iface, node_ids, gain_row):
        width_cols = state.shape[0]
        state_tiles = state.reshape(width_cols, block_count, block_size)
        summed = jnp.einsum(
            "iab,cib->cia", step_jac[:, 0], state_tiles, preferred_element_type=jnp.float32
        )
        near_tiles = state_tiles[:, block_cols, :]
        summed = summed + jnp.einsum(
            "ikab,cikb->cia", step_jac[:, 1:], near_tiles, preferred_element_type=jnp.float32
        )
        outgoing = state_tiles[:, send_rows, :]
        incoming = lax.all_to_all(outgoing, "net", split_axis=1, concat_axis=1, tiled=True)
        coupled = jnp.einsum(
            "qab,cqb->cqa", step_iface, incoming, preferred_element_type=jnp.float32
        )
        coupled = coupled * live_mask[None]
        summed = summed + jnp.einsum("cqa,qi->cia", coupled, receive_map, precision=highest)
        injection = gain_row[:, None] * (node_ids[:, None] == global_rows[None, :]).astype(
            jnp.float32
        )
        return (summed.reshape(width_cols, state_count) + injection).astype(jnp.bfloat16)

    panel_count = 1
    panel_cols = col_count // panel_count

    def one_round(r, carry):
        results, finished = carry
        arrived = from_behind(finished, "tm", 1)
        lag_rounds = r - section_index
        panel_index = jnp.clip(lag_rounds, 0, panel_count - 1)
        first_col = panel_index * panel_cols
        state = arrived
        produced = []
        for s in range(step_count):
            gain_row = ctrl_gain[s]
            state = advance(state, jac[s], iface_jac[s, 0], ctrl_node, gain_row)
            produced.append(state)
        new_steps = jnp.stack(produced)
        written = lax.dynamic_update_slice_in_dim(results, new_steps, first_col, 1)
        in_range = jnp.logical_and(lag_rounds >= 0, lag_rounds < panel_count)
        results = jnp.where(in_range, written, results)
        return (results, state)

    results = jnp.zeros((step_count, col_count, state_count), jnp.bfloat16)
    finished = jnp.zeros((panel_cols, state_count), jnp.bfloat16)
    results, finished = lax.fori_loop(0, tm_size + panel_count - 1, one_round, (results, finished))
    return results


def solution(mesh):
    return jax.shard_map(
        local,
        mesh=mesh,
        in_specs=(
            P("tm", "net", None, None, None),
            P("net", None),
            P("tm", "net", None, None, None),
            P("net", None),
            P("net", None),
            P("net", None),
            P("cols"),
            P("tm", "cols"),
        ),
        out_specs=P("tm", "cols", "net"),
        check_vma=False,
    )
```

profile of v0, /device:TPU:4, one launch (start us, length us, event | category | flops | bytes accessed | tf_op | source)
XLA Modules:
  0.0 84.0 jit_solution(4271954048221415923)
XLA Ops:
  0.0 1.2 %copy.39 = bf16[2,4,3,128,128]{4,3,1,2,0:T(8,128)(2,1)S(1)} copy(bf16[2,4,3,128,128]{4,3,2,1,0:T(8,128)(2,1)} %param.10) | data formatting | bytes 1572864
  2.0 81.2 %while.16 = (s32[]{:T(128)}, bf16[2,192,512]{2,1,0:T(8,128)(2,1)S(1)}, bf16[192,512]{1,0:T(8,128)(2,1)S(1)}, s32[]{:T(128)}, bf16[2,4,3,128,128]{4,3,1,2,0:T(8,1...) while((s32[]{:T(128)}, ...), condition=%wide.region_1.2_spmd.clone, body=%wide.region_0.1_spmd.clone.sunk | while | flops 213520480 | bytes 21963972 | solution.py:77
  2.0 1.3 %collective-permute-start = (bf16[192,512]{1,0:T(8,128)(2,1)S(1)}, bf16[192,512]{1,0:T(8,128)(2,1)S(1)}, u32[]{:S(2)}, u32[]{:S(2)}) collective-permute-start(bf16[192,512]{1,0:T(8,128)(2,1)S(1)} %broadcast_select_fusion.2), channel_id=1, source_target_pairs={{0,16},{1,17},{2,18},{3,19},{4,20},{5,21},{6,22},{7,23},{8,24},{9,... | collective-permute-start | bytes 589832 | tf_op jit(solution)/shard_map/while/body/eval_jaxpr/ppermute | solution.py:10
  4.0 6.5 %collective-permute-done = bf16[192,512]{1,0:T(8,128)(2,1)S(1)} collective-permute-done((bf16[192,512]{1,0:T(8,128)(2,1)S(1)}, bf16[192,512]{1,0:T(8,128)(2,1)S(1)}, u32[]{:S(2)}, u32[]{:S(2)}) %collective-permute-start) | collective-permute-done | bytes 196640 | tf_op jit(solution)/shard_map/while/body/eval_jaxpr/ppermute | solution.py:10
  10.6 1.2 %gather_fusion = bf16[4,192,128]{2,1,0:T(8,128)(2,1)} fusion(bf16[192,4,128]{2,0,1:T(8,128)(2,1)S(1)} %copy_bitcast_fusion.3, s32[1024]{0:T(1024)S(1)} %pad_clamp_fusion.4), kind=kCustom, calls=%fused_computation.1.clone.clone.1 | custom fusion | bytes 393232 | tf_op jit(solution)/shard_map/while/body/eval_jaxpr/gather | solution.py:42
  11.8 4.9 %all-to-all-start = ((bf16[192,4,128]{2,0,1:T(8,128)(2,1)}), bf16[192,4,128]{2,0,1:T(8,128)(2,1)S(1)}, u32[]{:S(2)}, u32[]{:S(2)}) async-start(bf16[192,4,128]{2,0,1:T(8,128)(2,1)} %bitcast.154), calls=%async_computation | async-start | bytes 393216 | tf_op jit(solution)/shard_map/while/body/eval_jaxpr/all_to_all | solution.py:43
  18.4 4.8 %all-to-all-done = bf16[192,4,128]{2,0,1:T(8,128)(2,1)S(1)} async-done(((bf16[192,4,128]{2,0,1:T(8,128)(2,1)}), bf16[192,4,128]{2,0,1:T(8,128)(2,1)S(1)}, u32[]{:S(2)}, u32[]{:S(2)}) %all-to-all-start) | async-done | bytes 196640 | tf_op jit(solution)/shard_map/while/body/eval_jaxpr/all_to_all | solution.py:43
  23.1 1.1 %fusion.98 = f32[192,4,128]{2,0,1:T(8,128)S(1)} fusion(bf16[192,4,128]{2,0,1:T(8,128)(2,1)S(1)} %all-to-all-done, f32[4,128]{1,0:T(4,128)S(1)} %fusion.97, bf16[2,1,4,128,128]{4,3,2,1,0:T(8,128)(2,1)} %get-tuple-element.476), kind=kOutput, calls=%fused_computation.13.clone.1 | convolution fusion | flops 25264128 | bytes 722944 | tf_op jit(solution)/shard_map/while/body/eval_jaxpr/qab,cqb->cqa/dot_general | solution.py:44
  24.9 1.0 %fusion.99 = f32[192,128,4]{1,2,0:T(4,128)S(1)} fusion(f32[192,4,128]{2,0,1:T(8,128)S(1)} %fusion.98, s32[4]{0:T(128)S(1)} %copy-done.10), kind=kOutput, calls=%fused_computation.30.clone.1 | convolution fusion | flops 4718624 | bytes 786448 | tf_op jit(solution)/shard_map/while/body/eval_jaxpr/cqa,qi->cia/dot_general | solution.py:48
  26.8 1.4 %gather_fusion.3 = bf16[4,192,128]{2,1,0:T(8,128)(2,1)} fusion(bf16[192,4,128]{2,0,1:T(8,128)(2,1)S(1)} %get-tuple-element.434, s32[1024]{0:T(1024)} %copy-done.7), kind=kCustom, calls=%fused_computation.3.clone.clone.1 | custom fusion | bytes 393232 | tf_op jit(solution)/shard_map/while/body/eval_jaxpr/gather | solution.py:42
  28.2 3.4 %all-to-all-start.1 = ((bf16[192,4,128]{2,0,1:T(8,128)(2,1)}), bf16[192,4,128]{2,0,1:T(8,128)(2,1)S(1)}, u32[]{:S(2)}, u32[]{:S(2)}) async-start(bf16[192,4,128]{2,0,1:T(8,128)(2,1)} %bitcast.157), calls=%async_computation.1 | async-start | bytes 393216 | tf_op jit(solution)/shard_map/while/body/eval_jaxpr/all_to_all | solution.py:43
  32.9 4.9 %all-to-all-done.1 = bf16[192,4,128]{2,0,1:T(8,128)(2,1)S(1)} async-done(((bf16[192,4,128]{2,0,1:T(8,128)(2,1)}), bf16[192,4,128]{2,0,1:T(8,128)(2,1)S(1)}, u32[]{:S(2)}, u32[]{:S(2)}) %all-to-all-start.1) | async-done | bytes 196640 | tf_op jit(solution)/shard_map/while/body/eval_jaxpr/all_to_all | solution.py:43
  37.8 1.1 %fusion.100 = f32[192,4,128]{2,0,1:T(8,128)S(1)} fusion(bf16[192,4,128]{2,0,1:T(8,128)(2,1)S(1)} %all-to-all-done.1, f32[4,128]{1,0:T(4,128)S(1)} %fusion.97, bf16[2,1,4,128,128]{4,3,2,1,0:T(8,128)(2,1)} %get-tuple-element.476), kind=kOutput, calls=%fused_computation.8.clone.1 | convolution fusion | flops 25264128 | bytes 722944 | tf_op jit(solution)/shard_map/while/body/eval_jaxpr/qab,cqb->cqa/dot_general | solution.py:44
  38.9 1.0 %fusion.101 = f32[192,128,4]{1,2,0:T(4,128)S(1)} fusion(f32[192,4,128]{2,0,1:T(8,128)S(1)} %fusion.100, s32[4]{0:T(128)S(1)} %copy-done.11), kind=kOutput, calls=%fused_computation.28.clone.1 | convolution fusion | flops 4718624 | bytes 786448 | tf_op jit(solution)/shard_map/while/body/eval_jaxpr/cqa,qi->cia/dot_general | solution.py:48
  40.6 1.5 %fusion.104 = bf16[192,512]{1,0:T(8,128)(2,1)} fusion(f32[192]{0:T(256)S(1)} %bitcast.161, s32[512]{0:T(512)S(1)} %iota_add_fusion.2, s32[192]{0:T(256)} %get-tuple-element.518, f32[192,4,128]{2,0,1:T(8,128)S(1)} %fusion.102), kind=kLoop, calls=%fused_computation.26.clone.1 | loop fusion | flops 393216 | bytes 593408 | tf_op jit(solution)/shard_map/while/body/eval_jaxpr/convert_element_type | solution.py:52
  42.1 0.8 fusion.103
  43.2 0.7 copy-done.1
  44.0 1.3 %collective-permute-start = (bf16[192,512]{1,0:T(8,128)(2,1)S(1)}, bf16[192,512]{1,0:T(8,128)(2,1)S(1)}, u32[]{:S(2)}, u32[]{:S(2)}) collective-permute-start(bf16[192,512]{1,0:T(8,128)(2,1)S(1)} %broadcast_select_fusion.2), channel_id=1, source_target_pairs={{0,16},{1,17},{2,18},{3,19},{4,20},{5,21},{6,22},{7,23},{8,24},{9,... | collective-permute-start | bytes 589832 | tf_op jit(solution)/shard_map/while/body/eval_jaxpr/ppermute | solution.py:10
  46.0 5.5 %collective-permute-done = bf16[192,512]{1,0:T(8,128)(2,1)S(1)} collective-permute-done((bf16[192,512]{1,0:T(8,128)(2,1)S(1)}, bf16[192,512]{1,0:T(8,128)(2,1)S(1)}, u32[]{:S(2)}, u32[]{:S(2)}) %collective-permute-start) | collective-permute-done | bytes 196640 | tf_op jit(solution)/shard_map/while/body/eval_jaxpr/ppermute | solution.py:10
  51.6 1.2 %gather_fusion = bf16[4,192,128]{2,1,0:T(8,128)(2,1)} fusion(bf16[192,4,128]{2,0,1:T(8,128)(2,1)S(1)} %copy_bitcast_fusion.3, s32[1024]{0:T(1024)S(1)} %pad_clamp_fusion.4), kind=kCustom, calls=%fused_computation.1.clone.clone.1 | custom fusion | bytes 393232 | tf_op jit(solution)/shard_map/while/body/eval_jaxpr/gather | solution.py:42
  52.8 3.4 %all-to-all-start = ((bf16[192,4,128]{2,0,1:T(8,128)(2,1)}), bf16[192,4,128]{2,0,1:T(8,128)(2,1)S(1)}, u32[]{:S(2)}, u32[]{:S(2)}) async-start(bf16[192,4,128]{2,0,1:T(8,128)(2,1)} %bitcast.154), calls=%async_computation | async-start | bytes 393216 | tf_op jit(solution)/shard_map/while/body/eval_jaxpr/all_to_all | solution.py:43
  57.9 4.5 %all-to-all-done = bf16[192,4,128]{2,0,1:T(8,128)(2,1)S(1)} async-done(((bf16[192,4,128]{2,0,1:T(8,128)(2,1)}), bf16[192,4,128]{2,0,1:T(8,128)(2,1)S(1)}, u32[]{:S(2)}, u32[]{:S(2)}) %all-to-all-start) | async-done | bytes 196640 | tf_op jit(solution)/shard_map/while/body/eval_jaxpr/all_to_all | solution.py:43
  62.4 1.1 %fusion.98 = f32[192,4,128]{2,0,1:T(8,128)S(1)} fusion(bf16[192,4,128]{2,0,1:T(8,128)(2,1)S(1)} %all-to-all-done, f32[4,128]{1,0:T(4,128)S(1)} %fusion.97, bf16[2,1,4,128,128]{4,3,2,1,0:T(8,128)(2,1)} %get-tuple-element.476), kind=kOutput, calls=%fused_computation.13.clone.1 | convolution fusion | flops 25264128 | bytes 722944 | tf_op jit(solution)/shard_map/while/body/eval_jaxpr/qab,cqb->cqa/dot_general | solution.py:44
  64.2 1.0 %fusion.99 = f32[192,128,4]{1,2,0:T(4,128)S(1)} fusion(f32[192,4,128]{2,0,1:T(8,128)S(1)} %fusion.98, s32[4]{0:T(128)S(1)} %copy-done.10), kind=kOutput, calls=%fused_computation.30.clone.1 | convolution fusion | flops 4718624 | bytes 786448 | tf_op jit(solution)/shard_map/while/body/eval_jaxpr/cqa,qi->cia/dot_general | solution.py:48
  66.1 1.4 %gather_fusion.3 = bf16[4,192,128]{2,1,0:T(8,128)(2,1)} fusion(bf16[192,4,128]{2,0,1:T(8,128)(2,1)S(1)} %get-tuple-element.434, s32[1024]{0:T(1024)} %copy-done.7), kind=kCustom, calls=%fused_computation.3.clone.clone.1 | custom fusion | bytes 393232 | tf_op jit(solution)/shard_map/while/body/eval_jaxpr/gather | solution.py:42
  67.5 3.4 %all-to-all-start.1 = ((bf16[192,4,128]{2,0,1:T(8,128)(2,1)}), bf16[192,4,128]{2,0,1:T(8,128)(2,1)S(1)}, u32[]{:S(2)}, u32[]{:S(2)}) async-start(bf16[192,4,128]{2,0,1:T(8,128)(2,1)} %bitcast.157), calls=%async_computation.1 | async-start | bytes 393216 | tf_op jit(solution)/shard_map/while/body/eval_jaxpr/all_to_all | solution.py:43
  72.2 4.9 %all-to-all-done.1 = bf16[192,4,128]{2,0,1:T(8,128)(2,1)S(1)} async-done(((bf16[192,4,128]{2,0,1:T(8,128)(2,1)}), bf16[192,4,128]{2,0,1:T(8,128)(2,1)S(1)}, u32[]{:S(2)}, u32[]{:S(2)}) %all-to-all-start.1) | async-done | bytes 196640 | tf_op jit(solution)/shard_map/while/body/eval_jaxpr/all_to_all | solution.py:43
  77.1 1.1 %fusion.100 = f32[192,4,128]{2,0,1:T(8,128)S(1)} fusion(bf16[192,4,128]{2,0,1:T(8,128)(2,1)S(1)} %all-to-all-done.1, f32[4,128]{1,0:T(4,128)S(1)} %fusion.97, bf16[2,1,4,128,128]{4,3,2,1,0:T(8,128)(2,1)} %get-tuple-element.476), kind=kOutput, calls=%fused_computation.8.clone.1 | convolution fusion | flops 25264128 | bytes 722944 | tf_op jit(solution)/shard_map/while/body/eval_jaxpr/qab,cqb->cqa/dot_general | solution.py:44
  78.2 1.0 %fusion.101 = f32[192,128,4]{1,2,0:T(4,128)S(1)} fusion(f32[192,4,128]{2,0,1:T(8,128)S(1)} %fusion.100, s32[4]{0:T(128)S(1)} %copy-done.11), kind=kOutput, calls=%fused_computation.28.clone.1 | convolution fusion | flops 4718624 | bytes 786448 | tf_op jit(solution)/shard_map/while/body/eval_jaxpr/cqa,qi->cia/dot_general | solution.py:48
  79.9 1.5 %fusion.104 = bf16[192,512]{1,0:T(8,128)(2,1)} fusion(f32[192]{0:T(256)S(1)} %bitcast.161, s32[512]{0:T(512)S(1)} %iota_add_fusion.2, s32[192]{0:T(256)} %get-tuple-element.518, f32[192,4,128]{2,0,1:T(8,128)S(1)} %fusion.102), kind=kLoop, calls=%fused_computation.26.clone.1 | loop fusion | flops 393216 | bytes 593408 | tf_op jit(solution)/shard_map/while/body/eval_jaxpr/convert_element_type | solution.py:52
  81.4 0.8 fusion.103
  83.2 0.7 copy-done
  (108 shorter events, 13.6 us)
Async XLA Ops:
  0.0 1.3 %copy-start.12 = (s32[4,2]{0,1:T(2,128)S(1)}, s32[4,2]{0,1:T(2,128)}, u32[]{:S(2)}) copy-start(s32[4,2]{0,1:T(2,128)} %param.11) | copy-start | bytes 100
  0.0 1.3 %copy-start.16 = (s32[1,4]{1,0:T(1,128)S(1)}, s32[1,4]{1,0:T(1,128)}, u32[]{:S(2)}) copy-start(s32[1,4]{1,0:T(1,128)} %param.13) | copy-start | bytes 52
  1.3 0.7 copy-start.8
  1.3 0.7 copy-start.2
  1.3 0.7 copy-start.14
  2.0 8.5 %collective-permute-start = (bf16[192,512]{1,0:T(8,128)(2,1)S(1)}, bf16[192,512]{1,0:T(8,128)(2,1)S(1)}, u32[]{:S(2)}, u32[]{:S(2)}) collective-permute-start(bf16[192,512]{1,0:T(8,128)(2,1)S(1)} %broadcast_select_fusion.2), channel_id=1, source_target_pairs={{0,16},{1,17},{2,18},{3,19},{4,20},{5,21},{6,22},{7,23},{8,24},{9,... | collective-permute-start | bytes 589832 | tf_op jit(solution)/shard_map/while/body/eval_jaxpr/ppermute | solution.py:10
  3.3 7.3 %copy-start.7 = (s32[1024]{0:T(1024)}, s32[1024]{0:T(1024)S(1)}, u32[]{:S(2)}) copy-start(s32[1024]{0:T(1024)S(1)} %pad_clamp_fusion.4) | copy-start | bytes 12292 | tf_op jit(solution)/shard_map/while
  11.8 11.3 %all-to-all-start = ((bf16[192,4,128]{2,0,1:T(8,128)(2,1)}), bf16[192,4,128]{2,0,1:T(8,128)(2,1)S(1)}, u32[]{:S(2)}, u32[]{:S(2)}) async-start(bf16[192,4,128]{2,0,1:T(8,128)(2,1)} %bitcast.154), calls=%async_computation | async-start | bytes 393216 | tf_op jit(solution)/shard_map/while/body/eval_jaxpr/all_to_all | solution.py:43
  25.9 0.7 copy-start.6
  28.2 9.6 %all-to-all-start.1 = ((bf16[192,4,128]{2,0,1:T(8,128)(2,1)}), bf16[192,4,128]{2,0,1:T(8,128)(2,1)S(1)}, u32[]{:S(2)}, u32[]{:S(2)}) async-start(bf16[192,4,128]{2,0,1:T(8,128)(2,1)} %bitcast.157), calls=%async_computation.1 | async-start | bytes 393216 | tf_op jit(solution)/shard_map/while/body/eval_jaxpr/all_to_all | solution.py:43
  32.9 6.0 %copy-start.11 = (s32[4]{0:T(128)S(1)}, s32[4]{0:T(128)}, u32[]{:S(2)}) copy-start(s32[4]{0:T(128)} %get-tuple-element.480) | copy-start | bytes 52 | tf_op jit(solution)/shard_map/while
  40.6 1.5 %copy-start.5 = (f32[1,192]{1,0:T(1,128)S(1)}, f32[1,192]{1,0:T(1,128)}, u32[]{:S(2)}) copy-start(f32[1,192]{1,0:T(1,128)} %get-tuple-element.431) | copy-start | bytes 2308 | tf_op jit(solution)/shard_map/while
  43.0 0.9 %copy-start.1 = (bf16[192,512]{1,0:T(8,128)(2,1)S(1)}, bf16[192,512]{1,0:T(8,128)(2,1)}, u32[]{:S(2)}) copy-start(bf16[192,512]{1,0:T(8,128)(2,1)} %fusion.104) | copy-start | bytes 589828 | tf_op jit(solution)/shard_map/while
  43.0 0.9 %copy-start.13 = (s32[4,2]{0,1:T(2,128)S(1)}, s32[4,2]{0,1:T(2,128)}, u32[]{:S(2)}) copy-start(s32[4,2]{0,1:T(2,128)} %get-tuple-element.553) | copy-start | bytes 100 | tf_op jit(solution)/shard_map/while
  43.0 0.9 %copy-start.17 = (s32[1,4]{1,0:T(1,128)S(1)}, s32[1,4]{1,0:T(1,128)}, u32[]{:S(2)}) copy-start(s32[1,4]{1,0:T(1,128)} %get-tuple-element.592) | copy-start | bytes 52 | tf_op jit(solution)/shard_map/while
  43.2 0.7 copy-start.9
  43.2 0.7 copy-start.3
  43.2 0.7 copy-start.15
  44.0 7.6 %collective-permute-start = (bf16[192,512]{1,0:T(8,128)(2,1)S(1)}, bf16[192,512]{1,0:T(8,128)(2,1)S(1)}, u32[]{:S(2)}, u32[]{:S(2)}) collective-permute-start(bf16[192,512]{1,0:T(8,128)(2,1)S(1)} %broadcast_select_fusion.2), channel_id=1, source_target_pairs={{0,16},{1,17},{2,18},{3,19},{4,20},{5,21},{6,22},{7,23},{8,24},{9,... | collective-permute-start | bytes 589832 | tf_op jit(solution)/shard_map/while/body/eval_jaxpr/ppermute | solution.py:10
  45.3 6.3 %copy-start.7 = (s32[1024]{0:T(1024)}, s32[1024]{0:T(1024)S(1)}, u32[]{:S(2)}) copy-start(s32[1024]{0:T(1024)S(1)} %pad_clamp_fusion.4) | copy-start | bytes 12292 | tf_op jit(solution)/shard_map/while
  52.8 9.6 %all-to-all-start = ((bf16[192,4,128]{2,0,1:T(8,128)(2,1)}), bf16[192,4,128]{2,0,1:T(8,128)(2,1)S(1)}, u32[]{:S(2)}, u32[]{:S(2)}) async-start(bf16[192,4,128]{2,0,1:T(8,128)(2,1)} %bitcast.154), calls=%async_computation | async-start | bytes 393216 | tf_op jit(solution)/shard_map/while/body/eval_jaxpr/all_to_all | solution.py:43
  65.2 0.7 copy-start.6
  67.5 9.6 %all-to-all-start.1 = ((bf16[192,4,128]{2,0,1:T(8,128)(2,1)}), bf16[192,4,128]{2,0,1:T(8,128)(2,1)S(1)}, u32[]{:S(2)}, u32[]{:S(2)}) async-start(bf16[192,4,128]{2,0,1:T(8,128)(2,1)} %bitcast.157), calls=%async_computation.1 | async-start | bytes 393216 | tf_op jit(solution)/shard_map/while/body/eval_jaxpr/all_to_all | solution.py:43
  72.2 6.0 %copy-start.11 = (s32[4]{0:T(128)S(1)}, s32[4]{0:T(128)}, u32[]{:S(2)}) copy-start(s32[4]{0:T(128)} %get-tuple-element.480) | copy-start | bytes 52 | tf_op jit(solution)/shard_map/while
  79.9 1.5 %copy-start.5 = (f32[1,192]{1,0:T(1,128)S(1)}, f32[1,192]{1,0:T(1,128)}, u32[]{:S(2)}) copy-start(f32[1,192]{1,0:T(1,128)} %get-tuple-element.431) | copy-start | bytes 2308 | tf_op jit(solution)/shard_map/while
  82.2 0.9 %copy-start.1 = (bf16[192,512]{1,0:T(8,128)(2,1)S(1)}, bf16[192,512]{1,0:T(8,128)(2,1)}, u32[]{:S(2)}) copy-start(bf16[192,512]{1,0:T(8,128)(2,1)} %fusion.104) | copy-start | bytes 589828 | tf_op jit(solution)/shard_map/while
  82.3 0.9 %copy-start.13 = (s32[4,2]{0,1:T(2,128)S(1)}, s32[4,2]{0,1:T(2,128)}, u32[]{:S(2)}) copy-start(s32[4,2]{0,1:T(2,128)} %get-tuple-element.553) | copy-start | bytes 100 | tf_op jit(solution)/shard_map/while
  82.3 0.9 %copy-start.17 = (s32[1,4]{1,0:T(1,128)S(1)}, s32[1,4]{1,0:T(1,128)}, u32[]{:S(2)}) copy-start(s32[1,4]{1,0:T(1,128)} %get-tuple-element.592) | copy-start | bytes 52 | tf_op jit(solution)/shard_map/while
  82.5 0.7 copy-start.9
  82.5 0.7 copy-start.3
  82.5 0.7 copy-start.15
  83.2 0.7 copy-start
  (4 other events, 2.7 us)
where the time goes:
time: 85.3 us; the launch traced here: 84 us
  waiting for transfers between devices  31.1 us (36%)
  local copies, waits for them, and re-layouts  17.8 us (21%)
  starting transfers between devices  17.6 us (21%)
  matrix products  10.5 us (12%)
  other arithmetic  6.41 us (8%)
    all_to_all x4, waiting for transfers between devices, advance(): lax.all_to_all(outgoing, 'net', split_axis=1, concat_axis=1, tiled=True)  19 us
    all_to_all x4, starting transfers between devices, advance(): lax.all_to_all(outgoing, 'net', split_axis=1, concat_axis=1, tiled=True)  15 us
    ppermute x2, waiting for transfers between devices, from_behind(): return lax.ppermute(value, axis, pairs)  12 us
    gather x4, local copies, waits for them, and re-layouts, advance(): outgoing = state_tiles[:, send_rows, :]  5.24 us
    convert_element_type x4, other arithmetic, advance(): (summed.reshape(width_cols, state_count) + injection).astype(jnp.bfloat16)  4.65 us
    dot_general x4, matrix products, advance(): jnp.einsum('qab,cqb->cqa', step_iface, incoming, preferred_element_type=j...  4.49 us
    while x48, local copies, waits for them, and re-layouts  4.09 us
    dot_general x4, matrix products, advance(): jnp.einsum('cqa,qi->cia', coupled, receive_map, precision=highest)  4.05 us
  transfers between devices with their start and end apart: 6, of which 6 were waited for; matrix products, arithmetic and copies ran while one was open for 9% of the time, Pallas kernels for 0%

commit v1 on v0

v1 whole, which is shorter than its diff:
```python
import functools

import jax
import jax.numpy as jnp
from jax import lax
from jax.experimental import pallas as pl
from jax.experimental.pallas import tpu as pltpu
from jax.sharding import PartitionSpec as P

VMEM = pl.BlockSpec(memory_space=pltpu.VMEM)
SMEM = pl.BlockSpec(memory_space=pltpu.SMEM)
HBM = pl.BlockSpec(memory_space=pltpu.HBM)
ANY = pl.BlockSpec(memory_space=pl.ANY)
LIMIT = pltpu.CompilerParams(vmem_limit_bytes=16 * 1024 * 1024)
DMA = pltpu.SemaphoreType.DMA

STATE, LANE, BLOCK, PART, GAIN = 0, 1, 2, 3, 4


def times_transposed(rows, block):
    return lax.dot_general(rows, block, (((1,), (1,)), ((), ())), preferred_element_type=jnp.float32)


def injected(table, step, first_state, width):
    lane = lax.broadcasted_iota(jnp.int32, (table.shape[0], width), 1)
    hit = table[:, STATE : STATE + 1] == (lane + first_state).astype(jnp.float32)
    return jnp.where(hit, table[:, GAIN + step : GAIN + step + 1], 0.0)


def own_sum(i, state_ref, jac_ref, cols_ref, table, step):
    blocks, _, width = state_ref.shape
    first = (lax.axis_index("net") * blocks + i) * width
    total = injected(table, step, first, width)
    total += times_transposed(state_ref[i], jac_ref[i, 0])
    for k in range(1, jac_ref.shape[1]):
        total += times_transposed(state_ref[cols_ref[k - 1, i]], jac_ref[i, k])
    return total


def add_coupled(incoming, block, live, recv, z_ref):
    lane = lax.broadcasted_iota(jnp.int32, z_ref.shape[1:], 1)
    term = times_transposed(incoming, block)
    z_ref[recv] += jnp.where(lane < live, term, 0.0)


def kept(table, partition, send_ref, n):
    part, block = table[:, PART : PART + 1], table[:, BLOCK : BLOCK + 1]
    keep = part == partition.astype(jnp.float32)
    for q in range(n):
        same = block == send_ref[q, partition].astype(jnp.float32)
        keep = jnp.logical_or(keep, jnp.logical_and(part == float(q), same))
    return keep


def second_kernel(
    jac_hbm, iface_hbm, cols_ref, send_ref, recv_ref, live_ref, node_ref, gain_ref, table_ref, state_ref, *refs
):
    *outgoing, jac_ref, iface_ref, first_ref, z_ref, sems = refs
    n = lax.axis_size("net")
    me = lax.axis_index("net")
    blocks, cols, width = state_ref.shape
    loads = [
        pltpu.make_async_copy(jac_hbm.at[1], jac_ref, sems.at[0]),
        pltpu.make_async_copy(iface_hbm.at[1, 0], iface_ref, sems.at[1]),
    ]
    for load in loads:
        load.start()
    node = node_ref[...]
    block_of = node // width
    rows = [
        node,
        node - block_of * width,
        block_of % blocks,
        block_of // blocks,
    ]
    steps = gain_ref.shape[0]
    fill = -(GAIN + steps) % 8
    rows = [row.astype(jnp.float32) for row in rows] + [gain_ref[...], jnp.zeros((fill, cols), jnp.float32)]
    table_ref[...] = jnp.concatenate(rows, axis=0).T
    table = table_ref[...]
    for i in range(blocks):
        first_ref[i] = injected(table, 0, (me * blocks + i) * width, width).astype(first_ref.dtype)
    lane = lax.broadcasted_iota(jnp.int32, (cols, width), 1).astype(jnp.float32)
    shot = jnp.where(lane == table[:, LANE : LANE + 1], table[:, GAIN : GAIN + 1], 0.0)
    loads[0].wait()
    for i in range(blocks):
        z_ref[i] = own_sum(i, first_ref, jac_ref, cols_ref, table, 1)
    loads[1].wait()
    part, block = table[:, PART : PART + 1], table[:, BLOCK : BLOCK + 1]
    mine = jnp.logical_or(part != me.astype(jnp.float32), block == send_ref[0, me].astype(jnp.float32))
    shot = jnp.where(mine, shot, 0.0)
    for q in range(n):
        sent = jnp.where(part == float(q), shot, 0.0).astype(first_ref.dtype)
        add_coupled(sent, iface_ref[q], live_ref[0, q], recv_ref[0, q], z_ref)
    state_ref[...] = z_ref[...].astype(state_ref.dtype)
    for d in range(1, n):
        outgoing[d - 1][...] = state_ref[send_ref[0, lax.rem(me + d, n)]]


def first_store_kernel(
    steps, jac_ref, iface_ref, cols_ref, recv_ref, live_ref, every_ref, table_ref, *refs
):
    *states, out_ref, zero_ref, z_ref, made_ref, sems = refs
    n = lax.axis_size("net")

    @pl.when(lax.axis_index("tm") == 0)
    def _():
        table = table_ref[...]
        zero_ref[...] = jnp.zeros_like(zero_ref)
        for i in range(z_ref.shape[0]):
            z_ref[i] = own_sum(i, zero_ref, jac_ref.at[0], cols_ref, table, 0)
        for q in range(n):
            add_coupled(zero_ref[0], iface_ref[0, 0, q], live_ref[0, q], recv_ref[0, q], z_ref)
        made_ref[0] = z_ref[...].astype(made_ref.dtype)
        keep = kept(table, lax.axis_index("net"), every_ref, n)
        for i in range(z_ref.shape[0]):
            made_ref[1, i] = jnp.where(keep, states[0][i], jnp.zeros_like(states[0][i]))
        write([made_ref.at[0], made_ref.at[1], *states[1:]], out_ref, sems)


def write(states, out_ref, sems):
    copies = write_start(states, 0, out_ref, sems)
    for copy in copies:
        copy.wait()


def write_start(states, first, out_ref, sems):
    copies = []
    for s, state_ref in enumerate(states, first):
        width = state_ref.shape[2]
        for i in range(state_ref.shape[0]):
            copies.append(
                pltpu.make_async_copy(state_ref.at[i], out_ref.at[s, :, pl.ds(i * width, width)], sems.at[s, i])
            )
    for copy in copies:
        copy.start()
    return copies


def own_kernel(step, fix, state_ref, jac_ref, cols_ref, table_ref, every_ref, z_ref, *fixed):
    table = table_ref[...]
    if fix:
        keep = kept(table, lax.axis_index("net"), every_ref, lax.axis_size("net"))
        for i in range(state_ref.shape[0]):
            fixed[0][i] = jnp.where(keep, state_ref[i], jnp.zeros_like(state_ref[i]))
        state_ref = fixed[0]
    for i in range(state_ref.shape[0]):
        z_ref[i] = own_sum(i, state_ref, jac_ref.at[step], cols_ref, table, step)


def join_kernel(step, fix, stacked, send_out, section, store, *refs):
    n = lax.axis_size("net")
    me = lax.axis_index("net")
    z_ref, iface_ref, send_ref, recv_ref, live_ref, every_ref, table_ref, state_in_ref, *refs = refs
    if stacked:
        arrived, *refs = refs
    else:
        arrived, refs = refs[: n - 1], refs[n - 1 :]
    acc_ref = refs.pop()
    if store:
        before, refs = refs[:store], refs[store:]
        _, out_ref, sems = refs.pop(0), refs.pop(0), refs.pop()
        here = lax.axis_index("tm") == section

        @pl.when(here)
        def _():
            write_start(before, 0, out_ref, sems)

    state_ref, *outgoing = refs
    acc_ref[...] = z_ref[...]
    add_coupled(state_in_ref[send_ref[0, me]], iface_ref[step, 0, me], live_ref[0, me], recv_ref[0, me], acc_ref)
    for d in range(1, n):
        q = lax.rem(me - d + n, n)
        block = arrived[q] if stacked else arrived[d - 1][...]
        if fix:
            block = jnp.where(kept(table_ref[...], q, every_ref, n), block, jnp.zeros_like(block))
        add_coupled(block, iface_ref[step, 0, q], live_ref[0, q], recv_ref[0, q], acc_ref)
    state_ref[...] = acc_ref[...].astype(state_ref.dtype)
    if send_out == "stack":
        for q in range(n):
            outgoing[0][q] = state_ref[send_ref[0, q]]
    if send_out == "each":
        for d in range(1, n):
            outgoing[d - 1][...] = state_ref[send_ref[0, lax.rem(me + d, n)]]
    if store:

        @pl.when(here)
        def _():
            last = write_start([state_ref], store, out_ref, sems)
            for s, ref in enumerate(before):
                for i in range(ref.shape[0]):
                    width = ref.shape[2]
                    pltpu.make_async_copy(
                        ref.at[i], out_ref.at[s, :, pl.ds(i * width, width)], sems.at[s, i]
                    ).wait()
            for copy in last:
                copy.wait()


def local(jac, block_cols, iface_jac, iface_send, iface_recv, iface_live, ctrl_node, ctrl_gain):
    steps, blocks, kinds, width, _ = jac.shape
    cols = ctrl_node.shape[0]
    tm = lax.axis_size("tm")
    n = lax.axis_size("net")
    node = ctrl_node[None]
    near = block_cols.T
    bf16 = functools.partial(jax.ShapeDtypeStruct, dtype=jnp.bfloat16)
    f32 = functools.partial(jax.ShapeDtypeStruct, dtype=jnp.float32)
    whole, one, stack = bf16((blocks, cols, width)), bf16((cols, width)), bf16((n, cols, width))
    table_rows = GAIN + steps + -(GAIN + steps) % 8
    written = bf16((steps, cols, blocks * width))

    every = lax.all_gather(iface_send, "net", axis=0, tiled=True)

    table, state, *outgoing = pl.pallas_call(
        second_kernel,
        out_shape=[f32((cols, table_rows)), whole] + [one] * (n - 1),
        in_specs=[HBM, HBM, SMEM, SMEM, SMEM, SMEM, VMEM, VMEM],
        out_specs=[VMEM] * (n + 1),
        scratch_shapes=[
            pltpu.VMEM((blocks, kinds, width, width), jnp.bfloat16),
            pltpu.VMEM((n, width, width), jnp.bfloat16),
            pltpu.VMEM(whole.shape, jnp.bfloat16),
            pltpu.VMEM(whole.shape, jnp.float32),
            DMA((2,)),
        ],
        compiler_params=LIMIT,
    )(jac, iface_jac, near, iface_send, iface_recv, iface_live, node, ctrl_gain)

    def own(state, step, fix):
        result = pl.pallas_call(
            functools.partial(own_kernel, step, fix),
            out_shape=[f32(whole.shape)] + ([whole] if fix else []),
            in_specs=[VMEM, VMEM, SMEM, VMEM, SMEM],
            out_specs=[VMEM] * (2 if fix else 1),
            compiler_params=LIMIT,
        )(state, jac, near, table_here, every)
        return result if fix else (result[0], state)

    def join(z, step, fix, state, arrived, send_out, section, before=(), out=None):
        stacked = not isinstance(arrived, list)
        arrays = [z, iface_jac, iface_send, iface_recv, iface_live, every, table_here, state]
        specs = [VMEM, VMEM, SMEM, SMEM, SMEM, SMEM, VMEM, VMEM]
        arrays += [arrived] if stacked else arrived
        specs += [VMEM] * (1 if stacked else n - 1)
        shapes = []
        scratch = [pltpu.VMEM(whole.shape, jnp.float32)]
        aliases = {}
        out_specs = []
        if out is not None:
            arrays += [*before, out]
            specs += [VMEM] * len(before) + [ANY]
            aliases = {len(arrays) - 1: 0}
            shapes.append(written)
            out_specs.append(ANY)
            scratch.insert(0, DMA((steps, blocks)))
        if send_out == "none":
            scratch.insert(0, pltpu.VMEM(whole.shape, jnp.bfloat16))
        else:
            shapes.append(whole)
        shapes += {"stack": [stack], "each": [one] * (n - 1), "none": []}[send_out]
        out_specs += [VMEM] * (len(shapes) - len(out_specs))
        return pl.pallas_call(
            functools.partial(join_kernel, step, fix, stacked, send_out, section, len(before)),
            out_shape=shapes,
            in_specs=specs,
            out_specs=out_specs,
            input_output_aliases=aliases,
            scratch_shapes=scratch,
            compiler_params=LIMIT,
        )(*arrays)

    def hand_over(blocks_to_send, section):
        return [
            lax.ppermute(
                block,
                ("tm", "net"),
                [((section - 1) * n + q, section * n + (q + d) % n) for q in range(n)],
            )
            for d, block in enumerate(blocks_to_send)
        ]

    fix = True
    table_here = table
    states = [state]
    out = None
    for r in range(tm):
        if r > 0:
            state, *arrived = hand_over([state, *outgoing], r)
            if out is None:
                out = pl.pallas_call(
                    functools.partial(first_store_kernel, steps),
                    out_shape=written,
                    in_specs=[VMEM, VMEM, SMEM, SMEM, SMEM, SMEM, VMEM] + [VMEM] * len(states),
                    out_specs=ANY,
                    scratch_shapes=[
                        pltpu.VMEM(whole.shape, jnp.bfloat16),
                        pltpu.VMEM(whole.shape, jnp.float32),
                        pltpu.VMEM((2, *whole.shape), jnp.bfloat16),
                        DMA((steps, blocks)),
                    ],
                    compiler_params=LIMIT,
                )(jac, iface_jac, near, iface_recv, iface_live, every, table, *states)
            states = []
        for s in range(2 if r == 0 else 0, steps):
            if s > 0:
                arrived = lax.all_to_all(outgoing, "net", split_axis=0, concat_axis=0, tiled=True)
            z, state = own(state, s, fix)
            end = s == steps - 1
            send_out = "stack" if not end else "each" if r < tm - 1 else "none"
            if end and r > 0:
                out, *rest = join(z, s, fix, state, arrived, send_out, r, states, out)
                state, *outgoing = rest or [None]
            else:
                state, *outgoing = join(z, s, fix, state, arrived, send_out, r)
            if send_out == "stack":
                outgoing = outgoing[0]
            fix = False
            states.append(state)
    return out


def solution(mesh):
    return jax.shard_map(
        local,
        mesh=mesh,
        in_specs=(
            P("tm", "net", None, None, None),
            P("net", None),
            P("tm", "net", None, None, None),
            P("net", None),
            P("net", None),
            P("net", None),
            P("cols"),
            P("tm", "cols"),
        ),
        out_specs=P("tm", "cols", "net"),
        check_vma=False,
    )
```

time: 85.3 us -> 39.7 us (0.47)
  the two profiles are of different devices: /device:TPU:4 before, /device:TPU:0 now
where the time goes in v1:
time: 39.7 us; the launch traced here: 39.4 us
  starting transfers between devices  15.2 us (38%)
  Pallas kernels  9.22 us (23%)
  blocking collectives  8.07 us (20%)
  local copies, waits for them, and re-layouts  3.49 us (9%)
  waiting for transfers between devices  3.29 us (8%)
    ppermute x4, starting transfers between devices, hand_over(): lax.ppermute(block, ('tm', 'net'), [((section - 1) * n + q, section * n +...  11.8 us
    all_gather x1, blocking collectives, local(): every = lax.all_gather(iface_send, 'net', axis=0, tiled=True)  8.07 us
    unnamed x20, local copies, waits for them, and re-layouts  3.49 us
    all_to_all x1, starting transfers between devices, local(): lax.all_to_all(outgoing, 'net', split_axis=0, concat_axis=0, tiled=True)  3.36 us
    all_to_all x1, waiting for transfers between devices, local(): lax.all_to_all(outgoing, 'net', split_axis=0, concat_axis=0, tiled=True)  3.28 us
    pallas_call x2, Pallas kernels, join(): pl.pallas_call(functools.partial(join_kernel, step, fix, stacked, send_ou...  3.06 us
    pallas_call x2, Pallas kernels, own(): pl.pallas_call(functools.partial(own_kernel, step, fix), out_shape=[f32(w...  2.13 us
    pallas_call x1, Pallas kernels, local(): pl.pallas_call(second_kernel, out_shape=[f32((cols, table_rows)), whole]...  2.08 us
  transfers between devices with their start and end apart: 5, of which 1 were waited for; matrix products, arithmetic and copies ran while one was open for 0% of the time, Pallas kernels for 10%

profile of v1, /device:TPU:0, one launch (start us, length us, event | category | flops | bytes accessed | tf_op | source)
XLA Modules:
  0.0 39.4 jit_solution(1262190040964936721)
XLA Ops:
  0.0 0.0 copy-start.6
  0.0 0.0 copy-start.7
  0.0 0.0 copy-start.9
  0.0 0.0 copy-start.4
  0.0 0.6 %copy-done.6 = s32[1,4]{1,0:T(1,128)S(1)} copy-done((s32[1,4]{1,0:T(1,128)S(1)}, s32[1,4]{1,0:T(1,128)}, u32[]{:S(2)}) %copy-start.6) | copy-done | bytes 40
  0.7 0.0 copy-done.7
  0.7 0.0 copy-done.9
  0.7 0.0 copy-done.4
  0.7 0.0 copy-done.5
  0.7 1.1 %copy-done = bf16[2,4,3,128,128]{4,3,2,1,0:T(8,128)(2,1)S(1)} copy-done((bf16[2,4,3,128,128]{4,3,2,1,0:T(8,128)(2,1)S(1)}, bf16[2,4,3,128,128]{4,3,2,1,0:T(8,128)(2,1)}, u32[]{:S(2)}) %copy-start) | copy-done | bytes 786456
  1.9 0.9 %copy-done.2 = bf16[2,1,4,128,128]{4,3,2,1,0:T(8,128)(2,1)S(1)} copy-done((bf16[2,1,4,128,128]{4,3,2,1,0:T(8,128)(2,1)S(1)}, bf16[2,1,4,128,128]{4,3,2,1,0:T(8,128)(2,1)}, u32[]{:S(2)}) %copy-start.2) | copy-done | bytes 262168
  2.8 0.7 %copy-done.8 = f32[2,192]{1,0:T(2,128)S(1)} copy-done((f32[2,192]{1,0:T(2,128)S(1)}, f32[2,192]{1,0:T(2,128)}, u32[]{:S(2)}) %copy-start.8) | copy-done | bytes 1560
  3.5 2.1 %shard_map.82 = (f32[192,8]{1,0:T(8,128)S(1)}, bf16[4,192,128]{2,1,0:T(8,128)(2,1)S(1)}, bf16[192,128]{1,0:T(8,128)(2,1)S(1)}, bf16[192,128]{1,0:T(8,128)(2,1)S(1)}, bf16[192,128]{1,0:T(8,128)(2,1)S(1)}) custom-call(bf16[2,4,3,128,128]{4,3,2,1,0:T(8,128)(2,1)S(1)} %copy-done, bf16[2,1,4,128,128]{4,3,2,1,0:T(8,128)(2,1)S(1)} %copy-done.2, ...), custom_call_target="tpu_custom_call" | custom-call | tf_op jit(solution)/shard_map/pallas_call | solution.py:215
  5.6 4.9 %collective-permute-start = (bf16[4,192,128]{2,1,0:T(8,128)(2,1)S(1)}, bf16[4,192,128]{2,1,0:T(8,128)(2,1)S(1)}, u32[]{:S(2)}, u32[]{:S(2)}) collective-permute-start(bf16[4,192,128]{2,1,0:T(8,128)(2,1)S(1)} %get-tuple-element.14.refs_0_), channel_id=1, source_target_pairs={{0,16},{4,20},{8,24},{12,28},{1,17},{5,21},{9,25},{13,29},{2,18},{... | collective-permute-start | bytes 589832 | tf_op jit(solution)/shard_map/ppermute | solution.py:275
  10.5 2.3 %collective-permute-start.1 = (bf16[192,128]{1,0:T(8,128)(2,1)S(1)}, bf16[192,128]{1,0:T(8,128)(2,1)S(1)}, u32[]{:S(2)}, u32[]{:S(2)}) collective-permute-start(bf16[192,128]{1,0:T(8,128)(2,1)S(1)} %get-tuple-element.18), channel_id=1, source_target_pairs={{0,20},{4,24},{8,28},{12,16},{1,21},{5,25},{9,29},{13,17},{2,22},{... | collective-permute-start | bytes 147464 | tf_op jit(solution)/shard_map/ppermute | solution.py:275
  12.8 2.3 %collective-permute-start.2 = (bf16[192,128]{1,0:T(8,128)(2,1)S(1)}, bf16[192,128]{1,0:T(8,128)(2,1)S(1)}, u32[]{:S(2)}, u32[]{:S(2)}) collective-permute-start(bf16[192,128]{1,0:T(8,128)(2,1)S(1)} %get-tuple-element.19), channel_id=1, source_target_pairs={{0,24},{4,28},{8,16},{12,20},{1,25},{5,29},{9,17},{13,21},{2,26},{... | collective-permute-start | bytes 147464 | tf_op jit(solution)/shard_map/ppermute | solution.py:275
  15.1 2.3 %collective-permute-start.3 = (bf16[192,128]{1,0:T(8,128)(2,1)S(1)}, bf16[192,128]{1,0:T(8,128)(2,1)S(1)}, u32[]{:S(2)}, u32[]{:S(2)}) collective-permute-start(bf16[192,128]{1,0:T(8,128)(2,1)S(1)} %get-tuple-element.20), channel_id=1, source_target_pairs={{0,28},{4,16},{8,20},{12,24},{1,29},{5,17},{9,21},{13,25},{2,30},{... | collective-permute-start | bytes 147464 | tf_op jit(solution)/shard_map/ppermute | solution.py:275
  17.4 8.1 %all-gather = s32[4,1,4]{2,1,0:T(1,128)S(1)} all-gather(s32[1,1,4]{2,1,0:T(1,128)S(1)} %bitcast.13), channel_id=1, replica_groups=mesh['tm'=2,'net'=4,'cols'=4] {'net'}, dimensions={0}, use_global_device_ids=true | all-gather | bytes 80 | tf_op jit(solution)/shard_map/all_gather | solution.py:213
  25.5 0.0 collective-permute-done.state_ref
  25.5 1.2 %shard_map.83 = (f32[4,192,128]{2,1,0:T(8,128)S(1)}, bf16[4,192,128]{2,1,0:T(8,128)(2,1)S(1)}) custom-call(bf16[4,192,128]{2,1,0:T(8,128)(2,1)S(1)} %collective-permute-done.state_ref, bf16[2,4,3,128,128]{4,3,2,1,0:T(8,128)(2,1)S(1)} %copy-done, s32[2,4]{1,0:T(2,128)S(1)} %bitcast.10, f32[192,8]{1,0:T(8,128)S(1)} %get-tuple-element.15.table_ref.refs_6_, ...), custom_call_target="tpu_custom_call" | custom-call | tf_op jit(solution)/shard_map/pallas_call | solution.py:231
  26.7 0.0 copy-start.1
  26.7 0.0 collective-permute-done.1.refs_8_
  26.7 0.0 collective-permute-done.2.refs_9_
  26.7 0.0 collective-permute-done.3.refs_10_
  26.7 0.0 copy-done.3
  26.7 2.1 %shard_map.84 = (bf16[4,192,128]{2,1,0:T(8,128)(2,1)S(1)}, bf16[4,192,128]{2,1,0:T(8,128)(2,1)}) custom-call(f32[4,192,128]{2,1,0:T(8,128)S(1)} %get-tuple-element.16.refs_0_, bf16[2,1,4,128,128]{4,3,2,1,0:T(8,128)(2,1)S(1)} %copy-done.3, s32[1,4]{1,0:T(1,128)S(1)} %copy-done.7, s32[1,4]{1,0:T(1,128)S(1)} %copy-done.5, s32[1,4]{1,0:T(1,128)S(1)} %copy-done.6, ...), custom_call_target="tpu_custom_call" | custom-call | tf_op jit(solution)/shard_map/pallas_call | solution.py:263
  28.8 3.4 %all-to-all-start = ((bf16[4,192,128]{2,1,0:T(8,128)(2,1)}), bf16[4,192,128]{2,1,0:T(8,128)(2,1)S(1)}, u32[]{:S(2)}, u32[]{:S(2)}) async-start(bf16[4,192,128]{2,1,0:T(8,128)(2,1)} %get-tuple-element.22), calls=%async_computation | async-start | bytes 393216 | tf_op jit(solution)/shard_map/all_to_all | solution.py:307
  32.2 0.0 copy-done.1
  32.2 2.0 %shard_map.86.refs_10_ = bf16[2,192,512]{2,1,0:T(8,128)(2,1)} custom-call(bf16[2,4,3,128,128]{4,3,2,1,0:T(8,128)(2,1)S(1)} %copy-done.1, bf16[2,1,4,128,128]{4,3,2,1,0:T(8,128)(2,1)S(1)} %copy-done.3, s32[2,4]{1,0:T(2,128)S(1)} %bitcast.11, s32[1,4]{1,0:T(1,128)S(1)} %copy-done.5, s32[1,4]{1,0:T(1,128)S(1)} %copy-done.6, s32[4,4]{1,0:T(4,128)S(1)} %bitcast.6, ...), custom_call_target="tpu_custom_call" | custom-call | tf_op jit(solution)/shard_map/pallas_call | solution.py:291
  34.2 1.0 %shard_map.85.refs_0_ = f32[4,192,128]{2,1,0:T(8,128)S(1)} custom-call(bf16[4,192,128]{2,1,0:T(8,128)(2,1)S(1)} %get-tuple-element.21.state_ref.refs_7_.refs_9_, bf16[2,4,3,128,128]{4,3,2,1,0:T(8,128)(2,1)S(1)} %copy-done.1, s32[2,4]{1,0:T(2,128)S(1)} %bitcast.12, f32[192,8]{1,0:T(8,128)S(1)} %get-tuple-element.15.table_ref.refs_6_, s32[4,4]{1,0:T(4,128)S(1)} %bitcast.7), custom_call_target="tpu_custom_call" | custom-call | tf_op jit(solution)/shard_map/pallas_call | solution.py:231
  35.1 3.3 %all-to-all-done.refs_8_ = bf16[4,192,128]{2,1,0:T(8,128)(2,1)S(1)} async-done(((bf16[4,192,128]{2,1,0:T(8,128)(2,1)}), bf16[4,192,128]{2,1,0:T(8,128)(2,1)S(1)}, u32[]{:S(2)}, u32[]{:S(2)}) %all-to-all-start) | async-done | bytes 196640 | tf_op jit(solution)/shard_map/all_to_all | solution.py:307
  38.4 0.9 %shard_map.87 = bf16[2,192,512]{2,1,0:T(8,128)(2,1)} custom-call(f32[4,192,128]{2,1,0:T(8,128)S(1)} %shard_map.85.refs_0_, bf16[2,1,4,128,128]{4,3,2,1,0:T(8,128)(2,1)S(1)} %copy-done.3, s32[1,4]{1,0:T(1,128)S(1)} %copy-done.7, s32[1,4]{1,0:T(1,128)S(1)} %copy-done.5, s32[1,4]{1,0:T(1,128)S(1)} %copy-done.6, ...), custom_call_target="tpu_custom_call", output_to_operand_aliasing={{}: (10, {})} | custom-call | tf_op jit(solution)/shard_map/pallas_call | solution.py:263
  (5 shorter events, 0.0 us)
Async XLA Ops:
  0.0 0.7 %copy-start.6 = (s32[1,4]{1,0:T(1,128)S(1)}, s32[1,4]{1,0:T(1,128)}, u32[]{:S(2)}) copy-start(s32[1,4]{1,0:T(1,128)} %refs_4_.3) | copy-start | bytes 52
  0.0 0.7 %copy-start.7 = (s32[1,4]{1,0:T(1,128)S(1)}, s32[1,4]{1,0:T(1,128)}, u32[]{:S(2)}) copy-start(s32[1,4]{1,0:T(1,128)} %refs_2_.3) | copy-start | bytes 52
  0.0 0.7 %copy-start.9 = (s32[192]{0:T(256)S(1)}, s32[192]{0:T(256)}, u32[]{:S(2)}) copy-start(s32[192]{0:T(256)} %param.14) | copy-start | bytes 2308
  0.0 0.7 %copy-start.4 = (s32[4,2]{0,1:T(2,128)S(1)}, s32[4,2]{0,1:T(2,128)}, u32[]{:S(2)}) copy-start(s32[4,2]{0,1:T(2,128)} %param.9) | copy-start | bytes 100
  0.0 0.7 %copy-start.5 = (s32[1,4]{1,0:T(1,128)S(1)}, s32[1,4]{1,0:T(1,128)}, u32[]{:S(2)}) copy-start(s32[1,4]{1,0:T(1,128)} %refs_3_.3) | copy-start | bytes 52
  0.7 1.1 %copy-start = (bf16[2,4,3,128,128]{4,3,2,1,0:T(8,128)(2,1)S(1)}, bf16[2,4,3,128,128]{4,3,2,1,0:T(8,128)(2,1)}, u32[]{:S(2)}) copy-start(bf16[2,4,3,128,128]{4,3,2,1,0:T(8,128)(2,1)} %jac_ref.5) | copy-start | bytes 2359300
  1.9 0.9 %copy-start.2 = (bf16[2,1,4,128,128]{4,3,2,1,0:T(8,128)(2,1)S(1)}, bf16[2,1,4,128,128]{4,3,2,1,0:T(8,128)(2,1)}, u32[]{:S(2)}) copy-start(bf16[2,1,4,128,128]{4,3,2,1,0:T(8,128)(2,1)} %refs_1_.3) | copy-start | bytes 786436
  2.8 0.7 %copy-start.8 = (f32[2,192]{1,0:T(2,128)S(1)}, f32[2,192]{1,0:T(2,128)}, u32[]{:S(2)}) copy-start(f32[2,192]{1,0:T(2,128)} %gain_ref.1) | copy-start | bytes 4612
  5.6 19.9 %collective-permute-start = (bf16[4,192,128]{2,1,0:T(8,128)(2,1)S(1)}, bf16[4,192,128]{2,1,0:T(8,128)(2,1)S(1)}, u32[]{:S(2)}, u32[]{:S(2)}) collective-permute-start(bf16[4,192,128]{2,1,0:T(8,128)(2,1)S(1)} %get-tuple-element.14.refs_0_), channel_id=1, source_target_pairs={{0,16},{4,20},{8,24},{12,28},{1,17},{5,21},{9,25},{13,29},{2,18},{... | collective-permute-start | bytes 589832 | tf_op jit(solution)/shard_map/ppermute | solution.py:275
  10.5 16.2 %collective-permute-start.1 = (bf16[192,128]{1,0:T(8,128)(2,1)S(1)}, bf16[192,128]{1,0:T(8,128)(2,1)S(1)}, u32[]{:S(2)}, u32[]{:S(2)}) collective-permute-start(bf16[192,128]{1,0:T(8,128)(2,1)S(1)} %get-tuple-element.18), channel_id=1, source_target_pairs={{0,20},{4,24},{8,28},{12,16},{1,21},{5,25},{9,29},{13,17},{2,22},{... | collective-permute-start | bytes 147464 | tf_op jit(solution)/shard_map/ppermute | solution.py:275
  12.8 13.9 %collective-permute-start.2 = (bf16[192,128]{1,0:T(8,128)(2,1)S(1)}, bf16[192,128]{1,0:T(8,128)(2,1)S(1)}, u32[]{:S(2)}, u32[]{:S(2)}) collective-permute-start(bf16[192,128]{1,0:T(8,128)(2,1)S(1)} %get-tuple-element.19), channel_id=1, source_target_pairs={{0,24},{4,28},{8,16},{12,20},{1,25},{5,29},{9,17},{13,21},{2,26},{... | collective-permute-start | bytes 147464 | tf_op jit(solution)/shard_map/ppermute | solution.py:275
  15.1 11.6 %collective-permute-start.3 = (bf16[192,128]{1,0:T(8,128)(2,1)S(1)}, bf16[192,128]{1,0:T(8,128)(2,1)S(1)}, u32[]{:S(2)}, u32[]{:S(2)}) collective-permute-start(bf16[192,128]{1,0:T(8,128)(2,1)S(1)} %get-tuple-element.20), channel_id=1, source_target_pairs={{0,28},{4,16},{8,20},{12,24},{1,29},{5,17},{9,21},{13,25},{2,30},{... | collective-permute-start | bytes 147464 | tf_op jit(solution)/shard_map/ppermute | solution.py:275
  25.5 1.2 %copy-start.3 = (bf16[2,1,4,128,128]{4,3,2,1,0:T(8,128)(2,1)S(1)}, bf16[2,1,4,128,128]{4,3,2,1,0:T(8,128)(2,1)}, u32[]{:S(2)}) copy-start(bf16[2,1,4,128,128]{4,3,2,1,0:T(8,128)(2,1)} %refs_1_.3) | copy-start | bytes 786436
  26.7 5.6 %copy-start.1 = (bf16[2,4,3,128,128]{4,3,2,1,0:T(8,128)(2,1)S(1)}, bf16[2,4,3,128,128]{4,3,2,1,0:T(8,128)(2,1)}, u32[]{:S(2)}) copy-start(bf16[2,4,3,128,128]{4,3,2,1,0:T(8,128)(2,1)} %jac_ref.5) | copy-start | bytes 2359300
  28.8 9.6 %all-to-all-start = ((bf16[4,192,128]{2,1,0:T(8,128)(2,1)}), bf16[4,192,128]{2,1,0:T(8,128)(2,1)S(1)}, u32[]{:S(2)}, u32[]{:S(2)}) async-start(bf16[4,192,128]{2,1,0:T(8,128)(2,1)} %get-tuple-element.22), calls=%async_computation | async-start | bytes 393216 | tf_op jit(solution)/shard_map/all_to_all | solution.py:307

commit v2 on v1

v2 whole, which is shorter than its diff:
```python
import functools

import jax
import jax.numpy as jnp
from jax import lax
from jax.experimental import pallas as pl
from jax.experimental.pallas import tpu as pltpu
from jax.sharding import PartitionSpec as P

VMEM = pl.BlockSpec(memory_space=pltpu.VMEM)
SMEM = pl.BlockSpec(memory_space=pltpu.SMEM)
HBM = pl.BlockSpec(memory_space=pltpu.HBM)
ANY = pl.BlockSpec(memory_space=pl.ANY)
LIMIT = pltpu.CompilerParams(vmem_limit_bytes=16 * 1024 * 1024)
LARGE = pltpu.CompilerParams(vmem_limit_bytes=60 * 1024 * 1024)
DMA = pltpu.SemaphoreType.DMA

STATE, LANE, BLOCK, PART, GAIN = 0, 1, 2, 3, 4
ROWS = 16


def times_transposed(rows, block):
    return lax.dot_general(rows, block, (((1,), (1,)), ((), ())), preferred_element_type=jnp.float32)


def injected(table, step, first_state, width):
    lane = lax.broadcasted_iota(jnp.int32, (table.shape[0], width), 1)
    hit = table[:, STATE : STATE + 1] == (lane + first_state).astype(jnp.float32)
    return jnp.where(hit, table[:, GAIN + step : GAIN + step + 1], 0.0)


def own_sum(i, state_ref, jac_ref, cols_ref, table, step):
    blocks, _, width = state_ref.shape
    first = (lax.axis_index("net") * blocks + i) * width
    total = injected(table, step, first, width)
    total += times_transposed(state_ref[i], jac_ref[i, 0])
    for k in range(1, jac_ref.shape[1]):
        total += times_transposed(state_ref[cols_ref[k - 1, i]], jac_ref[i, k])
    return total


def add_coupled(incoming, block, live, recv, z_ref):
    lane = lax.broadcasted_iota(jnp.int32, z_ref.shape[1:], 1)
    term = times_transposed(incoming, block)
    z_ref[recv] += jnp.where(lane < live, term, 0.0)


def table_row(send_ref, partition, width):
    n = lax.axis_size("net")
    lane = lax.broadcasted_iota(jnp.int32, (1, width), 1)
    row = jnp.zeros((1, width), jnp.float32)
    for e in range(n):
        row = jnp.where(lane == e, send_ref[0, lax.rem(partition - e + n, n)].astype(jnp.float32), row)
    return row


def kept(table, rows):
    n = lax.axis_size("net")
    me = lax.axis_index("net")
    part, block = table[:, PART : PART + 1], table[:, BLOCK : BLOCK + 1]
    back = me.astype(jnp.float32) - part
    back = jnp.where(back < 0.0, back + float(n), back)
    sent = jnp.broadcast_to(rows[0], (table.shape[0], rows[0].shape[1]))
    for d in range(1, n):
        sent = jnp.where(back == float(d), rows[d], sent)
    lane = lax.broadcasted_iota(jnp.int32, sent.shape, 1).astype(jnp.float32)
    return jnp.where(jnp.logical_or(back == lane, block == sent), 1.0, 0.0)


def second_kernel(
    jac_hbm, iface_hbm, cols_ref, send_ref, recv_ref, live_ref, node_ref, gain_ref, table_ref, state_ref, *refs
):
    *outgoing, jac_ref, iface_ref, first_ref, z_ref, sems = refs
    n = lax.axis_size("net")
    me = lax.axis_index("net")
    blocks, cols, width = state_ref.shape
    loads = [
        pltpu.make_async_copy(jac_hbm.at[1], jac_ref, sems.at[0]),
        pltpu.make_async_copy(iface_hbm.at[1, 0], iface_ref, sems.at[1]),
    ]
    for load in loads:
        load.start()
    node = node_ref[...]
    block_of = node // width
    rows = [
        node,
        node - block_of * width,
        block_of % blocks,
        block_of // blocks,
    ]
    steps = gain_ref.shape[0]
    fill = -(GAIN + steps) % 8
    rows = [row.astype(jnp.float32) for row in rows] + [gain_ref[...], jnp.zeros((fill, cols), jnp.float32)]
    table_ref[...] = jnp.concatenate(rows, axis=0).T
    table = table_ref[...]
    for i in range(blocks):
        first_ref[i] = injected(table, 0, (me * blocks + i) * width, width).astype(first_ref.dtype)
    lane = lax.broadcasted_iota(jnp.int32, (cols, width), 1).astype(jnp.float32)
    shot = jnp.where(lane == table[:, LANE : LANE + 1], table[:, GAIN : GAIN + 1], 0.0)
    loads[0].wait()
    for i in range(blocks):
        z_ref[i] = own_sum(i, first_ref, jac_ref, cols_ref, table, 1)
    loads[1].wait()
    part, block = table[:, PART : PART + 1], table[:, BLOCK : BLOCK + 1]
    mine = jnp.logical_or(part != me.astype(jnp.float32), block == send_ref[0, me].astype(jnp.float32))
    shot = jnp.where(mine, shot, 0.0)
    for q in range(n):
        sent = jnp.where(part == float(q), shot, 0.0).astype(first_ref.dtype)
        add_coupled(sent, iface_ref[q], live_ref[0, q], recv_ref[0, q], z_ref)
    state_ref[...] = z_ref[...].astype(state_ref.dtype)
    for d in range(1, n):
        target = lax.rem(me + d, n)
        outgoing[d - 1][pl.ds(0, cols)] = state_ref[send_ref[0, target]]
        row = table_row(send_ref, target, width).astype(state_ref.dtype)
        outgoing[d - 1][pl.ds(cols, ROWS)] = jnp.broadcast_to(row, (ROWS, width))


def write_start(states, first, out_ref, sems):
    copies = []
    for s, state_ref in enumerate(states, first):
        width = state_ref.shape[2]
        for i in range(state_ref.shape[0]):
            copies.append(
                pltpu.make_async_copy(state_ref.at[i], out_ref.at[s, :, pl.ds(i * width, width)], sems.at[s, i])
            )
    for copy in copies:
        copy.start()
    return copies


def own_kernel(step, state_ref, jac_ref, cols_ref, table_ref, z_ref):
    table = table_ref[...]
    for i in range(state_ref.shape[0]):
        z_ref[i] = own_sum(i, state_ref, jac_ref.at[step], cols_ref, table, step)


def first_states(states, jac_ref, iface_ref, cols_ref, send_ref, recv_ref, live_ref, table_ref, arrived, made_ref, z_ref):
    n = lax.axis_size("net")
    blocks, cols, width = z_ref.shape
    table = table_ref[...]
    made_ref[0] = jnp.zeros_like(made_ref[0])
    for i in range(blocks):
        z_ref[i] = own_sum(i, made_ref.at[0], jac_ref.at[0], cols_ref, table, 0)
    for q in range(n):
        add_coupled(made_ref[0, 0], iface_ref[0, 0, q], live_ref[0, q], recv_ref[0, q], z_ref)
    made_ref[0] = z_ref[...].astype(made_ref.dtype)
    me = lax.axis_index("net")
    rows = [table_row(send_ref, me, width)]
    for d in range(1, n):
        rows.append(arrived[lax.rem(me - d + n, n)][0:1].astype(jnp.float32))
    keep = kept(table, rows)[:, 0:1]
    for i in range(blocks):
        made_ref[1, i] = jnp.where(keep > 0.0, states[0][i], jnp.zeros_like(states[0][i]))
    return [made_ref.at[0], made_ref.at[1], *states[1:]]


def join_kernel(step, fix, stacked, send_out, section, firsts, store, *refs):
    n = lax.axis_size("net")
    me = lax.axis_index("net")
    tm = lax.axis_index("tm")
    z_ref, iface_ref, send_ref, recv_ref, live_ref, table_ref, state_in_ref, *refs = refs
    if stacked:
        arrived, *refs = refs
    else:
        arrived, refs = refs[: n - 1], refs[n - 1 :]
    acc_ref = refs.pop()
    blocks, cols, width = z_ref.shape
    before = []
    if store:
        sems = refs.pop()
        if firsts:
            made_ref = refs.pop()
            opening, refs = refs[:firsts], refs[firsts:]
            jac_ref, cols_ref = refs.pop(0), refs.pop(0)
        before, refs = refs[: store - 1], refs[store - 1 :]
        if not firsts:
            refs.pop(0)
        out_ref = refs.pop(0)
    state_ref, *outgoing = refs

    def join():
        if store:
            copies = write_start(before, 0, out_ref, sems)
        if fix:
            table = table_ref[...]
            rows = [table_row(send_ref, me, width)]
            rows += [arrived[d - 1][cols : cols + 1].astype(jnp.float32) for d in range(1, n)]
            keep = kept(table, rows)
            for i in range(blocks):
                acc_ref[i] = jnp.where(keep[:, 0:1] > 0.0, z_ref[i], 0.0)
        else:
            acc_ref[...] = z_ref[...]
        for d in range(n):
            q = lax.rem(me - d + n, n)
            if d == 0:
                block = state_in_ref[send_ref[0, me]]
            elif stacked:
                block = arrived[q]
            else:
                block = arrived[d - 1][pl.ds(0, cols)]
            if fix:
                block = jnp.where(keep[:, d : d + 1] > 0.0, block, jnp.zeros_like(block))
            add_coupled(block, iface_ref[step, 0, q], live_ref[0, q], recv_ref[0, q], acc_ref)
        state_ref[...] = acc_ref[...].astype(state_ref.dtype)
        if send_out == "stack":
            for q in range(n):
                outgoing[0][q] = state_ref[send_ref[0, q]]
        if send_out == "each":
            for d in range(1, n):
                outgoing[d - 1][...] = state_ref[send_ref[0, lax.rem(me + d, n)]]
        if store:
            copies += write_start([state_ref], store - 1, out_ref, sems)
            for copy in copies:
                copy.wait()

    if store:
        pl.when(tm == section)(join)
    else:
        join()
    if fix and send_out == "stack":

        @pl.when(tm == 0)
        def _():
            for q in range(n):
                row = table_row(send_ref, jnp.int32(q), width).astype(state_ref.dtype)
                outgoing[0][q, pl.ds(0, ROWS)] = jnp.broadcast_to(row, (ROWS, width))

    if firsts:

        @pl.when(tm == 0)
        def _():
            made = first_states(
                opening, jac_ref, iface_ref, cols_ref, send_ref, recv_ref, live_ref, table_ref, arrived, made_ref, acc_ref
            )
            for copy in write_start(made, 0, out_ref, sems):
                copy.wait()


def local(jac, block_cols, iface_jac, iface_send, iface_recv, iface_live, ctrl_node, ctrl_gain):
    steps, blocks, kinds, width, _ = jac.shape
    cols = ctrl_node.shape[0]
    tm = lax.axis_size("tm")
    n = lax.axis_size("net")
    node = ctrl_node[None]
    near = block_cols.T
    bf16 = functools.partial(jax.ShapeDtypeStruct, dtype=jnp.bfloat16)
    f32 = functools.partial(jax.ShapeDtypeStruct, dtype=jnp.float32)
    whole, one, stack = bf16((blocks, cols, width)), bf16((cols, width)), bf16((n, cols, width))
    table_rows = GAIN + steps + -(GAIN + steps) % 8
    written = bf16((steps, cols, blocks * width))

    table, state, *outgoing = pl.pallas_call(
        second_kernel,
        out_shape=[f32((cols, table_rows)), whole] + [bf16((cols + ROWS, width))] * (n - 1),
        in_specs=[ANY, ANY, SMEM, SMEM, SMEM, SMEM, VMEM, VMEM],
        out_specs=[VMEM] * (n + 1),
        scratch_shapes=[
            pltpu.VMEM((blocks, kinds, width, width), jnp.bfloat16),
            pltpu.VMEM((n, width, width), jnp.bfloat16),
            pltpu.VMEM(whole.shape, jnp.bfloat16),
            pltpu.VMEM(whole.shape, jnp.float32),
            DMA((2,)),
        ],
        compiler_params=LARGE,
    )(jac, iface_jac, near, iface_send, iface_recv, iface_live, node, ctrl_gain)

    def own(state, step):
        return pl.pallas_call(
            functools.partial(own_kernel, step),
            out_shape=f32(whole.shape),
            in_specs=[VMEM, VMEM, SMEM, VMEM],
            out_specs=VMEM,
            compiler_params=LIMIT,
        )(state, jac, near, table)

    def join(z, step, fix, state, arrived, send_out, section, opening=(), before=(), out=None, store=0):
        stacked = not isinstance(arrived, list)
        arrays = [z, iface_jac, iface_send, iface_recv, iface_live, table, state]
        specs = [VMEM, VMEM, SMEM, SMEM, SMEM, VMEM, VMEM]
        arrays += [arrived] if stacked else arrived
        specs += [VMEM] * (1 if stacked else n - 1)
        shapes = []
        scratch = [pltpu.VMEM(whole.shape, jnp.float32)]
        aliases = {}
        out_specs = []
        if store:
            if out is None:
                arrays += [*opening, jac, near]
                specs += [VMEM] * len(opening) + [VMEM, SMEM]
            arrays += before
            specs += [VMEM] * len(before)
            if out is not None:
                aliases = {len(arrays): 0}
                arrays.append(out)
                specs.append(ANY)
            shapes.append(written)
            out_specs.append(ANY)
            scratch.insert(0, DMA((steps, blocks)))
            if out is None:
                scratch.insert(0, pltpu.VMEM((2, *whole.shape), jnp.bfloat16))
        if send_out == "none":
            scratch.insert(0, pltpu.VMEM(whole.shape, jnp.bfloat16))
        else:
            shapes.append(whole)
        shapes += {"stack": [stack], "each": [one] * (n - 1), "none": []}[send_out]
        out_specs += [VMEM] * (len(shapes) - len(out_specs))
        firsts = len(opening) if store and out is None else 0
        return pl.pallas_call(
            functools.partial(join_kernel, step, fix, stacked, send_out, section, firsts, store),
            out_shape=shapes,
            in_specs=specs,
            out_specs=out_specs,
            input_output_aliases=aliases,
            scratch_shapes=scratch,
            compiler_params=LIMIT,
        )(*arrays)

    def hand_over(blocks_to_send, section):
        return [
            lax.ppermute(
                block,
                ("tm", "net"),
                [((section - 1) * n + q, section * n + (q + d) % n) for q in range(n)],
            )
            for d, block in enumerate(blocks_to_send)
        ]

    opening = [state]
    out = None
    for r in range(1, tm):
        state, *arrived = hand_over([state, *outgoing], r)
        before = []
        for s in range(steps):
            fix = r == 1 and s == 0
            if s > 0:
                arrived = lax.all_to_all(outgoing, "net", split_axis=0, concat_axis=0, tiled=True)
            z = own(state, s)
            if s < steps - 1:
                state, outgoing = join(z, s, fix, state, arrived, "stack", r)
                before.append(state)
            elif r < tm - 1:
                out, state, *outgoing = join(z, s, fix, state, arrived, "each", r, opening, before, out, steps)
            else:
                (out,) = join(z, s, fix, state, arrived, "none", r, opening, before, out, steps)
    return out


def solution(mesh):
    return jax.shard_map(
        local,
        mesh=mesh,
        in_specs=(
            P("tm", "net", None, None, None),
            P("net", None),
            P("tm", "net", None, None, None),
            P("net", None),
            P("net", None),
            P("net", None),
            P("cols"),
            P("tm", "cols"),
        ),
        out_specs=P("tm", "cols", "net"),
        check_vma=False,
    )
```

time: 39.7 us -> 32.2 us (0.81)
  blocking collectives: 8.07 us -> 0 us
  local copies, waits for them, and re-layouts: 3.49 us -> 0.92 us
  waiting for transfers between devices: 3.29 us -> 5.5 us
  starting transfers between devices: 15.2 us -> 16.4 us
    all_gather x1 -> x0, blocking collectives: 8.07 us -> none  [local(): every = lax.all_gather(iface_send, 'net', axis=0, tiled=True)]
    unnamed x20 -> x18, local copies, waits for them, and re-layouts: 3.49 us -> 0.92 us
    pallas_call x3 -> x2, Pallas kernels: 4.08 us -> 1.87 us  [own(): pl.pallas_call(functools.partial(own_kernel, step), out_shape=f32(whole.s...]
    all_to_all x1, waiting for transfers between devices: 3.28 us -> 5.32 us  [local(): lax.all_to_all(outgoing, 'net', split_axis=0, concat_axis=0, tiled=True)]
    pallas_call x1, Pallas kernels: 2.08 us -> 3.34 us  [local(): pl.pallas_call(second_kernel, out_shape=[f32((cols, table_rows)), whole]...]
    all_to_all x1, starting transfers between devices: 3.36 us -> 4.62 us  [local(): lax.all_to_all(outgoing, 'net', split_axis=0, concat_axis=0, tiled=True)]
    pallas_call x2, Pallas kernels: 3.06 us -> 3.69 us  [join(): pl.pallas_call(functools.partial(join_kernel, step, fix, stacked, send_ou...]
  transfers between devices with their start and end apart: 5 -> 5, of which waited for: 1 -> 2; matrix products, arithmetic and copies ran while one was open for 0% -> 0% of each run, Pallas kernels for 10% -> 6%
where the time goes in v2:
time: 32.2 us; the launch traced here: 31.9 us
  starting transfers between devices  16.4 us (51%)
  Pallas kernels  8.91 us (28%)
  waiting for transfers between devices  5.5 us (17%)
  local copies, waits for them, and re-layouts  0.92 us (3%)
    ppermute x4, starting transfers between devices, hand_over(): lax.ppermute(block, ('tm', 'net'), [((section - 1) * n + q, section * n +...  11.8 us
    all_to_all x1, waiting for transfers between devices, local(): lax.all_to_all(outgoing, 'net', split_axis=0, concat_axis=0, tiled=True)  5.32 us
    all_to_all x1, starting transfers between devices, local(): lax.all_to_all(outgoing, 'net', split_axis=0, concat_axis=0, tiled=True)  4.62 us
    pallas_call x2, Pallas kernels, join(): pl.pallas_call(functools.partial(join_kernel, step, fix, stacked, send_ou...  3.69 us
    pallas_call x1, Pallas kernels, local(): pl.pallas_call(second_kernel, out_shape=[f32((cols, table_rows)), whole]...  3.34 us
    pallas_call x2, Pallas kernels, own(): pl.pallas_call(functools.partial(own_kernel, step), out_shape=f32(whole.s...  1.87 us
    unnamed x18, local copies, waits for them, and re-layouts  0.92 us
  transfers between devices with their start and end apart: 5, of which 2 were waited for; matrix products, arithmetic and copies ran while one was open for 0% of the time, Pallas kernels for 6%

profile of v2, /device:TPU:0, one launch (start us, length us, event | category | flops | bytes accessed | tf_op | source)
XLA Modules:
  0.0 31.9 jit_solution(12343301030758034895)
XLA Ops:
  0.0 0.0 copy-start
  0.0 3.3 %shard_map.82 = (f32[192,8]{1,0:T(8,128)}, bf16[4,192,128]{2,1,0:T(8,128)(2,1)}, bf16[208,128]{1,0:T(8,128)(2,1)}, bf16[208,128]{1,0:T(8,128)(2,1)}, bf16[208,128]{1,0:T(8,128)(2,1)}) custom-call(bf16[2,4,3,128,128]{4,3,2,1,0:T(8,128)(2,1)} %refs_9_.1, bf16[2,1,4,128,128]{4,3,2,1,0:T(8,128)(2,1)} %refs_1_.3, s32[2,4]{1,0:T(2,128)} %bitcast.2, ...), custom_call_target="tpu_custom_call" | custom-call | tf_op jit(solution)/shard_map/pallas_call | solution.py:252
  3.4 4.9 %collective-permute-start = (bf16[4,192,128]{2,1,0:T(8,128)(2,1)}, bf16[4,192,128]{2,1,0:T(8,128)(2,1)S(1)}, u32[]{:S(2)}, u32[]{:S(2)}) collective-permute-start(bf16[4,192,128]{2,1,0:T(8,128)(2,1)} %get-tuple-element.12.refs_8_), channel_id=1, source_target_pairs={{0,16},{4,20},{8,24},{12,28},{1,17},{5,21},{9,25},{13,29},{2,18},{... | collective-permute-start | bytes 589832 | tf_op jit(solution)/shard_map/ppermute | solution.py:320
  8.2 2.3 %collective-permute-start.1 = (bf16[208,128]{1,0:T(8,128)(2,1)}, bf16[208,128]{1,0:T(8,128)(2,1)S(1)}, u32[]{:S(2)}, u32[]{:S(2)}) collective-permute-start(bf16[208,128]{1,0:T(8,128)(2,1)} %get-tuple-element.14), channel_id=1, source_target_pairs={{0,20},{4,24},{8,28},{12,16},{1,21},{5,25},{9,29},{13,17},{2,22},{... | collective-permute-start | bytes 159752 | tf_op jit(solution)/shard_map/ppermute | solution.py:320
  10.6 2.3 %collective-permute-start.2 = (bf16[208,128]{1,0:T(8,128)(2,1)}, bf16[208,128]{1,0:T(8,128)(2,1)S(1)}, u32[]{:S(2)}, u32[]{:S(2)}) collective-permute-start(bf16[208,128]{1,0:T(8,128)(2,1)} %get-tuple-element.15), channel_id=1, source_target_pairs={{0,24},{4,28},{8,16},{12,20},{1,25},{5,29},{9,17},{13,21},{2,26},{... | collective-permute-start | bytes 159752 | tf_op jit(solution)/shard_map/ppermute | solution.py:320
  12.9 0.0 copy-start.5
  12.9 2.3 %collective-permute-start.3 = (bf16[208,128]{1,0:T(8,128)(2,1)}, bf16[208,128]{1,0:T(8,128)(2,1)S(1)}, u32[]{:S(2)}, u32[]{:S(2)}) collective-permute-start(bf16[208,128]{1,0:T(8,128)(2,1)} %get-tuple-element.16), channel_id=1, source_target_pairs={{0,28},{4,16},{8,20},{12,24},{1,29},{5,17},{9,21},{13,25},{2,30},{... | collective-permute-start | bytes 159752 | tf_op jit(solution)/shard_map/ppermute | solution.py:320
  15.2 0.0 collective-permute-done.state_ref.refs_6_
  15.2 0.0 copy-done
  15.2 0.0 copy-done.5
  15.2 0.0 copy-start.2
  15.2 0.9 %copy-done.2 = f32[192,8]{1,0:T(8,128)S(1)} copy-done((f32[192,8]{1,0:T(8,128)S(1)}, f32[192,8]{1,0:T(8,128)}, u32[]{:S(2)}) %copy-start.2) | copy-done | bytes 6168
  16.1 0.0 copy-start.3
  16.1 0.0 copy-start.6
  16.1 0.0 copy-start.7
  16.1 0.0 copy-start.8
  16.1 0.9 %shard_map.83.refs_0_ = f32[4,192,128]{2,1,0:T(8,128)S(1)} custom-call(bf16[4,192,128]{2,1,0:T(8,128)(2,1)S(1)} %collective-permute-done.state_ref.refs_6_, bf16[2,4,3,128,128]{4,3,2,1,0:T(8,128)(2,1)S(1)} %copy-done, s32[2,4]{1,0:T(2,128)S(1)} %bitcast.3, f32[192,8]{1,0:T(8,128)S(1)} %copy-done.2), custom_call_target="tpu_custom_call" | custom-call | tf_op jit(solution)/shard_map/pallas_call | solution.py:268
  17.1 0.0 collective-permute-done.1.refs_7_
  17.1 0.0 collective-permute-done.2.refs_8_
  17.1 0.2 collective-permute-done.3.refs_9_
  17.3 0.0 copy-done.1
  17.3 0.0 copy-done.3
  17.3 0.0 copy-done.6
  17.3 0.0 copy-done.7
  17.3 0.0 copy-done.8
  17.3 1.8 %shard_map.84 = (bf16[4,192,128]{2,1,0:T(8,128)(2,1)S(1)}, bf16[4,192,128]{2,1,0:T(8,128)(2,1)}) custom-call(f32[4,192,128]{2,1,0:T(8,128)S(1)} %shard_map.83.refs_0_, bf16[2,1,4,128,128]{4,3,2,1,0:T(8,128)(2,1)S(1)} %copy-done.1, s32[1,4]{1,0:T(1,128)S(1)} %copy-done.6, s32[1,4]{1,0:T(1,128)S(1)} %copy-done.7, s32[1,4]{1,0:T(1,128)S(1)} %copy-done.8, ...), custom_call_target="tpu_custom_call" | custom-call | tf_op jit(solution)/shard_map/pallas_call | solution.py:308
  19.1 4.6 %all-to-all-start = ((bf16[4,192,128]{2,1,0:T(8,128)(2,1)}), bf16[4,192,128]{2,1,0:T(8,128)(2,1)S(1)}, u32[]{:S(2)}, u32[]{:S(2)}) async-start(bf16[4,192,128]{2,1,0:T(8,128)(2,1)} %get-tuple-element.18), calls=%async_computation | async-start | bytes 393216 | tf_op jit(solution)/shard_map/all_to_all | solution.py:336
  23.7 0.0 copy-start.4
  23.7 0.9 %shard_map.85.refs_0_ = f32[4,192,128]{2,1,0:T(8,128)S(1)} custom-call(bf16[4,192,128]{2,1,0:T(8,128)(2,1)S(1)} %get-tuple-element.17.state_ref.refs_6_.refs_11_, bf16[2,4,3,128,128]{4,3,2,1,0:T(8,128)(2,1)S(1)} %copy-done, s32[2,4]{1,0:T(2,128)S(1)} %bitcast.4, f32[192,8]{1,0:T(8,128)S(1)} %copy-done.3), custom_call_target="tpu_custom_call" | custom-call | tf_op jit(solution)/shard_map/pallas_call | solution.py:268
  24.6 5.3 %all-to-all-done.refs_7_ = bf16[4,192,128]{2,1,0:T(8,128)(2,1)S(1)} async-done(((bf16[4,192,128]{2,1,0:T(8,128)(2,1)}), bf16[4,192,128]{2,1,0:T(8,128)(2,1)S(1)}, u32[]{:S(2)}, u32[]{:S(2)}) %all-to-all-start) | async-done | bytes 196640 | tf_op jit(solution)/shard_map/all_to_all | solution.py:336
  30.0 0.0 copy-done.4
  30.0 1.9 %shard_map.86 = bf16[2,192,512]{2,1,0:T(8,128)(2,1)} custom-call(f32[4,192,128]{2,1,0:T(8,128)S(1)} %shard_map.85.refs_0_, bf16[2,1,4,128,128]{4,3,2,1,0:T(8,128)(2,1)S(1)} %copy-done.1, s32[1,4]{1,0:T(1,128)S(1)} %copy-done.6, s32[1,4]{1,0:T(1,128)S(1)} %copy-done.7, s32[1,4]{1,0:T(1,128)S(1)} %copy-done.8, f32[192,8]{1,0:T(8,128)S(1)} %copy-done.3, ...), custom_call_target="tpu_custom_call" | custom-call | tf_op jit(solution)/shard_map/pallas_call | solution.py:308
  (1 shorter events, 0.0 us)
Async XLA Ops:
  0.0 15.2 %copy-start = (bf16[2,4,3,128,128]{4,3,2,1,0:T(8,128)(2,1)S(1)}, bf16[2,4,3,128,128]{4,3,2,1,0:T(8,128)(2,1)}, u32[]{:S(2)}) copy-start(bf16[2,4,3,128,128]{4,3,2,1,0:T(8,128)(2,1)} %refs_9_.1) | copy-start | bytes 2359300
  3.4 11.8 %collective-permute-start = (bf16[4,192,128]{2,1,0:T(8,128)(2,1)}, bf16[4,192,128]{2,1,0:T(8,128)(2,1)S(1)}, u32[]{:S(2)}, u32[]{:S(2)}) collective-permute-start(bf16[4,192,128]{2,1,0:T(8,128)(2,1)} %get-tuple-element.12.refs_8_), channel_id=1, source_target_pairs={{0,16},{4,20},{8,24},{12,28},{1,17},{5,21},{9,25},{13,29},{2,18},{... | collective-permute-start | bytes 589832 | tf_op jit(solution)/shard_map/ppermute | solution.py:320
  8.2 8.8 %collective-permute-start.1 = (bf16[208,128]{1,0:T(8,128)(2,1)}, bf16[208,128]{1,0:T(8,128)(2,1)S(1)}, u32[]{:S(2)}, u32[]{:S(2)}) collective-permute-start(bf16[208,128]{1,0:T(8,128)(2,1)} %get-tuple-element.14), channel_id=1, source_target_pairs={{0,20},{4,24},{8,28},{12,16},{1,21},{5,25},{9,29},{13,17},{2,22},{... | collective-permute-start | bytes 159752 | tf_op jit(solution)/shard_map/ppermute | solution.py:320
  10.6 6.5 %collective-permute-start.2 = (bf16[208,128]{1,0:T(8,128)(2,1)}, bf16[208,128]{1,0:T(8,128)(2,1)S(1)}, u32[]{:S(2)}, u32[]{:S(2)}) collective-permute-start(bf16[208,128]{1,0:T(8,128)(2,1)} %get-tuple-element.15), channel_id=1, source_target_pairs={{0,24},{4,28},{8,16},{12,20},{1,25},{5,29},{9,17},{13,21},{2,26},{... | collective-permute-start | bytes 159752 | tf_op jit(solution)/shard_map/ppermute | solution.py:320
  12.9 2.3 %copy-start.5 = (s32[4,2]{0,1:T(2,128)S(1)}, s32[4,2]{0,1:T(2,128)}, u32[]{:S(2)}) copy-start(s32[4,2]{0,1:T(2,128)} %param.9) | copy-start | bytes 100
  12.9 4.4 %collective-permute-start.3 = (bf16[208,128]{1,0:T(8,128)(2,1)}, bf16[208,128]{1,0:T(8,128)(2,1)S(1)}, u32[]{:S(2)}, u32[]{:S(2)}) collective-permute-start(bf16[208,128]{1,0:T(8,128)(2,1)} %get-tuple-element.16), channel_id=1, source_target_pairs={{0,28},{4,16},{8,20},{12,24},{1,29},{5,17},{9,21},{13,25},{2,30},{... | collective-permute-start | bytes 159752 | tf_op jit(solution)/shard_map/ppermute | solution.py:320
  15.2 0.9 %copy-start.2 = (f32[192,8]{1,0:T(8,128)S(1)}, f32[192,8]{1,0:T(8,128)}, u32[]{:S(2)}) copy-start(f32[192,8]{1,0:T(8,128)} %get-tuple-element.13.table_ref.refs_5_) | copy-start | bytes 18436
  16.1 1.2 %copy-start.1 = (bf16[2,1,4,128,128]{4,3,2,1,0:T(8,128)(2,1)S(1)}, bf16[2,1,4,128,128]{4,3,2,1,0:T(8,128)(2,1)}, u32[]{:S(2)}) copy-start(bf16[2,1,4,128,128]{4,3,2,1,0:T(8,128)(2,1)} %refs_1_.3) | copy-start | bytes 786436
  16.1 1.2 %copy-start.3 = (f32[192,8]{1,0:T(8,128)S(1)}, f32[192,8]{1,0:T(8,128)}, u32[]{:S(2)}) copy-start(f32[192,8]{1,0:T(8,128)} %get-tuple-element.13.table_ref.refs_5_) | copy-start | bytes 18436
  16.1 1.2 %copy-start.6 = (s32[1,4]{1,0:T(1,128)S(1)}, s32[1,4]{1,0:T(1,128)}, u32[]{:S(2)}) copy-start(s32[1,4]{1,0:T(1,128)} %refs_2_.3) | copy-start | bytes 52
  16.1 1.2 %copy-start.7 = (s32[1,4]{1,0:T(1,128)S(1)}, s32[1,4]{1,0:T(1,128)}, u32[]{:S(2)}) copy-start(s32[1,4]{1,0:T(1,128)} %refs_3_.3) | copy-start | bytes 52
  16.1 1.2 %copy-start.8 = (s32[1,4]{1,0:T(1,128)S(1)}, s32[1,4]{1,0:T(1,128)}, u32[]{:S(2)}) copy-start(s32[1,4]{1,0:T(1,128)} %refs_4_.3) | copy-start | bytes 52
  19.1 10.9 %all-to-all-start = ((bf16[4,192,128]{2,1,0:T(8,128)(2,1)}), bf16[4,192,128]{2,1,0:T(8,128)(2,1)S(1)}, u32[]{:S(2)}, u32[]{:S(2)}) async-start(bf16[4,192,128]{2,1,0:T(8,128)(2,1)} %get-tuple-element.18), calls=%async_computation | async-start | bytes 393216 | tf_op jit(solution)/shard_map/all_to_all | solution.py:336
  23.7 6.3 %copy-start.4 = (bf16[4,192,128]{2,1,0:T(8,128)(2,1)S(1)}, bf16[4,192,128]{2,1,0:T(8,128)(2,1)}, u32[]{:S(2)}) copy-start(bf16[4,192,128]{2,1,0:T(8,128)(2,1)} %get-tuple-element.12.refs_8_) | copy-start | bytes 589828

commit v3 on v2

--- a/solution.py
+++ b/solution.py
@@ -12,7 +12,6 @@
 HBM = pl.BlockSpec(memory_space=pltpu.HBM)
 ANY = pl.BlockSpec(memory_space=pl.ANY)
 LIMIT = pltpu.CompilerParams(vmem_limit_bytes=16 * 1024 * 1024)
-LARGE = pltpu.CompilerParams(vmem_limit_bytes=60 * 1024 * 1024)
 DMA = pltpu.SemaphoreType.DMA
 
 STATE, LANE, BLOCK, PART, GAIN = 0, 1, 2, 3, 4
@@ -32,17 +31,18 @@
 def own_sum(i, state_ref, jac_ref, cols_ref, table, step):
     blocks, _, width = state_ref.shape
     first = (lax.axis_index("net") * blocks + i) * width
-    total = injected(table, step, first, width)
-    total += times_transposed(state_ref[i], jac_ref[i, 0])
-    for k in range(1, jac_ref.shape[1]):
-        total += times_transposed(state_ref[cols_ref[k - 1, i]], jac_ref[i, k])
-    return total
-
-
-def add_coupled(incoming, block, live, recv, z_ref):
-    lane = lax.broadcasted_iota(jnp.int32, z_ref.shape[1:], 1)
-    term = times_transposed(incoming, block)
-    z_ref[recv] += jnp.where(lane < live, term, 0.0)
+    kinds = jac_ref.shape[1]
+    rows = [state_ref[i]] + [state_ref[cols_ref[k - 1, i]] for k in range(1, kinds)]
+    row_blocks = [jac_ref[i, k] for k in range(kinds)]
+    total = times_transposed(jnp.concatenate(rows, axis=1), jnp.concatenate(row_blocks, axis=1))
+    return total + injected(table, step, first, width)
+
+
+def add_coupled(incoming, block, live, recv, z_ref, keep=None):
+    mask = lax.broadcasted_iota(jnp.int32, z_ref.shape[1:], 1) < live
+    if keep is not None:
+        mask = jnp.logical_and(mask, keep > 0.0)
+    z_ref[recv] += jnp.where(mask, times_transposed(incoming, block), 0.0)
 
 
 def table_row(send_ref, partition, width):
@@ -67,19 +67,24 @@
     return jnp.where(jnp.logical_or(back == lane, block == sent), 1.0, 0.0)
 
 
-def second_kernel(
-    jac_hbm, iface_hbm, cols_ref, send_ref, recv_ref, live_ref, node_ref, gain_ref, table_ref, state_ref, *refs
-):
-    *outgoing, jac_ref, iface_ref, first_ref, z_ref, sems = refs
+def second_kernel(*refs):
+    jac_hbm, iface_hbm, *small, table_ref, state_ref = refs[:10]
     n = lax.axis_size("net")
     me = lax.axis_index("net")
+    outgoing, refs = refs[10 : 9 + n], refs[9 + n :]
+    jac_ref, iface_ref, *loaded, first_ref, z_ref, sems = refs
+    cols_ref, send_ref, recv_ref, live_ref, node_ref, gain_ref = loaded
     blocks, cols, width = state_ref.shape
     loads = [
-        pltpu.make_async_copy(jac_hbm.at[1], jac_ref, sems.at[0]),
-        pltpu.make_async_copy(iface_hbm.at[1, 0], iface_ref, sems.at[1]),
+        pltpu.make_async_copy(source, target, sems.at[i])
+        for i, (source, target) in enumerate(
+            zip([jac_hbm.at[1], iface_hbm.at[1, 0], *small], [jac_ref, iface_ref, *loaded])
+        )
     ]
     for load in loads:
         load.start()
+    for load in loads[2:]:
+        load.wait()
     node = node_ref[...]
     block_of = node // width
     rows = [
@@ -198,9 +203,8 @@
                 block = arrived[q]
             else:
                 block = arrived[d - 1][pl.ds(0, cols)]
-            if fix:
-                block = jnp.where(keep[:, d : d + 1] > 0.0, block, jnp.zeros_like(block))
-            add_coupled(block, iface_ref[step, 0, q], live_ref[0, q], recv_ref[0, q], acc_ref)
+            stands = keep[:, d : d + 1] if fix else None
+            add_coupled(block, iface_ref[step, 0, q], live_ref[0, q], recv_ref[0, q], acc_ref, stands)
         state_ref[...] = acc_ref[...].astype(state_ref.dtype)
         if send_out == "stack":
             for q in range(n):
@@ -249,20 +253,26 @@
     table_rows = GAIN + steps + -(GAIN + steps) % 8
     written = bf16((steps, cols, blocks * width))
 
+    pinned = [
+        pltpu.with_memory_space_constraint(x, pltpu.HBM)
+        for x in (jac, iface_jac, near, iface_send, iface_recv, iface_live, node, ctrl_gain)
+    ]
     table, state, *outgoing = pl.pallas_call(
         second_kernel,
         out_shape=[f32((cols, table_rows)), whole] + [bf16((cols + ROWS, width))] * (n - 1),
-        in_specs=[ANY, ANY, SMEM, SMEM, SMEM, SMEM, VMEM, VMEM],
+        in_specs=[HBM] * len(pinned),
         out_specs=[VMEM] * (n + 1),
         scratch_shapes=[
             pltpu.VMEM((blocks, kinds, width, width), jnp.bfloat16),
             pltpu.VMEM((n, width, width), jnp.bfloat16),
+            *[pltpu.SMEM(x.shape, x.dtype) for x in (near, iface_send, iface_recv, iface_live)],
+            *[pltpu.VMEM(x.shape, x.dtype) for x in (node, ctrl_gain)],
             pltpu.VMEM(whole.shape, jnp.bfloat16),
             pltpu.VMEM(whole.shape, jnp.float32),
-            DMA((2,)),
+            DMA((len(pinned),)),
         ],
-        compiler_params=LARGE,
-    )(jac, iface_jac, near, iface_send, iface_recv, iface_live, node, ctrl_gain)
+        compiler_params=LIMIT,
+    )(*pinned)
 
     def own(state, step):
         return pl.pallas_call(

time: 32.2 us -> 29.7 us (0.922)
  the two profiles are of different devices: /device:TPU:0 before, /device:TPU:4 now
where the time goes in v3:
time: 29.7 us; the launch traced here: 29.5 us
  waiting for transfers between devices  12.9 us (43%)
  starting transfers between devices  9.28 us (31%)
  Pallas kernels  7.09 us (24%)
    ppermute x4, waiting for transfers between devices, hand_over(): lax.ppermute(block, ('tm', 'net'), [((section - 1) * n + q, section * n +...  7.25 us
    all_to_all x1, waiting for transfers between devices, local(): lax.all_to_all(outgoing, 'net', split_axis=0, concat_axis=0, tiled=True)  5.69 us
    ppermute x4, starting transfers between devices, hand_over(): lax.ppermute(block, ('tm', 'net'), [((section - 1) * n + q, section * n +...  5.17 us
    all_to_all x1, starting transfers between devices, local(): lax.all_to_all(outgoing, 'net', split_axis=0, concat_axis=0, tiled=True)  4.11 us
    pallas_call x2, Pallas kernels, join(): pl.pallas_call(functools.partial(join_kernel, step, fix, stacked, send_ou...  3.21 us
    pallas_call x1, Pallas kernels, local(): pl.pallas_call(second_kernel, out_shape=[f32((cols, table_rows)), whole]...  2.12 us
    pallas_call x2, Pallas kernels, own(): pl.pallas_call(functools.partial(own_kernel, step), out_shape=f32(whole.s...  1.76 us
  transfers between devices with their start and end apart: 5, of which 5 were waited for; matrix products, arithmetic and copies ran while one was open for 0% of the time, Pallas kernels for 6%

profile of v3, /device:TPU:4, one launch (start us, length us, event | category | flops | bytes accessed | tf_op | source)
XLA Modules:
  0.0 29.5 jit_solution(15785109255445505604)
XLA Ops:
  0.0 0.0 copy-start
  0.0 2.1 %shard_map.82 = (f32[192,8]{1,0:T(8,128)S(1)}, bf16[4,192,128]{2,1,0:T(8,128)(2,1)S(1)}, bf16[208,128]{1,0:T(8,128)(2,1)S(1)}, bf16[208,128]{1,0:T(8,128)(2,1)S(1)}, bf16[208,128]{1,0:T(8,128)(2,1)S(1)}) custom-call(bf16[2,4,3,128,128]{4,3,2,1,0:T(8,128)(2,1)} %refs_9_.1, bf16[2,1,4,128,128]{4,3,2,1,0:T(8,128)(2,1)} %refs_1_.5, s32[2,4]{1,0:T(2,128)} %bitcast.2, ...), custom_call_target="tpu_custom_call" | custom-call | tf_op jit(solution)/shard_map/pallas_call | solution.py:260
  2.1 1.3 %collective-permute-start = (bf16[4,192,128]{2,1,0:T(8,128)(2,1)S(1)}, bf16[4,192,128]{2,1,0:T(8,128)(2,1)S(1)}, u32[]{:S(2)}, u32[]{:S(2)}) collective-permute-start(bf16[4,192,128]{2,1,0:T(8,128)(2,1)S(1)} %get-tuple-element.12.refs_8_), channel_id=1, source_target_pairs={{0,16},{4,20},{8,24},{12,28},{1,17},{5,21},{9,25},{13,29},{2,18},{... | collective-permute-start | bytes 589832 | tf_op jit(solution)/shard_map/ppermute | solution.py:330
  3.4 1.3 %collective-permute-start.1 = (bf16[208,128]{1,0:T(8,128)(2,1)S(1)}, bf16[208,128]{1,0:T(8,128)(2,1)S(1)}, u32[]{:S(2)}, u32[]{:S(2)}) collective-permute-start(bf16[208,128]{1,0:T(8,128)(2,1)S(1)} %get-tuple-element.14), channel_id=1, source_target_pairs={{0,20},{4,24},{8,28},{12,16},{1,21},{5,25},{9,29},{13,17},{2,22},{... | collective-permute-start | bytes 159752 | tf_op jit(solution)/shard_map/ppermute | solution.py:330
  4.7 1.3 %collective-permute-start.2 = (bf16[208,128]{1,0:T(8,128)(2,1)S(1)}, bf16[208,128]{1,0:T(8,128)(2,1)S(1)}, u32[]{:S(2)}, u32[]{:S(2)}) collective-permute-start(bf16[208,128]{1,0:T(8,128)(2,1)S(1)} %get-tuple-element.15), channel_id=1, source_target_pairs={{0,24},{4,28},{8,16},{12,20},{1,25},{5,29},{9,17},{13,21},{2,26},{... | collective-permute-start | bytes 159752 | tf_op jit(solution)/shard_map/ppermute | solution.py:330
  6.0 0.0 copy-start.2
  6.0 1.3 %collective-permute-start.3 = (bf16[208,128]{1,0:T(8,128)(2,1)S(1)}, bf16[208,128]{1,0:T(8,128)(2,1)S(1)}, u32[]{:S(2)}, u32[]{:S(2)}) collective-permute-start(bf16[208,128]{1,0:T(8,128)(2,1)S(1)} %get-tuple-element.16), channel_id=1, source_target_pairs={{0,28},{4,16},{8,20},{12,24},{1,29},{5,17},{9,21},{13,25},{2,30},{... | collective-permute-start | bytes 159752 | tf_op jit(solution)/shard_map/ppermute | solution.py:330
  7.3 3.3 %collective-permute-done.state_ref.refs_6_ = bf16[4,192,128]{2,1,0:T(8,128)(2,1)S(1)} collective-permute-done((bf16[4,192,128]{2,1,0:T(8,128)(2,1)S(1)}, bf16[4,192,128]{2,1,0:T(8,128)(2,1)S(1)}, u32[]{:S(2)}, u32[]{:S(2)}) %collective-permute-start) | collective-permute-done | bytes 196640 | tf_op jit(solution)/shard_map/ppermute | solution.py:330
  10.7 0.0 copy-done
  10.7 0.0 copy-done.2
  10.7 0.0 copy-start.1
  10.7 0.0 copy-start.3
  10.7 0.0 copy-start.4
  10.7 0.0 copy-start.5
  10.7 0.9 %shard_map.83.refs_0_ = f32[4,192,128]{2,1,0:T(8,128)S(1)} custom-call(bf16[4,192,128]{2,1,0:T(8,128)(2,1)S(1)} %collective-permute-done.state_ref.refs_6_, bf16[2,4,3,128,128]{4,3,2,1,0:T(8,128)(2,1)S(1)} %copy-done, s32[2,4]{1,0:T(2,128)S(1)} %bitcast.3, f32[192,8]{1,0:T(8,128)S(1)} %get-tuple-element.13.table_ref.refs_5_), custom_call_target="tpu_custom_call" | custom-call | tf_op jit(solution)/shard_map/pallas_call | solution.py:278
  11.6 1.4 %collective-permute-done.1.refs_7_ = bf16[208,128]{1,0:T(8,128)(2,1)S(1)} collective-permute-done((bf16[208,128]{1,0:T(8,128)(2,1)S(1)}, bf16[208,128]{1,0:T(8,128)(2,1)S(1)}, u32[]{:S(2)}, u32[]{:S(2)}) %collective-permute-start.1) | collective-permute-done | bytes 53280 | tf_op jit(solution)/shard_map/ppermute | solution.py:330
  13.0 1.9 %collective-permute-done.2.refs_8_ = bf16[208,128]{1,0:T(8,128)(2,1)S(1)} collective-permute-done((bf16[208,128]{1,0:T(8,128)(2,1)S(1)}, bf16[208,128]{1,0:T(8,128)(2,1)S(1)}, u32[]{:S(2)}, u32[]{:S(2)}) %collective-permute-start.2) | collective-permute-done | bytes 53280 | tf_op jit(solution)/shard_map/ppermute | solution.py:330
  14.9 0.6 %collective-permute-done.3.refs_9_ = bf16[208,128]{1,0:T(8,128)(2,1)S(1)} collective-permute-done((bf16[208,128]{1,0:T(8,128)(2,1)S(1)}, bf16[208,128]{1,0:T(8,128)(2,1)S(1)}, u32[]{:S(2)}, u32[]{:S(2)}) %collective-permute-start.3) | collective-permute-done | bytes 53280 | tf_op jit(solution)/shard_map/ppermute | solution.py:330
  15.5 0.0 copy-done.1
  15.5 0.0 copy-done.3
  15.5 0.0 copy-done.4
  15.5 0.0 copy-done.5
  15.5 1.6 %shard_map.84 = (bf16[4,192,128]{2,1,0:T(8,128)(2,1)S(1)}, bf16[4,192,128]{2,1,0:T(8,128)(2,1)}) custom-call(f32[4,192,128]{2,1,0:T(8,128)S(1)} %shard_map.83.refs_0_, bf16[2,1,4,128,128]{4,3,2,1,0:T(8,128)(2,1)S(1)} %copy-done.1, s32[1,4]{1,0:T(1,128)S(1)} %copy-done.3, s32[1,4]{1,0:T(1,128)S(1)} %copy-done.4, s32[1,4]{1,0:T(1,128)S(1)} %copy-done.5, ...), custom_call_target="tpu_custom_call" | custom-call | tf_op jit(solution)/shard_map/pallas_call | solution.py:318
  17.2 4.1 %all-to-all-start = ((bf16[4,192,128]{2,1,0:T(8,128)(2,1)}), bf16[4,192,128]{2,1,0:T(8,128)(2,1)S(1)}, u32[]{:S(2)}, u32[]{:S(2)}) async-start(bf16[4,192,128]{2,1,0:T(8,128)(2,1)} %get-tuple-element.18), calls=%async_computation | async-start | bytes 393216 | tf_op jit(solution)/shard_map/all_to_all | solution.py:346
  21.3 0.9 %shard_map.85.refs_0_ = f32[4,192,128]{2,1,0:T(8,128)S(1)} custom-call(bf16[4,192,128]{2,1,0:T(8,128)(2,1)S(1)} %get-tuple-element.17.state_ref.refs_6_.refs_11_, bf16[2,4,3,128,128]{4,3,2,1,0:T(8,128)(2,1)S(1)} %copy-done, s32[2,4]{1,0:T(2,128)S(1)} %bitcast.4, f32[192,8]{1,0:T(8,128)S(1)} %get-tuple-element.13.table_ref.refs_5_), custom_call_target="tpu_custom_call" | custom-call | tf_op jit(solution)/shard_map/pallas_call | solution.py:278
  22.2 5.7 %all-to-all-done.refs_7_ = bf16[4,192,128]{2,1,0:T(8,128)(2,1)S(1)} async-done(((bf16[4,192,128]{2,1,0:T(8,128)(2,1)}), bf16[4,192,128]{2,1,0:T(8,128)(2,1)S(1)}, u32[]{:S(2)}, u32[]{:S(2)}) %all-to-all-start) | async-done | bytes 196640 | tf_op jit(solution)/shard_map/all_to_all | solution.py:346
  27.9 1.6 %shard_map.86 = bf16[2,192,512]{2,1,0:T(8,128)(2,1)} custom-call(f32[4,192,128]{2,1,0:T(8,128)S(1)} %shard_map.85.refs_0_, bf16[2,1,4,128,128]{4,3,2,1,0:T(8,128)(2,1)S(1)} %copy-done.1, s32[1,4]{1,0:T(1,128)S(1)} %copy-done.3, s32[1,4]{1,0:T(1,128)S(1)} %copy-done.4, s32[1,4]{1,0:T(1,128)S(1)} %copy-done.5, ...), custom_call_target="tpu_custom_call" | custom-call | tf_op jit(solution)/shard_map/pallas_call | solution.py:318
Async XLA Ops:
  0.0 10.7 %copy-start = (bf16[2,4,3,128,128]{4,3,2,1,0:T(8,128)(2,1)S(1)}, bf16[2,4,3,128,128]{4,3,2,1,0:T(8,128)(2,1)}, u32[]{:S(2)}) copy-start(bf16[2,4,3,128,128]{4,3,2,1,0:T(8,128)(2,1)} %refs_9_.1) | copy-start | bytes 2359300
  2.1 8.5 %collective-permute-start = (bf16[4,192,128]{2,1,0:T(8,128)(2,1)S(1)}, bf16[4,192,128]{2,1,0:T(8,128)(2,1)S(1)}, u32[]{:S(2)}, u32[]{:S(2)}) collective-permute-start(bf16[4,192,128]{2,1,0:T(8,128)(2,1)S(1)} %get-tuple-element.12.refs_8_), channel_id=1, source_target_pairs={{0,16},{4,20},{8,24},{12,28},{1,17},{5,21},{9,25},{13,29},{2,18},{... | collective-permute-start | bytes 589832 | tf_op jit(solution)/shard_map/ppermute | solution.py:330
  3.4 9.6 %collective-permute-start.1 = (bf16[208,128]{1,0:T(8,128)(2,1)S(1)}, bf16[208,128]{1,0:T(8,128)(2,1)S(1)}, u32[]{:S(2)}, u32[]{:S(2)}) collective-permute-start(bf16[208,128]{1,0:T(8,128)(2,1)S(1)} %get-tuple-element.14), channel_id=1, source_target_pairs={{0,20},{4,24},{8,28},{12,16},{1,21},{5,25},{9,29},{13,17},{2,22},{... | collective-permute-start | bytes 159752 | tf_op jit(solution)/shard_map/ppermute | solution.py:330
  4.7 10.2 %collective-permute-start.2 = (bf16[208,128]{1,0:T(8,128)(2,1)S(1)}, bf16[208,128]{1,0:T(8,128)(2,1)S(1)}, u32[]{:S(2)}, u32[]{:S(2)}) collective-permute-start(bf16[208,128]{1,0:T(8,128)(2,1)S(1)} %get-tuple-element.15), channel_id=1, source_target_pairs={{0,24},{4,28},{8,16},{12,20},{1,25},{5,29},{9,17},{13,21},{2,26},{... | collective-permute-start | bytes 159752 | tf_op jit(solution)/shard_map/ppermute | solution.py:330
  6.0 4.6 %copy-start.2 = (s32[4,2]{0,1:T(2,128)S(1)}, s32[4,2]{0,1:T(2,128)}, u32[]{:S(2)}) copy-start(s32[4,2]{0,1:T(2,128)} %param.9) | copy-start | bytes 100
  6.0 9.5 %collective-permute-start.3 = (bf16[208,128]{1,0:T(8,128)(2,1)S(1)}, bf16[208,128]{1,0:T(8,128)(2,1)S(1)}, u32[]{:S(2)}, u32[]{:S(2)}) collective-permute-start(bf16[208,128]{1,0:T(8,128)(2,1)S(1)} %get-tuple-element.16), channel_id=1, source_target_pairs={{0,28},{4,16},{8,20},{12,24},{1,29},{5,17},{9,21},{13,25},{2,30},{... | collective-permute-start | bytes 159752 | tf_op jit(solution)/shard_map/ppermute | solution.py:330
  10.7 4.8 %copy-start.1 = (bf16[2,1,4,128,128]{4,3,2,1,0:T(8,128)(2,1)S(1)}, bf16[2,1,4,128,128]{4,3,2,1,0:T(8,128)(2,1)}, u32[]{:S(2)}) copy-start(bf16[2,1,4,128,128]{4,3,2,1,0:T(8,128)(2,1)} %refs_1_.5) | copy-start | bytes 786436
  10.7 4.8 %copy-start.3 = (s32[1,4]{1,0:T(1,128)S(1)}, s32[1,4]{1,0:T(1,128)}, u32[]{:S(2)}) copy-start(s32[1,4]{1,0:T(1,128)} %refs_2_.3) | copy-start | bytes 52
  10.7 4.8 %copy-start.4 = (s32[1,4]{1,0:T(1,128)S(1)}, s32[1,4]{1,0:T(1,128)}, u32[]{:S(2)}) copy-start(s32[1,4]{1,0:T(1,128)} %refs_3_.5) | copy-start | bytes 52
  10.7 4.8 %copy-start.5 = (s32[1,4]{1,0:T(1,128)S(1)}, s32[1,4]{1,0:T(1,128)}, u32[]{:S(2)}) copy-start(s32[1,4]{1,0:T(1,128)} %refs_4_.5) | copy-start | bytes 52
  17.2 10.7 %all-to-all-start = ((bf16[4,192,128]{2,1,0:T(8,128)(2,1)}), bf16[4,192,128]{2,1,0:T(8,128)(2,1)S(1)}, u32[]{:S(2)}, u32[]{:S(2)}) async-start(bf16[4,192,128]{2,1,0:T(8,128)(2,1)} %get-tuple-element.18), calls=%async_computation | async-start | bytes 393216 | tf_op jit(solution)/shard_map/all_to_all | solution.py:346

commit v4 on v3

--- a/solution.py
+++ b/solution.py
@@ -332,13 +332,14 @@
                 ("tm", "net"),
                 [((section - 1) * n + q, section * n + (q + d) % n) for q in range(n)],
             )
-            for d, block in enumerate(blocks_to_send)
+            for d, block in enumerate(blocks_to_send, 1)
         ]
 
     opening = [state]
     out = None
     for r in range(1, tm):
-        state, *arrived = hand_over([state, *outgoing], r)
+        arrived = hand_over(outgoing, r)
+        state = lax.all_gather(state, "tm")[r - 1]
         before = []
         for s in range(steps):
             fix = r == 1 and s == 0

time: 29.7 us -> 35.8 us (1.21)
  the two profiles are of different devices: /device:TPU:4 before, /device:TPU:0 now
where the time goes in v4:
time: 35.8 us; the launch traced here: 35.5 us
  starting transfers between devices  13.9 us (39%)
  Pallas kernels  7.34 us (21%)
  blocking collectives  7.04 us (20%)
  waiting for transfers between devices  6.39 us (18%)
  local copies, waits for them, and re-layouts  0.72 us (2%)
    ppermute x3, starting transfers between devices, hand_over(): lax.ppermute(block, ('tm', 'net'), [((section - 1) * n + q, section * n +...  10.5 us
    all_gather x1, blocking collectives, local(): state = lax.all_gather(state, 'tm')[r - 1]  7.04 us
    all_to_all x1, waiting for transfers between devices, local(): lax.all_to_all(outgoing, 'net', split_axis=0, concat_axis=0, tiled=True)  6.38 us
    pallas_call x2, Pallas kernels, join(): pl.pallas_call(functools.partial(join_kernel, step, fix, stacked, send_ou...  3.46 us
    all_to_all x1, starting transfers between devices, local(): lax.all_to_all(outgoing, 'net', split_axis=0, concat_axis=0, tiled=True)  3.37 us
    pallas_call x1, Pallas kernels, local(): pl.pallas_call(second_kernel, out_shape=[f32((cols, table_rows)), whole]...  2.12 us
    pallas_call x2, Pallas kernels, own(): pl.pallas_call(functools.partial(own_kernel, step), out_shape=f32(whole.s...  1.76 us
  transfers between devices with their start and end apart: 4, of which 1 were waited for; matrix products, arithmetic and copies ran while one was open for 0% of the time, Pallas kernels for 5%

profile of v4, /device:TPU:0, one launch (start us, length us, event | category | flops | bytes accessed | tf_op | source)
XLA Modules:
  0.0 35.5 jit_solution(15342878684828182169)
XLA Ops:
  0.0 0.0 copy-start
  0.0 2.1 %shard_map.82 = (f32[192,8]{1,0:T(8,128)S(1)}, bf16[4,192,128]{2,1,0:T(8,128)(2,1)S(1)}, bf16[208,128]{1,0:T(8,128)(2,1)S(1)}, bf16[208,128]{1,0:T(8,128)(2,1)S(1)}, bf16[208,128]{1,0:T(8,128)(2,1)S(1)}) custom-call(bf16[2,4,3,128,128]{4,3,2,1,0:T(8,128)(2,1)} %refs_9_.1, bf16[2,1,4,128,128]{4,3,2,1,0:T(8,128)(2,1)} %refs_1_.5, s32[2,4]{1,0:T(2,128)} %bitcast.2, ...), custom_call_target="tpu_custom_call" | custom-call | tf_op jit(solution)/shard_map/pallas_call | solution.py:260
  2.1 5.9 %collective-permute-start = (bf16[208,128]{1,0:T(8,128)(2,1)S(1)}, bf16[208,128]{1,0:T(8,128)(2,1)S(1)}, u32[]{:S(2)}, u32[]{:S(2)}) collective-permute-start(bf16[208,128]{1,0:T(8,128)(2,1)S(1)} %get-tuple-element.14), channel_id=1, source_target_pairs={{0,20},{4,24},{8,28},{12,16},{1,21},{5,25},{9,29},{13,17},{2,22},{... | collective-permute-start | bytes 159752 | tf_op jit(solution)/shard_map/ppermute | solution.py:330
  8.0 2.3 %collective-permute-start.1 = (bf16[208,128]{1,0:T(8,128)(2,1)S(1)}, bf16[208,128]{1,0:T(8,128)(2,1)S(1)}, u32[]{:S(2)}, u32[]{:S(2)}) collective-permute-start(bf16[208,128]{1,0:T(8,128)(2,1)S(1)} %get-tuple-element.15), channel_id=1, source_target_pairs={{0,24},{4,28},{8,16},{12,20},{1,25},{5,29},{9,17},{13,21},{2,26},{... | collective-permute-start | bytes 159752 | tf_op jit(solution)/shard_map/ppermute | solution.py:330
  10.3 2.3 %collective-permute-start.2 = (bf16[208,128]{1,0:T(8,128)(2,1)S(1)}, bf16[208,128]{1,0:T(8,128)(2,1)S(1)}, u32[]{:S(2)}, u32[]{:S(2)}) collective-permute-start(bf16[208,128]{1,0:T(8,128)(2,1)S(1)} %get-tuple-element.16), channel_id=1, source_target_pairs={{0,28},{4,16},{8,20},{12,24},{1,29},{5,17},{9,21},{13,25},{2,30},{... | collective-permute-start | bytes 159752 | tf_op jit(solution)/shard_map/ppermute | solution.py:330
  12.6 7.0 %all-gather = bf16[8,192,128]{2,1,0:T(8,128)(2,1)S(1)} all-gather(bf16[4,192,128]{2,1,0:T(8,128)(2,1)S(1)} %get-tuple-element.12.refs_8_), channel_id=2, replica_groups=mesh['tm'=2,'net'=4,'cols'=4] {'tm'}, dimensions={0}, use_global_device_ids=true | all-gather | bytes 589824 | tf_op jit(solution)/shard_map/all_gather | solution.py:342
  19.7 0.0 copy-start.2
  19.7 0.0 copy-done
  19.7 0.7 %copy-done.2 = s32[4,2]{0,1:T(2,128)S(1)} copy-done((s32[4,2]{0,1:T(2,128)S(1)}, s32[4,2]{0,1:T(2,128)}, u32[]{:S(2)}) %copy-start.2) | copy-done | bytes 56
  20.4 0.0 copy-start.1
  20.4 0.0 copy-start.3
  20.4 0.0 copy-start.4
  20.4 0.0 copy-start.5
  20.4 0.9 %shard_map.83.refs_0_ = f32[4,192,128]{2,1,0:T(8,128)S(1)} custom-call(bf16[4,192,128]{2,1,0:T(8,128)(2,1)S(1)} %slice.5.state_ref.refs_6_, bf16[2,4,3,128,128]{4,3,2,1,0:T(8,128)(2,1)S(1)} %copy-done, s32[2,4]{1,0:T(2,128)S(1)} %bitcast.3, f32[192,8]{1,0:T(8,128)S(1)} %get-tuple-element.13.table_ref.refs_5_), custom_call_target="tpu_custom_call" | custom-call | tf_op jit(solution)/shard_map/pallas_call | solution.py:278
  21.3 0.0 collective-permute-done.refs_7_
  21.3 0.0 collective-permute-done.1.refs_8_
  21.3 0.0 collective-permute-done.2.refs_9_
  21.3 0.0 copy-done.1
  21.3 0.0 copy-done.3
  21.3 0.0 copy-done.4
  21.3 0.0 copy-done.5
  21.4 1.6 %shard_map.84 = (bf16[4,192,128]{2,1,0:T(8,128)(2,1)S(1)}, bf16[4,192,128]{2,1,0:T(8,128)(2,1)}) custom-call(f32[4,192,128]{2,1,0:T(8,128)S(1)} %shard_map.83.refs_0_, bf16[2,1,4,128,128]{4,3,2,1,0:T(8,128)(2,1)S(1)} %copy-done.1, s32[1,4]{1,0:T(1,128)S(1)} %copy-done.3, s32[1,4]{1,0:T(1,128)S(1)} %copy-done.4, s32[1,4]{1,0:T(1,128)S(1)} %copy-done.5, ...), custom_call_target="tpu_custom_call" | custom-call | tf_op jit(solution)/shard_map/pallas_call | solution.py:318
  23.0 3.4 %all-to-all-start = ((bf16[4,192,128]{2,1,0:T(8,128)(2,1)}), bf16[4,192,128]{2,1,0:T(8,128)(2,1)S(1)}, u32[]{:S(2)}, u32[]{:S(2)}) async-start(bf16[4,192,128]{2,1,0:T(8,128)(2,1)} %get-tuple-element.18), calls=%async_computation | async-start | bytes 393216 | tf_op jit(solution)/shard_map/all_to_all | solution.py:347
  26.4 0.9 %shard_map.85.refs_0_ = f32[4,192,128]{2,1,0:T(8,128)S(1)} custom-call(bf16[4,192,128]{2,1,0:T(8,128)(2,1)S(1)} %get-tuple-element.17.state_ref.refs_6_.refs_11_, bf16[2,4,3,128,128]{4,3,2,1,0:T(8,128)(2,1)S(1)} %copy-done, s32[2,4]{1,0:T(2,128)S(1)} %bitcast.4, f32[192,8]{1,0:T(8,128)S(1)} %get-tuple-element.13.table_ref.refs_5_), custom_call_target="tpu_custom_call" | custom-call | tf_op jit(solution)/shard_map/pallas_call | solution.py:278
  27.3 6.4 %all-to-all-done.refs_7_ = bf16[4,192,128]{2,1,0:T(8,128)(2,1)S(1)} async-done(((bf16[4,192,128]{2,1,0:T(8,128)(2,1)}), bf16[4,192,128]{2,1,0:T(8,128)(2,1)S(1)}, u32[]{:S(2)}, u32[]{:S(2)}) %all-to-all-start) | async-done | bytes 196640 | tf_op jit(solution)/shard_map/all_to_all | solution.py:347
  33.6 1.8 %shard_map.86 = bf16[2,192,512]{2,1,0:T(8,128)(2,1)} custom-call(f32[4,192,128]{2,1,0:T(8,128)S(1)} %shard_map.85.refs_0_, bf16[2,1,4,128,128]{4,3,2,1,0:T(8,128)(2,1)S(1)} %copy-done.1, s32[1,4]{1,0:T(1,128)S(1)} %copy-done.3, s32[1,4]{1,0:T(1,128)S(1)} %copy-done.4, s32[1,4]{1,0:T(1,128)S(1)} %copy-done.5, ...), custom_call_target="tpu_custom_call" | custom-call | tf_op jit(solution)/shard_map/pallas_call | solution.py:318
  (1 shorter events, 0.0 us)
Async XLA Ops:
  0.0 19.7 %copy-start = (bf16[2,4,3,128,128]{4,3,2,1,0:T(8,128)(2,1)S(1)}, bf16[2,4,3,128,128]{4,3,2,1,0:T(8,128)(2,1)}, u32[]{:S(2)}) copy-start(bf16[2,4,3,128,128]{4,3,2,1,0:T(8,128)(2,1)} %refs_9_.1) | copy-start | bytes 2359300
  2.1 19.2 %collective-permute-start = (bf16[208,128]{1,0:T(8,128)(2,1)S(1)}, bf16[208,128]{1,0:T(8,128)(2,1)S(1)}, u32[]{:S(2)}, u32[]{:S(2)}) collective-permute-start(bf16[208,128]{1,0:T(8,128)(2,1)S(1)} %get-tuple-element.14), channel_id=1, source_target_pairs={{0,20},{4,24},{8,28},{12,16},{1,21},{5,25},{9,29},{13,17},{2,22},{... | collective-permute-start | bytes 159752 | tf_op jit(solution)/shard_map/ppermute | solution.py:330
  8.0 13.3 %collective-permute-start.1 = (bf16[208,128]{1,0:T(8,128)(2,1)S(1)}, bf16[208,128]{1,0:T(8,128)(2,1)S(1)}, u32[]{:S(2)}, u32[]{:S(2)}) collective-permute-start(bf16[208,128]{1,0:T(8,128)(2,1)S(1)} %get-tuple-element.15), channel_id=1, source_target_pairs={{0,24},{4,28},{8,16},{12,20},{1,25},{5,29},{9,17},{13,21},{2,26},{... | collective-permute-start | bytes 159752 | tf_op jit(solution)/shard_map/ppermute | solution.py:330
  10.3 11.0 %collective-permute-start.2 = (bf16[208,128]{1,0:T(8,128)(2,1)S(1)}, bf16[208,128]{1,0:T(8,128)(2,1)S(1)}, u32[]{:S(2)}, u32[]{:S(2)}) collective-permute-start(bf16[208,128]{1,0:T(8,128)(2,1)S(1)} %get-tuple-element.16), channel_id=1, source_target_pairs={{0,28},{4,16},{8,20},{12,24},{1,29},{5,17},{9,21},{13,25},{2,30},{... | collective-permute-start | bytes 159752 | tf_op jit(solution)/shard_map/ppermute | solution.py:330
  19.7 0.7 %copy-start.2 = (s32[4,2]{0,1:T(2,128)S(1)}, s32[4,2]{0,1:T(2,128)}, u32[]{:S(2)}) copy-start(s32[4,2]{0,1:T(2,128)} %param.9) | copy-start | bytes 100
  20.4 0.9 %copy-start.1 = (bf16[2,1,4,128,128]{4,3,2,1,0:T(8,128)(2,1)S(1)}, bf16[2,1,4,128,128]{4,3,2,1,0:T(8,128)(2,1)}, u32[]{:S(2)}) copy-start(bf16[2,1,4,128,128]{4,3,2,1,0:T(8,128)(2,1)} %refs_1_.5) | copy-start | bytes 786436
  20.4 1.0 %copy-start.3 = (s32[1,4]{1,0:T(1,128)S(1)}, s32[1,4]{1,0:T(1,128)}, u32[]{:S(2)}) copy-start(s32[1,4]{1,0:T(1,128)} %refs_2_.3) | copy-start | bytes 52
  20.4 1.0 %copy-start.4 = (s32[1,4]{1,0:T(1,128)S(1)}, s32[1,4]{1,0:T(1,128)}, u32[]{:S(2)}) copy-start(s32[1,4]{1,0:T(1,128)} %refs_3_.5) | copy-start | bytes 52
  20.4 1.0 %copy-start.5 = (s32[1,4]{1,0:T(1,128)S(1)}, s32[1,4]{1,0:T(1,128)}, u32[]{:S(2)}) copy-start(s32[1,4]{1,0:T(1,128)} %refs_4_.5) | copy-start | bytes 52
  23.0 10.6 %all-to-all-start = ((bf16[4,192,128]{2,1,0:T(8,128)(2,1)}), bf16[4,192,128]{2,1,0:T(8,128)(2,1)S(1)}, u32[]{:S(2)}, u32[]{:S(2)}) async-start(bf16[4,192,128]{2,1,0:T(8,128)(2,1)} %get-tuple-element.18), calls=%async_computation | async-start | bytes 393216 | tf_op jit(solution)/shard_map/all_to_all | solution.py:347

commit v5 on v3

--- a/solution.py
+++ b/solution.py
@@ -14,7 +14,7 @@
 LIMIT = pltpu.CompilerParams(vmem_limit_bytes=16 * 1024 * 1024)
 DMA = pltpu.SemaphoreType.DMA
 
-STATE, LANE, BLOCK, PART, GAIN = 0, 1, 2, 3, 4
+STATE, LANE, BLOCK, AWAY, GAIN = 0, 1, 2, 3, 4
 ROWS = 16
 
 
@@ -46,25 +46,20 @@
 
 
 def table_row(send_ref, partition, width):
-    n = lax.axis_size("net")
     lane = lax.broadcasted_iota(jnp.int32, (1, width), 1)
     row = jnp.zeros((1, width), jnp.float32)
-    for e in range(n):
-        row = jnp.where(lane == e, send_ref[0, lax.rem(partition - e + n, n)].astype(jnp.float32), row)
+    for e in range(lax.axis_size("net")):
+        row = jnp.where(lane == e, send_ref[0, partition ^ e].astype(jnp.float32), row)
     return row
 
 
 def kept(table, rows):
-    n = lax.axis_size("net")
-    me = lax.axis_index("net")
-    part, block = table[:, PART : PART + 1], table[:, BLOCK : BLOCK + 1]
-    back = me.astype(jnp.float32) - part
-    back = jnp.where(back < 0.0, back + float(n), back)
+    away, block = table[:, AWAY : AWAY + 1], table[:, BLOCK : BLOCK + 1]
     sent = jnp.broadcast_to(rows[0], (table.shape[0], rows[0].shape[1]))
-    for d in range(1, n):
-        sent = jnp.where(back == float(d), rows[d], sent)
+    for d in range(1, len(rows)):
+        sent = jnp.where(away == float(d), rows[d], sent)
     lane = lax.broadcasted_iota(jnp.int32, sent.shape, 1).astype(jnp.float32)
-    return jnp.where(jnp.logical_or(back == lane, block == sent), 1.0, 0.0)
+    return jnp.where(jnp.logical_or(away == lane, block == sent), 1.0, 0.0)
 
 
 def second_kernel(*refs):
@@ -81,7 +76,14 @@
             zip([jac_hbm.at[1], iface_hbm.at[1, 0], *small], [jac_ref, iface_ref, *loaded])
         )
     ]
-    for load in loads:
+    here = lax.axis_index("tm") == 0
+
+    @pl.when(here)
+    def _():
+        for load in loads[:2]:
+            load.start()
+
+    for load in loads[2:]:
         load.start()
     for load in loads[2:]:
         load.wait()
@@ -91,33 +93,36 @@
         node,
         node - block_of * width,
         block_of % blocks,
-        block_of // blocks,
+        (block_of // blocks) ^ me,
     ]
     steps = gain_ref.shape[0]
     fill = -(GAIN + steps) % 8
     rows = [row.astype(jnp.float32) for row in rows] + [gain_ref[...], jnp.zeros((fill, cols), jnp.float32)]
     table_ref[...] = jnp.concatenate(rows, axis=0).T
-    table = table_ref[...]
-    for i in range(blocks):
-        first_ref[i] = injected(table, 0, (me * blocks + i) * width, width).astype(first_ref.dtype)
-    lane = lax.broadcasted_iota(jnp.int32, (cols, width), 1).astype(jnp.float32)
-    shot = jnp.where(lane == table[:, LANE : LANE + 1], table[:, GAIN : GAIN + 1], 0.0)
-    loads[0].wait()
-    for i in range(blocks):
-        z_ref[i] = own_sum(i, first_ref, jac_ref, cols_ref, table, 1)
-    loads[1].wait()
-    part, block = table[:, PART : PART + 1], table[:, BLOCK : BLOCK + 1]
-    mine = jnp.logical_or(part != me.astype(jnp.float32), block == send_ref[0, me].astype(jnp.float32))
-    shot = jnp.where(mine, shot, 0.0)
-    for q in range(n):
-        sent = jnp.where(part == float(q), shot, 0.0).astype(first_ref.dtype)
-        add_coupled(sent, iface_ref[q], live_ref[0, q], recv_ref[0, q], z_ref)
-    state_ref[...] = z_ref[...].astype(state_ref.dtype)
-    for d in range(1, n):
-        target = lax.rem(me + d, n)
-        outgoing[d - 1][pl.ds(0, cols)] = state_ref[send_ref[0, target]]
-        row = table_row(send_ref, target, width).astype(state_ref.dtype)
-        outgoing[d - 1][pl.ds(cols, ROWS)] = jnp.broadcast_to(row, (ROWS, width))
+
+    @pl.when(here)
+    def _():
+        table = table_ref[...]
+        for i in range(blocks):
+            first_ref[i] = injected(table, 0, (me * blocks + i) * width, width).astype(first_ref.dtype)
+        lane = lax.broadcasted_iota(jnp.int32, (cols, width), 1).astype(jnp.float32)
+        shot = jnp.where(lane == table[:, LANE : LANE + 1], table[:, GAIN : GAIN + 1], 0.0)
+        loads[0].wait()
+        for i in range(blocks):
+            z_ref[i] = own_sum(i, first_ref, jac_ref, cols_ref, table, 1)
+        loads[1].wait()
+        away, block = table[:, AWAY : AWAY + 1], table[:, BLOCK : BLOCK + 1]
+        mine = jnp.logical_or(away != 0.0, block == send_ref[0, me].astype(jnp.float32))
+        shot = jnp.where(mine, shot, 0.0)
+        for d in range(n):
+            q = me ^ d
+            sent = jnp.where(away == float(d), shot, 0.0).astype(first_ref.dtype)
+            add_coupled(sent, iface_ref[q], live_ref[0, q], recv_ref[0, q], z_ref)
+        state_ref[...] = z_ref[...].astype(state_ref.dtype)
+        for d in range(1, n):
+            outgoing[d - 1][pl.ds(0, cols)] = state_ref[send_ref[0, me ^ d]]
+            row = table_row(send_ref, me ^ d, width).astype(state_ref.dtype)
+            outgoing[d - 1][pl.ds(cols, ROWS)] = jnp.broadcast_to(row, (ROWS, width))
 
 
 def write_start(states, first, out_ref, sems):
@@ -151,23 +156,19 @@
     made_ref[0] = z_ref[...].astype(made_ref.dtype)
     me = lax.axis_index("net")
     rows = [table_row(send_ref, me, width)]
-    for d in range(1, n):
-        rows.append(arrived[lax.rem(me - d + n, n)][0:1].astype(jnp.float32))
+    rows += [block[0:1].astype(jnp.float32) for block in arrived]
     keep = kept(table, rows)[:, 0:1]
     for i in range(blocks):
         made_ref[1, i] = jnp.where(keep > 0.0, states[0][i], jnp.zeros_like(states[0][i]))
     return [made_ref.at[0], made_ref.at[1], *states[1:]]
 
 
-def join_kernel(step, fix, stacked, send_out, section, firsts, store, *refs):
+def join_kernel(step, fix, send, section, firsts, store, *refs):
     n = lax.axis_size("net")
     me = lax.axis_index("net")
     tm = lax.axis_index("tm")
     z_ref, iface_ref, send_ref, recv_ref, live_ref, table_ref, state_in_ref, *refs = refs
-    if stacked:
-        arrived, *refs = refs
-    else:
-        arrived, refs = refs[: n - 1], refs[n - 1 :]
+    arrived, refs = refs[: n - 1], refs[n - 1 :]
     acc_ref = refs.pop()
     blocks, cols, width = z_ref.shape
     before = []
@@ -196,22 +197,14 @@
         else:
             acc_ref[...] = z_ref[...]
         for d in range(n):
-            q = lax.rem(me - d + n, n)
-            if d == 0:
-                block = state_in_ref[send_ref[0, me]]
-            elif stacked:
-                block = arrived[q]
-            else:
-                block = arrived[d - 1][pl.ds(0, cols)]
+            q = me ^ d
+            block = arrived[d - 1][pl.ds(0, cols)] if d else state_in_ref[send_ref[0, me]]
             stands = keep[:, d : d + 1] if fix else None
             add_coupled(block, iface_ref[step, 0, q], live_ref[0, q], recv_ref[0, q], acc_ref, stands)
         state_ref[...] = acc_ref[...].astype(state_ref.dtype)
-        if send_out == "stack":
-            for q in range(n):
-                outgoing[0][q] = state_ref[send_ref[0, q]]
-        if send_out == "each":
+        if send:
             for d in range(1, n):
-                outgoing[d - 1][...] = state_ref[send_ref[0, lax.rem(me + d, n)]]
+                outgoing[d - 1][...] = state_ref[send_ref[0, me ^ d]]
         if store:
             copies += write_start([state_ref], store - 1, out_ref, sems)
             for copy in copies:
@@ -221,13 +214,13 @@
         pl.when(tm == section)(join)
     else:
         join()
-    if fix and send_out == "stack":
+    if fix:
 
         @pl.when(tm == 0)
         def _():
-            for q in range(n):
-                row = table_row(send_ref, jnp.int32(q), width).astype(state_ref.dtype)
-                outgoing[0][q, pl.ds(0, ROWS)] = jnp.broadcast_to(row, (ROWS, width))
+            for d in range(1, n):
+                row = table_row(send_ref, me ^ d, width).astype(state_ref.dtype)
+                outgoing[d - 1][pl.ds(0, ROWS)] = jnp.broadcast_to(row, (ROWS, width))
 
     if firsts:
 
@@ -249,7 +242,7 @@
     near = block_cols.T
     bf16 = functools.partial(jax.ShapeDtypeStruct, dtype=jnp.bfloat16)
     f32 = functools.partial(jax.ShapeDtypeStruct, dtype=jnp.float32)
-    whole, one, stack = bf16((blocks, cols, width)), bf16((cols, width)), bf16((n, cols, width))
+    whole, one = bf16((blocks, cols, width)), bf16((cols, width))
     table_rows = GAIN + steps + -(GAIN + steps) % 8
     written = bf16((steps, cols, blocks * width))
 
@@ -283,12 +276,11 @@
             compiler_params=LIMIT,
         )(state, jac, near, table)
 
-    def join(z, step, fix, state, arrived, send_out, section, opening=(), before=(), out=None, store=0):
-        stacked = not isinstance(arrived, list)
+    def join(z, step, fix, state, arrived, send, section, opening=(), before=(), out=None, store=0):
         arrays = [z, iface_jac, iface_send, iface_recv, iface_live, table, state]
         specs = [VMEM, VMEM, SMEM, SMEM, SMEM, VMEM, VMEM]
-        arrays += [arrived] if stacked else arrived
-        specs += [VMEM] * (1 if stacked else n - 1)
+        arrays += arrived
+        specs += [VMEM] * (n - 1)
         shapes = []
         scratch = [pltpu.VMEM(whole.shape, jnp.float32)]
         aliases = {}
@@ -308,15 +300,14 @@
             scratch.insert(0, DMA((steps, blocks)))
             if out is None:
                 scratch.insert(0, pltpu.VMEM((2, *whole.shape), jnp.bfloat16))
-        if send_out == "none":
+        if send:
+            shapes += [whole] + [one] * (n - 1)
+        else:
             scratch.insert(0, pltpu.VMEM(whole.shape, jnp.bfloat16))
-        else:
-            shapes.append(whole)
-        shapes += {"stack": [stack], "each": [one] * (n - 1), "none": []}[send_out]
         out_specs += [VMEM] * (len(shapes) - len(out_specs))
         firsts = len(opening) if store and out is None else 0
         return pl.pallas_call(
-            functools.partial(join_kernel, step, fix, stacked, send_out, section, firsts, store),
+            functools.partial(join_kernel, step, fix, send, section, firsts, store),
             out_shape=shapes,
             in_specs=specs,
             out_specs=out_specs,
@@ -325,33 +316,32 @@
             compiler_params=LIMIT,
         )(*arrays)
 
-    def hand_over(blocks_to_send, section):
+    def swap(outgoing, sections):
         return [
             lax.ppermute(
-                block,
-                ("tm", "net"),
-                [((section - 1) * n + q, section * n + (q + d) % n) for q in range(n)],
+                block, ("tm", "net"), [(a * n + q, b * n + (q ^ d)) for a, b in sections for q in range(n)]
             )
-            for d, block in enumerate(blocks_to_send)
+            for d, block in enumerate(outgoing, 1)
         ]
 
     opening = [state]
     out = None
     for r in range(1, tm):
-        state, *arrived = hand_over([state, *outgoing], r)
+        state = lax.ppermute(state, "tm", [(r - 1, r)])
+        arrived = swap(outgoing, [(r - 1, r)])
         before = []
         for s in range(steps):
             fix = r == 1 and s == 0
             if s > 0:
-                arrived = lax.all_to_all(outgoing, "net", split_axis=0, concat_axis=0, tiled=True)
+                arrived = swap(outgoing, [(0, 0), (r, r)] if r == 1 else [(r, r)])
             z = own(state, s)
             if s < steps - 1:
-                state, outgoing = join(z, s, fix, state, arrived, "stack", r)
+                state, *outgoing = join(z, s, fix, state, arrived, True, r)
                 before.append(state)
             elif r < tm - 1:
-                out, state, *outgoing = join(z, s, fix, state, arrived, "each", r, opening, before, out, steps)
+                out, state, *outgoing = join(z, s, fix, state, arrived, True, r, opening, before, out, steps)
             else:
-                (out,) = join(z, s, fix, state, arrived, "none", r, opening, before, out, steps)
+                (out,) = join(z, s, fix, state, arrived, False, r, opening, before, out, steps)
     return out
 
 

time: 29.7 us -> 26.7 us (0.90)
  Pallas kernels: 7.09 us -> 5.33 us
  waiting for transfers between devices: 12.9 us -> 11.4 us
  starting transfers between devices: 9.28 us -> 9.62 us
    all_to_all x1 -> x0, waiting for transfers between devices: 5.69 us -> none  [local(): lax.all_to_all(outgoing, 'net', split_axis=0, concat_axis=0, tiled=True)]
    ppermute x4 -> x7, starting transfers between devices: 5.17 us -> 9.62 us  [the longest x6 8.33 us: swap(): lax.ppermute(block, ('tm', 'net'), [(a * n + q, b * n + (q ^ d)) for a, b...]
    all_to_all x1 -> x0, starting transfers between devices: 4.11 us -> none  [local(): lax.all_to_all(outgoing, 'net', split_axis=0, concat_axis=0, tiled=True)]
    ppermute x4 -> x7, waiting for transfers between devices: 7.25 us -> 11.4 us  [the longest x6 6.89 us: swap(): lax.ppermute(block, ('tm', 'net'), [(a * n + q, b * n + (q ^ d)) for a, b...]
    pallas_call x1, Pallas kernels: 2.12 us -> 1.05 us  [local(): pl.pallas_call(second_kernel, out_shape=[f32((cols, table_rows)), whole]...]
    pallas_call x2, Pallas kernels: 3.21 us -> 2.52 us  [join(): pl.pallas_call(functools.partial(join_kernel, step, fix, send, section, f...]
  transfers between devices with their start and end apart: 5 -> 7, of which waited for: 5 -> 4; matrix products, arithmetic and copies ran while one was open for 0% -> 0% of each run, Pallas kernels for 6% -> 7%
where the time goes in v5:
time: 26.7 us; the launch traced here: 26.5 us
  waiting for transfers between devices  11.4 us (43%)
  starting transfers between devices  9.62 us (36%)
  Pallas kernels  5.33 us (20%)
    ppermute x6, starting transfers between devices, swap(): lax.ppermute(block, ('tm', 'net'), [(a * n + q, b * n + (q ^ d)) for a, b...  8.33 us
    ppermute x6, waiting for transfers between devices, swap(): lax.ppermute(block, ('tm', 'net'), [(a * n + q, b * n + (q ^ d)) for a, b...  6.89 us
    ppermute x1, waiting for transfers between devices, local(): state = lax.ppermute(state, 'tm', [(r - 1, r)])  4.46 us
    pallas_call x2, Pallas kernels, join(): pl.pallas_call(functools.partial(join_kernel, step, fix, send, section, f...  2.52 us
    pallas_call x2, Pallas kernels, own(): pl.pallas_call(functools.partial(own_kernel, step), out_shape=f32(whole.s...  1.76 us
    ppermute x1, starting transfers between devices, local(): state = lax.ppermute(state, 'tm', [(r - 1, r)])  1.29 us
    pallas_call x1, Pallas kernels, local(): pl.pallas_call(second_kernel, out_shape=[f32((cols, table_rows)), whole]...  1.05 us
  transfers between devices with their start and end apart: 7, of which 4 were waited for; matrix products, arithmetic and copies ran while one was open for 0% of the time, Pallas kernels for 7%

profile of v5, /device:TPU:4, one launch (start us, length us, event | category | flops | bytes accessed | tf_op | source)
XLA Modules:
  0.0 26.5 jit_solution(1854380695802197027)
XLA Ops:
  0.0 0.0 copy-start
  0.0 1.1 %shard_map.82 = (f32[192,8]{1,0:T(8,128)S(1)}, bf16[4,192,128]{2,1,0:T(8,128)(2,1)S(1)}, bf16[208,128]{1,0:T(8,128)(2,1)S(1)}, bf16[208,128]{1,0:T(8,128)(2,1)S(1)}, bf16[208,128]{1,0:T(8,128)(2,1)S(1)}) custom-call(bf16[2,4,3,128,128]{4,3,2,1,0:T(8,128)(2,1)} %refs_11_.1, bf16[2,1,4,128,128]{4,3,2,1,0:T(8,128)(2,1)} %refs_1_.5, s32[2,4]{1,0:T(2,128)} %bitcast.2, ...), custom_call_target="tpu_custom_call" | custom-call | tf_op jit(solution)/shard_map/pallas_call | solution.py:253
  1.1 1.3 %collective-permute-start = (bf16[4,192,128]{2,1,0:T(8,128)(2,1)S(1)}, bf16[4,192,128]{2,1,0:T(8,128)(2,1)S(1)}, u32[]{:S(2)}, u32[]{:S(2)}) collective-permute-start(bf16[4,192,128]{2,1,0:T(8,128)(2,1)S(1)} %get-tuple-element.14.refs_10_), channel_id=1, source_target_pairs={{0,16},{1,17},{2,18},{3,19},{4,20},{5,21},{6,22},{7,23},{8,24},{9,... | collective-permute-start | bytes 589832 | tf_op jit(solution)/shard_map/ppermute | solution.py:330
  2.4 1.3 %collective-permute-start.1 = (bf16[208,128]{1,0:T(8,128)(2,1)S(1)}, bf16[208,128]{1,0:T(8,128)(2,1)S(1)}, u32[]{:S(2)}, u32[]{:S(2)}) collective-permute-start(bf16[208,128]{1,0:T(8,128)(2,1)S(1)} %get-tuple-element.16), channel_id=1, source_target_pairs={{0,20},{4,16},{8,28},{12,24},{1,21},{5,17},{9,29},{13,25},{2,22},{... | collective-permute-start | bytes 159752 | tf_op jit(solution)/shard_map/ppermute | solution.py:321
  3.7 1.3 %collective-permute-start.2 = (bf16[208,128]{1,0:T(8,128)(2,1)S(1)}, bf16[208,128]{1,0:T(8,128)(2,1)S(1)}, u32[]{:S(2)}, u32[]{:S(2)}) collective-permute-start(bf16[208,128]{1,0:T(8,128)(2,1)S(1)} %get-tuple-element.17), channel_id=1, source_target_pairs={{0,24},{4,28},{8,16},{12,20},{1,25},{5,29},{9,17},{13,21},{2,26},{... | collective-permute-start | bytes 159752 | tf_op jit(solution)/shard_map/ppermute | solution.py:321
  5.0 0.0 copy-start.2
  5.0 1.3 %collective-permute-start.3 = (bf16[208,128]{1,0:T(8,128)(2,1)S(1)}, bf16[208,128]{1,0:T(8,128)(2,1)S(1)}, u32[]{:S(2)}, u32[]{:S(2)}) collective-permute-start(bf16[208,128]{1,0:T(8,128)(2,1)S(1)} %get-tuple-element.18), channel_id=1, source_target_pairs={{0,28},{4,24},{8,20},{12,16},{1,29},{5,25},{9,21},{13,17},{2,30},{... | collective-permute-start | bytes 159752 | tf_op jit(solution)/shard_map/ppermute | solution.py:321
  6.3 4.5 %collective-permute-done.state_ref.refs_6_ = bf16[4,192,128]{2,1,0:T(8,128)(2,1)S(1)} collective-permute-done((bf16[4,192,128]{2,1,0:T(8,128)(2,1)S(1)}, bf16[4,192,128]{2,1,0:T(8,128)(2,1)S(1)}, u32[]{:S(2)}, u32[]{:S(2)}) %collective-permute-start) | collective-permute-done | bytes 196640 | tf_op jit(solution)/shard_map/ppermute | solution.py:330
  10.7 0.0 copy-done
  10.7 0.0 copy-done.2
  10.7 0.0 copy-start.1
  10.7 0.0 copy-start.3
  10.8 0.0 copy-start.4
  10.8 0.0 copy-start.5
  10.8 0.9 %shard_map.83.refs_0_ = f32[4,192,128]{2,1,0:T(8,128)S(1)} custom-call(bf16[4,192,128]{2,1,0:T(8,128)(2,1)S(1)} %collective-permute-done.state_ref.refs_6_, bf16[2,4,3,128,128]{4,3,2,1,0:T(8,128)(2,1)S(1)} %copy-done, s32[2,4]{1,0:T(2,128)S(1)} %bitcast.3, f32[192,8]{1,0:T(8,128)S(1)} %get-tuple-element.15.table_ref.refs_5_), custom_call_target="tpu_custom_call" | custom-call | tf_op jit(solution)/shard_map/pallas_call | solution.py:271
  11.7 0.0 collective-permute-done.1.refs_7_
  11.7 3.3 %collective-permute-done.2.refs_8_ = bf16[208,128]{1,0:T(8,128)(2,1)S(1)} collective-permute-done((bf16[208,128]{1,0:T(8,128)(2,1)S(1)}, bf16[208,128]{1,0:T(8,128)(2,1)S(1)}, u32[]{:S(2)}, u32[]{:S(2)}) %collective-permute-start.2) | collective-permute-done | bytes 53280 | tf_op jit(solution)/shard_map/ppermute | solution.py:321
  15.0 0.0 collective-permute-done.3.refs_9_
  15.0 0.0 copy-done.1
  15.0 0.0 copy-done.3
  15.0 0.0 copy-done.4
  15.0 0.0 copy-done.5
  15.0 0.9 %shard_map.84 = (bf16[4,192,128]{2,1,0:T(8,128)(2,1)S(1)}, bf16[192,128]{1,0:T(8,128)(2,1)S(1)}, bf16[192,128]{1,0:T(8,128)(2,1)S(1)}, bf16[192,128]{1,0:T(8,128)(2,1)S(1)}) custom-call(f32[4,192,128]{2,1,0:T(8,128)S(1)} %shard_map.83.refs_0_, bf16[2,1,4,128,128]{4,3,2,1,0:T(8,128)(2,1)S(1)} %copy-done.1, s32[1,4]{1,0:T(1,128)S(1)} %copy-done.3, ...), custom_call_target="tpu_custom_call" | custom-call | tf_op jit(solution)/shard_map/pallas_call | solution.py:309
  16.0 1.2 %collective-permute-start.4 = (bf16[192,128]{1,0:T(8,128)(2,1)S(1)}, bf16[192,128]{1,0:T(8,128)(2,1)S(1)}, u32[]{:S(2)}, u32[]{:S(2)}) collective-permute-start(bf16[192,128]{1,0:T(8,128)(2,1)S(1)} %get-tuple-element.20), channel_id=1, source_target_pairs={{0,4},{4,0},{8,12},{12,8},{16,20},{20,16},{24,28},{28,24},{1,5},{5... | collective-permute-start | bytes 147464 | tf_op jit(solution)/shard_map/ppermute | solution.py:321
  17.2 1.8 %collective-permute-start.5 = (bf16[192,128]{1,0:T(8,128)(2,1)S(1)}, bf16[192,128]{1,0:T(8,128)(2,1)S(1)}, u32[]{:S(2)}, u32[]{:S(2)}) collective-permute-start(bf16[192,128]{1,0:T(8,128)(2,1)S(1)} %get-tuple-element.21), channel_id=1, source_target_pairs={{0,8},{4,12},{8,0},{12,4},{16,24},{20,28},{24,16},{28,20},{1,9},{5... | collective-permute-start | bytes 147464 | tf_op jit(solution)/shard_map/ppermute | solution.py:321
  19.0 1.4 %collective-permute-start.6 = (bf16[192,128]{1,0:T(8,128)(2,1)S(1)}, bf16[192,128]{1,0:T(8,128)(2,1)S(1)}, u32[]{:S(2)}, u32[]{:S(2)}) collective-permute-start(bf16[192,128]{1,0:T(8,128)(2,1)S(1)} %get-tuple-element.22), channel_id=1, source_target_pairs={{0,12},{4,8},{8,4},{12,0},{16,28},{20,24},{24,20},{28,16},{1,13},{... | collective-permute-start | bytes 147464 | tf_op jit(solution)/shard_map/ppermute | solution.py:321
  20.5 0.9 %shard_map.85.refs_0_ = f32[4,192,128]{2,1,0:T(8,128)S(1)} custom-call(bf16[4,192,128]{2,1,0:T(8,128)(2,1)S(1)} %get-tuple-element.19.state_ref.refs_6_.refs_13_, bf16[2,4,3,128,128]{4,3,2,1,0:T(8,128)(2,1)S(1)} %copy-done, s32[2,4]{1,0:T(2,128)S(1)} %bitcast.4, f32[192,8]{1,0:T(8,128)S(1)} %get-tuple-element.15.table_ref.refs_5_), custom_call_target="tpu_custom_call" | custom-call | tf_op jit(solution)/shard_map/pallas_call | solution.py:271
  21.3 0.0 collective-permute-done.4.refs_7_
  21.3 1.8 %collective-permute-done.5.refs_8_ = bf16[192,128]{1,0:T(8,128)(2,1)S(1)} collective-permute-done((bf16[192,128]{1,0:T(8,128)(2,1)S(1)}, bf16[192,128]{1,0:T(8,128)(2,1)S(1)}, u32[]{:S(2)}, u32[]{:S(2)}) %collective-permute-start.5) | collective-permute-done | bytes 49184 | tf_op jit(solution)/shard_map/ppermute | solution.py:321
  23.1 1.8 %collective-permute-done.6.refs_9_ = bf16[192,128]{1,0:T(8,128)(2,1)S(1)} collective-permute-done((bf16[192,128]{1,0:T(8,128)(2,1)S(1)}, bf16[192,128]{1,0:T(8,128)(2,1)S(1)}, u32[]{:S(2)}, u32[]{:S(2)}) %collective-permute-start.6) | collective-permute-done | bytes 49184 | tf_op jit(solution)/shard_map/ppermute | solution.py:321
  24.9 1.6 %shard_map.86 = bf16[2,192,512]{2,1,0:T(8,128)(2,1)} custom-call(f32[4,192,128]{2,1,0:T(8,128)S(1)} %shard_map.85.refs_0_, bf16[2,1,4,128,128]{4,3,2,1,0:T(8,128)(2,1)S(1)} %copy-done.1, s32[1,4]{1,0:T(1,128)S(1)} %copy-done.3, s32[1,4]{1,0:T(1,128)S(1)} %copy-done.4, s32[1,4]{1,0:T(1,128)S(1)} %copy-done.5, ...), custom_call_target="tpu_custom_call" | custom-call | tf_op jit(solution)/shard_map/pallas_call | solution.py:309
Async XLA Ops:
  0.0 10.7 %copy-start = (bf16[2,4,3,128,128]{4,3,2,1,0:T(8,128)(2,1)S(1)}, bf16[2,4,3,128,128]{4,3,2,1,0:T(8,128)(2,1)}, u32[]{:S(2)}) copy-start(bf16[2,4,3,128,128]{4,3,2,1,0:T(8,128)(2,1)} %refs_11_.1) | copy-start | bytes 2359300
  1.1 9.7 %collective-permute-start = (bf16[4,192,128]{2,1,0:T(8,128)(2,1)S(1)}, bf16[4,192,128]{2,1,0:T(8,128)(2,1)S(1)}, u32[]{:S(2)}, u32[]{:S(2)}) collective-permute-start(bf16[4,192,128]{2,1,0:T(8,128)(2,1)S(1)} %get-tuple-element.14.refs_10_), channel_id=1, source_target_pairs={{0,16},{1,17},{2,18},{3,19},{4,20},{5,21},{6,22},{7,23},{8,24},{9,... | collective-permute-start | bytes 589832 | tf_op jit(solution)/shard_map/ppermute | solution.py:330
  2.4 9.3 %collective-permute-start.1 = (bf16[208,128]{1,0:T(8,128)(2,1)S(1)}, bf16[208,128]{1,0:T(8,128)(2,1)S(1)}, u32[]{:S(2)}, u32[]{:S(2)}) collective-permute-start(bf16[208,128]{1,0:T(8,128)(2,1)S(1)} %get-tuple-element.16), channel_id=1, source_target_pairs={{0,20},{4,16},{8,28},{12,24},{1,21},{5,17},{9,29},{13,25},{2,22},{... | collective-permute-start | bytes 159752 | tf_op jit(solution)/shard_map/ppermute | solution.py:321
  3.7 11.3 %collective-permute-start.2 = (bf16[208,128]{1,0:T(8,128)(2,1)S(1)}, bf16[208,128]{1,0:T(8,128)(2,1)S(1)}, u32[]{:S(2)}, u32[]{:S(2)}) collective-permute-start(bf16[208,128]{1,0:T(8,128)(2,1)S(1)} %get-tuple-element.17), channel_id=1, source_target_pairs={{0,24},{4,28},{8,16},{12,20},{1,25},{5,29},{9,17},{13,21},{2,26},{... | collective-permute-start | bytes 159752 | tf_op jit(solution)/shard_map/ppermute | solution.py:321
  5.0 5.8 %copy-start.2 = (s32[4,2]{0,1:T(2,128)S(1)}, s32[4,2]{0,1:T(2,128)}, u32[]{:S(2)}) copy-start(s32[4,2]{0,1:T(2,128)} %param.9) | copy-start | bytes 100
  5.0 10.0 %collective-permute-start.3 = (bf16[208,128]{1,0:T(8,128)(2,1)S(1)}, bf16[208,128]{1,0:T(8,128)(2,1)S(1)}, u32[]{:S(2)}, u32[]{:S(2)}) collective-permute-start(bf16[208,128]{1,0:T(8,128)(2,1)S(1)} %get-tuple-element.18), channel_id=1, source_target_pairs={{0,28},{4,24},{8,20},{12,16},{1,29},{5,25},{9,21},{13,17},{2,30},{... | collective-permute-start | bytes 159752 | tf_op jit(solution)/shard_map/ppermute | solution.py:321
  10.7 4.3 %copy-start.1 = (bf16[2,1,4,128,128]{4,3,2,1,0:T(8,128)(2,1)S(1)}, bf16[2,1,4,128,128]{4,3,2,1,0:T(8,128)(2,1)}, u32[]{:S(2)}) copy-start(bf16[2,1,4,128,128]{4,3,2,1,0:T(8,128)(2,1)} %refs_1_.5) | copy-start | bytes 786436
  10.7 4.3 %copy-start.3 = (s32[1,4]{1,0:T(1,128)S(1)}, s32[1,4]{1,0:T(1,128)}, u32[]{:S(2)}) copy-start(s32[1,4]{1,0:T(1,128)} %refs_2_.3) | copy-start | bytes 52
  10.8 4.3 %copy-start.4 = (s32[1,4]{1,0:T(1,128)S(1)}, s32[1,4]{1,0:T(1,128)}, u32[]{:S(2)}) copy-start(s32[1,4]{1,0:T(1,128)} %refs_3_.5) | copy-start | bytes 52
  10.8 4.3 %copy-start.5 = (s32[1,4]{1,0:T(1,128)S(1)}, s32[1,4]{1,0:T(1,128)}, u32[]{:S(2)}) copy-start(s32[1,4]{1,0:T(1,128)} %refs_4_.5) | copy-start | bytes 52
  16.0 5.3 %collective-permute-start.4 = (bf16[192,128]{1,0:T(8,128)(2,1)S(1)}, bf16[192,128]{1,0:T(8,128)(2,1)S(1)}, u32[]{:S(2)}, u32[]{:S(2)}) collective-permute-start(bf16[192,128]{1,0:T(8,128)(2,1)S(1)} %get-tuple-element.20), channel_id=1, source_target_pairs={{0,4},{4,0},{8,12},{12,8},{16,20},{20,16},{24,28},{28,24},{1,5},{5... | collective-permute-start | bytes 147464 | tf_op jit(solution)/shard_map/ppermute | solution.py:321
  17.2 5.9 %collective-permute-start.5 = (bf16[192,128]{1,0:T(8,128)(2,1)S(1)}, bf16[192,128]{1,0:T(8,128)(2,1)S(1)}, u32[]{:S(2)}, u32[]{:S(2)}) collective-permute-start(bf16[192,128]{1,0:T(8,128)(2,1)S(1)} %get-tuple-element.21), channel_id=1, source_target_pairs={{0,8},{4,12},{8,0},{12,4},{16,24},{20,28},{24,16},{28,20},{1,9},{5... | collective-permute-start | bytes 147464 | tf_op jit(solution)/shard_map/ppermute | solution.py:321
  19.0 5.9 %collective-permute-start.6 = (bf16[192,128]{1,0:T(8,128)(2,1)S(1)}, bf16[192,128]{1,0:T(8,128)(2,1)S(1)}, u32[]{:S(2)}, u32[]{:S(2)}) collective-permute-start(bf16[192,128]{1,0:T(8,128)(2,1)S(1)} %get-tuple-element.22), channel_id=1, source_target_pairs={{0,12},{4,8},{8,4},{12,0},{16,28},{20,24},{24,20},{28,16},{1,13},{... | collective-permute-start | bytes 147464 | tf_op jit(solution)/shard_map/ppermute | solution.py:321

commit v6 on v5

--- a/solution.py
+++ b/solution.py
@@ -317,18 +317,17 @@
         )(*arrays)
 
     def swap(outgoing, sections):
-        return [
-            lax.ppermute(
-                block, ("tm", "net"), [(a * n + q, b * n + (q ^ d)) for a, b in sections for q in range(n)]
-            )
-            for d, block in enumerate(outgoing, 1)
-        ]
+        arrived = {}
+        for d in reversed(range(1, n)):
+            pairs = [(a * n + q, b * n + (q ^ d)) for a, b in sections for q in range(n)]
+            arrived[d] = lax.ppermute(outgoing[d - 1], ("tm", "net"), pairs)
+        return [arrived[d] for d in range(1, n)]
 
     opening = [state]
     out = None
     for r in range(1, tm):
-        state = lax.ppermute(state, "tm", [(r - 1, r)])
-        arrived = swap(outgoing, [(r - 1, r)])
+        state = lax.ppermute(state, "tm", [(r - 1, r), (r, r - 1)])
+        arrived = swap(outgoing, [(r - 1, r), (r, r - 1)])
         before = []
         for s in range(steps):
             fix = r == 1 and s == 0

time: 26.7 us -> 27.7 us (1.037)
  the two profiles are of different devices: /device:TPU:4 before, /device:TPU:0 now
where the time goes in v6:
time: 27.7 us; the launch traced here: 27.5 us
  starting transfers between devices  11.5 us (42%)
  waiting for transfers between devices  9.29 us (34%)
  Pallas kernels  6.58 us (24%)
    ppermute x6, starting transfers between devices, swap(): arrived[d] = lax.ppermute(outgoing[d - 1], ('tm', 'net'), pairs)  9.51 us
    ppermute x6, waiting for transfers between devices, swap(): arrived[d] = lax.ppermute(outgoing[d - 1], ('tm', 'net'), pairs)  7.36 us
    pallas_call x2, Pallas kernels, join(): pl.pallas_call(functools.partial(join_kernel, step, fix, send, section, f...  2.77 us
    pallas_call x1, Pallas kernels, local(): pl.pallas_call(second_kernel, out_shape=[f32((cols, table_rows)), whole]...  2.05 us
    ppermute x1, starting transfers between devices, local(): state = lax.ppermute(state, 'tm', [(r - 1, r), (r, r - 1)])  2.04 us
    ppermute x1, waiting for transfers between devices, local(): state = lax.ppermute(state, 'tm', [(r - 1, r), (r, r - 1)])  1.93 us
    pallas_call x2, Pallas kernels, own(): pl.pallas_call(functools.partial(own_kernel, step), out_shape=f32(whole.s...  1.77 us
  transfers between devices with their start and end apart: 7, of which 4 were waited for; matrix products, arithmetic and copies ran while one was open for 0% of the time, Pallas kernels for 6%

profile of v6, /device:TPU:0, one launch (start us, length us, event | category | flops | bytes accessed | tf_op | source)
XLA Modules:
  0.0 27.5 jit_solution(4765953686609814336)
XLA Ops:
  0.0 0.0 copy-start
  0.0 2.0 %shard_map.82 = (f32[192,8]{1,0:T(8,128)S(1)}, bf16[4,192,128]{2,1,0:T(8,128)(2,1)S(1)}, bf16[208,128]{1,0:T(8,128)(2,1)S(1)}, bf16[208,128]{1,0:T(8,128)(2,1)S(1)}, bf16[208,128]{1,0:T(8,128)(2,1)S(1)}) custom-call(bf16[2,4,3,128,128]{4,3,2,1,0:T(8,128)(2,1)} %refs_11_.1, bf16[2,1,4,128,128]{4,3,2,1,0:T(8,128)(2,1)} %refs_1_.5, s32[2,4]{1,0:T(2,128)} %bitcast.2, ...), custom_call_target="tpu_custom_call" | custom-call | tf_op jit(solution)/shard_map/pallas_call | solution.py:253
  2.1 2.0 %collective-permute-start = (bf16[4,192,128]{2,1,0:T(8,128)(2,1)S(1)}, bf16[4,192,128]{2,1,0:T(8,128)(2,1)S(1)}, u32[]{:S(2)}, u32[]{:S(2)}) collective-permute-start(bf16[4,192,128]{2,1,0:T(8,128)(2,1)S(1)} %get-tuple-element.14.refs_10_), channel_id=1, source_target_pairs={{0,16},{16,0},{1,17},{17,1},{2,18},{18,2},{3,19},{19,3},{4,20},{20... | collective-permute-start | bytes 589832 | tf_op jit(solution)/shard_map/ppermute | solution.py:329
  4.1 2.5 %collective-permute-start.1 = (bf16[208,128]{1,0:T(8,128)(2,1)S(1)}, bf16[208,128]{1,0:T(8,128)(2,1)S(1)}, u32[]{:S(2)}, u32[]{:S(2)}) collective-permute-start(bf16[208,128]{1,0:T(8,128)(2,1)S(1)} %get-tuple-element.16), channel_id=1, source_target_pairs={{0,20},{4,16},{8,28},{12,24},{16,4},{20,0},{24,12},{28,8},{1,21},{... | collective-permute-start | bytes 159752 | tf_op jit(solution)/shard_map/ppermute | solution.py:323
  6.6 2.6 %collective-permute-start.2 = (bf16[208,128]{1,0:T(8,128)(2,1)S(1)}, bf16[208,128]{1,0:T(8,128)(2,1)S(1)}, u32[]{:S(2)}, u32[]{:S(2)}) collective-permute-start(bf16[208,128]{1,0:T(8,128)(2,1)S(1)} %get-tuple-element.17), channel_id=1, source_target_pairs={{0,24},{4,28},{8,16},{12,20},{16,8},{20,12},{24,0},{28,4},{1,25},{... | collective-permute-start | bytes 159752 | tf_op jit(solution)/shard_map/ppermute | solution.py:323
  9.2 0.0 copy-start.2
  9.2 0.0 collective-permute-start.3
  9.2 1.9 %collective-permute-done.state_ref.refs_6_ = bf16[4,192,128]{2,1,0:T(8,128)(2,1)S(1)} collective-permute-done((bf16[4,192,128]{2,1,0:T(8,128)(2,1)S(1)}, bf16[4,192,128]{2,1,0:T(8,128)(2,1)S(1)}, u32[]{:S(2)}, u32[]{:S(2)}) %collective-permute-start) | collective-permute-done | bytes 196640 | tf_op jit(solution)/shard_map/ppermute | solution.py:329
  11.1 0.0 copy-done
  11.1 0.0 copy-done.2
  11.1 0.0 copy-start.1
  11.1 0.0 copy-start.3
  11.1 0.0 copy-start.4
  11.1 0.0 copy-start.5
  11.1 0.9 %shard_map.83.refs_0_ = f32[4,192,128]{2,1,0:T(8,128)S(1)} custom-call(bf16[4,192,128]{2,1,0:T(8,128)(2,1)S(1)} %collective-permute-done.state_ref.refs_6_, bf16[2,4,3,128,128]{4,3,2,1,0:T(8,128)(2,1)S(1)} %copy-done, s32[2,4]{1,0:T(2,128)S(1)} %bitcast.3, f32[192,8]{1,0:T(8,128)S(1)} %get-tuple-element.15.table_ref.refs_5_), custom_call_target="tpu_custom_call" | custom-call | tf_op jit(solution)/shard_map/pallas_call | solution.py:271
  12.0 0.0 collective-permute-done.1.refs_7_
  12.0 0.8 %collective-permute-done.2.refs_8_ = bf16[208,128]{1,0:T(8,128)(2,1)S(1)} collective-permute-done((bf16[208,128]{1,0:T(8,128)(2,1)S(1)}, bf16[208,128]{1,0:T(8,128)(2,1)S(1)}, u32[]{:S(2)}, u32[]{:S(2)}) %collective-permute-start.2) | collective-permute-done | bytes 53280 | tf_op jit(solution)/shard_map/ppermute | solution.py:323
  12.9 3.1 %collective-permute-done.3.refs_9_ = bf16[208,128]{1,0:T(8,128)(2,1)S(1)} collective-permute-done((bf16[208,128]{1,0:T(8,128)(2,1)S(1)}, bf16[208,128]{1,0:T(8,128)(2,1)S(1)}, u32[]{:S(2)}, u32[]{:S(2)}) %collective-permute-start.3) | collective-permute-done | bytes 53280 | tf_op jit(solution)/shard_map/ppermute | solution.py:323
  16.0 0.0 copy-done.1
  16.0 0.0 copy-done.3
  16.0 0.0 copy-done.4
  16.0 0.0 copy-done.5
  16.0 1.0 %shard_map.84 = (bf16[4,192,128]{2,1,0:T(8,128)(2,1)S(1)}, bf16[192,128]{1,0:T(8,128)(2,1)S(1)}, bf16[192,128]{1,0:T(8,128)(2,1)S(1)}, bf16[192,128]{1,0:T(8,128)(2,1)S(1)}) custom-call(f32[4,192,128]{2,1,0:T(8,128)S(1)} %shard_map.83.refs_0_, bf16[2,1,4,128,128]{4,3,2,1,0:T(8,128)(2,1)S(1)} %copy-done.1, s32[1,4]{1,0:T(1,128)S(1)} %copy-done.3, ...), custom_call_target="tpu_custom_call" | custom-call | tf_op jit(solution)/shard_map/pallas_call | solution.py:309
  17.0 0.1 collective-permute-start.4
  17.1 2.8 %collective-permute-start.5 = (bf16[192,128]{1,0:T(8,128)(2,1)S(1)}, bf16[192,128]{1,0:T(8,128)(2,1)S(1)}, u32[]{:S(2)}, u32[]{:S(2)}) collective-permute-start(bf16[192,128]{1,0:T(8,128)(2,1)S(1)} %get-tuple-element.21), channel_id=1, source_target_pairs={{0,8},{4,12},{8,0},{12,4},{16,24},{20,28},{24,16},{28,20},{1,9},{5... | collective-permute-start | bytes 147464 | tf_op jit(solution)/shard_map/ppermute | solution.py:323
  19.8 1.6 %collective-permute-start.6 = (bf16[192,128]{1,0:T(8,128)(2,1)S(1)}, bf16[192,128]{1,0:T(8,128)(2,1)S(1)}, u32[]{:S(2)}, u32[]{:S(2)}) collective-permute-start(bf16[192,128]{1,0:T(8,128)(2,1)S(1)} %get-tuple-element.22), channel_id=1, source_target_pairs={{0,12},{4,8},{8,4},{12,0},{16,28},{20,24},{24,20},{28,16},{1,13},{... | collective-permute-start | bytes 147464 | tf_op jit(solution)/shard_map/ppermute | solution.py:323
  21.4 0.9 %shard_map.85.refs_0_ = f32[4,192,128]{2,1,0:T(8,128)S(1)} custom-call(bf16[4,192,128]{2,1,0:T(8,128)(2,1)S(1)} %get-tuple-element.19.state_ref.refs_6_.refs_13_, bf16[2,4,3,128,128]{4,3,2,1,0:T(8,128)(2,1)S(1)} %copy-done, s32[2,4]{1,0:T(2,128)S(1)} %bitcast.4, f32[192,8]{1,0:T(8,128)S(1)} %get-tuple-element.15.table_ref.refs_5_), custom_call_target="tpu_custom_call" | custom-call | tf_op jit(solution)/shard_map/pallas_call | solution.py:271
  22.3 0.0 collective-permute-done.4.refs_7_
  22.3 0.0 collective-permute-done.5.refs_8_
  22.3 3.4 %collective-permute-done.6.refs_9_ = bf16[192,128]{1,0:T(8,128)(2,1)S(1)} collective-permute-done((bf16[192,128]{1,0:T(8,128)(2,1)S(1)}, bf16[192,128]{1,0:T(8,128)(2,1)S(1)}, u32[]{:S(2)}, u32[]{:S(2)}) %collective-permute-start.6) | collective-permute-done | bytes 49184 | tf_op jit(solution)/shard_map/ppermute | solution.py:323
  25.7 1.8 %shard_map.86 = bf16[2,192,512]{2,1,0:T(8,128)(2,1)} custom-call(f32[4,192,128]{2,1,0:T(8,128)S(1)} %shard_map.85.refs_0_, bf16[2,1,4,128,128]{4,3,2,1,0:T(8,128)(2,1)S(1)} %copy-done.1, s32[1,4]{1,0:T(1,128)S(1)} %copy-done.3, s32[1,4]{1,0:T(1,128)S(1)} %copy-done.4, s32[1,4]{1,0:T(1,128)S(1)} %copy-done.5, ...), custom_call_target="tpu_custom_call" | custom-call | tf_op jit(solution)/shard_map/pallas_call | solution.py:309
Async XLA Ops:
  0.0 11.1 %copy-start = (bf16[2,4,3,128,128]{4,3,2,1,0:T(8,128)(2,1)S(1)}, bf16[2,4,3,128,128]{4,3,2,1,0:T(8,128)(2,1)}, u32[]{:S(2)}) copy-start(bf16[2,4,3,128,128]{4,3,2,1,0:T(8,128)(2,1)} %refs_11_.1) | copy-start | bytes 2359300
  2.1 9.0 %collective-permute-start = (bf16[4,192,128]{2,1,0:T(8,128)(2,1)S(1)}, bf16[4,192,128]{2,1,0:T(8,128)(2,1)S(1)}, u32[]{:S(2)}, u32[]{:S(2)}) collective-permute-start(bf16[4,192,128]{2,1,0:T(8,128)(2,1)S(1)} %get-tuple-element.14.refs_10_), channel_id=1, source_target_pairs={{0,16},{16,0},{1,17},{17,1},{2,18},{18,2},{3,19},{19,3},{4,20},{20... | collective-permute-start | bytes 589832 | tf_op jit(solution)/shard_map/ppermute | solution.py:329
  4.1 7.9 %collective-permute-start.1 = (bf16[208,128]{1,0:T(8,128)(2,1)S(1)}, bf16[208,128]{1,0:T(8,128)(2,1)S(1)}, u32[]{:S(2)}, u32[]{:S(2)}) collective-permute-start(bf16[208,128]{1,0:T(8,128)(2,1)S(1)} %get-tuple-element.16), channel_id=1, source_target_pairs={{0,20},{4,16},{8,28},{12,24},{16,4},{20,0},{24,12},{28,8},{1,21},{... | collective-permute-start | bytes 159752 | tf_op jit(solution)/shard_map/ppermute | solution.py:323
  6.6 6.3 %collective-permute-start.2 = (bf16[208,128]{1,0:T(8,128)(2,1)S(1)}, bf16[208,128]{1,0:T(8,128)(2,1)S(1)}, u32[]{:S(2)}, u32[]{:S(2)}) collective-permute-start(bf16[208,128]{1,0:T(8,128)(2,1)S(1)} %get-tuple-element.17), channel_id=1, source_target_pairs={{0,24},{4,28},{8,16},{12,20},{16,8},{20,12},{24,0},{28,4},{1,25},{... | collective-permute-start | bytes 159752 | tf_op jit(solution)/shard_map/ppermute | solution.py:323
  9.2 1.9 %copy-start.2 = (s32[4,2]{0,1:T(2,128)S(1)}, s32[4,2]{0,1:T(2,128)}, u32[]{:S(2)}) copy-start(s32[4,2]{0,1:T(2,128)} %param.9) | copy-start | bytes 100
  9.2 6.8 %collective-permute-start.3 = (bf16[208,128]{1,0:T(8,128)(2,1)S(1)}, bf16[208,128]{1,0:T(8,128)(2,1)S(1)}, u32[]{:S(2)}, u32[]{:S(2)}) collective-permute-start(bf16[208,128]{1,0:T(8,128)(2,1)S(1)} %get-tuple-element.18), channel_id=1, source_target_pairs={{0,28},{4,24},{8,20},{12,16},{16,12},{20,8},{24,4},{28,0},{1,29},{... | collective-permute-start | bytes 159752 | tf_op jit(solution)/shard_map/ppermute | solution.py:323
  11.1 4.9 %copy-start.1 = (bf16[2,1,4,128,128]{4,3,2,1,0:T(8,128)(2,1)S(1)}, bf16[2,1,4,128,128]{4,3,2,1,0:T(8,128)(2,1)}, u32[]{:S(2)}) copy-start(bf16[2,1,4,128,128]{4,3,2,1,0:T(8,128)(2,1)} %refs_1_.5) | copy-start | bytes 786436
  11.1 4.9 %copy-start.3 = (s32[1,4]{1,0:T(1,128)S(1)}, s32[1,4]{1,0:T(1,128)}, u32[]{:S(2)}) copy-start(s32[1,4]{1,0:T(1,128)} %refs_2_.3) | copy-start | bytes 52
  11.1 4.9 %copy-start.4 = (s32[1,4]{1,0:T(1,128)S(1)}, s32[1,4]{1,0:T(1,128)}, u32[]{:S(2)}) copy-start(s32[1,4]{1,0:T(1,128)} %refs_3_.5) | copy-start | bytes 52
  11.1 4.9 %copy-start.5 = (s32[1,4]{1,0:T(1,128)S(1)}, s32[1,4]{1,0:T(1,128)}, u32[]{:S(2)}) copy-start(s32[1,4]{1,0:T(1,128)} %refs_4_.5) | copy-start | bytes 52
  17.0 5.3 %collective-permute-start.4 = (bf16[192,128]{1,0:T(8,128)(2,1)S(1)}, bf16[192,128]{1,0:T(8,128)(2,1)S(1)}, u32[]{:S(2)}, u32[]{:S(2)}) collective-permute-start(bf16[192,128]{1,0:T(8,128)(2,1)S(1)} %get-tuple-element.20), channel_id=1, source_target_pairs={{0,4},{4,0},{8,12},{12,8},{16,20},{20,16},{24,28},{28,24},{1,5},{5... | collective-permute-start | bytes 147464 | tf_op jit(solution)/shard_map/ppermute | solution.py:323
  17.1 5.3 %collective-permute-start.5 = (bf16[192,128]{1,0:T(8,128)(2,1)S(1)}, bf16[192,128]{1,0:T(8,128)(2,1)S(1)}, u32[]{:S(2)}, u32[]{:S(2)}) collective-permute-start(bf16[192,128]{1,0:T(8,128)(2,1)S(1)} %get-tuple-element.21), channel_id=1, source_target_pairs={{0,8},{4,12},{8,0},{12,4},{16,24},{20,28},{24,16},{28,20},{1,9},{5... | collective-permute-start | bytes 147464 | tf_op jit(solution)/shard_map/ppermute | solution.py:323
  19.8 5.9 %collective-permute-start.6 = (bf16[192,128]{1,0:T(8,128)(2,1)S(1)}, bf16[192,128]{1,0:T(8,128)(2,1)S(1)}, u32[]{:S(2)}, u32[]{:S(2)}) collective-permute-start(bf16[192,128]{1,0:T(8,128)(2,1)S(1)} %get-tuple-element.22), channel_id=1, source_target_pairs={{0,12},{4,8},{8,4},{12,0},{16,28},{20,24},{24,20},{28,16},{1,13},{... | collective-permute-start | bytes 147464 | tf_op jit(solution)/shard_map/ppermute | solution.py:323

commit v7 on v6

--- a/solution.py
+++ b/solution.py
@@ -121,8 +121,10 @@
         state_ref[...] = z_ref[...].astype(state_ref.dtype)
         for d in range(1, n):
             outgoing[d - 1][pl.ds(0, cols)] = state_ref[send_ref[0, me ^ d]]
-            row = table_row(send_ref, me ^ d, width).astype(state_ref.dtype)
-            outgoing[d - 1][pl.ds(cols, ROWS)] = jnp.broadcast_to(row, (ROWS, width))
+
+    for d in range(1, n):
+        row = table_row(send_ref, me ^ d, width).astype(state_ref.dtype)
+        outgoing[d - 1][pl.ds(cols, ROWS)] = jnp.broadcast_to(row, (ROWS, width))
 
 
 def write_start(states, first, out_ref, sems):
@@ -144,7 +146,7 @@
         z_ref[i] = own_sum(i, state_ref, jac_ref.at[step], cols_ref, table, step)
 
 
-def first_states(states, jac_ref, iface_ref, cols_ref, send_ref, recv_ref, live_ref, table_ref, arrived, made_ref, z_ref):
+def first_states(states, jac_ref, iface_ref, cols_ref, send_ref, recv_ref, live_ref, table_ref, handed, made_ref, z_ref):
     n = lax.axis_size("net")
     blocks, cols, width = z_ref.shape
     table = table_ref[...]
@@ -156,7 +158,7 @@
     made_ref[0] = z_ref[...].astype(made_ref.dtype)
     me = lax.axis_index("net")
     rows = [table_row(send_ref, me, width)]
-    rows += [block[0:1].astype(jnp.float32) for block in arrived]
+    rows += [block[cols : cols + 1].astype(jnp.float32) for block in handed]
     keep = kept(table, rows)[:, 0:1]
     for i in range(blocks):
         made_ref[1, i] = jnp.where(keep > 0.0, states[0][i], jnp.zeros_like(states[0][i]))
@@ -177,6 +179,7 @@
         if firsts:
             made_ref = refs.pop()
             opening, refs = refs[:firsts], refs[firsts:]
+            handed, refs = refs[: n - 1], refs[n - 1 :]
             jac_ref, cols_ref = refs.pop(0), refs.pop(0)
         before, refs = refs[: store - 1], refs[store - 1 :]
         if not firsts:
@@ -214,20 +217,12 @@
         pl.when(tm == section)(join)
     else:
         join()
-    if fix:
-
-        @pl.when(tm == 0)
-        def _():
-            for d in range(1, n):
-                row = table_row(send_ref, me ^ d, width).astype(state_ref.dtype)
-                outgoing[d - 1][pl.ds(0, ROWS)] = jnp.broadcast_to(row, (ROWS, width))
-
     if firsts:
 
         @pl.when(tm == 0)
         def _():
             made = first_states(
-                opening, jac_ref, iface_ref, cols_ref, send_ref, recv_ref, live_ref, table_ref, arrived, made_ref, acc_ref
+                opening, jac_ref, iface_ref, cols_ref, send_ref, recv_ref, live_ref, table_ref, handed, made_ref, acc_ref
             )
             for copy in write_start(made, 0, out_ref, sems):
                 copy.wait()
@@ -287,8 +282,8 @@
         out_specs = []
         if store:
             if out is None:
-                arrays += [*opening, jac, near]
-                specs += [VMEM] * len(opening) + [VMEM, SMEM]
+                arrays += [*opening, *handed, jac, near]
+                specs += [VMEM] * (len(opening) + n - 1) + [VMEM, SMEM]
             arrays += before
             specs += [VMEM] * len(before)
             if out is not None:
@@ -328,11 +323,13 @@
     for r in range(1, tm):
         state = lax.ppermute(state, "tm", [(r - 1, r), (r, r - 1)])
         arrived = swap(outgoing, [(r - 1, r), (r, r - 1)])
+        if r == 1:
+            handed = arrived
         before = []
         for s in range(steps):
             fix = r == 1 and s == 0
             if s > 0:
-                arrived = swap(outgoing, [(0, 0), (r, r)] if r == 1 else [(r, r)])
+                arrived = swap(outgoing, [(r, r)])
             z = own(state, s)
             if s < steps - 1:
                 state, *outgoing = join(z, s, fix, state, arrived, True, r)

time: 27.7 us -> 30.7 us (1.11)
  the two profiles are of different devices: /device:TPU:0 before, /device:TPU:4 now
where the time goes in v7:
time: 30.7 us; the launch traced here: 30.5 us
  starting transfers between devices  16.9 us (55%)
  waiting for transfers between devices  8.1 us (26%)
  Pallas kernels  5.37 us (17%)
    ppermute x6, starting transfers between devices, swap(): arrived[d] = lax.ppermute(outgoing[d - 1], ('tm', 'net'), pairs)  16.8 us
    ppermute x6, waiting for transfers between devices, swap(): arrived[d] = lax.ppermute(outgoing[d - 1], ('tm', 'net'), pairs)  6.5 us
    pallas_call x2, Pallas kernels, join(): pl.pallas_call(functools.partial(join_kernel, step, fix, send, section, f...  2.52 us
    pallas_call x2, Pallas kernels, own(): pl.pallas_call(functools.partial(own_kernel, step), out_shape=f32(whole.s...  1.78 us
    ppermute x1, waiting for transfers between devices, local(): state = lax.ppermute(state, 'tm', [(r - 1, r), (r, r - 1)])  1.6 us
    pallas_call x1, Pallas kernels, local(): pl.pallas_call(second_kernel, out_shape=[f32((cols, table_rows)), whole]...  1.06 us
  transfers between devices with their start and end apart: 7, of which 4 were waited for; matrix products, arithmetic and copies ran while one was open for 0% of the time, Pallas kernels for 6%

profile of v7, /device:TPU:4, one launch (start us, length us, event | category | flops | bytes accessed | tf_op | source)
XLA Modules:
  0.0 30.5 jit_solution(1807455795146106124)
XLA Ops:
  0.0 0.0 copy-start
  0.0 1.1 %shard_map.82 = (f32[192,8]{1,0:T(8,128)S(1)}, bf16[4,192,128]{2,1,0:T(8,128)(2,1)S(1)}, bf16[208,128]{1,0:T(8,128)(2,1)S(1)}, bf16[208,128]{1,0:T(8,128)(2,1)S(1)}, bf16[208,128]{1,0:T(8,128)(2,1)S(1)}) custom-call(bf16[2,4,3,128,128]{4,3,2,1,0:T(8,128)(2,1)} %refs_14_.1, bf16[2,1,4,128,128]{4,3,2,1,0:T(8,128)(2,1)} %refs_1_.5, s32[2,4]{1,0:T(2,128)} %bitcast.2, ...), custom_call_target="tpu_custom_call" | custom-call | tf_op jit(solution)/shard_map/pallas_call | solution.py:248
  1.1 0.1 collective-permute-start
  1.2 3.0 %collective-permute-start.1 = (bf16[208,128]{1,0:T(8,128)(2,1)S(1)}, bf16[208,128]{1,0:T(8,128)(2,1)S(1)}, u32[]{:S(2)}, u32[]{:S(2)}) collective-permute-start(bf16[208,128]{1,0:T(8,128)(2,1)S(1)} %get-tuple-element.16), channel_id=1, source_target_pairs={{0,20},{4,16},{8,28},{12,24},{16,4},{20,0},{24,12},{28,8},{1,21},{... | collective-permute-start | bytes 159752 | tf_op jit(solution)/shard_map/ppermute | solution.py:318
  4.2 3.5 %collective-permute-start.2 = (bf16[208,128]{1,0:T(8,128)(2,1)S(1)}, bf16[208,128]{1,0:T(8,128)(2,1)S(1)}, u32[]{:S(2)}, u32[]{:S(2)}) collective-permute-start(bf16[208,128]{1,0:T(8,128)(2,1)S(1)} %get-tuple-element.17), channel_id=1, source_target_pairs={{0,24},{4,28},{8,16},{12,20},{16,8},{20,12},{24,0},{28,4},{1,25},{... | collective-permute-start | bytes 159752 | tf_op jit(solution)/shard_map/ppermute | solution.py:318
  7.7 0.0 copy-start.2
  7.7 0.2 collective-permute-start.3
  7.9 1.6 %collective-permute-done.state_ref.refs_6_ = bf16[4,192,128]{2,1,0:T(8,128)(2,1)S(1)} collective-permute-done((bf16[4,192,128]{2,1,0:T(8,128)(2,1)S(1)}, bf16[4,192,128]{2,1,0:T(8,128)(2,1)S(1)}, u32[]{:S(2)}, u32[]{:S(2)}) %collective-permute-start) | collective-permute-done | bytes 196640 | tf_op jit(solution)/shard_map/ppermute | solution.py:324
  9.5 0.0 copy-done
  9.5 0.0 copy-done.2
  9.5 0.0 copy-start.1
  9.5 0.0 copy-start.3
  9.5 0.0 copy-start.4
  9.5 0.0 copy-start.5
  9.5 0.9 %shard_map.83.refs_0_ = f32[4,192,128]{2,1,0:T(8,128)S(1)} custom-call(bf16[4,192,128]{2,1,0:T(8,128)(2,1)S(1)} %collective-permute-done.state_ref.refs_6_, bf16[2,4,3,128,128]{4,3,2,1,0:T(8,128)(2,1)S(1)} %copy-done, s32[2,4]{1,0:T(2,128)S(1)} %bitcast.3, f32[192,8]{1,0:T(8,128)S(1)} %get-tuple-element.15.table_ref.refs_5_), custom_call_target="tpu_custom_call" | custom-call | tf_op jit(solution)/shard_map/pallas_call | solution.py:266
  10.4 0.0 collective-permute-done.1.refs_7_.refs_11_
  10.4 0.5 %collective-permute-done.2.refs_8_.refs_12_ = bf16[208,128]{1,0:T(8,128)(2,1)S(1)} collective-permute-done((bf16[208,128]{1,0:T(8,128)(2,1)S(1)}, bf16[208,128]{1,0:T(8,128)(2,1)S(1)}, u32[]{:S(2)}, u32[]{:S(2)}) %collective-permute-start.2) | collective-permute-done | bytes 53280 | tf_op jit(solution)/shard_map/ppermute | solution.py:318
  11.0 3.6 %collective-permute-done.3.refs_9_.refs_13_ = bf16[208,128]{1,0:T(8,128)(2,1)S(1)} collective-permute-done((bf16[208,128]{1,0:T(8,128)(2,1)S(1)}, bf16[208,128]{1,0:T(8,128)(2,1)S(1)}, u32[]{:S(2)}, u32[]{:S(2)}) %collective-permute-start.3) | collective-permute-done | bytes 53280 | tf_op jit(solution)/shard_map/ppermute | solution.py:318
  14.5 0.0 copy-done.1
  14.5 0.0 copy-done.3
  14.5 0.0 copy-done.4
  14.5 0.0 copy-done.5
  14.6 0.9 %shard_map.84 = (bf16[4,192,128]{2,1,0:T(8,128)(2,1)S(1)}, bf16[192,128]{1,0:T(8,128)(2,1)S(1)}, bf16[192,128]{1,0:T(8,128)(2,1)S(1)}, bf16[192,128]{1,0:T(8,128)(2,1)S(1)}) custom-call(f32[4,192,128]{2,1,0:T(8,128)S(1)} %shard_map.83.refs_0_, bf16[2,1,4,128,128]{4,3,2,1,0:T(8,128)(2,1)S(1)} %copy-done.1, s32[1,4]{1,0:T(1,128)S(1)} %copy-done.3, ...), custom_call_target="tpu_custom_call" | custom-call | tf_op jit(solution)/shard_map/pallas_call | solution.py:304
  15.5 1.9 %collective-permute-start.4 = (bf16[192,128]{1,0:T(8,128)(2,1)S(1)}, bf16[192,128]{1,0:T(8,128)(2,1)S(1)}, u32[]{:S(2)}, u32[]{:S(2)}) collective-permute-start(bf16[192,128]{1,0:T(8,128)(2,1)S(1)} %get-tuple-element.20), channel_id=1, source_target_pairs={{16,20},{20,16},{24,28},{28,24},{17,21},{21,17},{25,29},{29,25},{1... | collective-permute-start | bytes 147464 | tf_op jit(solution)/shard_map/ppermute | solution.py:318
  17.4 3.7 %collective-permute-start.5 = (bf16[192,128]{1,0:T(8,128)(2,1)S(1)}, bf16[192,128]{1,0:T(8,128)(2,1)S(1)}, u32[]{:S(2)}, u32[]{:S(2)}) collective-permute-start(bf16[192,128]{1,0:T(8,128)(2,1)S(1)} %get-tuple-element.21), channel_id=1, source_target_pairs={{16,24},{20,28},{24,16},{28,20},{17,25},{21,29},{25,17},{29,21},{1... | collective-permute-start | bytes 147464 | tf_op jit(solution)/shard_map/ppermute | solution.py:318
  21.2 4.5 %collective-permute-start.6 = (bf16[192,128]{1,0:T(8,128)(2,1)S(1)}, bf16[192,128]{1,0:T(8,128)(2,1)S(1)}, u32[]{:S(2)}, u32[]{:S(2)}) collective-permute-start(bf16[192,128]{1,0:T(8,128)(2,1)S(1)} %get-tuple-element.22), channel_id=1, source_target_pairs={{16,28},{20,24},{24,20},{28,16},{17,29},{21,25},{25,21},{29,17},{1... | collective-permute-start | bytes 147464 | tf_op jit(solution)/shard_map/ppermute | solution.py:318
  25.6 0.9 %shard_map.85.refs_0_ = f32[4,192,128]{2,1,0:T(8,128)S(1)} custom-call(bf16[4,192,128]{2,1,0:T(8,128)(2,1)S(1)} %get-tuple-element.19.state_ref.refs_6_.refs_16_, bf16[2,4,3,128,128]{4,3,2,1,0:T(8,128)(2,1)S(1)} %copy-done, s32[2,4]{1,0:T(2,128)S(1)} %bitcast.4, f32[192,8]{1,0:T(8,128)S(1)} %get-tuple-element.15.table_ref.refs_5_), custom_call_target="tpu_custom_call" | custom-call | tf_op jit(solution)/shard_map/pallas_call | solution.py:266
  26.5 0.0 collective-permute-done.4.refs_7_
  26.5 0.0 collective-permute-done.5.refs_8_
  26.6 2.4 %collective-permute-done.6.refs_9_ = bf16[192,128]{1,0:T(8,128)(2,1)S(1)} collective-permute-done((bf16[192,128]{1,0:T(8,128)(2,1)S(1)}, bf16[192,128]{1,0:T(8,128)(2,1)S(1)}, u32[]{:S(2)}, u32[]{:S(2)}) %collective-permute-start.6) | collective-permute-done | bytes 49184 | tf_op jit(solution)/shard_map/ppermute | solution.py:318
  29.0 1.6 %shard_map.86 = bf16[2,192,512]{2,1,0:T(8,128)(2,1)} custom-call(f32[4,192,128]{2,1,0:T(8,128)S(1)} %shard_map.85.refs_0_, bf16[2,1,4,128,128]{4,3,2,1,0:T(8,128)(2,1)S(1)} %copy-done.1, s32[1,4]{1,0:T(1,128)S(1)} %copy-done.3, s32[1,4]{1,0:T(1,128)S(1)} %copy-done.4, s32[1,4]{1,0:T(1,128)S(1)} %copy-done.5, ...), custom_call_target="tpu_custom_call" | custom-call | tf_op jit(solution)/shard_map/pallas_call | solution.py:304
Async XLA Ops:
  0.0 9.5 %copy-start = (bf16[2,4,3,128,128]{4,3,2,1,0:T(8,128)(2,1)S(1)}, bf16[2,4,3,128,128]{4,3,2,1,0:T(8,128)(2,1)}, u32[]{:S(2)}) copy-start(bf16[2,4,3,128,128]{4,3,2,1,0:T(8,128)(2,1)} %refs_14_.1) | copy-start | bytes 2359300
  1.1 8.4 %collective-permute-start = (bf16[4,192,128]{2,1,0:T(8,128)(2,1)S(1)}, bf16[4,192,128]{2,1,0:T(8,128)(2,1)S(1)}, u32[]{:S(2)}, u32[]{:S(2)}) collective-permute-start(bf16[4,192,128]{2,1,0:T(8,128)(2,1)S(1)} %get-tuple-element.14.refs_10_), channel_id=1, source_target_pairs={{0,16},{16,0},{1,17},{17,1},{2,18},{18,2},{3,19},{19,3},{4,20},{20... | collective-permute-start | bytes 589832 | tf_op jit(solution)/shard_map/ppermute | solution.py:324
  1.2 9.2 %collective-permute-start.1 = (bf16[208,128]{1,0:T(8,128)(2,1)S(1)}, bf16[208,128]{1,0:T(8,128)(2,1)S(1)}, u32[]{:S(2)}, u32[]{:S(2)}) collective-permute-start(bf16[208,128]{1,0:T(8,128)(2,1)S(1)} %get-tuple-element.16), channel_id=1, source_target_pairs={{0,20},{4,16},{8,28},{12,24},{16,4},{20,0},{24,12},{28,8},{1,21},{... | collective-permute-start | bytes 159752 | tf_op jit(solution)/shard_map/ppermute | solution.py:318
  4.2 6.8 %collective-permute-start.2 = (bf16[208,128]{1,0:T(8,128)(2,1)S(1)}, bf16[208,128]{1,0:T(8,128)(2,1)S(1)}, u32[]{:S(2)}, u32[]{:S(2)}) collective-permute-start(bf16[208,128]{1,0:T(8,128)(2,1)S(1)} %get-tuple-element.17), channel_id=1, source_target_pairs={{0,24},{4,28},{8,16},{12,20},{16,8},{20,12},{24,0},{28,4},{1,25},{... | collective-permute-start | bytes 159752 | tf_op jit(solution)/shard_map/ppermute | solution.py:318
  7.7 1.8 %copy-start.2 = (s32[4,2]{0,1:T(2,128)S(1)}, s32[4,2]{0,1:T(2,128)}, u32[]{:S(2)}) copy-start(s32[4,2]{0,1:T(2,128)} %param.9) | copy-start | bytes 100
  7.7 6.8 %collective-permute-start.3 = (bf16[208,128]{1,0:T(8,128)(2,1)S(1)}, bf16[208,128]{1,0:T(8,128)(2,1)S(1)}, u32[]{:S(2)}, u32[]{:S(2)}) collective-permute-start(bf16[208,128]{1,0:T(8,128)(2,1)S(1)} %get-tuple-element.18), channel_id=1, source_target_pairs={{0,28},{4,24},{8,20},{12,16},{16,12},{20,8},{24,4},{28,0},{1,29},{... | collective-permute-start | bytes 159752 | tf_op jit(solution)/shard_map/ppermute | solution.py:318
  9.5 5.0 %copy-start.1 = (bf16[2,1,4,128,128]{4,3,2,1,0:T(8,128)(2,1)S(1)}, bf16[2,1,4,128,128]{4,3,2,1,0:T(8,128)(2,1)}, u32[]{:S(2)}) copy-start(bf16[2,1,4,128,128]{4,3,2,1,0:T(8,128)(2,1)} %refs_1_.5) | copy-start | bytes 786436
  9.5 5.0 %copy-start.3 = (s32[1,4]{1,0:T(1,128)S(1)}, s32[1,4]{1,0:T(1,128)}, u32[]{:S(2)}) copy-start(s32[1,4]{1,0:T(1,128)} %refs_2_.3) | copy-start | bytes 52
  9.5 5.0 %copy-start.4 = (s32[1,4]{1,0:T(1,128)S(1)}, s32[1,4]{1,0:T(1,128)}, u32[]{:S(2)}) copy-start(s32[1,4]{1,0:T(1,128)} %refs_3_.5) | copy-start | bytes 52
  9.5 5.0 %copy-start.5 = (s32[1,4]{1,0:T(1,128)S(1)}, s32[1,4]{1,0:T(1,128)}, u32[]{:S(2)}) copy-start(s32[1,4]{1,0:T(1,128)} %refs_4_.5) | copy-start | bytes 52
  15.5 11.0 %collective-permute-start.4 = (bf16[192,128]{1,0:T(8,128)(2,1)S(1)}, bf16[192,128]{1,0:T(8,128)(2,1)S(1)}, u32[]{:S(2)}, u32[]{:S(2)}) collective-permute-start(bf16[192,128]{1,0:T(8,128)(2,1)S(1)} %get-tuple-element.20), channel_id=1, source_target_pairs={{16,20},{20,16},{24,28},{28,24},{17,21},{21,17},{25,29},{29,25},{1... | collective-permute-start | bytes 147464 | tf_op jit(solution)/shard_map/ppermute | solution.py:318
  17.4 9.1 %collective-permute-start.5 = (bf16[192,128]{1,0:T(8,128)(2,1)S(1)}, bf16[192,128]{1,0:T(8,128)(2,1)S(1)}, u32[]{:S(2)}, u32[]{:S(2)}) collective-permute-start(bf16[192,128]{1,0:T(8,128)(2,1)S(1)} %get-tuple-element.21), channel_id=1, source_target_pairs={{16,24},{20,28},{24,16},{28,20},{17,25},{21,29},{25,17},{29,21},{1... | collective-permute-start | bytes 147464 | tf_op jit(solution)/shard_map/ppermute | solution.py:318
  21.2 7.8 %collective-permute-start.6 = (bf16[192,128]{1,0:T(8,128)(2,1)S(1)}, bf16[192,128]{1,0:T(8,128)(2,1)S(1)}, u32[]{:S(2)}, u32[]{:S(2)}) collective-permute-start(bf16[192,128]{1,0:T(8,128)(2,1)S(1)} %get-tuple-element.22), channel_id=1, source_target_pairs={{16,28},{20,24},{24,20},{28,16},{17,29},{21,25},{25,21},{29,17},{1... | collective-permute-start | bytes 147464 | tf_op jit(solution)/shard_map/ppermute | solution.py:318

commit v8 on v7

--- a/solution.py
+++ b/solution.py
@@ -311,25 +311,27 @@
             compiler_params=LIMIT,
         )(*arrays)
 
-    def swap(outgoing, sections):
-        arrived = {}
-        for d in reversed(range(1, n)):
-            pairs = [(a * n + q, b * n + (q ^ d)) for a, b in sections for q in range(n)]
-            arrived[d] = lax.ppermute(outgoing[d - 1], ("tm", "net"), pairs)
-        return [arrived[d] for d in range(1, n)]
+    def swap(block, first, second, d):
+        other = {first: second, second: first}
+        pairs = [(a * n + q, other[a] * n + (q ^ d) if a in other else a * n + q) for a in range(tm) for q in range(n)]
+        return lax.ppermute(block, ("tm", "net"), pairs)
+
+    def exchange(outgoing, first, second):
+        arrived = [swap(outgoing[d - 1], first, second, d) for d in reversed(range(1, n))]
+        return arrived[::-1]
 
     opening = [state]
     out = None
     for r in range(1, tm):
-        state = lax.ppermute(state, "tm", [(r - 1, r), (r, r - 1)])
-        arrived = swap(outgoing, [(r - 1, r), (r, r - 1)])
+        state = swap(state, r - 1, r, 0)
+        arrived = exchange(outgoing, r - 1, r)
         if r == 1:
             handed = arrived
         before = []
         for s in range(steps):
             fix = r == 1 and s == 0
             if s > 0:
-                arrived = swap(outgoing, [(r, r)])
+                arrived = exchange(outgoing, r, r)
             z = own(state, s)
             if s < steps - 1:
                 state, *outgoing = join(z, s, fix, state, arrived, True, r)

time: 30.7 us -> 30.7 us (level)
  no operation moved by 1% of the time
where the time goes in v8:
time: 30.7 us; the launch traced here: 30.5 us
  starting transfers between devices  16.9 us (55%)
  waiting for transfers between devices  8.1 us (26%)
  Pallas kernels  5.37 us (17%)
    ppermute x7, starting transfers between devices, swap(): return lax.ppermute(block, ('tm', 'net'), pairs)  16.9 us
    ppermute x7, waiting for transfers between devices, swap(): return lax.ppermute(block, ('tm', 'net'), pairs)  8.1 us
    pallas_call x2, Pallas kernels, join(): pl.pallas_call(functools.partial(join_kernel, step, fix, send, section, f...  2.53 us
    pallas_call x2, Pallas kernels, own(): pl.pallas_call(functools.partial(own_kernel, step), out_shape=f32(whole.s...  1.78 us
    pallas_call x1, Pallas kernels, local(): pl.pallas_call(second_kernel, out_shape=[f32((cols, table_rows)), whole]...  1.06 us
  transfers between devices with their start and end apart: 7, of which 4 were waited for; matrix products, arithmetic and copies ran while one was open for 0% of the time, Pallas kernels for 6%

profile of v8, /device:TPU:4, one launch (start us, length us, event | category | flops | bytes accessed | tf_op | source)
XLA Modules:
  0.0 30.5 jit_solution(13871606001743355415)
XLA Ops:
  0.0 0.0 copy-start
  0.0 1.1 %shard_map.82 = (f32[192,8]{1,0:T(8,128)S(1)}, bf16[4,192,128]{2,1,0:T(8,128)(2,1)S(1)}, bf16[208,128]{1,0:T(8,128)(2,1)S(1)}, bf16[208,128]{1,0:T(8,128)(2,1)S(1)}, bf16[208,128]{1,0:T(8,128)(2,1)S(1)}) custom-call(bf16[2,4,3,128,128]{4,3,2,1,0:T(8,128)(2,1)} %refs_14_.1, bf16[2,1,4,128,128]{4,3,2,1,0:T(8,128)(2,1)} %refs_1_.5, s32[2,4]{1,0:T(2,128)} %bitcast.2, ...), custom_call_target="tpu_custom_call" | custom-call | tf_op jit(solution)/shard_map/pallas_call | solution.py:248
  1.1 0.1 collective-permute-start
  1.2 3.0 %collective-permute-start.1 = (bf16[208,128]{1,0:T(8,128)(2,1)S(1)}, bf16[208,128]{1,0:T(8,128)(2,1)S(1)}, u32[]{:S(2)}, u32[]{:S(2)}) collective-permute-start(bf16[208,128]{1,0:T(8,128)(2,1)S(1)} %get-tuple-element.16), channel_id=1, source_target_pairs={{0,20},{4,16},{8,28},{12,24},{16,4},{20,0},{24,12},{28,8},{1,21},{... | collective-permute-start | bytes 159752 | tf_op jit(solution)/shard_map/ppermute | solution.py:317
  4.2 3.5 %collective-permute-start.2 = (bf16[208,128]{1,0:T(8,128)(2,1)S(1)}, bf16[208,128]{1,0:T(8,128)(2,1)S(1)}, u32[]{:S(2)}, u32[]{:S(2)}) collective-permute-start(bf16[208,128]{1,0:T(8,128)(2,1)S(1)} %get-tuple-element.17), channel_id=1, source_target_pairs={{0,24},{4,28},{8,16},{12,20},{16,8},{20,12},{24,0},{28,4},{1,25},{... | collective-permute-start | bytes 159752 | tf_op jit(solution)/shard_map/ppermute | solution.py:317
  7.7 0.0 copy-start.2
  7.7 0.2 collective-permute-start.3
  7.9 1.6 %collective-permute-done.state_ref.refs_6_ = bf16[4,192,128]{2,1,0:T(8,128)(2,1)S(1)} collective-permute-done((bf16[4,192,128]{2,1,0:T(8,128)(2,1)S(1)}, bf16[4,192,128]{2,1,0:T(8,128)(2,1)S(1)}, u32[]{:S(2)}, u32[]{:S(2)}) %collective-permute-start) | collective-permute-done | bytes 196640 | tf_op jit(solution)/shard_map/ppermute | solution.py:317
  9.5 0.0 copy-done
  9.5 0.0 copy-done.2
  9.5 0.0 copy-start.1
  9.5 0.0 copy-start.3
  9.5 0.0 copy-start.4
  9.5 0.0 copy-start.5
  9.5 0.9 %shard_map.83.refs_0_ = f32[4,192,128]{2,1,0:T(8,128)S(1)} custom-call(bf16[4,192,128]{2,1,0:T(8,128)(2,1)S(1)} %collective-permute-done.state_ref.refs_6_, bf16[2,4,3,128,128]{4,3,2,1,0:T(8,128)(2,1)S(1)} %copy-done, s32[2,4]{1,0:T(2,128)S(1)} %bitcast.3, f32[192,8]{1,0:T(8,128)S(1)} %get-tuple-element.15.table_ref.refs_5_), custom_call_target="tpu_custom_call" | custom-call | tf_op jit(solution)/shard_map/pallas_call | solution.py:266
  10.4 0.0 collective-permute-done.1.refs_7_.refs_11_
  10.4 0.5 %collective-permute-done.2.refs_8_.refs_12_ = bf16[208,128]{1,0:T(8,128)(2,1)S(1)} collective-permute-done((bf16[208,128]{1,0:T(8,128)(2,1)S(1)}, bf16[208,128]{1,0:T(8,128)(2,1)S(1)}, u32[]{:S(2)}, u32[]{:S(2)}) %collective-permute-start.2) | collective-permute-done | bytes 53280 | tf_op jit(solution)/shard_map/ppermute | solution.py:317
  11.0 3.6 %collective-permute-done.3.refs_9_.refs_13_ = bf16[208,128]{1,0:T(8,128)(2,1)S(1)} collective-permute-done((bf16[208,128]{1,0:T(8,128)(2,1)S(1)}, bf16[208,128]{1,0:T(8,128)(2,1)S(1)}, u32[]{:S(2)}, u32[]{:S(2)}) %collective-permute-start.3) | collective-permute-done | bytes 53280 | tf_op jit(solution)/shard_map/ppermute | solution.py:317
  14.5 0.0 copy-done.1
  14.5 0.0 copy-done.3
  14.5 0.0 copy-done.4
  14.6 0.0 copy-done.5
  14.6 0.9 %shard_map.84 = (bf16[4,192,128]{2,1,0:T(8,128)(2,1)S(1)}, bf16[192,128]{1,0:T(8,128)(2,1)S(1)}, bf16[192,128]{1,0:T(8,128)(2,1)S(1)}, bf16[192,128]{1,0:T(8,128)(2,1)S(1)}) custom-call(f32[4,192,128]{2,1,0:T(8,128)S(1)} %shard_map.83.refs_0_, bf16[2,1,4,128,128]{4,3,2,1,0:T(8,128)(2,1)S(1)} %copy-done.1, s32[1,4]{1,0:T(1,128)S(1)} %copy-done.3, ...), custom_call_target="tpu_custom_call" | custom-call | tf_op jit(solution)/shard_map/pallas_call | solution.py:304
  15.5 1.9 %collective-permute-start.4 = (bf16[192,128]{1,0:T(8,128)(2,1)S(1)}, bf16[192,128]{1,0:T(8,128)(2,1)S(1)}, u32[]{:S(2)}, u32[]{:S(2)}) collective-permute-start(bf16[192,128]{1,0:T(8,128)(2,1)S(1)} %get-tuple-element.20), channel_id=1, source_target_pairs={{0,0},{4,4},{8,8},{12,12},{16,20},{20,16},{24,28},{28,24},{1,1},{5... | collective-permute-start | bytes 147464 | tf_op jit(solution)/shard_map/ppermute | solution.py:317
  17.4 3.7 %collective-permute-start.5 = (bf16[192,128]{1,0:T(8,128)(2,1)S(1)}, bf16[192,128]{1,0:T(8,128)(2,1)S(1)}, u32[]{:S(2)}, u32[]{:S(2)}) collective-permute-start(bf16[192,128]{1,0:T(8,128)(2,1)S(1)} %get-tuple-element.21), channel_id=1, source_target_pairs={{0,0},{4,4},{8,8},{12,12},{16,24},{20,28},{24,16},{28,20},{1,1},{5... | collective-permute-start | bytes 147464 | tf_op jit(solution)/shard_map/ppermute | solution.py:317
  21.2 4.5 %collective-permute-start.6 = (bf16[192,128]{1,0:T(8,128)(2,1)S(1)}, bf16[192,128]{1,0:T(8,128)(2,1)S(1)}, u32[]{:S(2)}, u32[]{:S(2)}) collective-permute-start(bf16[192,128]{1,0:T(8,128)(2,1)S(1)} %get-tuple-element.22), channel_id=1, source_target_pairs={{0,0},{4,4},{8,8},{12,12},{16,28},{20,24},{24,20},{28,16},{1,1},{5... | collective-permute-start | bytes 147464 | tf_op jit(solution)/shard_map/ppermute | solution.py:317
  25.7 0.9 %shard_map.85.refs_0_ = f32[4,192,128]{2,1,0:T(8,128)S(1)} custom-call(bf16[4,192,128]{2,1,0:T(8,128)(2,1)S(1)} %get-tuple-element.19.state_ref.refs_6_.refs_16_, bf16[2,4,3,128,128]{4,3,2,1,0:T(8,128)(2,1)S(1)} %copy-done, s32[2,4]{1,0:T(2,128)S(1)} %bitcast.4, f32[192,8]{1,0:T(8,128)S(1)} %get-tuple-element.15.table_ref.refs_5_), custom_call_target="tpu_custom_call" | custom-call | tf_op jit(solution)/shard_map/pallas_call | solution.py:266
  26.5 0.0 collective-permute-done.4.refs_7_
  26.6 0.0 collective-permute-done.5.refs_8_
  26.6 2.4 %collective-permute-done.6.refs_9_ = bf16[192,128]{1,0:T(8,128)(2,1)S(1)} collective-permute-done((bf16[192,128]{1,0:T(8,128)(2,1)S(1)}, bf16[192,128]{1,0:T(8,128)(2,1)S(1)}, u32[]{:S(2)}, u32[]{:S(2)}) %collective-permute-start.6) | collective-permute-done | bytes 49184 | tf_op jit(solution)/shard_map/ppermute | solution.py:317
  29.0 1.6 %shard_map.86 = bf16[2,192,512]{2,1,0:T(8,128)(2,1)} custom-call(f32[4,192,128]{2,1,0:T(8,128)S(1)} %shard_map.85.refs_0_, bf16[2,1,4,128,128]{4,3,2,1,0:T(8,128)(2,1)S(1)} %copy-done.1, s32[1,4]{1,0:T(1,128)S(1)} %copy-done.3, s32[1,4]{1,0:T(1,128)S(1)} %copy-done.4, s32[1,4]{1,0:T(1,128)S(1)} %copy-done.5, ...), custom_call_target="tpu_custom_call" | custom-call | tf_op jit(solution)/shard_map/pallas_call | solution.py:304
Async XLA Ops:
  0.0 9.5 %copy-start = (bf16[2,4,3,128,128]{4,3,2,1,0:T(8,128)(2,1)S(1)}, bf16[2,4,3,128,128]{4,3,2,1,0:T(8,128)(2,1)}, u32[]{:S(2)}) copy-start(bf16[2,4,3,128,128]{4,3,2,1,0:T(8,128)(2,1)} %refs_14_.1) | copy-start | bytes 2359300
  1.1 8.4 %collective-permute-start = (bf16[4,192,128]{2,1,0:T(8,128)(2,1)S(1)}, bf16[4,192,128]{2,1,0:T(8,128)(2,1)S(1)}, u32[]{:S(2)}, u32[]{:S(2)}) collective-permute-start(bf16[4,192,128]{2,1,0:T(8,128)(2,1)S(1)} %get-tuple-element.14.refs_10_), channel_id=1, source_target_pairs={{0,16},{4,20},{8,24},{12,28},{16,0},{20,4},{24,8},{28,12},{1,17},{... | collective-permute-start | bytes 589832 | tf_op jit(solution)/shard_map/ppermute | solution.py:317
  1.2 9.2 %collective-permute-start.1 = (bf16[208,128]{1,0:T(8,128)(2,1)S(1)}, bf16[208,128]{1,0:T(8,128)(2,1)S(1)}, u32[]{:S(2)}, u32[]{:S(2)}) collective-permute-start(bf16[208,128]{1,0:T(8,128)(2,1)S(1)} %get-tuple-element.16), channel_id=1, source_target_pairs={{0,20},{4,16},{8,28},{12,24},{16,4},{20,0},{24,12},{28,8},{1,21},{... | collective-permute-start | bytes 159752 | tf_op jit(solution)/shard_map/ppermute | solution.py:317
  4.2 6.8 %collective-permute-start.2 = (bf16[208,128]{1,0:T(8,128)(2,1)S(1)}, bf16[208,128]{1,0:T(8,128)(2,1)S(1)}, u32[]{:S(2)}, u32[]{:S(2)}) collective-permute-start(bf16[208,128]{1,0:T(8,128)(2,1)S(1)} %get-tuple-element.17), channel_id=1, source_target_pairs={{0,24},{4,28},{8,16},{12,20},{16,8},{20,12},{24,0},{28,4},{1,25},{... | collective-permute-start | bytes 159752 | tf_op jit(solution)/shard_map/ppermute | solution.py:317
  7.7 1.8 %copy-start.2 = (s32[4,2]{0,1:T(2,128)S(1)}, s32[4,2]{0,1:T(2,128)}, u32[]{:S(2)}) copy-start(s32[4,2]{0,1:T(2,128)} %param.9) | copy-start | bytes 100
  7.7 6.8 %collective-permute-start.3 = (bf16[208,128]{1,0:T(8,128)(2,1)S(1)}, bf16[208,128]{1,0:T(8,128)(2,1)S(1)}, u32[]{:S(2)}, u32[]{:S(2)}) collective-permute-start(bf16[208,128]{1,0:T(8,128)(2,1)S(1)} %get-tuple-element.18), channel_id=1, source_target_pairs={{0,28},{4,24},{8,20},{12,16},{16,12},{20,8},{24,4},{28,0},{1,29},{... | collective-permute-start | bytes 159752 | tf_op jit(solution)/shard_map/ppermute | solution.py:317
  9.5 5.0 %copy-start.1 = (bf16[2,1,4,128,128]{4,3,2,1,0:T(8,128)(2,1)S(1)}, bf16[2,1,4,128,128]{4,3,2,1,0:T(8,128)(2,1)}, u32[]{:S(2)}) copy-start(bf16[2,1,4,128,128]{4,3,2,1,0:T(8,128)(2,1)} %refs_1_.5) | copy-start | bytes 786436
  9.5 5.0 %copy-start.3 = (s32[1,4]{1,0:T(1,128)S(1)}, s32[1,4]{1,0:T(1,128)}, u32[]{:S(2)}) copy-start(s32[1,4]{1,0:T(1,128)} %refs_2_.3) | copy-start | bytes 52
  9.5 5.0 %copy-start.4 = (s32[1,4]{1,0:T(1,128)S(1)}, s32[1,4]{1,0:T(1,128)}, u32[]{:S(2)}) copy-start(s32[1,4]{1,0:T(1,128)} %refs_3_.5) | copy-start | bytes 52
  9.5 5.0 %copy-start.5 = (s32[1,4]{1,0:T(1,128)S(1)}, s32[1,4]{1,0:T(1,128)}, u32[]{:S(2)}) copy-start(s32[1,4]{1,0:T(1,128)} %refs_4_.5) | copy-start | bytes 52
  15.5 11.0 %collective-permute-start.4 = (bf16[192,128]{1,0:T(8,128)(2,1)S(1)}, bf16[192,128]{1,0:T(8,128)(2,1)S(1)}, u32[]{:S(2)}, u32[]{:S(2)}) collective-permute-start(bf16[192,128]{1,0:T(8,128)(2,1)S(1)} %get-tuple-element.20), channel_id=1, source_target_pairs={{0,0},{4,4},{8,8},{12,12},{16,20},{20,16},{24,28},{28,24},{1,1},{5... | collective-permute-start | bytes 147464 | tf_op jit(solution)/shard_map/ppermute | solution.py:317
  17.4 9.1 %collective-permute-start.5 = (bf16[192,128]{1,0:T(8,128)(2,1)S(1)}, bf16[192,128]{1,0:T(8,128)(2,1)S(1)}, u32[]{:S(2)}, u32[]{:S(2)}) collective-permute-start(bf16[192,128]{1,0:T(8,128)(2,1)S(1)} %get-tuple-element.21), channel_id=1, source_target_pairs={{0,0},{4,4},{8,8},{12,12},{16,24},{20,28},{24,16},{28,20},{1,1},{5... | collective-permute-start | bytes 147464 | tf_op jit(solution)/shard_map/ppermute | solution.py:317
  21.2 7.8 %collective-permute-start.6 = (bf16[192,128]{1,0:T(8,128)(2,1)S(1)}, bf16[192,128]{1,0:T(8,128)(2,1)S(1)}, u32[]{:S(2)}, u32[]{:S(2)}) collective-permute-start(bf16[192,128]{1,0:T(8,128)(2,1)S(1)} %get-tuple-element.22), channel_id=1, source_target_pairs={{0,0},{4,4},{8,8},{12,12},{16,28},{20,24},{24,20},{28,16},{1,1},{5... | collective-permute-start | bytes 147464 | tf_op jit(solution)/shard_map/ppermute | solution.py:317

commit v9 on v8

--- a/solution.py
+++ b/solution.py
@@ -233,6 +233,7 @@
     cols = ctrl_node.shape[0]
     tm = lax.axis_size("tm")
     n = lax.axis_size("net")
+    col_parts = lax.axis_size("cols")
     node = ctrl_node[None]
     near = block_cols.T
     bf16 = functools.partial(jax.ShapeDtypeStruct, dtype=jnp.bfloat16)
@@ -313,8 +314,13 @@
 
     def swap(block, first, second, d):
         other = {first: second, second: first}
-        pairs = [(a * n + q, other[a] * n + (q ^ d) if a in other else a * n + q) for a in range(tm) for q in range(n)]
-        return lax.ppermute(block, ("tm", "net"), pairs)
+        pairs = []
+        for a in range(tm):
+            for q in range(n):
+                for c in range(col_parts):
+                    to = (other[a] * n + (q ^ d)) * col_parts + c if a in other else (a * n + q) * col_parts + (c ^ 1)
+                    pairs.append(((a * n + q) * col_parts + c, to))
+        return lax.ppermute(block, ("tm", "net", "cols"), pairs)
 
     def exchange(outgoing, first, second):
         arrived = [swap(outgoing[d - 1], first, second, d) for d in reversed(range(1, n))]

time: 30.7 us -> 25 us (0.81)
  starting transfers between devices: 16.9 us -> 11.3 us
    ppermute x7, starting transfers between devices: 16.9 us -> 11.3 us  [swap(): return lax.ppermute(block, ('tm', 'net', 'cols'), pairs)]
  transfers between devices with their start and end apart: 7 -> 7, of which waited for: 4 -> 4; matrix products, arithmetic and copies ran while one was open for 0% -> 0% of each run, Pallas kernels for 6% -> 7%
where the time goes in v9:
time: 25 us; the launch traced here: 24.9 us
  starting transfers between devices  11.3 us (45%)
  waiting for transfers between devices  8.13 us (33%)
  Pallas kernels  5.37 us (21%)
    ppermute x7, starting transfers between devices, swap(): return lax.ppermute(block, ('tm', 'net', 'cols'), pairs)  11.3 us
    ppermute x7, waiting for transfers between devices, swap(): return lax.ppermute(block, ('tm', 'net', 'cols'), pairs)  8.13 us
    pallas_call x2, Pallas kernels, join(): pl.pallas_call(functools.partial(join_kernel, step, fix, send, section, f...  2.53 us
    pallas_call x2, Pallas kernels, own(): pl.pallas_call(functools.partial(own_kernel, step), out_shape=f32(whole.s...  1.78 us
    pallas_call x1, Pallas kernels, local(): pl.pallas_call(second_kernel, out_shape=[f32((cols, table_rows)), whole]...  1.06 us
  transfers between devices with their start and end apart: 7, of which 4 were waited for; matrix products, arithmetic and copies ran while one was open for 0% of the time, Pallas kernels for 7%

profile of v9, /device:TPU:4, one launch (start us, length us, event | category | flops | bytes accessed | tf_op | source)
XLA Modules:
  0.0 24.9 jit_solution(3601062317865991831)
XLA Ops:
  0.0 0.0 copy-start
  0.0 1.1 %shard_map.82 = (f32[192,8]{1,0:T(8,128)S(1)}, bf16[4,192,128]{2,1,0:T(8,128)(2,1)S(1)}, bf16[208,128]{1,0:T(8,128)(2,1)S(1)}, bf16[208,128]{1,0:T(8,128)(2,1)S(1)}, bf16[208,128]{1,0:T(8,128)(2,1)S(1)}) custom-call(bf16[2,4,3,128,128]{4,3,2,1,0:T(8,128)(2,1)} %refs_14_.1, bf16[2,1,4,128,128]{4,3,2,1,0:T(8,128)(2,1)} %refs_1_.5, s32[2,4]{1,0:T(2,128)} %bitcast.2, ...), custom_call_target="tpu_custom_call" | custom-call | tf_op jit(solution)/shard_map/pallas_call | solution.py:249
  1.1 0.1 collective-permute-start
  1.2 3.0 %collective-permute-start.1 = (bf16[208,128]{1,0:T(8,128)(2,1)S(1)}, bf16[208,128]{1,0:T(8,128)(2,1)S(1)}, u32[]{:S(2)}, u32[]{:S(2)}) collective-permute-start(bf16[208,128]{1,0:T(8,128)(2,1)S(1)} %get-tuple-element.16), channel_id=1, source_target_pairs={{0,20},{1,21},{2,22},{3,23},{4,16},{5,17},{6,18},{7,19},{8,28},{9,... | collective-permute-start | bytes 159752 | tf_op jit(solution)/shard_map/ppermute | solution.py:323
  4.2 3.5 %collective-permute-start.2 = (bf16[208,128]{1,0:T(8,128)(2,1)S(1)}, bf16[208,128]{1,0:T(8,128)(2,1)S(1)}, u32[]{:S(2)}, u32[]{:S(2)}) collective-permute-start(bf16[208,128]{1,0:T(8,128)(2,1)S(1)} %get-tuple-element.17), channel_id=1, source_target_pairs={{0,24},{1,25},{2,26},{3,27},{4,28},{5,29},{6,30},{7,31},{8,16},{9,... | collective-permute-start | bytes 159752 | tf_op jit(solution)/shard_map/ppermute | solution.py:323
  7.7 0.0 copy-start.2
  7.7 0.2 collective-permute-start.3
  7.9 1.6 %collective-permute-done.state_ref.refs_6_ = bf16[4,192,128]{2,1,0:T(8,128)(2,1)S(1)} collective-permute-done((bf16[4,192,128]{2,1,0:T(8,128)(2,1)S(1)}, bf16[4,192,128]{2,1,0:T(8,128)(2,1)S(1)}, u32[]{:S(2)}, u32[]{:S(2)}) %collective-permute-start) | collective-permute-done | bytes 196640 | tf_op jit(solution)/shard_map/ppermute | solution.py:323
  9.5 0.0 copy-done
  9.5 0.0 copy-done.2
  9.5 0.0 copy-start.1
  9.5 0.0 copy-start.3
  9.5 0.0 copy-start.4
  9.5 0.0 copy-start.5
  9.5 0.9 %shard_map.83.refs_0_ = f32[4,192,128]{2,1,0:T(8,128)S(1)} custom-call(bf16[4,192,128]{2,1,0:T(8,128)(2,1)S(1)} %collective-permute-done.state_ref.refs_6_, bf16[2,4,3,128,128]{4,3,2,1,0:T(8,128)(2,1)S(1)} %copy-done, s32[2,4]{1,0:T(2,128)S(1)} %bitcast.3, f32[192,8]{1,0:T(8,128)S(1)} %get-tuple-element.15.table_ref.refs_5_), custom_call_target="tpu_custom_call" | custom-call | tf_op jit(solution)/shard_map/pallas_call | solution.py:267
  10.4 0.0 collective-permute-done.1.refs_7_.refs_11_
  10.4 0.5 %collective-permute-done.2.refs_8_.refs_12_ = bf16[208,128]{1,0:T(8,128)(2,1)S(1)} collective-permute-done((bf16[208,128]{1,0:T(8,128)(2,1)S(1)}, bf16[208,128]{1,0:T(8,128)(2,1)S(1)}, u32[]{:S(2)}, u32[]{:S(2)}) %collective-permute-start.2) | collective-permute-done | bytes 53280 | tf_op jit(solution)/shard_map/ppermute | solution.py:323
  11.0 3.6 %collective-permute-done.3.refs_9_.refs_13_ = bf16[208,128]{1,0:T(8,128)(2,1)S(1)} collective-permute-done((bf16[208,128]{1,0:T(8,128)(2,1)S(1)}, bf16[208,128]{1,0:T(8,128)(2,1)S(1)}, u32[]{:S(2)}, u32[]{:S(2)}) %collective-permute-start.3) | collective-permute-done | bytes 53280 | tf_op jit(solution)/shard_map/ppermute | solution.py:323
  14.5 0.0 copy-done.1
  14.5 0.0 copy-done.3
  14.5 0.0 copy-done.4
  14.6 0.0 copy-done.5
  14.6 0.9 %shard_map.84 = (bf16[4,192,128]{2,1,0:T(8,128)(2,1)S(1)}, bf16[192,128]{1,0:T(8,128)(2,1)S(1)}, bf16[192,128]{1,0:T(8,128)(2,1)S(1)}, bf16[192,128]{1,0:T(8,128)(2,1)S(1)}) custom-call(f32[4,192,128]{2,1,0:T(8,128)S(1)} %shard_map.83.refs_0_, bf16[2,1,4,128,128]{4,3,2,1,0:T(8,128)(2,1)S(1)} %copy-done.1, s32[1,4]{1,0:T(1,128)S(1)} %copy-done.3, ...), custom_call_target="tpu_custom_call" | custom-call | tf_op jit(solution)/shard_map/pallas_call | solution.py:305
  15.5 0.1 collective-permute-start.4
  15.6 1.8 %collective-permute-start.5 = (bf16[192,128]{1,0:T(8,128)(2,1)S(1)}, bf16[192,128]{1,0:T(8,128)(2,1)S(1)}, u32[]{:S(2)}, u32[]{:S(2)}) collective-permute-start(bf16[192,128]{1,0:T(8,128)(2,1)S(1)} %get-tuple-element.21), channel_id=1, source_target_pairs={{0,1},{1,0},{2,3},{3,2},{4,5},{5,4},{6,7},{7,6},{8,9},{9,8},{10,11... | collective-permute-start | bytes 147464 | tf_op jit(solution)/shard_map/ppermute | solution.py:323
  17.4 2.6 %collective-permute-start.6 = (bf16[192,128]{1,0:T(8,128)(2,1)S(1)}, bf16[192,128]{1,0:T(8,128)(2,1)S(1)}, u32[]{:S(2)}, u32[]{:S(2)}) collective-permute-start(bf16[192,128]{1,0:T(8,128)(2,1)S(1)} %get-tuple-element.22), channel_id=1, source_target_pairs={{0,1},{1,0},{2,3},{3,2},{4,5},{5,4},{6,7},{7,6},{8,9},{9,8},{10,11... | collective-permute-start | bytes 147464 | tf_op jit(solution)/shard_map/ppermute | solution.py:323
  20.0 0.9 %shard_map.85.refs_0_ = f32[4,192,128]{2,1,0:T(8,128)S(1)} custom-call(bf16[4,192,128]{2,1,0:T(8,128)(2,1)S(1)} %get-tuple-element.19.state_ref.refs_6_.refs_16_, bf16[2,4,3,128,128]{4,3,2,1,0:T(8,128)(2,1)S(1)} %copy-done, s32[2,4]{1,0:T(2,128)S(1)} %bitcast.4, f32[192,8]{1,0:T(8,128)S(1)} %get-tuple-element.15.table_ref.refs_5_), custom_call_target="tpu_custom_call" | custom-call | tf_op jit(solution)/shard_map/pallas_call | solution.py:267
  20.9 0.0 collective-permute-done.4.refs_7_
  20.9 0.0 collective-permute-done.5.refs_8_
  20.9 2.4 %collective-permute-done.6.refs_9_ = bf16[192,128]{1,0:T(8,128)(2,1)S(1)} collective-permute-done((bf16[192,128]{1,0:T(8,128)(2,1)S(1)}, bf16[192,128]{1,0:T(8,128)(2,1)S(1)}, u32[]{:S(2)}, u32[]{:S(2)}) %collective-permute-start.6) | collective-permute-done | bytes 49184 | tf_op jit(solution)/shard_map/ppermute | solution.py:323
  23.3 1.6 %shard_map.86 = bf16[2,192,512]{2,1,0:T(8,128)(2,1)} custom-call(f32[4,192,128]{2,1,0:T(8,128)S(1)} %shard_map.85.refs_0_, bf16[2,1,4,128,128]{4,3,2,1,0:T(8,128)(2,1)S(1)} %copy-done.1, s32[1,4]{1,0:T(1,128)S(1)} %copy-done.3, s32[1,4]{1,0:T(1,128)S(1)} %copy-done.4, s32[1,4]{1,0:T(1,128)S(1)} %copy-done.5, ...), custom_call_target="tpu_custom_call" | custom-call | tf_op jit(solution)/shard_map/pallas_call | solution.py:305
Async XLA Ops:
  0.0 9.5 %copy-start = (bf16[2,4,3,128,128]{4,3,2,1,0:T(8,128)(2,1)S(1)}, bf16[2,4,3,128,128]{4,3,2,1,0:T(8,128)(2,1)}, u32[]{:S(2)}) copy-start(bf16[2,4,3,128,128]{4,3,2,1,0:T(8,128)(2,1)} %refs_14_.1) | copy-start | bytes 2359300
  1.1 8.4 %collective-permute-start = (bf16[4,192,128]{2,1,0:T(8,128)(2,1)S(1)}, bf16[4,192,128]{2,1,0:T(8,128)(2,1)S(1)}, u32[]{:S(2)}, u32[]{:S(2)}) collective-permute-start(bf16[4,192,128]{2,1,0:T(8,128)(2,1)S(1)} %get-tuple-element.14.refs_10_), channel_id=1, source_target_pairs={{0,16},{1,17},{2,18},{3,19},{4,20},{5,21},{6,22},{7,23},{8,24},{9,... | collective-permute-start | bytes 589832 | tf_op jit(solution)/shard_map/ppermute | solution.py:323
  1.2 9.2 %collective-permute-start.1 = (bf16[208,128]{1,0:T(8,128)(2,1)S(1)}, bf16[208,128]{1,0:T(8,128)(2,1)S(1)}, u32[]{:S(2)}, u32[]{:S(2)}) collective-permute-start(bf16[208,128]{1,0:T(8,128)(2,1)S(1)} %get-tuple-element.16), channel_id=1, source_target_pairs={{0,20},{1,21},{2,22},{3,23},{4,16},{5,17},{6,18},{7,19},{8,28},{9,... | collective-permute-start | bytes 159752 | tf_op jit(solution)/shard_map/ppermute | solution.py:323
  4.2 6.8 %collective-permute-start.2 = (bf16[208,128]{1,0:T(8,128)(2,1)S(1)}, bf16[208,128]{1,0:T(8,128)(2,1)S(1)}, u32[]{:S(2)}, u32[]{:S(2)}) collective-permute-start(bf16[208,128]{1,0:T(8,128)(2,1)S(1)} %get-tuple-element.17), channel_id=1, source_target_pairs={{0,24},{1,25},{2,26},{3,27},{4,28},{5,29},{6,30},{7,31},{8,16},{9,... | collective-permute-start | bytes 159752 | tf_op jit(solution)/shard_map/ppermute | solution.py:323
  7.7 1.8 %copy-start.2 = (s32[4,2]{0,1:T(2,128)S(1)}, s32[4,2]{0,1:T(2,128)}, u32[]{:S(2)}) copy-start(s32[4,2]{0,1:T(2,128)} %param.9) | copy-start | bytes 100
  7.7 6.8 %collective-permute-start.3 = (bf16[208,128]{1,0:T(8,128)(2,1)S(1)}, bf16[208,128]{1,0:T(8,128)(2,1)S(1)}, u32[]{:S(2)}, u32[]{:S(2)}) collective-permute-start(bf16[208,128]{1,0:T(8,128)(2,1)S(1)} %get-tuple-element.18), channel_id=1, source_target_pairs={{0,28},{1,29},{2,30},{3,31},{4,24},{5,25},{6,26},{7,27},{8,20},{9,... | collective-permute-start | bytes 159752 | tf_op jit(solution)/shard_map/ppermute | solution.py:323
  9.5 5.0 %copy-start.1 = (bf16[2,1,4,128,128]{4,3,2,1,0:T(8,128)(2,1)S(1)}, bf16[2,1,4,128,128]{4,3,2,1,0:T(8,128)(2,1)}, u32[]{:S(2)}) copy-start(bf16[2,1,4,128,128]{4,3,2,1,0:T(8,128)(2,1)} %refs_1_.5) | copy-start | bytes 786436
  9.5 5.0 %copy-start.3 = (s32[1,4]{1,0:T(1,128)S(1)}, s32[1,4]{1,0:T(1,128)}, u32[]{:S(2)}) copy-start(s32[1,4]{1,0:T(1,128)} %refs_2_.3) | copy-start | bytes 52
  9.5 5.0 %copy-start.4 = (s32[1,4]{1,0:T(1,128)S(1)}, s32[1,4]{1,0:T(1,128)}, u32[]{:S(2)}) copy-start(s32[1,4]{1,0:T(1,128)} %refs_3_.5) | copy-start | bytes 52
  9.5 5.0 %copy-start.5 = (s32[1,4]{1,0:T(1,128)S(1)}, s32[1,4]{1,0:T(1,128)}, u32[]{:S(2)}) copy-start(s32[1,4]{1,0:T(1,128)} %refs_4_.5) | copy-start | bytes 52
  15.5 5.3 %collective-permute-start.4 = (bf16[192,128]{1,0:T(8,128)(2,1)S(1)}, bf16[192,128]{1,0:T(8,128)(2,1)S(1)}, u32[]{:S(2)}, u32[]{:S(2)}) collective-permute-start(bf16[192,128]{1,0:T(8,128)(2,1)S(1)} %get-tuple-element.20), channel_id=1, source_target_pairs={{0,1},{1,0},{2,3},{3,2},{4,5},{5,4},{6,7},{7,6},{8,9},{9,8},{10,11... | collective-permute-start | bytes 147464 | tf_op jit(solution)/shard_map/ppermute | solution.py:323
  15.6 5.3 %collective-permute-start.5 = (bf16[192,128]{1,0:T(8,128)(2,1)S(1)}, bf16[192,128]{1,0:T(8,128)(2,1)S(1)}, u32[]{:S(2)}, u32[]{:S(2)}) collective-permute-start(bf16[192,128]{1,0:T(8,128)(2,1)S(1)} %get-tuple-element.21), channel_id=1, source_target_pairs={{0,1},{1,0},{2,3},{3,2},{4,5},{5,4},{6,7},{7,6},{8,9},{9,8},{10,11... | collective-permute-start | bytes 147464 | tf_op jit(solution)/shard_map/ppermute | solution.py:323
  17.4 5.9 %collective-permute-start.6 = (bf16[192,128]{1,0:T(8,128)(2,1)S(1)}, bf16[192,128]{1,0:T(8,128)(2,1)S(1)}, u32[]{:S(2)}, u32[]{:S(2)}) collective-permute-start(bf16[192,128]{1,0:T(8,128)(2,1)S(1)} %get-tuple-element.22), channel_id=1, source_target_pairs={{0,1},{1,0},{2,3},{3,2},{4,5},{5,4},{6,7},{7,6},{8,9},{9,8},{10,11... | collective-permute-start | bytes 147464 | tf_op jit(solution)/shard_map/ppermute | solution.py:323

commit v10 on v9

--- a/solution.py
+++ b/solution.py
@@ -169,10 +169,14 @@
     n = lax.axis_size("net")
     me = lax.axis_index("net")
     tm = lax.axis_index("tm")
-    z_ref, iface_ref, send_ref, recv_ref, live_ref, table_ref, state_in_ref, *refs = refs
+    if fix:
+        jac_ref, cols_ref, *refs = refs
+    else:
+        z_ref, *refs = refs
+    iface_ref, send_ref, recv_ref, live_ref, table_ref, state_in_ref, *refs = refs
     arrived, refs = refs[: n - 1], refs[n - 1 :]
     acc_ref = refs.pop()
-    blocks, cols, width = z_ref.shape
+    blocks, cols, width = acc_ref.shape
     before = []
     if store:
         sems = refs.pop()
@@ -196,7 +200,8 @@
             rows += [arrived[d - 1][cols : cols + 1].astype(jnp.float32) for d in range(1, n)]
             keep = kept(table, rows)
             for i in range(blocks):
-                acc_ref[i] = jnp.where(keep[:, 0:1] > 0.0, z_ref[i], 0.0)
+                own = own_sum(i, state_in_ref, jac_ref.at[step], cols_ref, table, step)
+                acc_ref[i] = jnp.where(keep[:, 0:1] > 0.0, own, 0.0)
         else:
             acc_ref[...] = z_ref[...]
         for d in range(n):
@@ -273,8 +278,8 @@
         )(state, jac, near, table)
 
     def join(z, step, fix, state, arrived, send, section, opening=(), before=(), out=None, store=0):
-        arrays = [z, iface_jac, iface_send, iface_recv, iface_live, table, state]
-        specs = [VMEM, VMEM, SMEM, SMEM, SMEM, VMEM, VMEM]
+        arrays = [*([jac, near] if fix else [z]), iface_jac, iface_send, iface_recv, iface_live, table, state]
+        specs = [*([VMEM, SMEM] if fix else [VMEM]), VMEM, SMEM, SMEM, SMEM, VMEM, VMEM]
         arrays += arrived
         specs += [VMEM] * (n - 1)
         shapes = []
@@ -329,8 +334,8 @@
     opening = [state]
     out = None
     for r in range(1, tm):
+        arrived = exchange(outgoing, r - 1, r)
         state = swap(state, r - 1, r, 0)
-        arrived = exchange(outgoing, r - 1, r)
         if r == 1:
             handed = arrived
         before = []
@@ -338,7 +343,7 @@
             fix = r == 1 and s == 0
             if s > 0:
                 arrived = exchange(outgoing, r, r)
-            z = own(state, s)
+            z = None if fix else own(state, s)
             if s < steps - 1:
                 state, *outgoing = join(z, s, fix, state, arrived, True, r)
                 before.append(state)

time: 25 us -> 24.5 us (0.980)
  Pallas kernels: 5.37 us -> 4.58 us
    pallas_call x2 -> x1, Pallas kernels: 1.78 us -> 0.89 us  [own(): pl.pallas_call(functools.partial(own_kernel, step), out_shape=f32(whole.s...]
  transfers between devices with their start and end apart: 7 -> 7, of which waited for: 4 -> 3; matrix products, arithmetic and copies ran while one was open for 0% -> 0% of each run, Pallas kernels for 7% -> 4%
where the time goes in v10:
time: 24.5 us; the launch traced here: 24.4 us
  starting transfers between devices  11.3 us (46%)
  waiting for transfers between devices  8.35 us (34%)
  Pallas kernels  4.58 us (19%)
    ppermute x7, starting transfers between devices, swap(): return lax.ppermute(block, ('tm', 'net', 'cols'), pairs)  11.3 us
    ppermute x7, waiting for transfers between devices, swap(): return lax.ppermute(block, ('tm', 'net', 'cols'), pairs)  8.35 us
    pallas_call x2, Pallas kernels, join(): pl.pallas_call(functools.partial(join_kernel, step, fix, send, section, f...  2.63 us
    pallas_call x1, Pallas kernels, local(): pl.pallas_call(second_kernel, out_shape=[f32((cols, table_rows)), whole]...  1.06 us
    pallas_call x1, Pallas kernels, own(): pl.pallas_call(functools.partial(own_kernel, step), out_shape=f32(whole.s...  0.89 us
  transfers between devices with their start and end apart: 7, of which 3 were waited for; matrix products, arithmetic and copies ran while one was open for 0% of the time, Pallas kernels for 4%

profile of v10, /device:TPU:4, one launch (start us, length us, event | category | flops | bytes accessed | tf_op | source)
XLA Modules:
  0.0 24.4 jit_solution(13991084125967541116)
XLA Ops:
  0.0 0.0 copy-start
  0.0 0.0 copy-start.1
  0.0 1.1 %shard_map.82 = (f32[192,8]{1,0:T(8,128)S(1)}, bf16[4,192,128]{2,1,0:T(8,128)(2,1)S(1)}, bf16[208,128]{1,0:T(8,128)(2,1)S(1)}, bf16[208,128]{1,0:T(8,128)(2,1)S(1)}, bf16[208,128]{1,0:T(8,128)(2,1)S(1)}) custom-call(bf16[2,4,3,128,128]{4,3,2,1,0:T(8,128)(2,1)} %refs_14_.1, bf16[2,1,4,128,128]{4,3,2,1,0:T(8,128)(2,1)} %refs_1_.3, s32[2,4]{1,0:T(2,128)} %bitcast.2, ...), custom_call_target="tpu_custom_call" | custom-call | tf_op jit(solution)/shard_map/pallas_call | solution.py:254
  1.1 0.1 collective-permute-start
  1.2 3.0 %collective-permute-start.1 = (bf16[208,128]{1,0:T(8,128)(2,1)S(1)}, bf16[208,128]{1,0:T(8,128)(2,1)S(1)}, u32[]{:S(2)}, u32[]{:S(2)}) collective-permute-start(bf16[208,128]{1,0:T(8,128)(2,1)S(1)} %get-tuple-element.16), channel_id=1, source_target_pairs={{0,20},{1,21},{2,22},{3,23},{4,16},{5,17},{6,18},{7,19},{8,28},{9,... | collective-permute-start | bytes 159752 | tf_op jit(solution)/shard_map/ppermute | solution.py:328
  4.2 3.5 %collective-permute-start.2 = (bf16[208,128]{1,0:T(8,128)(2,1)S(1)}, bf16[208,128]{1,0:T(8,128)(2,1)S(1)}, u32[]{:S(2)}, u32[]{:S(2)}) collective-permute-start(bf16[208,128]{1,0:T(8,128)(2,1)S(1)} %get-tuple-element.17), channel_id=1, source_target_pairs={{0,24},{1,25},{2,26},{3,27},{4,28},{5,29},{6,30},{7,31},{8,16},{9,... | collective-permute-start | bytes 159752 | tf_op jit(solution)/shard_map/ppermute | solution.py:328
  7.7 0.0 copy-start.4
  7.7 0.0 copy-start.5
  7.7 0.0 copy-start.2
  7.7 0.0 copy-start.3
  7.7 0.2 collective-permute-start.3
  8.0 0.0 collective-permute-done.1.refs_8_.refs_11_
  8.0 3.0 %collective-permute-done.2.refs_9_.refs_12_ = bf16[208,128]{1,0:T(8,128)(2,1)S(1)} collective-permute-done((bf16[208,128]{1,0:T(8,128)(2,1)S(1)}, bf16[208,128]{1,0:T(8,128)(2,1)S(1)}, u32[]{:S(2)}, u32[]{:S(2)}) %collective-permute-start.2) | collective-permute-done | bytes 53280 | tf_op jit(solution)/shard_map/ppermute | solution.py:328
  11.0 3.7 %collective-permute-done.3.refs_10_.refs_13_ = bf16[208,128]{1,0:T(8,128)(2,1)S(1)} collective-permute-done((bf16[208,128]{1,0:T(8,128)(2,1)S(1)}, bf16[208,128]{1,0:T(8,128)(2,1)S(1)}, u32[]{:S(2)}, u32[]{:S(2)}) %collective-permute-start.3) | collective-permute-done | bytes 53280 | tf_op jit(solution)/shard_map/ppermute | solution.py:328
  14.6 0.0 collective-permute-done.refs_7_
  14.6 0.0 copy-done
  14.6 0.0 copy-done.1
  14.6 0.0 copy-done.4
  14.7 0.0 copy-done.5
  14.7 0.0 copy-done.2
  14.7 0.0 copy-done.3
  14.7 1.0 %shard_map.83 = (bf16[4,192,128]{2,1,0:T(8,128)(2,1)S(1)}, bf16[192,128]{1,0:T(8,128)(2,1)S(1)}, bf16[192,128]{1,0:T(8,128)(2,1)S(1)}, bf16[192,128]{1,0:T(8,128)(2,1)S(1)}) custom-call(bf16[2,4,3,128,128]{4,3,2,1,0:T(8,128)(2,1)S(1)} %copy-done, s32[2,4]{1,0:T(2,128)S(1)} %bitcast.3, bf16[2,1,4,128,128]{4,3,2,1,0:T(8,128)(2,1)S(1)} %copy-done.1, ...), custom_call_target="tpu_custom_call" | custom-call | tf_op jit(solution)/shard_map/pallas_call | solution.py:310
  15.7 0.1 collective-permute-start.4
  15.8 0.7 %collective-permute-start.5 = (bf16[192,128]{1,0:T(8,128)(2,1)S(1)}, bf16[192,128]{1,0:T(8,128)(2,1)S(1)}, u32[]{:S(2)}, u32[]{:S(2)}) collective-permute-start(bf16[192,128]{1,0:T(8,128)(2,1)S(1)} %get-tuple-element.21), channel_id=1, source_target_pairs={{0,1},{1,0},{2,3},{3,2},{4,5},{5,4},{6,7},{7,6},{8,9},{9,8},{10,11... | collective-permute-start | bytes 147464 | tf_op jit(solution)/shard_map/ppermute | solution.py:328
  16.5 3.7 %collective-permute-start.6 = (bf16[192,128]{1,0:T(8,128)(2,1)S(1)}, bf16[192,128]{1,0:T(8,128)(2,1)S(1)}, u32[]{:S(2)}, u32[]{:S(2)}) collective-permute-start(bf16[192,128]{1,0:T(8,128)(2,1)S(1)} %get-tuple-element.22), channel_id=1, source_target_pairs={{0,1},{1,0},{2,3},{3,2},{4,5},{5,4},{6,7},{7,6},{8,9},{9,8},{10,11... | collective-permute-start | bytes 147464 | tf_op jit(solution)/shard_map/ppermute | solution.py:328
  20.2 0.9 %shard_map.84.refs_0_ = f32[4,192,128]{2,1,0:T(8,128)S(1)} custom-call(bf16[4,192,128]{2,1,0:T(8,128)(2,1)S(1)} %get-tuple-element.19.state_ref.refs_6_.refs_16_, bf16[2,4,3,128,128]{4,3,2,1,0:T(8,128)(2,1)S(1)} %copy-done, s32[2,4]{1,0:T(2,128)S(1)} %bitcast.4, f32[192,8]{1,0:T(8,128)S(1)} %get-tuple-element.14.refs_6_.table_ref.refs_5_), custom_call_target="tpu_custom_call" | custom-call | tf_op jit(solution)/shard_map/pallas_call | solution.py:272
  21.1 0.0 collective-permute-done.4.refs_7_
  21.1 0.0 collective-permute-done.5.refs_8_
  21.1 1.7 %collective-permute-done.6.refs_9_ = bf16[192,128]{1,0:T(8,128)(2,1)S(1)} collective-permute-done((bf16[192,128]{1,0:T(8,128)(2,1)S(1)}, bf16[192,128]{1,0:T(8,128)(2,1)S(1)}, u32[]{:S(2)}, u32[]{:S(2)}) %collective-permute-start.6) | collective-permute-done | bytes 49184 | tf_op jit(solution)/shard_map/ppermute | solution.py:328
  22.8 1.6 %shard_map.85 = bf16[2,192,512]{2,1,0:T(8,128)(2,1)} custom-call(f32[4,192,128]{2,1,0:T(8,128)S(1)} %shard_map.84.refs_0_, bf16[2,1,4,128,128]{4,3,2,1,0:T(8,128)(2,1)S(1)} %copy-done.1, s32[1,4]{1,0:T(1,128)S(1)} %copy-done.3, s32[1,4]{1,0:T(1,128)S(1)} %copy-done.4, s32[1,4]{1,0:T(1,128)S(1)} %copy-done.5, ...), custom_call_target="tpu_custom_call" | custom-call | tf_op jit(solution)/shard_map/pallas_call | solution.py:310
Async XLA Ops:
  0.0 14.6 %copy-start = (bf16[2,4,3,128,128]{4,3,2,1,0:T(8,128)(2,1)S(1)}, bf16[2,4,3,128,128]{4,3,2,1,0:T(8,128)(2,1)}, u32[]{:S(2)}) copy-start(bf16[2,4,3,128,128]{4,3,2,1,0:T(8,128)(2,1)} %refs_14_.1) | copy-start | bytes 2359300
  0.0 14.6 %copy-start.1 = (bf16[2,1,4,128,128]{4,3,2,1,0:T(8,128)(2,1)S(1)}, bf16[2,1,4,128,128]{4,3,2,1,0:T(8,128)(2,1)}, u32[]{:S(2)}) copy-start(bf16[2,1,4,128,128]{4,3,2,1,0:T(8,128)(2,1)} %refs_1_.3) | copy-start | bytes 786436
  1.1 13.6 %collective-permute-start = (bf16[4,192,128]{2,1,0:T(8,128)(2,1)S(1)}, bf16[4,192,128]{2,1,0:T(8,128)(2,1)S(1)}, u32[]{:S(2)}, u32[]{:S(2)}) collective-permute-start(bf16[4,192,128]{2,1,0:T(8,128)(2,1)S(1)} %get-tuple-element.15.refs_10_), channel_id=1, source_target_pairs={{0,16},{1,17},{2,18},{3,19},{4,20},{5,21},{6,22},{7,23},{8,24},{9,... | collective-permute-start | bytes 589832 | tf_op jit(solution)/shard_map/ppermute | solution.py:328
  1.2 6.8 %collective-permute-start.1 = (bf16[208,128]{1,0:T(8,128)(2,1)S(1)}, bf16[208,128]{1,0:T(8,128)(2,1)S(1)}, u32[]{:S(2)}, u32[]{:S(2)}) collective-permute-start(bf16[208,128]{1,0:T(8,128)(2,1)S(1)} %get-tuple-element.16), channel_id=1, source_target_pairs={{0,20},{1,21},{2,22},{3,23},{4,16},{5,17},{6,18},{7,19},{8,28},{9,... | collective-permute-start | bytes 159752 | tf_op jit(solution)/shard_map/ppermute | solution.py:328
  4.2 6.8 %collective-permute-start.2 = (bf16[208,128]{1,0:T(8,128)(2,1)S(1)}, bf16[208,128]{1,0:T(8,128)(2,1)S(1)}, u32[]{:S(2)}, u32[]{:S(2)}) collective-permute-start(bf16[208,128]{1,0:T(8,128)(2,1)S(1)} %get-tuple-element.17), channel_id=1, source_target_pairs={{0,24},{1,25},{2,26},{3,27},{4,28},{5,29},{6,30},{7,31},{8,16},{9,... | collective-permute-start | bytes 159752 | tf_op jit(solution)/shard_map/ppermute | solution.py:328
  7.7 6.9 %copy-start.4 = (s32[1,4]{1,0:T(1,128)S(1)}, s32[1,4]{1,0:T(1,128)}, u32[]{:S(2)}) copy-start(s32[1,4]{1,0:T(1,128)} %refs_3_.5) | copy-start | bytes 52
  7.7 6.9 %copy-start.5 = (s32[1,4]{1,0:T(1,128)S(1)}, s32[1,4]{1,0:T(1,128)}, u32[]{:S(2)}) copy-start(s32[1,4]{1,0:T(1,128)} %refs_4_.5) | copy-start | bytes 52
  7.7 6.9 %copy-start.2 = (s32[4,2]{0,1:T(2,128)S(1)}, s32[4,2]{0,1:T(2,128)}, u32[]{:S(2)}) copy-start(s32[4,2]{0,1:T(2,128)} %param.9) | copy-start | bytes 100
  7.7 6.9 %copy-start.3 = (s32[1,4]{1,0:T(1,128)S(1)}, s32[1,4]{1,0:T(1,128)}, u32[]{:S(2)}) copy-start(s32[1,4]{1,0:T(1,128)} %refs_2_.3) | copy-start | bytes 52
  7.7 6.9 %collective-permute-start.3 = (bf16[208,128]{1,0:T(8,128)(2,1)S(1)}, bf16[208,128]{1,0:T(8,128)(2,1)S(1)}, u32[]{:S(2)}, u32[]{:S(2)}) collective-permute-start(bf16[208,128]{1,0:T(8,128)(2,1)S(1)} %get-tuple-element.18), channel_id=1, source_target_pairs={{0,28},{1,29},{2,30},{3,31},{4,24},{5,25},{6,26},{7,27},{8,20},{9,... | collective-permute-start | bytes 159752 | tf_op jit(solution)/shard_map/ppermute | solution.py:328
  15.7 5.3 %collective-permute-start.4 = (bf16[192,128]{1,0:T(8,128)(2,1)S(1)}, bf16[192,128]{1,0:T(8,128)(2,1)S(1)}, u32[]{:S(2)}, u32[]{:S(2)}) collective-permute-start(bf16[192,128]{1,0:T(8,128)(2,1)S(1)} %get-tuple-element.20), channel_id=1, source_target_pairs={{0,1},{1,0},{2,3},{3,2},{4,5},{5,4},{6,7},{7,6},{8,9},{9,8},{10,11... | collective-permute-start | bytes 147464 | tf_op jit(solution)/shard_map/ppermute | solution.py:328
  15.8 5.3 %collective-permute-start.5 = (bf16[192,128]{1,0:T(8,128)(2,1)S(1)}, bf16[192,128]{1,0:T(8,128)(2,1)S(1)}, u32[]{:S(2)}, u32[]{:S(2)}) collective-permute-start(bf16[192,128]{1,0:T(8,128)(2,1)S(1)} %get-tuple-element.21), channel_id=1, source_target_pairs={{0,1},{1,0},{2,3},{3,2},{4,5},{5,4},{6,7},{7,6},{8,9},{9,8},{10,11... | collective-permute-start | bytes 147464 | tf_op jit(solution)/shard_map/ppermute | solution.py:328
  16.5 6.3 %collective-permute-start.6 = (bf16[192,128]{1,0:T(8,128)(2,1)S(1)}, bf16[192,128]{1,0:T(8,128)(2,1)S(1)}, u32[]{:S(2)}, u32[]{:S(2)}) collective-permute-start(bf16[192,128]{1,0:T(8,128)(2,1)S(1)} %get-tuple-element.22), channel_id=1, source_target_pairs={{0,1},{1,0},{2,3},{3,2},{4,5},{5,4},{6,7},{7,6},{8,9},{9,8},{10,11... | collective-permute-start | bytes 147464 | tf_op jit(solution)/shard_map/ppermute | solution.py:328

commit v11 on v10

--- a/solution.py
+++ b/solution.py
@@ -63,13 +63,13 @@
 
 
 def second_kernel(*refs):
-    jac_hbm, iface_hbm, *small, table_ref, state_ref = refs[:10]
+    jac_hbm, iface_hbm, *small, table_ref = refs[:9]
     n = lax.axis_size("net")
     me = lax.axis_index("net")
-    outgoing, refs = refs[10 : 9 + n], refs[9 + n :]
-    jac_ref, iface_ref, *loaded, first_ref, z_ref, sems = refs
+    jac_ref, iface_ref, *loaded, first_ref, state_ref, z_ref, sems = refs[-12:]
     cols_ref, send_ref, recv_ref, live_ref, node_ref, gain_ref = loaded
     blocks, cols, width = state_ref.shape
+    states, outgoing = refs[9 : 9 + blocks], refs[9 + blocks : -12]
     loads = [
         pltpu.make_async_copy(source, target, sems.at[i])
         for i, (source, target) in enumerate(
@@ -119,6 +119,8 @@
             sent = jnp.where(away == float(d), shot, 0.0).astype(first_ref.dtype)
             add_coupled(sent, iface_ref[q], live_ref[0, q], recv_ref[0, q], z_ref)
         state_ref[...] = z_ref[...].astype(state_ref.dtype)
+        for i in range(blocks):
+            states[i][...] = state_ref[i]
         for d in range(1, n):
             outgoing[d - 1][pl.ds(0, cols)] = state_ref[send_ref[0, me ^ d]]
 
@@ -146,7 +148,7 @@
         z_ref[i] = own_sum(i, state_ref, jac_ref.at[step], cols_ref, table, step)
 
 
-def first_states(states, jac_ref, iface_ref, cols_ref, send_ref, recv_ref, live_ref, table_ref, handed, made_ref, z_ref):
+def first_states(second, jac_ref, iface_ref, cols_ref, send_ref, recv_ref, live_ref, table_ref, handed, made_ref, z_ref):
     n = lax.axis_size("net")
     blocks, cols, width = z_ref.shape
     table = table_ref[...]
@@ -161,8 +163,8 @@
     rows += [block[cols : cols + 1].astype(jnp.float32) for block in handed]
     keep = kept(table, rows)[:, 0:1]
     for i in range(blocks):
-        made_ref[1, i] = jnp.where(keep > 0.0, states[0][i], jnp.zeros_like(states[0][i]))
-    return [made_ref.at[0], made_ref.at[1], *states[1:]]
+        made_ref[1, i] = jnp.where(keep > 0.0, second[i][...], jnp.zeros_like(second[i]))
+    return [made_ref.at[0], made_ref.at[1]]
 
 
 def join_kernel(step, fix, send, section, firsts, store, *refs):
@@ -173,10 +175,16 @@
         jac_ref, cols_ref, *refs = refs
     else:
         z_ref, *refs = refs
-    iface_ref, send_ref, recv_ref, live_ref, table_ref, state_in_ref, *refs = refs
-    arrived, refs = refs[: n - 1], refs[n - 1 :]
+    iface_ref, send_ref, recv_ref, live_ref, table_ref, *refs = refs
     acc_ref = refs.pop()
     blocks, cols, width = acc_ref.shape
+    if fix:
+        state_in_ref = refs.pop()
+        for i in range(blocks):
+            state_in_ref[i] = refs.pop(0)[...]
+    else:
+        state_in_ref = refs.pop(0)
+    arrived, refs = refs[: n - 1], refs[n - 1 :]
     before = []
     if store:
         sems = refs.pop()
@@ -251,16 +259,17 @@
         pltpu.with_memory_space_constraint(x, pltpu.HBM)
         for x in (jac, iface_jac, near, iface_send, iface_recv, iface_live, node, ctrl_gain)
     ]
-    table, state, *outgoing = pl.pallas_call(
+    table, *outgoing = pl.pallas_call(
         second_kernel,
-        out_shape=[f32((cols, table_rows)), whole] + [bf16((cols + ROWS, width))] * (n - 1),
+        out_shape=[f32((cols, table_rows))] + [one] * blocks + [bf16((cols + ROWS, width))] * (n - 1),
         in_specs=[HBM] * len(pinned),
-        out_specs=[VMEM] * (n + 1),
+        out_specs=[VMEM] * (blocks + n),
         scratch_shapes=[
             pltpu.VMEM((blocks, kinds, width, width), jnp.bfloat16),
             pltpu.VMEM((n, width, width), jnp.bfloat16),
             *[pltpu.SMEM(x.shape, x.dtype) for x in (near, iface_send, iface_recv, iface_live)],
             *[pltpu.VMEM(x.shape, x.dtype) for x in (node, ctrl_gain)],
+            pltpu.VMEM(whole.shape, jnp.bfloat16),
             pltpu.VMEM(whole.shape, jnp.bfloat16),
             pltpu.VMEM(whole.shape, jnp.float32),
             DMA((len(pinned),)),
@@ -278,12 +287,16 @@
         )(state, jac, near, table)
 
     def join(z, step, fix, state, arrived, send, section, opening=(), before=(), out=None, store=0):
-        arrays = [*([jac, near] if fix else [z]), iface_jac, iface_send, iface_recv, iface_live, table, state]
-        specs = [*([VMEM, SMEM] if fix else [VMEM]), VMEM, SMEM, SMEM, SMEM, VMEM, VMEM]
+        arrays = [*([jac, near] if fix else [z]), iface_jac, iface_send, iface_recv, iface_live, table]
+        specs = [*([VMEM, SMEM] if fix else [VMEM]), VMEM, SMEM, SMEM, SMEM, VMEM]
+        states = state if fix else [state]
+        arrays += states
+        specs += [VMEM] * len(states)
         arrays += arrived
         specs += [VMEM] * (n - 1)
         shapes = []
-        scratch = [pltpu.VMEM(whole.shape, jnp.float32)]
+        scratch = [pltpu.VMEM(whole.shape, jnp.bfloat16)] if fix else []
+        scratch.append(pltpu.VMEM(whole.shape, jnp.float32))
         aliases = {}
         out_specs = []
         if store:
@@ -331,13 +344,15 @@
         arrived = [swap(outgoing[d - 1], first, second, d) for d in reversed(range(1, n))]
         return arrived[::-1]
 
-    opening = [state]
+    opening, outgoing = outgoing[:blocks], outgoing[blocks:]
     out = None
     for r in range(1, tm):
         arrived = exchange(outgoing, r - 1, r)
-        state = swap(state, r - 1, r, 0)
         if r == 1:
             handed = arrived
+            state = [swap(block, 0, 1, 0) for block in opening]
+        else:
+            state = swap(state, r - 1, r, 0)
         before = []
         for s in range(steps):
             fix = r == 1 and s == 0

time: 24.5 us -> 27.1 us (1.11)
  starting transfers between devices: 11.3 us -> 13.7 us
    ppermute x7 -> x10, starting transfers between devices: 11.3 us -> 13.7 us  [swap(): return lax.ppermute(block, ('tm', 'net', 'cols'), pairs)]
    ppermute x7 -> x10, waiting for transfers between devices: 8.35 us -> 8.54 us  [swap(): return lax.ppermute(block, ('tm', 'net', 'cols'), pairs)]
  transfers between devices with their start and end apart: 7 -> 10, of which waited for: 3 -> 4; matrix products, arithmetic and copies ran while one was open for 0% -> 0% of each run, Pallas kernels for 4% -> 3%
where the time goes in v11:
time: 27.1 us; the launch traced here: 26.9 us
  starting transfers between devices  13.7 us (51%)
  waiting for transfers between devices  8.54 us (32%)
  Pallas kernels  4.59 us (17%)
    ppermute x10, starting transfers between devices, swap(): return lax.ppermute(block, ('tm', 'net', 'cols'), pairs)  13.7 us
    ppermute x10, waiting for transfers between devices, swap(): return lax.ppermute(block, ('tm', 'net', 'cols'), pairs)  8.54 us
    pallas_call x2, Pallas kernels, join(): pl.pallas_call(functools.partial(join_kernel, step, fix, send, section, f...  2.64 us
    pallas_call x1, Pallas kernels, local(): pl.pallas_call(second_kernel, out_shape=[f32((cols, table_rows))] + [one]...  1.06 us
    pallas_call x1, Pallas kernels, own(): pl.pallas_call(functools.partial(own_kernel, step), out_shape=f32(whole.s...  0.89 us
  transfers between devices with their start and end apart: 10, of which 4 were waited for; matrix products, arithmetic and copies ran while one was open for 0% of the time, Pallas kernels for 3%

profile of v11, /device:TPU:4, one launch (start us, length us, event | category | flops | bytes accessed | tf_op | source)
XLA Modules:
  0.0 26.9 jit_solution(15315643294044645531)
XLA Ops:
  0.0 0.0 copy-start
  0.0 1.1 %shard_map.82 = (f32[192,8]{1,0:T(8,128)S(1)}, bf16[192,128]{1,0:T(8,128)(2,1)S(1)}, bf16[192,128]{1,0:T(8,128)(2,1)S(1)}, bf16[192,128]{1,0:T(8,128)(2,1)S(1)},...) custom-call(bf16[2,4,3,128,128]{4,3,2,1,0:T(8,128)(2,1)} %refs_17_.1, ...), custom_call_target="tpu_custom_call" | custom-call | tf_op jit(solution)/shard_map/pallas_call | solution.py:262
  1.1 0.1 collective-permute-start
  1.2 1.9 %collective-permute-start.1 = (bf16[192,128]{1,0:T(8,128)(2,1)S(1)}, bf16[192,128]{1,0:T(8,128)(2,1)S(1)}, u32[]{:S(2)}, u32[]{:S(2)}) collective-permute-start(bf16[192,128]{1,0:T(8,128)(2,1)S(1)} %get-tuple-element.19.refs_11_), channel_id=1, source_target_pairs={{0,16},{1,17},{2,18},{3,19},{4,20},{5,21},{6,22},{7,23},{8,24},{9,... | collective-permute-start | bytes 147464 | tf_op jit(solution)/shard_map/ppermute | solution.py:341
  3.2 2.5 %collective-permute-start.4 = (bf16[208,128]{1,0:T(8,128)(2,1)S(1)}, bf16[208,128]{1,0:T(8,128)(2,1)S(1)}, u32[]{:S(2)}, u32[]{:S(2)}) collective-permute-start(bf16[208,128]{1,0:T(8,128)(2,1)S(1)} %get-tuple-element.22), channel_id=1, source_target_pairs={{0,20},{1,21},{2,22},{3,23},{4,16},{5,17},{6,18},{7,19},{8,28},{9,... | collective-permute-start | bytes 159752 | tf_op jit(solution)/shard_map/ppermute | solution.py:341
  5.7 2.5 %collective-permute-start.5 = (bf16[208,128]{1,0:T(8,128)(2,1)S(1)}, bf16[208,128]{1,0:T(8,128)(2,1)S(1)}, u32[]{:S(2)}, u32[]{:S(2)}) collective-permute-start(bf16[208,128]{1,0:T(8,128)(2,1)S(1)} %get-tuple-element.23), channel_id=1, source_target_pairs={{0,24},{1,25},{2,26},{3,27},{4,28},{5,29},{6,30},{7,31},{8,16},{9,... | collective-permute-start | bytes 159752 | tf_op jit(solution)/shard_map/ppermute | solution.py:341
  8.2 0.0 collective-permute-start.6
  8.2 0.0 collective-permute-done.refs_7_
  8.2 1.7 %collective-permute-start.2 = (bf16[192,128]{1,0:T(8,128)(2,1)S(1)}, bf16[192,128]{1,0:T(8,128)(2,1)S(1)}, u32[]{:S(2)}, u32[]{:S(2)}) collective-permute-start(bf16[192,128]{1,0:T(8,128)(2,1)S(1)} %get-tuple-element.20.refs_12_), channel_id=1, source_target_pairs={{0,16},{1,17},{2,18},{3,19},{4,20},{5,21},{6,22},{7,23},{8,24},{9,... | collective-permute-start | bytes 147464 | tf_op jit(solution)/shard_map/ppermute | solution.py:341
  9.9 0.0 collective-permute-done.1.refs_8_
  9.9 0.0 copy-start.3
  9.9 0.4 %collective-permute-start.3 = (bf16[192,128]{1,0:T(8,128)(2,1)S(1)}, bf16[192,128]{1,0:T(8,128)(2,1)S(1)}, u32[]{:S(2)}, u32[]{:S(2)}) collective-permute-start(bf16[192,128]{1,0:T(8,128)(2,1)S(1)} %get-tuple-element.21.refs_13_), channel_id=1, source_target_pairs={{0,16},{1,17},{2,18},{3,19},{4,20},{5,21},{6,22},{7,23},{8,24},{9,... | collective-permute-start | bytes 147464 | tf_op jit(solution)/shard_map/ppermute | solution.py:341
  10.4 2.7 %collective-permute-done.2.refs_9_ = bf16[192,128]{1,0:T(8,128)(2,1)S(1)} collective-permute-done((bf16[192,128]{1,0:T(8,128)(2,1)S(1)}, bf16[192,128]{1,0:T(8,128)(2,1)S(1)}, u32[]{:S(2)}, u32[]{:S(2)}) %collective-permute-start.2) | collective-permute-done | bytes 49184 | tf_op jit(solution)/shard_map/ppermute | solution.py:341
  13.1 1.0 %collective-permute-done.3.refs_10_ = bf16[192,128]{1,0:T(8,128)(2,1)S(1)} collective-permute-done((bf16[192,128]{1,0:T(8,128)(2,1)S(1)}, bf16[192,128]{1,0:T(8,128)(2,1)S(1)}, u32[]{:S(2)}, u32[]{:S(2)}) %collective-permute-start.3) | collective-permute-done | bytes 49184 | tf_op jit(solution)/shard_map/ppermute | solution.py:341
  14.1 0.0 collective-permute-done.4.refs_11_.refs_14_
  14.1 0.0 collective-permute-done.5.refs_12_.refs_15_
  14.1 1.0 %collective-permute-done.6.refs_13_.refs_16_ = bf16[208,128]{1,0:T(8,128)(2,1)S(1)} collective-permute-done((bf16[208,128]{1,0:T(8,128)(2,1)S(1)}, bf16[208,128]{1,0:T(8,128)(2,1)S(1)}, u32[]{:S(2)}, u32[]{:S(2)}) %collective-permute-start.6) | collective-permute-done | bytes 53280 | tf_op jit(solution)/shard_map/ppermute | solution.py:341
  15.1 0.0 copy-done
  15.1 0.0 copy-done.1
  15.1 0.0 copy-done.4
  15.1 0.0 copy-done.5
  15.1 0.0 copy-done.2
  15.1 0.0 copy-done.3
  15.1 1.1 %shard_map.83 = (bf16[4,192,128]{2,1,0:T(8,128)(2,1)S(1)}, bf16[192,128]{1,0:T(8,128)(2,1)S(1)}, bf16[192,128]{1,0:T(8,128)(2,1)S(1)}, bf16[192,128]{1,0:T(8,128)(2,1)S(1)}) custom-call(bf16[2,4,3,128,128]{4,3,2,1,0:T(8,128)(2,1)S(1)} %copy-done, s32[2,4]{1,0:T(2,128)S(1)} %bitcast.3, bf16[2,1,4,128,128]{4,3,2,1,0:T(8,128)(2,1)S(1)} %copy-done.1, ...), custom_call_target="tpu_custom_call" | custom-call | tf_op jit(solution)/shard_map/pallas_call | solution.py:323
  16.2 0.1 collective-permute-start.7
  16.3 3.2 %collective-permute-start.8 = (bf16[192,128]{1,0:T(8,128)(2,1)S(1)}, bf16[192,128]{1,0:T(8,128)(2,1)S(1)}, u32[]{:S(2)}, u32[]{:S(2)}) collective-permute-start(bf16[192,128]{1,0:T(8,128)(2,1)S(1)} %get-tuple-element.27), channel_id=1, source_target_pairs={{0,1},{1,0},{2,3},{3,2},{4,5},{5,4},{6,7},{7,6},{8,9},{9,8},{10,11... | collective-permute-start | bytes 147464 | tf_op jit(solution)/shard_map/ppermute | solution.py:341
  19.5 1.2 %collective-permute-start.9 = (bf16[192,128]{1,0:T(8,128)(2,1)S(1)}, bf16[192,128]{1,0:T(8,128)(2,1)S(1)}, u32[]{:S(2)}, u32[]{:S(2)}) collective-permute-start(bf16[192,128]{1,0:T(8,128)(2,1)S(1)} %get-tuple-element.28), channel_id=1, source_target_pairs={{0,1},{1,0},{2,3},{3,2},{4,5},{5,4},{6,7},{7,6},{8,9},{9,8},{10,11... | collective-permute-start | bytes 147464 | tf_op jit(solution)/shard_map/ppermute | solution.py:341
  20.6 0.9 %shard_map.84.refs_0_ = f32[4,192,128]{2,1,0:T(8,128)S(1)} custom-call(bf16[4,192,128]{2,1,0:T(8,128)(2,1)S(1)} %get-tuple-element.25.state_ref.refs_6_.refs_19_, bf16[2,4,3,128,128]{4,3,2,1,0:T(8,128)(2,1)S(1)} %copy-done, s32[2,4]{1,0:T(2,128)S(1)} %bitcast.4, f32[192,8]{1,0:T(8,128)S(1)} %get-tuple-element.17.refs_6_.table_ref.refs_5_), custom_call_target="tpu_custom_call" | custom-call | tf_op jit(solution)/shard_map/pallas_call | solution.py:281
  21.5 0.0 collective-permute-done.7.refs_7_
  21.5 0.0 collective-permute-done.8.refs_8_
  21.6 3.8 %collective-permute-done.9.refs_9_ = bf16[192,128]{1,0:T(8,128)(2,1)S(1)} collective-permute-done((bf16[192,128]{1,0:T(8,128)(2,1)S(1)}, bf16[192,128]{1,0:T(8,128)(2,1)S(1)}, u32[]{:S(2)}, u32[]{:S(2)}) %collective-permute-start.9) | collective-permute-done | bytes 49184 | tf_op jit(solution)/shard_map/ppermute | solution.py:341
  25.4 1.6 %shard_map.85 = bf16[2,192,512]{2,1,0:T(8,128)(2,1)} custom-call(f32[4,192,128]{2,1,0:T(8,128)S(1)} %shard_map.84.refs_0_, bf16[2,1,4,128,128]{4,3,2,1,0:T(8,128)(2,1)S(1)} %copy-done.1, s32[1,4]{1,0:T(1,128)S(1)} %copy-done.3, s32[1,4]{1,0:T(1,128)S(1)} %copy-done.4, s32[1,4]{1,0:T(1,128)S(1)} %copy-done.5, ...), custom_call_target="tpu_custom_call" | custom-call | tf_op jit(solution)/shard_map/pallas_call | solution.py:323
  (4 shorter events, 0.0 us)
Async XLA Ops:
  0.0 15.1 %copy-start = (bf16[2,4,3,128,128]{4,3,2,1,0:T(8,128)(2,1)S(1)}, bf16[2,4,3,128,128]{4,3,2,1,0:T(8,128)(2,1)}, u32[]{:S(2)}) copy-start(bf16[2,4,3,128,128]{4,3,2,1,0:T(8,128)(2,1)} %refs_17_.1) | copy-start | bytes 2359300
  0.0 15.1 %copy-start.1 = (bf16[2,1,4,128,128]{4,3,2,1,0:T(8,128)(2,1)S(1)}, bf16[2,1,4,128,128]{4,3,2,1,0:T(8,128)(2,1)}, u32[]{:S(2)}) copy-start(bf16[2,1,4,128,128]{4,3,2,1,0:T(8,128)(2,1)} %refs_1_.3) | copy-start | bytes 786436
  1.1 7.2 %collective-permute-start = (bf16[192,128]{1,0:T(8,128)(2,1)S(1)}, bf16[192,128]{1,0:T(8,128)(2,1)S(1)}, u32[]{:S(2)}, u32[]{:S(2)}) collective-permute-start(bf16[192,128]{1,0:T(8,128)(2,1)S(1)} %get-tuple-element.18.refs_10_), channel_id=1, source_target_pairs={{0,16},{1,17},{2,18},{3,19},{4,20},{5,21},{6,22},{7,23},{8,24},{9,... | collective-permute-start | bytes 147464 | tf_op jit(solution)/shard_map/ppermute | solution.py:341
  1.2 8.7 %collective-permute-start.1 = (bf16[192,128]{1,0:T(8,128)(2,1)S(1)}, bf16[192,128]{1,0:T(8,128)(2,1)S(1)}, u32[]{:S(2)}, u32[]{:S(2)}) collective-permute-start(bf16[192,128]{1,0:T(8,128)(2,1)S(1)} %get-tuple-element.19.refs_11_), channel_id=1, source_target_pairs={{0,16},{1,17},{2,18},{3,19},{4,20},{5,21},{6,22},{7,23},{8,24},{9,... | collective-permute-start | bytes 147464 | tf_op jit(solution)/shard_map/ppermute | solution.py:341
  3.2 10.9 %collective-permute-start.4 = (bf16[208,128]{1,0:T(8,128)(2,1)S(1)}, bf16[208,128]{1,0:T(8,128)(2,1)S(1)}, u32[]{:S(2)}, u32[]{:S(2)}) collective-permute-start(bf16[208,128]{1,0:T(8,128)(2,1)S(1)} %get-tuple-element.22), channel_id=1, source_target_pairs={{0,20},{1,21},{2,22},{3,23},{4,16},{5,17},{6,18},{7,19},{8,28},{9,... | collective-permute-start | bytes 159752 | tf_op jit(solution)/shard_map/ppermute | solution.py:341
  5.7 8.4 %collective-permute-start.5 = (bf16[208,128]{1,0:T(8,128)(2,1)S(1)}, bf16[208,128]{1,0:T(8,128)(2,1)S(1)}, u32[]{:S(2)}, u32[]{:S(2)}) collective-permute-start(bf16[208,128]{1,0:T(8,128)(2,1)S(1)} %get-tuple-element.23), channel_id=1, source_target_pairs={{0,24},{1,25},{2,26},{3,27},{4,28},{5,29},{6,30},{7,31},{8,16},{9,... | collective-permute-start | bytes 159752 | tf_op jit(solution)/shard_map/ppermute | solution.py:341
  8.2 6.8 %collective-permute-start.6 = (bf16[208,128]{1,0:T(8,128)(2,1)S(1)}, bf16[208,128]{1,0:T(8,128)(2,1)S(1)}, u32[]{:S(2)}, u32[]{:S(2)}) collective-permute-start(bf16[208,128]{1,0:T(8,128)(2,1)S(1)} %get-tuple-element.24), channel_id=1, source_target_pairs={{0,28},{1,29},{2,30},{3,31},{4,24},{5,25},{6,26},{7,27},{8,20},{9,... | collective-permute-start | bytes 159752 | tf_op jit(solution)/shard_map/ppermute | solution.py:341
  8.2 4.8 %collective-permute-start.2 = (bf16[192,128]{1,0:T(8,128)(2,1)S(1)}, bf16[192,128]{1,0:T(8,128)(2,1)S(1)}, u32[]{:S(2)}, u32[]{:S(2)}) collective-permute-start(bf16[192,128]{1,0:T(8,128)(2,1)S(1)} %get-tuple-element.20.refs_12_), channel_id=1, source_target_pairs={{0,16},{1,17},{2,18},{3,19},{4,20},{5,21},{6,22},{7,23},{8,24},{9,... | collective-permute-start | bytes 147464 | tf_op jit(solution)/shard_map/ppermute | solution.py:341
  9.9 5.1 %copy-start.4 = (s32[1,4]{1,0:T(1,128)S(1)}, s32[1,4]{1,0:T(1,128)}, u32[]{:S(2)}) copy-start(s32[1,4]{1,0:T(1,128)} %refs_3_.5) | copy-start | bytes 52
  9.9 5.2 %copy-start.5 = (s32[1,4]{1,0:T(1,128)S(1)}, s32[1,4]{1,0:T(1,128)}, u32[]{:S(2)}) copy-start(s32[1,4]{1,0:T(1,128)} %refs_4_.5) | copy-start | bytes 52
  9.9 5.2 %copy-start.2 = (s32[4,2]{0,1:T(2,128)S(1)}, s32[4,2]{0,1:T(2,128)}, u32[]{:S(2)}) copy-start(s32[4,2]{0,1:T(2,128)} %param.9) | copy-start | bytes 100
  9.9 5.2 %copy-start.3 = (s32[1,4]{1,0:T(1,128)S(1)}, s32[1,4]{1,0:T(1,128)}, u32[]{:S(2)}) copy-start(s32[1,4]{1,0:T(1,128)} %refs_2_.3) | copy-start | bytes 52
  9.9 4.2 %collective-permute-start.3 = (bf16[192,128]{1,0:T(8,128)(2,1)S(1)}, bf16[192,128]{1,0:T(8,128)(2,1)S(1)}, u32[]{:S(2)}, u32[]{:S(2)}) collective-permute-start(bf16[192,128]{1,0:T(8,128)(2,1)S(1)} %get-tuple-element.21.refs_13_), channel_id=1, source_target_pairs={{0,16},{1,17},{2,18},{3,19},{4,20},{5,21},{6,22},{7,23},{8,24},{9,... | collective-permute-start | bytes 147464 | tf_op jit(solution)/shard_map/ppermute | solution.py:341
  16.2 5.3 %collective-permute-start.7 = (bf16[192,128]{1,0:T(8,128)(2,1)S(1)}, bf16[192,128]{1,0:T(8,128)(2,1)S(1)}, u32[]{:S(2)}, u32[]{:S(2)}) collective-permute-start(bf16[192,128]{1,0:T(8,128)(2,1)S(1)} %get-tuple-element.26), channel_id=1, source_target_pairs={{0,1},{1,0},{2,3},{3,2},{4,5},{5,4},{6,7},{7,6},{8,9},{9,8},{10,11... | collective-permute-start | bytes 147464 | tf_op jit(solution)/shard_map/ppermute | solution.py:341
  16.3 5.3 %collective-permute-start.8 = (bf16[192,128]{1,0:T(8,128)(2,1)S(1)}, bf16[192,128]{1,0:T(8,128)(2,1)S(1)}, u32[]{:S(2)}, u32[]{:S(2)}) collective-permute-start(bf16[192,128]{1,0:T(8,128)(2,1)S(1)} %get-tuple-element.27), channel_id=1, source_target_pairs={{0,1},{1,0},{2,3},{3,2},{4,5},{5,4},{6,7},{7,6},{8,9},{9,8},{10,11... | collective-permute-start | bytes 147464 | tf_op jit(solution)/shard_map/ppermute | solution.py:341
  19.5 5.9 %collective-permute-start.9 = (bf16[192,128]{1,0:T(8,128)(2,1)S(1)}, bf16[192,128]{1,0:T(8,128)(2,1)S(1)}, u32[]{:S(2)}, u32[]{:S(2)}) collective-permute-start(bf16[192,128]{1,0:T(8,128)(2,1)S(1)} %get-tuple-element.28), channel_id=1, source_target_pairs={{0,1},{1,0},{2,3},{3,2},{4,5},{5,4},{6,7},{7,6},{8,9},{9,8},{10,11... | collective-permute-start | bytes 147464 | tf_op jit(solution)/shard_map/ppermute | solution.py:341

commit v12 on v10

--- a/solution.py
+++ b/solution.py
@@ -328,8 +328,9 @@
         return lax.ppermute(block, ("tm", "net", "cols"), pairs)
 
     def exchange(outgoing, first, second):
-        arrived = [swap(outgoing[d - 1], first, second, d) for d in reversed(range(1, n))]
-        return arrived[::-1]
+        order = range(1, n) if first != second else reversed(range(1, n))
+        arrived = {d: swap(outgoing[d - 1], first, second, d) for d in order}
+        return [arrived[d] for d in range(1, n)]
 
     opening = [state]
     out = None

time: 24.5 us -> 24.5 us (level)
  no operation moved by 1% of the time
where the time goes in v12:
time: 24.5 us; the launch traced here: 24.4 us
  starting transfers between devices  11.3 us (46%)
  waiting for transfers between devices  8.35 us (34%)
  Pallas kernels  4.58 us (19%)
    ppermute x7, starting transfers between devices, swap(): return lax.ppermute(block, ('tm', 'net', 'cols'), pairs)  11.3 us
    ppermute x7, waiting for transfers between devices, swap(): return lax.ppermute(block, ('tm', 'net', 'cols'), pairs)  8.35 us
    pallas_call x2, Pallas kernels, join(): pl.pallas_call(functools.partial(join_kernel, step, fix, send, section, f...  2.63 us
    pallas_call x1, Pallas kernels, local(): pl.pallas_call(second_kernel, out_shape=[f32((cols, table_rows)), whole]...  1.06 us
    pallas_call x1, Pallas kernels, own(): pl.pallas_call(functools.partial(own_kernel, step), out_shape=f32(whole.s...  0.89 us
  transfers between devices with their start and end apart: 7, of which 3 were waited for; matrix products, arithmetic and copies ran while one was open for 0% of the time, Pallas kernels for 4%

profile of v12, /device:TPU:4, one launch (start us, length us, event | category | flops | bytes accessed | tf_op | source)
XLA Modules:
  0.0 24.4 jit_solution(13991084125967541116)
XLA Ops:
  0.0 0.0 copy-start
  0.0 0.0 copy-start.1
  0.0 1.1 %shard_map.82 = (f32[192,8]{1,0:T(8,128)S(1)}, bf16[4,192,128]{2,1,0:T(8,128)(2,1)S(1)}, bf16[208,128]{1,0:T(8,128)(2,1)S(1)}, bf16[208,128]{1,0:T(8,128)(2,1)S(1)}, bf16[208,128]{1,0:T(8,128)(2,1)S(1)}) custom-call(bf16[2,4,3,128,128]{4,3,2,1,0:T(8,128)(2,1)} %refs_14_.1, bf16[2,1,4,128,128]{4,3,2,1,0:T(8,128)(2,1)} %refs_1_.3, s32[2,4]{1,0:T(2,128)} %bitcast.2, ...), custom_call_target="tpu_custom_call" | custom-call | tf_op jit(solution)/shard_map/pallas_call | solution.py:254
  1.1 0.1 collective-permute-start
  1.2 3.0 %collective-permute-start.1 = (bf16[208,128]{1,0:T(8,128)(2,1)S(1)}, bf16[208,128]{1,0:T(8,128)(2,1)S(1)}, u32[]{:S(2)}, u32[]{:S(2)}) collective-permute-start(bf16[208,128]{1,0:T(8,128)(2,1)S(1)} %get-tuple-element.16), channel_id=1, source_target_pairs={{0,20},{1,21},{2,22},{3,23},{4,16},{5,17},{6,18},{7,19},{8,28},{9,... | collective-permute-start | bytes 159752 | tf_op jit(solution)/shard_map/ppermute | solution.py:328
  4.2 3.5 %collective-permute-start.2 = (bf16[208,128]{1,0:T(8,128)(2,1)S(1)}, bf16[208,128]{1,0:T(8,128)(2,1)S(1)}, u32[]{:S(2)}, u32[]{:S(2)}) collective-permute-start(bf16[208,128]{1,0:T(8,128)(2,1)S(1)} %get-tuple-element.17), channel_id=1, source_target_pairs={{0,24},{1,25},{2,26},{3,27},{4,28},{5,29},{6,30},{7,31},{8,16},{9,... | collective-permute-start | bytes 159752 | tf_op jit(solution)/shard_map/ppermute | solution.py:328
  7.7 0.0 copy-start.4
  7.7 0.0 copy-start.5
  7.7 0.0 copy-start.2
  7.7 0.0 copy-start.3
  7.7 0.2 collective-permute-start.3
  8.0 0.0 collective-permute-done.1.refs_8_.refs_11_
  8.0 3.0 %collective-permute-done.2.refs_9_.refs_12_ = bf16[208,128]{1,0:T(8,128)(2,1)S(1)} collective-permute-done((bf16[208,128]{1,0:T(8,128)(2,1)S(1)}, bf16[208,128]{1,0:T(8,128)(2,1)S(1)}, u32[]{:S(2)}, u32[]{:S(2)}) %collective-permute-start.2) | collective-permute-done | bytes 53280 | tf_op jit(solution)/shard_map/ppermute | solution.py:328
  11.0 3.7 %collective-permute-done.3.refs_10_.refs_13_ = bf16[208,128]{1,0:T(8,128)(2,1)S(1)} collective-permute-done((bf16[208,128]{1,0:T(8,128)(2,1)S(1)}, bf16[208,128]{1,0:T(8,128)(2,1)S(1)}, u32[]{:S(2)}, u32[]{:S(2)}) %collective-permute-start.3) | collective-permute-done | bytes 53280 | tf_op jit(solution)/shard_map/ppermute | solution.py:328
  14.6 0.0 collective-permute-done.refs_7_
  14.6 0.0 copy-done
  14.6 0.0 copy-done.1
  14.6 0.0 copy-done.4
  14.7 0.0 copy-done.5
  14.7 0.0 copy-done.2
  14.7 0.0 copy-done.3
  14.7 1.0 %shard_map.83 = (bf16[4,192,128]{2,1,0:T(8,128)(2,1)S(1)}, bf16[192,128]{1,0:T(8,128)(2,1)S(1)}, bf16[192,128]{1,0:T(8,128)(2,1)S(1)}, bf16[192,128]{1,0:T(8,128)(2,1)S(1)}) custom-call(bf16[2,4,3,128,128]{4,3,2,1,0:T(8,128)(2,1)S(1)} %copy-done, s32[2,4]{1,0:T(2,128)S(1)} %bitcast.3, bf16[2,1,4,128,128]{4,3,2,1,0:T(8,128)(2,1)S(1)} %copy-done.1, ...), custom_call_target="tpu_custom_call" | custom-call | tf_op jit(solution)/shard_map/pallas_call | solution.py:310
  15.7 0.1 collective-permute-start.4
  15.8 0.7 %collective-permute-start.5 = (bf16[192,128]{1,0:T(8,128)(2,1)S(1)}, bf16[192,128]{1,0:T(8,128)(2,1)S(1)}, u32[]{:S(2)}, u32[]{:S(2)}) collective-permute-start(bf16[192,128]{1,0:T(8,128)(2,1)S(1)} %get-tuple-element.21), channel_id=1, source_target_pairs={{0,1},{1,0},{2,3},{3,2},{4,5},{5,4},{6,7},{7,6},{8,9},{9,8},{10,11... | collective-permute-start | bytes 147464 | tf_op jit(solution)/shard_map/ppermute | solution.py:328
  16.5 3.7 %collective-permute-start.6 = (bf16[192,128]{1,0:T(8,128)(2,1)S(1)}, bf16[192,128]{1,0:T(8,128)(2,1)S(1)}, u32[]{:S(2)}, u32[]{:S(2)}) collective-permute-start(bf16[192,128]{1,0:T(8,128)(2,1)S(1)} %get-tuple-element.22), channel_id=1, source_target_pairs={{0,1},{1,0},{2,3},{3,2},{4,5},{5,4},{6,7},{7,6},{8,9},{9,8},{10,11... | collective-permute-start | bytes 147464 | tf_op jit(solution)/shard_map/ppermute | solution.py:328
  20.2 0.9 %shard_map.84.refs_0_ = f32[4,192,128]{2,1,0:T(8,128)S(1)} custom-call(bf16[4,192,128]{2,1,0:T(8,128)(2,1)S(1)} %get-tuple-element.19.state_ref.refs_6_.refs_16_, bf16[2,4,3,128,128]{4,3,2,1,0:T(8,128)(2,1)S(1)} %copy-done, s32[2,4]{1,0:T(2,128)S(1)} %bitcast.4, f32[192,8]{1,0:T(8,128)S(1)} %get-tuple-element.14.refs_6_.table_ref.refs_5_), custom_call_target="tpu_custom_call" | custom-call | tf_op jit(solution)/shard_map/pallas_call | solution.py:272
  21.1 0.0 collective-permute-done.4.refs_7_
  21.1 0.0 collective-permute-done.5.refs_8_
  21.1 1.7 %collective-permute-done.6.refs_9_ = bf16[192,128]{1,0:T(8,128)(2,1)S(1)} collective-permute-done((bf16[192,128]{1,0:T(8,128)(2,1)S(1)}, bf16[192,128]{1,0:T(8,128)(2,1)S(1)}, u32[]{:S(2)}, u32[]{:S(2)}) %collective-permute-start.6) | collective-permute-done | bytes 49184 | tf_op jit(solution)/shard_map/ppermute | solution.py:328
  22.8 1.6 %shard_map.85 = bf16[2,192,512]{2,1,0:T(8,128)(2,1)} custom-call(f32[4,192,128]{2,1,0:T(8,128)S(1)} %shard_map.84.refs_0_, bf16[2,1,4,128,128]{4,3,2,1,0:T(8,128)(2,1)S(1)} %copy-done.1, s32[1,4]{1,0:T(1,128)S(1)} %copy-done.3, s32[1,4]{1,0:T(1,128)S(1)} %copy-done.4, s32[1,4]{1,0:T(1,128)S(1)} %copy-done.5, ...), custom_call_target="tpu_custom_call" | custom-call | tf_op jit(solution)/shard_map/pallas_call | solution.py:310
Async XLA Ops:
  0.0 14.6 %copy-start = (bf16[2,4,3,128,128]{4,3,2,1,0:T(8,128)(2,1)S(1)}, bf16[2,4,3,128,128]{4,3,2,1,0:T(8,128)(2,1)}, u32[]{:S(2)}) copy-start(bf16[2,4,3,128,128]{4,3,2,1,0:T(8,128)(2,1)} %refs_14_.1) | copy-start | bytes 2359300
  0.0 14.6 %copy-start.1 = (bf16[2,1,4,128,128]{4,3,2,1,0:T(8,128)(2,1)S(1)}, bf16[2,1,4,128,128]{4,3,2,1,0:T(8,128)(2,1)}, u32[]{:S(2)}) copy-start(bf16[2,1,4,128,128]{4,3,2,1,0:T(8,128)(2,1)} %refs_1_.3) | copy-start | bytes 786436
  1.1 13.6 %collective-permute-start = (bf16[4,192,128]{2,1,0:T(8,128)(2,1)S(1)}, bf16[4,192,128]{2,1,0:T(8,128)(2,1)S(1)}, u32[]{:S(2)}, u32[]{:S(2)}) collective-permute-start(bf16[4,192,128]{2,1,0:T(8,128)(2,1)S(1)} %get-tuple-element.15.refs_10_), channel_id=1, source_target_pairs={{0,16},{1,17},{2,18},{3,19},{4,20},{5,21},{6,22},{7,23},{8,24},{9,... | collective-permute-start | bytes 589832 | tf_op jit(solution)/shard_map/ppermute | solution.py:328
  1.2 6.8 %collective-permute-start.1 = (bf16[208,128]{1,0:T(8,128)(2,1)S(1)}, bf16[208,128]{1,0:T(8,128)(2,1)S(1)}, u32[]{:S(2)}, u32[]{:S(2)}) collective-permute-start(bf16[208,128]{1,0:T(8,128)(2,1)S(1)} %get-tuple-element.16), channel_id=1, source_target_pairs={{0,20},{1,21},{2,22},{3,23},{4,16},{5,17},{6,18},{7,19},{8,28},{9,... | collective-permute-start | bytes 159752 | tf_op jit(solution)/shard_map/ppermute | solution.py:328
  4.2 6.8 %collective-permute-start.2 = (bf16[208,128]{1,0:T(8,128)(2,1)S(1)}, bf16[208,128]{1,0:T(8,128)(2,1)S(1)}, u32[]{:S(2)}, u32[]{:S(2)}) collective-permute-start(bf16[208,128]{1,0:T(8,128)(2,1)S(1)} %get-tuple-element.17), channel_id=1, source_target_pairs={{0,24},{1,25},{2,26},{3,27},{4,28},{5,29},{6,30},{7,31},{8,16},{9,... | collective-permute-start | bytes 159752 | tf_op jit(solution)/shard_map/ppermute | solution.py:328
  7.7 6.9 %copy-start.4 = (s32[1,4]{1,0:T(1,128)S(1)}, s32[1,4]{1,0:T(1,128)}, u32[]{:S(2)}) copy-start(s32[1,4]{1,0:T(1,128)} %refs_3_.5) | copy-start | bytes 52
  7.7 6.9 %copy-start.5 = (s32[1,4]{1,0:T(1,128)S(1)}, s32[1,4]{1,0:T(1,128)}, u32[]{:S(2)}) copy-start(s32[1,4]{1,0:T(1,128)} %refs_4_.5) | copy-start | bytes 52
  7.7 6.9 %copy-start.2 = (s32[4,2]{0,1:T(2,128)S(1)}, s32[4,2]{0,1:T(2,128)}, u32[]{:S(2)}) copy-start(s32[4,2]{0,1:T(2,128)} %param.9) | copy-start | bytes 100
  7.7 6.9 %copy-start.3 = (s32[1,4]{1,0:T(1,128)S(1)}, s32[1,4]{1,0:T(1,128)}, u32[]{:S(2)}) copy-start(s32[1,4]{1,0:T(1,128)} %refs_2_.3) | copy-start | bytes 52
  7.7 6.9 %collective-permute-start.3 = (bf16[208,128]{1,0:T(8,128)(2,1)S(1)}, bf16[208,128]{1,0:T(8,128)(2,1)S(1)}, u32[]{:S(2)}, u32[]{:S(2)}) collective-permute-start(bf16[208,128]{1,0:T(8,128)(2,1)S(1)} %get-tuple-element.18), channel_id=1, source_target_pairs={{0,28},{1,29},{2,30},{3,31},{4,24},{5,25},{6,26},{7,27},{8,20},{9,... | collective-permute-start | bytes 159752 | tf_op jit(solution)/shard_map/ppermute | solution.py:328
  15.7 5.4 %collective-permute-start.4 = (bf16[192,128]{1,0:T(8,128)(2,1)S(1)}, bf16[192,128]{1,0:T(8,128)(2,1)S(1)}, u32[]{:S(2)}, u32[]{:S(2)}) collective-permute-start(bf16[192,128]{1,0:T(8,128)(2,1)S(1)} %get-tuple-element.20), channel_id=1, source_target_pairs={{0,1},{1,0},{2,3},{3,2},{4,5},{5,4},{6,7},{7,6},{8,9},{9,8},{10,11... | collective-permute-start | bytes 147464 | tf_op jit(solution)/shard_map/ppermute | solution.py:328
  15.8 5.3 %collective-permute-start.5 = (bf16[192,128]{1,0:T(8,128)(2,1)S(1)}, bf16[192,128]{1,0:T(8,128)(2,1)S(1)}, u32[]{:S(2)}, u32[]{:S(2)}) collective-permute-start(bf16[192,128]{1,0:T(8,128)(2,1)S(1)} %get-tuple-element.21), channel_id=1, source_target_pairs={{0,1},{1,0},{2,3},{3,2},{4,5},{5,4},{6,7},{7,6},{8,9},{9,8},{10,11... | collective-permute-start | bytes 147464 | tf_op jit(solution)/shard_map/ppermute | solution.py:328
  16.5 6.3 %collective-permute-start.6 = (bf16[192,128]{1,0:T(8,128)(2,1)S(1)}, bf16[192,128]{1,0:T(8,128)(2,1)S(1)}, u32[]{:S(2)}, u32[]{:S(2)}) collective-permute-start(bf16[192,128]{1,0:T(8,128)(2,1)S(1)} %get-tuple-element.22), channel_id=1, source_target_pairs={{0,1},{1,0},{2,3},{3,2},{4,5},{5,4},{6,7},{7,6},{8,9},{9,8},{10,11... | collective-permute-start | bytes 147464 | tf_op jit(solution)/shard_map/ppermute | solution.py:328

commit v13 on v10

--- a/solution.py
+++ b/solution.py
@@ -173,8 +173,8 @@
         jac_ref, cols_ref, *refs = refs
     else:
         z_ref, *refs = refs
-    iface_ref, send_ref, recv_ref, live_ref, table_ref, state_in_ref, *refs = refs
-    arrived, refs = refs[: n - 1], refs[n - 1 :]
+    iface_ref, send_ref, recv_ref, live_ref, table_ref, *refs = refs
+    arrived, state_in_ref, refs = refs[: n - 1][::-1], refs[n - 1], refs[n:]
     acc_ref = refs.pop()
     blocks, cols, width = acc_ref.shape
     before = []
@@ -278,10 +278,10 @@
         )(state, jac, near, table)
 
     def join(z, step, fix, state, arrived, send, section, opening=(), before=(), out=None, store=0):
-        arrays = [*([jac, near] if fix else [z]), iface_jac, iface_send, iface_recv, iface_live, table, state]
-        specs = [*([VMEM, SMEM] if fix else [VMEM]), VMEM, SMEM, SMEM, SMEM, VMEM, VMEM]
-        arrays += arrived
-        specs += [VMEM] * (n - 1)
+        arrays = [*([jac, near] if fix else [z]), iface_jac, iface_send, iface_recv, iface_live, table]
+        specs = [*([VMEM, SMEM] if fix else [VMEM]), VMEM, SMEM, SMEM, SMEM, VMEM]
+        arrays += [*arrived[::-1], state]
+        specs += [VMEM] * n
         shapes = []
         scratch = [pltpu.VMEM(whole.shape, jnp.float32)]
         aliases = {}
@@ -328,8 +328,7 @@
         return lax.ppermute(block, ("tm", "net", "cols"), pairs)
 
     def exchange(outgoing, first, second):
-        arrived = [swap(outgoing[d - 1], first, second, d) for d in reversed(range(1, n))]
-        return arrived[::-1]
+        return [swap(outgoing[d - 1], first, second, d) for d in range(1, n)]
 
     opening = [state]
     out = None

time: 24.5 us -> 23.2 us (0.947)
  waiting for transfers between devices: 8.35 us -> 7.06 us
    ppermute x7, waiting for transfers between devices: 8.35 us -> 7.06 us  [swap(): return lax.ppermute(block, ('tm', 'net', 'cols'), pairs)]
  transfers between devices with their start and end apart: 7 -> 7, of which waited for: 3 -> 4; matrix products, arithmetic and copies ran while one was open for 0% -> 0% of each run, Pallas kernels for 4% -> 4%
where the time goes in v13:
time: 23.2 us; the launch traced here: 23.1 us
  starting transfers between devices  11.3 us (49%)
  waiting for transfers between devices  7.06 us (30%)
  Pallas kernels  4.56 us (20%)
    ppermute x7, starting transfers between devices, swap(): return lax.ppermute(block, ('tm', 'net', 'cols'), pairs)  11.3 us
    ppermute x7, waiting for transfers between devices, swap(): return lax.ppermute(block, ('tm', 'net', 'cols'), pairs)  7.06 us
    pallas_call x2, Pallas kernels, join(): pl.pallas_call(functools.partial(join_kernel, step, fix, send, section, f...  2.62 us
    pallas_call x1, Pallas kernels, local(): pl.pallas_call(second_kernel, out_shape=[f32((cols, table_rows)), whole]...  1.06 us
    pallas_call x1, Pallas kernels, own(): pl.pallas_call(functools.partial(own_kernel, step), out_shape=f32(whole.s...  0.89 us
  transfers between devices with their start and end apart: 7, of which 4 were waited for; matrix products, arithmetic and copies ran while one was open for 0% of the time, Pallas kernels for 4%

profile of v13, /device:TPU:4, one launch (start us, length us, event | category | flops | bytes accessed | tf_op | source)
XLA Modules:
  0.0 23.1 jit_solution(9002721567838849125)
XLA Ops:
  0.0 0.0 copy-start
  0.0 0.0 copy-start.1
  0.0 1.1 %shard_map.82 = (f32[192,8]{1,0:T(8,128)S(1)}, bf16[4,192,128]{2,1,0:T(8,128)(2,1)S(1)}, bf16[208,128]{1,0:T(8,128)(2,1)S(1)}, bf16[208,128]{1,0:T(8,128)(2,1)S(1)}, bf16[208,128]{1,0:T(8,128)(2,1)S(1)}) custom-call(bf16[2,4,3,128,128]{4,3,2,1,0:T(8,128)(2,1)} %refs_14_.1, bf16[2,1,4,128,128]{4,3,2,1,0:T(8,128)(2,1)} %refs_1_.3, s32[2,4]{1,0:T(2,128)} %bitcast.2, ...), custom_call_target="tpu_custom_call" | custom-call | tf_op jit(solution)/shard_map/pallas_call | solution.py:254
  1.1 0.1 collective-permute-start.3
  1.2 5.0 %collective-permute-start = (bf16[208,128]{1,0:T(8,128)(2,1)S(1)}, bf16[208,128]{1,0:T(8,128)(2,1)S(1)}, u32[]{:S(2)}, u32[]{:S(2)}) collective-permute-start(bf16[208,128]{1,0:T(8,128)(2,1)S(1)} %get-tuple-element.15), channel_id=1, source_target_pairs={{0,28},{1,29},{2,30},{3,31},{4,24},{5,25},{6,26},{7,27},{8,20},{9,... | collective-permute-start | bytes 159752 | tf_op jit(solution)/shard_map/ppermute | solution.py:328
  6.2 0.4 %collective-permute-start.1 = (bf16[208,128]{1,0:T(8,128)(2,1)S(1)}, bf16[208,128]{1,0:T(8,128)(2,1)S(1)}, u32[]{:S(2)}, u32[]{:S(2)}) collective-permute-start(bf16[208,128]{1,0:T(8,128)(2,1)S(1)} %get-tuple-element.16), channel_id=1, source_target_pairs={{0,24},{1,25},{2,26},{3,27},{4,28},{5,29},{6,30},{7,31},{8,16},{9,... | collective-permute-start | bytes 159752 | tf_op jit(solution)/shard_map/ppermute | solution.py:328
  6.6 0.0 copy-start.4
  6.6 0.0 copy-start.5
  6.6 0.0 copy-start.2
  6.6 0.0 copy-start.3
  6.6 1.4 %collective-permute-start.2 = (bf16[208,128]{1,0:T(8,128)(2,1)S(1)}, bf16[208,128]{1,0:T(8,128)(2,1)S(1)}, u32[]{:S(2)}, u32[]{:S(2)}) collective-permute-start(bf16[208,128]{1,0:T(8,128)(2,1)S(1)} %get-tuple-element.17), channel_id=1, source_target_pairs={{0,20},{1,21},{2,22},{3,23},{4,16},{5,17},{6,18},{7,19},{8,28},{9,... | collective-permute-start | bytes 159752 | tf_op jit(solution)/shard_map/ppermute | solution.py:328
  8.0 0.5 %collective-permute-done.refs_7_.refs_13_ = bf16[208,128]{1,0:T(8,128)(2,1)S(1)} collective-permute-done((bf16[208,128]{1,0:T(8,128)(2,1)S(1)}, bf16[208,128]{1,0:T(8,128)(2,1)S(1)}, u32[]{:S(2)}, u32[]{:S(2)}) %collective-permute-start) | collective-permute-done | bytes 53280 | tf_op jit(solution)/shard_map/ppermute | solution.py:328
  8.4 3.8 %collective-permute-done.1.refs_8_.refs_12_ = bf16[208,128]{1,0:T(8,128)(2,1)S(1)} collective-permute-done((bf16[208,128]{1,0:T(8,128)(2,1)S(1)}, bf16[208,128]{1,0:T(8,128)(2,1)S(1)}, u32[]{:S(2)}, u32[]{:S(2)}) %collective-permute-start.1) | collective-permute-done | bytes 53280 | tf_op jit(solution)/shard_map/ppermute | solution.py:328
  12.2 0.0 collective-permute-done.2.refs_9_.refs_11_
  12.3 0.0 collective-permute-done.3.refs_10_
  12.3 0.0 copy-done
  12.3 0.0 copy-done.1
  12.3 0.0 copy-done.4
  12.3 0.0 copy-done.5
  12.3 0.0 copy-done.2
  12.3 0.0 copy-done.3
  12.3 1.0 %shard_map.83 = (bf16[4,192,128]{2,1,0:T(8,128)(2,1)S(1)}, bf16[192,128]{1,0:T(8,128)(2,1)S(1)}, bf16[192,128]{1,0:T(8,128)(2,1)S(1)}, bf16[192,128]{1,0:T(8,128)(2,1)S(1)}) custom-call(bf16[2,4,3,128,128]{4,3,2,1,0:T(8,128)(2,1)S(1)} %copy-done, s32[2,4]{1,0:T(2,128)S(1)} %bitcast.3, bf16[2,1,4,128,128]{4,3,2,1,0:T(8,128)(2,1)S(1)} %copy-done.1, ...), custom_call_target="tpu_custom_call" | custom-call | tf_op jit(solution)/shard_map/pallas_call | solution.py:310
  13.4 2.6 %collective-permute-start.4 = (bf16[192,128]{1,0:T(8,128)(2,1)S(1)}, bf16[192,128]{1,0:T(8,128)(2,1)S(1)}, u32[]{:S(2)}, u32[]{:S(2)}) collective-permute-start(bf16[192,128]{1,0:T(8,128)(2,1)S(1)} %get-tuple-element.20), channel_id=1, source_target_pairs={{0,1},{1,0},{2,3},{3,2},{4,5},{5,4},{6,7},{7,6},{8,9},{9,8},{10,11... | collective-permute-start | bytes 147464 | tf_op jit(solution)/shard_map/ppermute | solution.py:328
  16.0 0.5 %collective-permute-start.5 = (bf16[192,128]{1,0:T(8,128)(2,1)S(1)}, bf16[192,128]{1,0:T(8,128)(2,1)S(1)}, u32[]{:S(2)}, u32[]{:S(2)}) collective-permute-start(bf16[192,128]{1,0:T(8,128)(2,1)S(1)} %get-tuple-element.21), channel_id=1, source_target_pairs={{0,1},{1,0},{2,3},{3,2},{4,5},{5,4},{6,7},{7,6},{8,9},{9,8},{10,11... | collective-permute-start | bytes 147464 | tf_op jit(solution)/shard_map/ppermute | solution.py:328
  16.4 1.4 %collective-permute-start.6 = (bf16[192,128]{1,0:T(8,128)(2,1)S(1)}, bf16[192,128]{1,0:T(8,128)(2,1)S(1)}, u32[]{:S(2)}, u32[]{:S(2)}) collective-permute-start(bf16[192,128]{1,0:T(8,128)(2,1)S(1)} %get-tuple-element.22), channel_id=1, source_target_pairs={{0,1},{1,0},{2,3},{3,2},{4,5},{5,4},{6,7},{7,6},{8,9},{9,8},{10,11... | collective-permute-start | bytes 147464 | tf_op jit(solution)/shard_map/ppermute | solution.py:328
  17.8 0.9 %shard_map.84.refs_0_ = f32[4,192,128]{2,1,0:T(8,128)S(1)} custom-call(bf16[4,192,128]{2,1,0:T(8,128)(2,1)S(1)} %get-tuple-element.19.state_ref.refs_9_.refs_16_, bf16[2,4,3,128,128]{4,3,2,1,0:T(8,128)(2,1)S(1)} %copy-done, s32[2,4]{1,0:T(2,128)S(1)} %bitcast.4, f32[192,8]{1,0:T(8,128)S(1)} %get-tuple-element.14.refs_6_.table_ref.refs_5_), custom_call_target="tpu_custom_call" | custom-call | tf_op jit(solution)/shard_map/pallas_call | solution.py:272
  18.7 0.7 %collective-permute-done.4.refs_6_ = bf16[192,128]{1,0:T(8,128)(2,1)S(1)} collective-permute-done((bf16[192,128]{1,0:T(8,128)(2,1)S(1)}, bf16[192,128]{1,0:T(8,128)(2,1)S(1)}, u32[]{:S(2)}, u32[]{:S(2)}) %collective-permute-start.4) | collective-permute-done | bytes 49184 | tf_op jit(solution)/shard_map/ppermute | solution.py:328
  19.4 2.0 %collective-permute-done.5.refs_7_ = bf16[192,128]{1,0:T(8,128)(2,1)S(1)} collective-permute-done((bf16[192,128]{1,0:T(8,128)(2,1)S(1)}, bf16[192,128]{1,0:T(8,128)(2,1)S(1)}, u32[]{:S(2)}, u32[]{:S(2)}) %collective-permute-start.5) | collective-permute-done | bytes 49184 | tf_op jit(solution)/shard_map/ppermute | solution.py:328
  21.5 0.0 collective-permute-done.6.refs_8_
  21.5 1.6 %shard_map.85 = bf16[2,192,512]{2,1,0:T(8,128)(2,1)} custom-call(f32[4,192,128]{2,1,0:T(8,128)S(1)} %shard_map.84.refs_0_, bf16[2,1,4,128,128]{4,3,2,1,0:T(8,128)(2,1)S(1)} %copy-done.1, s32[1,4]{1,0:T(1,128)S(1)} %copy-done.3, s32[1,4]{1,0:T(1,128)S(1)} %copy-done.4, s32[1,4]{1,0:T(1,128)S(1)} %copy-done.5, ...), custom_call_target="tpu_custom_call" | custom-call | tf_op jit(solution)/shard_map/pallas_call | solution.py:310
Async XLA Ops:
  0.0 12.3 %copy-start = (bf16[2,4,3,128,128]{4,3,2,1,0:T(8,128)(2,1)S(1)}, bf16[2,4,3,128,128]{4,3,2,1,0:T(8,128)(2,1)}, u32[]{:S(2)}) copy-start(bf16[2,4,3,128,128]{4,3,2,1,0:T(8,128)(2,1)} %refs_14_.1) | copy-start | bytes 2359300
  0.0 12.3 %copy-start.1 = (bf16[2,1,4,128,128]{4,3,2,1,0:T(8,128)(2,1)S(1)}, bf16[2,1,4,128,128]{4,3,2,1,0:T(8,128)(2,1)}, u32[]{:S(2)}) copy-start(bf16[2,1,4,128,128]{4,3,2,1,0:T(8,128)(2,1)} %refs_1_.3) | copy-start | bytes 786436
  1.1 11.2 %collective-permute-start.3 = (bf16[4,192,128]{2,1,0:T(8,128)(2,1)S(1)}, bf16[4,192,128]{2,1,0:T(8,128)(2,1)S(1)}, u32[]{:S(2)}, u32[]{:S(2)}) collective-permute-start(bf16[4,192,128]{2,1,0:T(8,128)(2,1)S(1)} %get-tuple-element.18.refs_10_), channel_id=1, source_target_pairs={{0,16},{1,17},{2,18},{3,19},{4,20},{5,21},{6,22},{7,23},{8,24},{9,... | collective-permute-start | bytes 589832 | tf_op jit(solution)/shard_map/ppermute | solution.py:328
  1.2 7.2 %collective-permute-start = (bf16[208,128]{1,0:T(8,128)(2,1)S(1)}, bf16[208,128]{1,0:T(8,128)(2,1)S(1)}, u32[]{:S(2)}, u32[]{:S(2)}) collective-permute-start(bf16[208,128]{1,0:T(8,128)(2,1)S(1)} %get-tuple-element.15), channel_id=1, source_target_pairs={{0,28},{1,29},{2,30},{3,31},{4,24},{5,25},{6,26},{7,27},{8,20},{9,... | collective-permute-start | bytes 159752 | tf_op jit(solution)/shard_map/ppermute | solution.py:328
  6.2 6.0 %collective-permute-start.1 = (bf16[208,128]{1,0:T(8,128)(2,1)S(1)}, bf16[208,128]{1,0:T(8,128)(2,1)S(1)}, u32[]{:S(2)}, u32[]{:S(2)}) collective-permute-start(bf16[208,128]{1,0:T(8,128)(2,1)S(1)} %get-tuple-element.16), channel_id=1, source_target_pairs={{0,24},{1,25},{2,26},{3,27},{4,28},{5,29},{6,30},{7,31},{8,16},{9,... | collective-permute-start | bytes 159752 | tf_op jit(solution)/shard_map/ppermute | solution.py:328
  6.6 5.7 %copy-start.4 = (s32[1,4]{1,0:T(1,128)S(1)}, s32[1,4]{1,0:T(1,128)}, u32[]{:S(2)}) copy-start(s32[1,4]{1,0:T(1,128)} %refs_3_.5) | copy-start | bytes 52
  6.6 5.7 %copy-start.5 = (s32[1,4]{1,0:T(1,128)S(1)}, s32[1,4]{1,0:T(1,128)}, u32[]{:S(2)}) copy-start(s32[1,4]{1,0:T(1,128)} %refs_4_.5) | copy-start | bytes 52
  6.6 5.7 %copy-start.2 = (s32[4,2]{0,1:T(2,128)S(1)}, s32[4,2]{0,1:T(2,128)}, u32[]{:S(2)}) copy-start(s32[4,2]{0,1:T(2,128)} %param.9) | copy-start | bytes 100
  6.6 5.7 %copy-start.3 = (s32[1,4]{1,0:T(1,128)S(1)}, s32[1,4]{1,0:T(1,128)}, u32[]{:S(2)}) copy-start(s32[1,4]{1,0:T(1,128)} %refs_2_.3) | copy-start | bytes 52
  6.6 5.7 %collective-permute-start.2 = (bf16[208,128]{1,0:T(8,128)(2,1)S(1)}, bf16[208,128]{1,0:T(8,128)(2,1)S(1)}, u32[]{:S(2)}, u32[]{:S(2)}) collective-permute-start(bf16[208,128]{1,0:T(8,128)(2,1)S(1)} %get-tuple-element.17), channel_id=1, source_target_pairs={{0,20},{1,21},{2,22},{3,23},{4,16},{5,17},{6,18},{7,19},{8,28},{9,... | collective-permute-start | bytes 159752 | tf_op jit(solution)/shard_map/ppermute | solution.py:328
  13.4 6.1 %collective-permute-start.4 = (bf16[192,128]{1,0:T(8,128)(2,1)S(1)}, bf16[192,128]{1,0:T(8,128)(2,1)S(1)}, u32[]{:S(2)}, u32[]{:S(2)}) collective-permute-start(bf16[192,128]{1,0:T(8,128)(2,1)S(1)} %get-tuple-element.20), channel_id=1, source_target_pairs={{0,1},{1,0},{2,3},{3,2},{4,5},{5,4},{6,7},{7,6},{8,9},{9,8},{10,11... | collective-permute-start | bytes 147464 | tf_op jit(solution)/shard_map/ppermute | solution.py:328
  16.0 5.5 %collective-permute-start.5 = (bf16[192,128]{1,0:T(8,128)(2,1)S(1)}, bf16[192,128]{1,0:T(8,128)(2,1)S(1)}, u32[]{:S(2)}, u32[]{:S(2)}) collective-permute-start(bf16[192,128]{1,0:T(8,128)(2,1)S(1)} %get-tuple-element.21), channel_id=1, source_target_pairs={{0,1},{1,0},{2,3},{3,2},{4,5},{5,4},{6,7},{7,6},{8,9},{9,8},{10,11... | collective-permute-start | bytes 147464 | tf_op jit(solution)/shard_map/ppermute | solution.py:328
  16.4 5.0 %collective-permute-start.6 = (bf16[192,128]{1,0:T(8,128)(2,1)S(1)}, bf16[192,128]{1,0:T(8,128)(2,1)S(1)}, u32[]{:S(2)}, u32[]{:S(2)}) collective-permute-start(bf16[192,128]{1,0:T(8,128)(2,1)S(1)} %get-tuple-element.22), channel_id=1, source_target_pairs={{0,1},{1,0},{2,3},{3,2},{4,5},{5,4},{6,7},{7,6},{8,9},{9,8},{10,11... | collective-permute-start | bytes 147464 | tf_op jit(solution)/shard_map/ppermute | solution.py:328

commit v14 on v9

v14 whole, which is shorter than its diff:
```python
import functools

import jax
import jax.numpy as jnp
from jax import lax
from jax.experimental import pallas as pl
from jax.experimental.pallas import tpu as pltpu
from jax.sharding import PartitionSpec as P

VMEM = pl.BlockSpec(memory_space=pltpu.VMEM)
SMEM = pl.BlockSpec(memory_space=pltpu.SMEM)
HBM = pl.BlockSpec(memory_space=pltpu.HBM)
ANY = pl.BlockSpec(memory_space=pl.ANY)
LIMIT = pltpu.CompilerParams(vmem_limit_bytes=16 * 1024 * 1024)
DMA = pltpu.SemaphoreType.DMA

STATE, LANE, BLOCK, AWAY, GAIN = 0, 1, 2, 3, 4
ROWS = 16


def times_transposed(rows, block):
    return lax.dot_general(rows, block, (((1,), (1,)), ((), ())), preferred_element_type=jnp.float32)


def injected(table, step, first_state, width):
    lane = lax.broadcasted_iota(jnp.int32, (table.shape[0], width), 1)
    hit = table[:, STATE : STATE + 1] == (lane + first_state).astype(jnp.float32)
    return jnp.where(hit, table[:, GAIN + step : GAIN + step + 1], 0.0)


def near_by(state_ref, cols_ref):
    return lambda i, k: state_ref[cols_ref[k, i]]


def own_sum(i, state_ref, jac_ref, near, table, step):
    blocks, _, width = state_ref.shape
    first = (lax.axis_index("net") * blocks + i) * width
    kinds = jac_ref.shape[1]
    rows = [state_ref[i]] + [near(i, k) for k in range(kinds - 1)]
    row_blocks = [jac_ref[i, k] for k in range(kinds)]
    total = times_transposed(jnp.concatenate(rows, axis=1), jnp.concatenate(row_blocks, axis=1))
    return total + injected(table, step, first, width)


def picked(blocks, marks):
    total = blocks[0] * marks[0]
    for block, mark in zip(blocks[1:], marks[1:]):
        total += block * mark
    return total


def marks_layout(n, blocks, kinds):
    sent = n * blocks
    near = sent + n * blocks
    row = near + blocks * (kinds - 1) * blocks
    return sent, near, row, row + 1 + -(row + 1) % 8


def make_marks(marks_ref, blocks, kinds, cols_ref, send_ref, recv_ref, live_ref):
    n = lax.axis_size("net")
    me = lax.axis_index("net")
    width = marks_ref.shape[1]
    lane = lax.broadcasted_iota(jnp.int32, (1, width), 1)
    sent, near, own_row, _ = marks_layout(n, blocks, kinds)

    def put(row, mask):
        marks_ref[pl.ds(row, 1)] = jnp.where(mask, 1.0, 0.0)

    for d in range(n):
        q = me ^ d
        for i in range(blocks):
            put(d * blocks + i, lane < jnp.where(recv_ref[0, q] == i, live_ref[0, q], 0))
            put(sent + d * blocks + i, lane < jnp.where(send_ref[0, q] == i, width, 0))
    for i in range(blocks):
        for k in range(kinds - 1):
            for j in range(blocks):
                put(near + (i * (kinds - 1) + k) * blocks + j, lane < jnp.where(cols_ref[k, i] == j, width, 0))
    marks_ref[pl.ds(own_row, 1)] = table_row(send_ref, me, width)


def add_coupled(incoming, block, live, recv, z_ref):
    mask = lax.broadcasted_iota(jnp.int32, z_ref.shape[1:], 1) < live
    z_ref[recv] += jnp.where(mask, times_transposed(incoming, block), 0.0)


def table_row(send_ref, partition, width):
    lane = lax.broadcasted_iota(jnp.int32, (1, width), 1)
    row = jnp.zeros((1, width), jnp.float32)
    for e in range(lax.axis_size("net")):
        row = jnp.where(lane == e, send_ref[0, partition ^ e].astype(jnp.float32), row)
    return row


def kept(table, rows):
    away, block = table[:, AWAY : AWAY + 1], table[:, BLOCK : BLOCK + 1]
    sent = jnp.broadcast_to(rows[0], (table.shape[0], rows[0].shape[1]))
    for d in range(1, len(rows)):
        sent = jnp.where(away == float(d), rows[d], sent)
    lane = lax.broadcasted_iota(jnp.int32, sent.shape, 1).astype(jnp.float32)
    return jnp.where(jnp.logical_or(away == lane, block == sent), 1.0, 0.0)


def second_kernel(*refs):
    jac_hbm, iface_hbm, *small, table_ref, marks_ref, state_ref = refs[:11]
    n = lax.axis_size("net")
    me = lax.axis_index("net")
    outgoing, refs = refs[11 : 10 + n], refs[10 + n :]
    jac_ref, iface_ref, *loaded, first_ref, sems = refs
    cols_ref, send_ref, recv_ref, live_ref, node_ref, gain_ref = loaded
    blocks, cols, width = state_ref.shape
    loads = [
        pltpu.make_async_copy(source, target, sems.at[i])
        for i, (source, target) in enumerate(
            zip([jac_hbm.at[1], iface_hbm.at[1, 0], *small], [jac_ref, iface_ref, *loaded])
        )
    ]
    here = lax.axis_index("tm") == 0

    @pl.when(here)
    def _():
        for load in loads[:2]:
            load.start()

    for load in loads[2:]:
        load.start()
    for load in loads[2:]:
        load.wait()
    node = node_ref[...]
    block_of = node // width
    rows = [
        node,
        node - block_of * width,
        block_of % blocks,
        (block_of // blocks) ^ me,
    ]
    steps = gain_ref.shape[0]
    fill = -(GAIN + steps) % 8
    rows = [row.astype(jnp.float32) for row in rows] + [gain_ref[...], jnp.zeros((fill, cols), jnp.float32)]
    table_ref[...] = jnp.concatenate(rows, axis=0).T

    @pl.when(here)
    def _():
        table = table_ref[...]
        for i in range(blocks):
            first_ref[i] = injected(table, 0, (me * blocks + i) * width, width).astype(first_ref.dtype)
        lane = lax.broadcasted_iota(jnp.int32, (cols, width), 1).astype(jnp.float32)
        shot = jnp.where(lane == table[:, LANE : LANE + 1], table[:, GAIN : GAIN + 1], 0.0)
        away, block = table[:, AWAY : AWAY + 1], table[:, BLOCK : BLOCK + 1]
        mine = jnp.logical_or(away != 0.0, block == send_ref[0, me].astype(jnp.float32))
        shot = jnp.where(mine, shot, 0.0)
        live = recv = jnp.zeros_like(away)
        for d in range(n):
            live = jnp.where(away == float(d), live_ref[0, me ^ d].astype(jnp.float32), live)
            recv = jnp.where(away == float(d), recv_ref[0, me ^ d].astype(jnp.float32), recv)
        sent = [jnp.where(away == float(d), shot, 0.0).astype(first_ref.dtype) for d in range(n)]
        loads[1].wait()
        ifaces = jnp.concatenate([iface_ref[me ^ d] for d in range(n)], axis=1)
        coupled = times_transposed(jnp.concatenate(sent, axis=1), ifaces)
        coupled = jnp.where(lane < live, coupled, 0.0)
        loads[0].wait()
        for i in range(blocks):
            own = own_sum(i, first_ref, jac_ref, near_by(first_ref, cols_ref), table, 1)
            state_ref[i] = (own + jnp.where(recv == float(i), coupled, 0.0)).astype(state_ref.dtype)
        for d in range(1, n):
            outgoing[d - 1][pl.ds(0, cols)] = state_ref[send_ref[0, me ^ d]]

    @pl.when(jnp.logical_not(here))
    def _():
        make_marks(marks_ref, blocks, jac_ref.shape[1], cols_ref, send_ref, recv_ref, live_ref)

    for d in range(1, n):
        row = table_row(send_ref, me ^ d, width).astype(state_ref.dtype)
        outgoing[d - 1][pl.ds(cols, ROWS)] = jnp.broadcast_to(row, (ROWS, width))


def write_start(states, first, out_ref, sems):
    copies = []
    for s, state_ref in enumerate(states, first):
        width = state_ref.shape[2]
        for i in range(state_ref.shape[0]):
            copies.append(
                pltpu.make_async_copy(state_ref.at[i], out_ref.at[s, :, pl.ds(i * width, width)], sems.at[s, i])
            )
    for copy in copies:
        copy.start()
    return copies


def own_kernel(step, state_ref, jac_ref, cols_ref, table_ref, z_ref):
    table = table_ref[...]
    for i in range(state_ref.shape[0]):
        z_ref[i] = own_sum(i, state_ref, jac_ref.at[step], near_by(state_ref, cols_ref), table, step)


def first_states(opening, handed, jac_ref, iface_ref, ints, table_ref, made_ref, z_ref):
    cols_ref, send_ref, recv_ref, live_ref = ints
    n = lax.axis_size("net")
    blocks, cols, width = z_ref.shape
    table = table_ref[...]
    made_ref[0] = jnp.zeros_like(made_ref[0])
    for i in range(blocks):
        z_ref[i] = own_sum(i, made_ref.at[0], jac_ref.at[0], near_by(made_ref.at[0], cols_ref), table, 0)
    for q in range(n):
        add_coupled(made_ref[0, 0], iface_ref[0, 0, q], live_ref[0, q], recv_ref[0, q], z_ref)
    made_ref[0] = z_ref[...].astype(made_ref.dtype)
    rows = [table_row(send_ref, lax.axis_index("net"), width)]
    rows += [block[cols : cols + 1].astype(jnp.float32) for block in handed]
    keep = kept(table, rows)[:, 0:1]
    for i in range(blocks):
        made_ref[1, i] = jnp.where(keep > 0.0, opening[i], jnp.zeros_like(opening[i]))
    return [made_ref.at[0], made_ref.at[1]]


def joined(sums, step, iface_ref, marks_ref, state_ref, arrived, keep=None):
    n = lax.axis_size("net")
    me = lax.axis_index("net")
    blocks, cols, _ = state_ref.shape
    sent = marks_layout(n, blocks, 1)[0]
    for d in range(n):
        if d:
            block = arrived[d - 1][pl.ds(0, cols)]
        else:
            marks = [marks_ref[pl.ds(sent + j, 1)].astype(state_ref.dtype) for j in range(blocks)]
            block = picked([state_ref[j] for j in range(blocks)], marks)
        term = times_transposed(block, iface_ref[step, 0, me ^ d])
        if keep is not None:
            term *= keep[:, d : d + 1]
        sums = [total + term * marks_ref[pl.ds(d * blocks + i, 1)] for i, total in enumerate(sums)]
    return [total.astype(state_ref.dtype) for total in sums]


def give(made, marks_ref, state_ref, outgoing):
    blocks = len(made)
    n = lax.axis_size("net")
    sent = marks_layout(n, blocks, 1)[0]
    for i in range(blocks):
        state_ref[i] = made[i]
    for d in range(1, n) if outgoing else ():
        marks = [marks_ref[pl.ds(sent + d * blocks + j, 1)].astype(made[j].dtype) for j in range(blocks)]
        outgoing[d - 1][...] = picked(made, marks)


def join_kernel(step, fix, section, *refs):
    n = lax.axis_size("net")
    first_ref, iface_ref, table_ref, marks_ref, *refs = refs
    arrived, state_in_ref, state_ref, outgoing = refs[: n - 1][::-1], refs[n - 1], refs[n], refs[n + 1 :]
    blocks, cols, _ = state_in_ref.shape

    @pl.when(lax.axis_index("tm") == section)
    def _():
        keep = None
        if fix:
            kinds = first_ref.shape[2]
            table = table_ref[...]
            _, near, own_row, _ = marks_layout(n, blocks, kinds)
            state = [state_in_ref[j] for j in range(blocks)]

            def near_block(i, k):
                rows = [near + (i * (kinds - 1) + k) * blocks + j for j in range(blocks)]
                return picked(state, [marks_ref[pl.ds(row, 1)].astype(state_ref.dtype) for row in rows])

            rows = [marks_ref[pl.ds(own_row, 1)]]
            rows += [block[cols : cols + 1].astype(jnp.float32) for block in arrived]
            keep = kept(table, rows)
            sums = [
                own_sum(i, state_in_ref, first_ref.at[step], near_block, table, step) * keep[:, 0:1]
                for i in range(blocks)
            ]
        else:
            sums = [first_ref[i] for i in range(blocks)]
        made = joined(sums, step, iface_ref, marks_ref, state_in_ref, arrived, keep)
        give(made, marks_ref, state_ref, outgoing)


def close_kernel(step, section, firsts, send, before, *refs):
    n = lax.axis_size("net")
    *refs, sems = refs
    if firsts:
        *refs, made_ref, acc_ref, cols_ref, send_ref, recv_ref, live_ref, load_sems = refs
        ints = [cols_ref, send_ref, recv_ref, live_ref]
    z_ref, iface_ref, table_ref, marks_ref, *refs = refs
    arrived, state_in_ref, refs = refs[: n - 1][::-1], refs[n - 1], refs[n:]
    before, refs = refs[:before], refs[before:]
    if firsts:
        opening_ref, handed, jac_ref, sources, refs = refs[0], refs[1:n], refs[n], refs[n + 1 : n + 5], refs[n + 5 :]
    else:
        refs = refs[1:]
    out_ref, state_ref, *outgoing = refs

    @pl.when(lax.axis_index("tm") == section)
    def _():
        copies = write_start(before, 0, out_ref, sems)
        sums = [z_ref[i] for i in range(z_ref.shape[0])]
        made = joined(sums, step, iface_ref, marks_ref, state_in_ref, arrived)
        give(made, marks_ref, state_ref, outgoing)
        copies += write_start([state_ref], len(before), out_ref, sems)
        for copy in copies:
            copy.wait()

    if firsts:

        @pl.when(lax.axis_index("tm") == 0)
        def _():
            loads = [
                pltpu.make_async_copy(source, target, load_sems.at[i])
                for i, (source, target) in enumerate(zip(sources, ints))
            ]
            for load in loads:
                load.start()
            for load in loads:
                load.wait()
            made = first_states(opening_ref, handed, jac_ref, iface_ref, ints, table_ref, made_ref, acc_ref)
            for copy in write_start(made, 0, out_ref, sems):
                copy.wait()


def local(jac, block_cols, iface_jac, iface_send, iface_recv, iface_live, ctrl_node, ctrl_gain):
    steps, blocks, kinds, width, _ = jac.shape
    cols = ctrl_node.shape[0]
    tm = lax.axis_size("tm")
    n = lax.axis_size("net")
    col_parts = lax.axis_size("cols")
    node = ctrl_node[None]
    near = block_cols.T
    bf16 = functools.partial(jax.ShapeDtypeStruct, dtype=jnp.bfloat16)
    f32 = functools.partial(jax.ShapeDtypeStruct, dtype=jnp.float32)
    whole, one = bf16((blocks, cols, width)), bf16((cols, width))
    table_rows = GAIN + steps + -(GAIN + steps) % 8
    written = bf16((steps, cols, blocks * width))

    pinned = [
        pltpu.with_memory_space_constraint(x, pltpu.HBM)
        for x in (jac, iface_jac, near, iface_send, iface_recv, iface_live, node, ctrl_gain)
    ]
    marks_rows = marks_layout(n, blocks, kinds)[-1]
    table, marks, state, *outgoing = pl.pallas_call(
        second_kernel,
        out_shape=[f32((cols, table_rows)), f32((marks_rows, width)), whole]
        + [bf16((cols + ROWS, width))] * (n - 1),
        in_specs=[HBM] * len(pinned),
        out_specs=[VMEM] * (n + 2),
        scratch_shapes=[
            pltpu.VMEM((blocks, kinds, width, width), jnp.bfloat16),
            pltpu.VMEM((n, width, width), jnp.bfloat16),
            *[pltpu.SMEM(x.shape, x.dtype) for x in (near, iface_send, iface_recv, iface_live)],
            *[pltpu.VMEM(x.shape, x.dtype) for x in (node, ctrl_gain)],
            pltpu.VMEM(whole.shape, jnp.bfloat16),
            DMA((len(pinned),)),
        ],
        compiler_params=LIMIT,
    )(*pinned)

    def own(state, step):
        return pl.pallas_call(
            functools.partial(own_kernel, step),
            out_shape=f32(whole.shape),
            in_specs=[VMEM, VMEM, SMEM, VMEM],
            out_specs=VMEM,
            compiler_params=LIMIT,
        )(state, jac, near, table)

    def join(first, step, fix, state, arrived, section):
        return pl.pallas_call(
            functools.partial(join_kernel, step, fix, section),
            out_shape=[whole] + [one] * (n - 1),
            in_specs=[VMEM] * (n + 4),
            out_specs=[VMEM] * n,
            compiler_params=LIMIT,
        )(first, iface_jac, table, marks, *arrived[::-1], state)

    def close(z, step, state, arrived, section, before, out, send):
        firsts = out is None
        arrays = [z, iface_jac, table, marks, *arrived[::-1], state, *before]
        specs = [VMEM] * len(arrays)
        scratch = [DMA((steps, blocks))]
        aliases = {}
        if firsts:
            arrays += [opening, *handed, jac, *pinned[2:6]]
            specs += [VMEM] * (n + 1) + [HBM] * 4
            scratch = [
                pltpu.VMEM((2, *whole.shape), jnp.bfloat16),
                pltpu.VMEM(whole.shape, jnp.float32),
                *[pltpu.SMEM(x.shape, x.dtype) for x in pinned[2:6]],
                DMA((4,)),
            ] + scratch
        else:
            aliases = {len(arrays): 0}
            arrays.append(out)
            specs.append(ANY)
        shapes, out_specs = [written], [ANY]
        if send:
            shapes += [whole] + [one] * (n - 1)
            out_specs += [VMEM] * n
        else:
            scratch.insert(0, pltpu.VMEM(whole.shape, jnp.bfloat16))
        return pl.pallas_call(
            functools.partial(close_kernel, step, section, firsts, send, len(before)),
            out_shape=shapes,
            in_specs=specs,
            out_specs=out_specs,
            input_output_aliases=aliases,
            scratch_shapes=scratch,
            compiler_params=LIMIT,
        )(*arrays)

    def swap(block, first, second, d):
        other = {first: second, second: first}
        pairs = []
        for a in range(tm):
            for q in range(n):
                for c in range(col_parts):
                    to = (other[a] * n + (q ^ d)) * col_parts + c if a in other else (a * n + q) * col_parts + (c ^ 1)
                    pairs.append(((a * n + q) * col_parts + c, to))
        return lax.ppermute(block, ("tm", "net", "cols"), pairs)

    def exchange(outgoing, first, second):
        return [swap(outgoing[d - 1], first, second, d) for d in range(1, n)]

    opening = state
    out = None
    for r in range(1, tm):
        arrived = exchange(outgoing, r - 1, r)
        state = swap(state, r - 1, r, 0)
        if r == 1:
            handed = arrived
        before = []
        for s in range(steps):
            fix = r == 1 and s == 0
            if s > 0:
                arrived = exchange(outgoing, r, r)
            first = jac if fix else own(state, s)
            if s < steps - 1:
                state, *outgoing = join(first, s, fix, state, arrived, r)
                before.append(state)
            else:
                out, *rest = close(first, s, state, arrived, r, before, out, r < tm - 1)
                state, *outgoing = rest or [None]
    return out


def solution(mesh):
    return jax.shard_map(
        local,
        mesh=mesh,
        in_specs=(
            P("tm", "net", None, None, None),
            P("net", None),
            P("tm", "net", None, None, None),
            P("net", None),
            P("net", None),
            P("net", None),
            P("cols"),
            P("tm", "cols"),
        ),
        out_specs=P("tm", "cols", "net"),
        check_vma=False,
    )
```

time: 25 us -> 22.4 us (0.90)
  Pallas kernels: 5.37 us -> 3.73 us
  waiting for transfers between devices: 8.13 us -> 7.13 us
    ppermute x7, waiting for transfers between devices: 8.13 us -> 7.13 us  [swap(): return lax.ppermute(block, ('tm', 'net', 'cols'), pairs)]
    pallas_call x2 -> x1, Pallas kernels: 1.78 us -> 0.88 us  [own(): pl.pallas_call(functools.partial(own_kernel, step), out_shape=f32(whole.s...]
    pallas_call x3, Pallas kernels: 3.59 us -> 2.84 us  [the longest x1 1.13 us: local(): pl.pallas_call(second_kernel, out_shape=[f32((cols, table_rows)), f32((ma...]
  transfers between devices with their start and end apart: 7 -> 7, of which waited for: 4 -> 4; matrix products, arithmetic and copies ran while one was open for 0% -> 0% of each run, Pallas kernels for 7% -> 4%
where the time goes in v14:
time: 22.4 us; the launch traced here: 22.2 us
  starting transfers between devices  11.3 us (50%)
  waiting for transfers between devices  7.13 us (32%)
  Pallas kernels  3.73 us (17%)
    ppermute x7, starting transfers between devices, swap(): return lax.ppermute(block, ('tm', 'net', 'cols'), pairs)  11.3 us
    ppermute x7, waiting for transfers between devices, swap(): return lax.ppermute(block, ('tm', 'net', 'cols'), pairs)  7.13 us
    pallas_call x1, Pallas kernels, local(): pl.pallas_call(second_kernel, out_shape=[f32((cols, table_rows)), f32((ma...  1.13 us
    pallas_call x1, Pallas kernels, close(): pl.pallas_call(functools.partial(close_kernel, step, section, firsts, sen...  1.06 us
    pallas_call x1, Pallas kernels, own(): pl.pallas_call(functools.partial(own_kernel, step), out_shape=f32(whole.s...  0.88 us
    pallas_call x1, Pallas kernels, join(): pl.pallas_call(functools.partial(join_kernel, step, fix, section), out_sh...  0.65 us
  transfers between devices with their start and end apart: 7, of which 4 were waited for; matrix products, arithmetic and copies ran while one was open for 0% of the time, Pallas kernels for 4%

profile of v14, /device:TPU:4, one launch (start us, length us, event | category | flops | bytes accessed | tf_op | source)
XLA Modules:
  0.0 22.2 jit_solution(12138652636730122853)
XLA Ops:
  0.0 0.0 copy-start
  0.0 0.0 copy-start.1
  0.0 1.1 %shard_map.82 = (f32[192,8]{1,0:T(8,128)S(1)}, f32[72,128]{1,0:T(8,128)S(1)}, bf16[4,192,128]{2,1,0:T(8,128)(2,1)S(1)}, bf16[208,128]{1,0:T(8,128)(2,1)S(1)}, bf...) custom-call(bf16[2,4,3,128,128]{4,3,2,1,0:T(8,128)(2,1)} %refs_13_.1, bf16[2,1,4,128,128]{4,3,2,1,0:T(8,128)(2,1)} %refs_1_.5, ...), custom_call_target="tpu_custom_call" | custom-call | tf_op jit(solution)/shard_map/pallas_call | solution.py:336
  1.1 0.2 collective-permute-start.3
  1.3 5.0 %collective-permute-start = (bf16[208,128]{1,0:T(8,128)(2,1)S(1)}, bf16[208,128]{1,0:T(8,128)(2,1)S(1)}, u32[]{:S(2)}, u32[]{:S(2)}) collective-permute-start(bf16[208,128]{1,0:T(8,128)(2,1)S(1)} %get-tuple-element.17), channel_id=1, source_target_pairs={{0,28},{1,29},{2,30},{3,31},{4,24},{5,25},{6,26},{7,27},{8,20},{9,... | collective-permute-start | bytes 159752 | tf_op jit(solution)/shard_map/ppermute | solution.py:414
  6.3 0.4 %collective-permute-start.1 = (bf16[208,128]{1,0:T(8,128)(2,1)S(1)}, bf16[208,128]{1,0:T(8,128)(2,1)S(1)}, u32[]{:S(2)}, u32[]{:S(2)}) collective-permute-start(bf16[208,128]{1,0:T(8,128)(2,1)S(1)} %get-tuple-element.18), channel_id=1, source_target_pairs={{0,24},{1,25},{2,26},{3,27},{4,28},{5,29},{6,30},{7,31},{8,16},{9,... | collective-permute-start | bytes 159752 | tf_op jit(solution)/shard_map/ppermute | solution.py:414
  6.7 1.3 %collective-permute-start.2 = (bf16[208,128]{1,0:T(8,128)(2,1)S(1)}, bf16[208,128]{1,0:T(8,128)(2,1)S(1)}, u32[]{:S(2)}, u32[]{:S(2)}) collective-permute-start(bf16[208,128]{1,0:T(8,128)(2,1)S(1)} %get-tuple-element.19), channel_id=1, source_target_pairs={{0,20},{1,21},{2,22},{3,23},{4,16},{5,17},{6,18},{7,19},{8,28},{9,... | collective-permute-start | bytes 159752 | tf_op jit(solution)/shard_map/ppermute | solution.py:414
  8.0 0.5 %collective-permute-done.refs_4_.refs_12_ = bf16[208,128]{1,0:T(8,128)(2,1)S(1)} collective-permute-done((bf16[208,128]{1,0:T(8,128)(2,1)S(1)}, bf16[208,128]{1,0:T(8,128)(2,1)S(1)}, u32[]{:S(2)}, u32[]{:S(2)}) %collective-permute-start) | collective-permute-done | bytes 53280 | tf_op jit(solution)/shard_map/ppermute | solution.py:414
  8.4 3.9 %collective-permute-done.1.refs_5_.refs_11_ = bf16[208,128]{1,0:T(8,128)(2,1)S(1)} collective-permute-done((bf16[208,128]{1,0:T(8,128)(2,1)S(1)}, bf16[208,128]{1,0:T(8,128)(2,1)S(1)}, u32[]{:S(2)}, u32[]{:S(2)}) %collective-permute-start.1) | collective-permute-done | bytes 53280 | tf_op jit(solution)/shard_map/ppermute | solution.py:414
  12.3 0.0 collective-permute-done.2.refs_6_.refs_10_
  12.3 0.0 collective-permute-done.3.refs_7_
  12.3 0.0 copy-done
  12.3 0.0 copy-done.1
  12.3 0.7 %shard_map.83 = (bf16[4,192,128]{2,1,0:T(8,128)(2,1)S(1)}, bf16[192,128]{1,0:T(8,128)(2,1)S(1)}, bf16[192,128]{1,0:T(8,128)(2,1)S(1)}, bf16[192,128]{1,0:T(8,128)(2,1)S(1)}) custom-call(bf16[2,4,3,128,128]{4,3,2,1,0:T(8,128)(2,1)S(1)} %copy-done, bf16[2,1,4,128,128]{4,3,2,1,0:T(8,128)(2,1)S(1)} %copy-done.1, ...), custom_call_target="tpu_custom_call" | custom-call | tf_op jit(solution)/shard_map/pallas_call | solution.py:363
  13.0 2.6 %collective-permute-start.4 = (bf16[192,128]{1,0:T(8,128)(2,1)S(1)}, bf16[192,128]{1,0:T(8,128)(2,1)S(1)}, u32[]{:S(2)}, u32[]{:S(2)}) collective-permute-start(bf16[192,128]{1,0:T(8,128)(2,1)S(1)} %get-tuple-element.22), channel_id=1, source_target_pairs={{0,1},{1,0},{2,3},{3,2},{4,5},{5,4},{6,7},{7,6},{8,9},{9,8},{10,11... | collective-permute-start | bytes 147464 | tf_op jit(solution)/shard_map/ppermute | solution.py:414
  15.6 0.4 %collective-permute-start.5 = (bf16[192,128]{1,0:T(8,128)(2,1)S(1)}, bf16[192,128]{1,0:T(8,128)(2,1)S(1)}, u32[]{:S(2)}, u32[]{:S(2)}) collective-permute-start(bf16[192,128]{1,0:T(8,128)(2,1)S(1)} %get-tuple-element.23), channel_id=1, source_target_pairs={{0,1},{1,0},{2,3},{3,2},{4,5},{5,4},{6,7},{7,6},{8,9},{9,8},{10,11... | collective-permute-start | bytes 147464 | tf_op jit(solution)/shard_map/ppermute | solution.py:414
  16.0 0.0 copy-start.2
  16.0 1.4 %collective-permute-start.6 = (bf16[192,128]{1,0:T(8,128)(2,1)S(1)}, bf16[192,128]{1,0:T(8,128)(2,1)S(1)}, u32[]{:S(2)}, u32[]{:S(2)}) collective-permute-start(bf16[192,128]{1,0:T(8,128)(2,1)S(1)} %get-tuple-element.24), channel_id=1, source_target_pairs={{0,1},{1,0},{2,3},{3,2},{4,5},{5,4},{6,7},{7,6},{8,9},{9,8},{10,11... | collective-permute-start | bytes 147464 | tf_op jit(solution)/shard_map/ppermute | solution.py:414
  17.4 0.0 copy-done.2
  17.4 0.9 %shard_map.84.refs_0_ = f32[4,192,128]{2,1,0:T(8,128)S(1)} custom-call(bf16[4,192,128]{2,1,0:T(8,128)(2,1)S(1)} %get-tuple-element.21.state_ref.refs_7_.refs_8_, bf16[2,4,3,128,128]{4,3,2,1,0:T(8,128)(2,1)S(1)} %copy-done, s32[2,4]{1,0:T(2,128)S(1)} %bitcast.4, f32[192,8]{1,0:T(8,128)S(1)} %get-tuple-element.15.refs_2_.table_ref), custom_call_target="tpu_custom_call" | custom-call | tf_op jit(solution)/shard_map/pallas_call | solution.py:354
  18.3 0.8 %collective-permute-done.4.refs_4_ = bf16[192,128]{1,0:T(8,128)(2,1)S(1)} collective-permute-done((bf16[192,128]{1,0:T(8,128)(2,1)S(1)}, bf16[192,128]{1,0:T(8,128)(2,1)S(1)}, u32[]{:S(2)}, u32[]{:S(2)}) %collective-permute-start.4) | collective-permute-done | bytes 49184 | tf_op jit(solution)/shard_map/ppermute | solution.py:414
  19.1 2.0 %collective-permute-done.5.refs_5_ = bf16[192,128]{1,0:T(8,128)(2,1)S(1)} collective-permute-done((bf16[192,128]{1,0:T(8,128)(2,1)S(1)}, bf16[192,128]{1,0:T(8,128)(2,1)S(1)}, u32[]{:S(2)}, u32[]{:S(2)}) %collective-permute-start.5) | collective-permute-done | bytes 49184 | tf_op jit(solution)/shard_map/ppermute | solution.py:414
  21.1 0.0 collective-permute-done.6.refs_6_
  21.1 1.1 %shard_map.85 = bf16[2,192,512]{2,1,0:T(8,128)(2,1)} custom-call(f32[4,192,128]{2,1,0:T(8,128)S(1)} %shard_map.84.refs_0_, bf16[2,1,4,128,128]{4,3,2,1,0:T(8,128)(2,1)S(1)} %copy-done.1, f32[192,8]{1,0:T(8,128)S(1)} %get-tuple-element.15.refs_2_.table_ref, f32[72,128]{1,0:T(8,128)S(1)} %get-tuple-element.16.refs_3_, ...), custom_call_target="tpu_custom_call" | custom-call | tf_op jit(solution)/shard_map/pallas_call | solution.py:396
Async XLA Ops:
  0.0 12.3 %copy-start = (bf16[2,4,3,128,128]{4,3,2,1,0:T(8,128)(2,1)S(1)}, bf16[2,4,3,128,128]{4,3,2,1,0:T(8,128)(2,1)}, u32[]{:S(2)}) copy-start(bf16[2,4,3,128,128]{4,3,2,1,0:T(8,128)(2,1)} %refs_13_.1) | copy-start | bytes 2359300
  0.0 12.3 %copy-start.1 = (bf16[2,1,4,128,128]{4,3,2,1,0:T(8,128)(2,1)S(1)}, bf16[2,1,4,128,128]{4,3,2,1,0:T(8,128)(2,1)}, u32[]{:S(2)}) copy-start(bf16[2,1,4,128,128]{4,3,2,1,0:T(8,128)(2,1)} %refs_1_.5) | copy-start | bytes 786436
  1.1 11.2 %collective-permute-start.3 = (bf16[4,192,128]{2,1,0:T(8,128)(2,1)S(1)}, bf16[4,192,128]{2,1,0:T(8,128)(2,1)S(1)}, u32[]{:S(2)}, u32[]{:S(2)}) collective-permute-start(bf16[4,192,128]{2,1,0:T(8,128)(2,1)S(1)} %get-tuple-element.20.refs_9_), channel_id=1, source_target_pairs={{0,16},{1,17},{2,18},{3,19},{4,20},{5,21},{6,22},{7,23},{8,24},{9,... | collective-permute-start | bytes 589832 | tf_op jit(solution)/shard_map/ppermute | solution.py:414
  1.3 7.1 %collective-permute-start = (bf16[208,128]{1,0:T(8,128)(2,1)S(1)}, bf16[208,128]{1,0:T(8,128)(2,1)S(1)}, u32[]{:S(2)}, u32[]{:S(2)}) collective-permute-start(bf16[208,128]{1,0:T(8,128)(2,1)S(1)} %get-tuple-element.17), channel_id=1, source_target_pairs={{0,28},{1,29},{2,30},{3,31},{4,24},{5,25},{6,26},{7,27},{8,20},{9,... | collective-permute-start | bytes 159752 | tf_op jit(solution)/shard_map/ppermute | solution.py:414
  6.3 6.0 %collective-permute-start.1 = (bf16[208,128]{1,0:T(8,128)(2,1)S(1)}, bf16[208,128]{1,0:T(8,128)(2,1)S(1)}, u32[]{:S(2)}, u32[]{:S(2)}) collective-permute-start(bf16[208,128]{1,0:T(8,128)(2,1)S(1)} %get-tuple-element.18), channel_id=1, source_target_pairs={{0,24},{1,25},{2,26},{3,27},{4,28},{5,29},{6,30},{7,31},{8,16},{9,... | collective-permute-start | bytes 159752 | tf_op jit(solution)/shard_map/ppermute | solution.py:414
  6.7 5.6 %collective-permute-start.2 = (bf16[208,128]{1,0:T(8,128)(2,1)S(1)}, bf16[208,128]{1,0:T(8,128)(2,1)S(1)}, u32[]{:S(2)}, u32[]{:S(2)}) collective-permute-start(bf16[208,128]{1,0:T(8,128)(2,1)S(1)} %get-tuple-element.19), channel_id=1, source_target_pairs={{0,20},{1,21},{2,22},{3,23},{4,16},{5,17},{6,18},{7,19},{8,28},{9,... | collective-permute-start | bytes 159752 | tf_op jit(solution)/shard_map/ppermute | solution.py:414
  13.0 6.1 %collective-permute-start.4 = (bf16[192,128]{1,0:T(8,128)(2,1)S(1)}, bf16[192,128]{1,0:T(8,128)(2,1)S(1)}, u32[]{:S(2)}, u32[]{:S(2)}) collective-permute-start(bf16[192,128]{1,0:T(8,128)(2,1)S(1)} %get-tuple-element.22), channel_id=1, source_target_pairs={{0,1},{1,0},{2,3},{3,2},{4,5},{5,4},{6,7},{7,6},{8,9},{9,8},{10,11... | collective-permute-start | bytes 147464 | tf_op jit(solution)/shard_map/ppermute | solution.py:414
  15.6 5.5 %collective-permute-start.5 = (bf16[192,128]{1,0:T(8,128)(2,1)S(1)}, bf16[192,128]{1,0:T(8,128)(2,1)S(1)}, u32[]{:S(2)}, u32[]{:S(2)}) collective-permute-start(bf16[192,128]{1,0:T(8,128)(2,1)S(1)} %get-tuple-element.23), channel_id=1, source_target_pairs={{0,1},{1,0},{2,3},{3,2},{4,5},{5,4},{6,7},{7,6},{8,9},{9,8},{10,11... | collective-permute-start | bytes 147464 | tf_op jit(solution)/shard_map/ppermute | solution.py:414
  16.0 1.4 %copy-start.2 = (s32[4,2]{0,1:T(2,128)S(1)}, s32[4,2]{0,1:T(2,128)}, u32[]{:S(2)}) copy-start(s32[4,2]{0,1:T(2,128)} %param.9) | copy-start | bytes 100
  16.0 5.1 %collective-permute-start.6 = (bf16[192,128]{1,0:T(8,128)(2,1)S(1)}, bf16[192,128]{1,0:T(8,128)(2,1)S(1)}, u32[]{:S(2)}, u32[]{:S(2)}) collective-permute-start(bf16[192,128]{1,0:T(8,128)(2,1)S(1)} %get-tuple-element.24), channel_id=1, source_target_pairs={{0,1},{1,0},{2,3},{3,2},{4,5},{5,4},{6,7},{7,6},{8,9},{9,8},{10,11... | collective-permute-start | bytes 147464 | tf_op jit(solution)/shard_map/ppermute | solution.py:414

commit v15 on v14

--- a/solution.py
+++ b/solution.py
@@ -420,7 +420,7 @@
     out = None
     for r in range(1, tm):
         arrived = exchange(outgoing, r - 1, r)
-        state = swap(state, r - 1, r, 0)
+        state = lax.ppermute(state, "tm", [(r - 1, r)])
         if r == 1:
             handed = arrived
         before = []

time: 22.4 us -> 23.7 us (1.058)
  starting transfers between devices: 11.3 us -> 13.2 us
  waiting for transfers between devices: 7.13 us -> 6.51 us
    ppermute x0 -> x1, starting transfers between devices: none -> 1.29 us  [local(): state = lax.ppermute(state, 'tm', [(r - 1, r)])]
    ppermute x7 -> x6, starting transfers between devices: 11.3 us -> 11.9 us  [swap(): return lax.ppermute(block, ('tm', 'net', 'cols'), pairs)]
    ppermute x7 -> x6, waiting for transfers between devices: 7.13 us -> 6.5 us  [swap(): return lax.ppermute(block, ('tm', 'net', 'cols'), pairs)]
where the time goes in v15:
time: 23.7 us; the launch traced here: 23.5 us
  starting transfers between devices  13.2 us (56%)
  waiting for transfers between devices  6.51 us (27%)
  Pallas kernels  3.73 us (16%)
    ppermute x6, starting transfers between devices, swap(): return lax.ppermute(block, ('tm', 'net', 'cols'), pairs)  11.9 us
    ppermute x6, waiting for transfers between devices, swap(): return lax.ppermute(block, ('tm', 'net', 'cols'), pairs)  6.5 us
    ppermute x1, starting transfers between devices, local(): state = lax.ppermute(state, 'tm', [(r - 1, r)])  1.29 us
    pallas_call x1, Pallas kernels, local(): pl.pallas_call(second_kernel, out_shape=[f32((cols, table_rows)), f32((ma...  1.13 us
    pallas_call x1, Pallas kernels, close(): pl.pallas_call(functools.partial(close_kernel, step, section, firsts, sen...  1.06 us
    pallas_call x1, Pallas kernels, own(): pl.pallas_call(functools.partial(own_kernel, step), out_shape=f32(whole.s...  0.88 us
    pallas_call x1, Pallas kernels, join(): pl.pallas_call(functools.partial(join_kernel, step, fix, section), out_sh...  0.65 us
  transfers between devices with their start and end apart: 7, of which 4 were waited for; matrix products, arithmetic and copies ran while one was open for 0% of the time, Pallas kernels for 4%

profile of v15, /device:TPU:4, one launch (start us, length us, event | category | flops | bytes accessed | tf_op | source)
XLA Modules:
  0.0 23.5 jit_solution(15243654590466877327)
XLA Ops:
  0.0 0.0 copy-start
  0.0 0.0 copy-start.1
  0.0 1.1 %shard_map.82 = (f32[192,8]{1,0:T(8,128)S(1)}, f32[72,128]{1,0:T(8,128)S(1)}, bf16[4,192,128]{2,1,0:T(8,128)(2,1)S(1)}, bf16[208,128]{1,0:T(8,128)(2,1)S(1)}, bf...) custom-call(bf16[2,4,3,128,128]{4,3,2,1,0:T(8,128)(2,1)} %refs_13_.1, bf16[2,1,4,128,128]{4,3,2,1,0:T(8,128)(2,1)} %refs_1_.5, ...), custom_call_target="tpu_custom_call" | custom-call | tf_op jit(solution)/shard_map/pallas_call | solution.py:336
  1.1 1.3 %collective-permute-start.3 = (bf16[4,192,128]{2,1,0:T(8,128)(2,1)S(1)}, bf16[4,192,128]{2,1,0:T(8,128)(2,1)S(1)}, u32[]{:S(2)}, u32[]{:S(2)}) collective-permute-start(bf16[4,192,128]{2,1,0:T(8,128)(2,1)S(1)} %get-tuple-element.20.refs_9_), channel_id=1, source_target_pairs={{0,16},{1,17},{2,18},{3,19},{4,20},{5,21},{6,22},{7,23},{8,24},{9,... | collective-permute-start | bytes 589832 | tf_op jit(solution)/shard_map/ppermute | solution.py:423
  2.4 5.8 %collective-permute-start = (bf16[208,128]{1,0:T(8,128)(2,1)S(1)}, bf16[208,128]{1,0:T(8,128)(2,1)S(1)}, u32[]{:S(2)}, u32[]{:S(2)}) collective-permute-start(bf16[208,128]{1,0:T(8,128)(2,1)S(1)} %get-tuple-element.17), channel_id=1, source_target_pairs={{0,28},{1,29},{2,30},{3,31},{4,24},{5,25},{6,26},{7,27},{8,20},{9,... | collective-permute-start | bytes 159752 | tf_op jit(solution)/shard_map/ppermute | solution.py:414
  8.2 0.0 collective-permute-start.1
  8.2 1.7 %collective-permute-start.2 = (bf16[208,128]{1,0:T(8,128)(2,1)S(1)}, bf16[208,128]{1,0:T(8,128)(2,1)S(1)}, u32[]{:S(2)}, u32[]{:S(2)}) collective-permute-start(bf16[208,128]{1,0:T(8,128)(2,1)S(1)} %get-tuple-element.19), channel_id=1, source_target_pairs={{0,20},{1,21},{2,22},{3,23},{4,16},{5,17},{6,18},{7,19},{8,28},{9,... | collective-permute-start | bytes 159752 | tf_op jit(solution)/shard_map/ppermute | solution.py:414
  9.9 0.5 %collective-permute-done.refs_4_.refs_12_ = bf16[208,128]{1,0:T(8,128)(2,1)S(1)} collective-permute-done((bf16[208,128]{1,0:T(8,128)(2,1)S(1)}, bf16[208,128]{1,0:T(8,128)(2,1)S(1)}, u32[]{:S(2)}, u32[]{:S(2)}) %collective-permute-start) | collective-permute-done | bytes 53280 | tf_op jit(solution)/shard_map/ppermute | solution.py:414
  10.4 3.7 %collective-permute-done.1.refs_5_.refs_11_ = bf16[208,128]{1,0:T(8,128)(2,1)S(1)} collective-permute-done((bf16[208,128]{1,0:T(8,128)(2,1)S(1)}, bf16[208,128]{1,0:T(8,128)(2,1)S(1)}, u32[]{:S(2)}, u32[]{:S(2)}) %collective-permute-start.1) | collective-permute-done | bytes 53280 | tf_op jit(solution)/shard_map/ppermute | solution.py:414
  14.1 0.0 collective-permute-done.2.refs_6_.refs_10_
  14.1 0.0 collective-permute-done.3.refs_7_
  14.1 0.0 copy-done
  14.1 0.0 copy-done.1
  14.2 0.7 %shard_map.83 = (bf16[4,192,128]{2,1,0:T(8,128)(2,1)S(1)}, bf16[192,128]{1,0:T(8,128)(2,1)S(1)}, bf16[192,128]{1,0:T(8,128)(2,1)S(1)}, bf16[192,128]{1,0:T(8,128)(2,1)S(1)}) custom-call(bf16[2,4,3,128,128]{4,3,2,1,0:T(8,128)(2,1)S(1)} %copy-done, bf16[2,1,4,128,128]{4,3,2,1,0:T(8,128)(2,1)S(1)} %copy-done.1, ...), custom_call_target="tpu_custom_call" | custom-call | tf_op jit(solution)/shard_map/pallas_call | solution.py:363
  14.8 2.6 %collective-permute-start.4 = (bf16[192,128]{1,0:T(8,128)(2,1)S(1)}, bf16[192,128]{1,0:T(8,128)(2,1)S(1)}, u32[]{:S(2)}, u32[]{:S(2)}) collective-permute-start(bf16[192,128]{1,0:T(8,128)(2,1)S(1)} %get-tuple-element.22), channel_id=1, source_target_pairs={{0,1},{1,0},{2,3},{3,2},{4,5},{5,4},{6,7},{7,6},{8,9},{9,8},{10,11... | collective-permute-start | bytes 147464 | tf_op jit(solution)/shard_map/ppermute | solution.py:414
  17.4 0.0 collective-permute-start.5
  17.4 0.0 copy-start.2
  17.4 1.8 %collective-permute-start.6 = (bf16[192,128]{1,0:T(8,128)(2,1)S(1)}, bf16[192,128]{1,0:T(8,128)(2,1)S(1)}, u32[]{:S(2)}, u32[]{:S(2)}) collective-permute-start(bf16[192,128]{1,0:T(8,128)(2,1)S(1)} %get-tuple-element.24), channel_id=1, source_target_pairs={{0,1},{1,0},{2,3},{3,2},{4,5},{5,4},{6,7},{7,6},{8,9},{9,8},{10,11... | collective-permute-start | bytes 147464 | tf_op jit(solution)/shard_map/ppermute | solution.py:414
  19.3 0.0 copy-done.2
  19.3 0.9 %shard_map.84.refs_0_ = f32[4,192,128]{2,1,0:T(8,128)S(1)} custom-call(bf16[4,192,128]{2,1,0:T(8,128)(2,1)S(1)} %get-tuple-element.21.state_ref.refs_7_.refs_8_, bf16[2,4,3,128,128]{4,3,2,1,0:T(8,128)(2,1)S(1)} %copy-done, s32[2,4]{1,0:T(2,128)S(1)} %bitcast.4, f32[192,8]{1,0:T(8,128)S(1)} %get-tuple-element.15.refs_2_.table_ref), custom_call_target="tpu_custom_call" | custom-call | tf_op jit(solution)/shard_map/pallas_call | solution.py:354
  20.2 0.7 %collective-permute-done.4.refs_4_ = bf16[192,128]{1,0:T(8,128)(2,1)S(1)} collective-permute-done((bf16[192,128]{1,0:T(8,128)(2,1)S(1)}, bf16[192,128]{1,0:T(8,128)(2,1)S(1)}, u32[]{:S(2)}, u32[]{:S(2)}) %collective-permute-start.4) | collective-permute-done | bytes 49184 | tf_op jit(solution)/shard_map/ppermute | solution.py:414
  20.9 1.5 %collective-permute-done.5.refs_5_ = bf16[192,128]{1,0:T(8,128)(2,1)S(1)} collective-permute-done((bf16[192,128]{1,0:T(8,128)(2,1)S(1)}, bf16[192,128]{1,0:T(8,128)(2,1)S(1)}, u32[]{:S(2)}, u32[]{:S(2)}) %collective-permute-start.5) | collective-permute-done | bytes 49184 | tf_op jit(solution)/shard_map/ppermute | solution.py:414
  22.4 0.0 collective-permute-done.6.refs_6_
  22.4 1.1 %shard_map.85 = bf16[2,192,512]{2,1,0:T(8,128)(2,1)} custom-call(f32[4,192,128]{2,1,0:T(8,128)S(1)} %shard_map.84.refs_0_, bf16[2,1,4,128,128]{4,3,2,1,0:T(8,128)(2,1)S(1)} %copy-done.1, f32[192,8]{1,0:T(8,128)S(1)} %get-tuple-element.15.refs_2_.table_ref, f32[72,128]{1,0:T(8,128)S(1)} %get-tuple-element.16.refs_3_, ...), custom_call_target="tpu_custom_call" | custom-call | tf_op jit(solution)/shard_map/pallas_call | solution.py:396
Async XLA Ops:
  0.0 14.1 %copy-start = (bf16[2,4,3,128,128]{4,3,2,1,0:T(8,128)(2,1)S(1)}, bf16[2,4,3,128,128]{4,3,2,1,0:T(8,128)(2,1)}, u32[]{:S(2)}) copy-start(bf16[2,4,3,128,128]{4,3,2,1,0:T(8,128)(2,1)} %refs_13_.1) | copy-start | bytes 2359300
  0.0 14.1 %copy-start.1 = (bf16[2,1,4,128,128]{4,3,2,1,0:T(8,128)(2,1)S(1)}, bf16[2,1,4,128,128]{4,3,2,1,0:T(8,128)(2,1)}, u32[]{:S(2)}) copy-start(bf16[2,1,4,128,128]{4,3,2,1,0:T(8,128)(2,1)} %refs_1_.5) | copy-start | bytes 786436
  1.1 13.0 %collective-permute-start.3 = (bf16[4,192,128]{2,1,0:T(8,128)(2,1)S(1)}, bf16[4,192,128]{2,1,0:T(8,128)(2,1)S(1)}, u32[]{:S(2)}, u32[]{:S(2)}) collective-permute-start(bf16[4,192,128]{2,1,0:T(8,128)(2,1)S(1)} %get-tuple-element.20.refs_9_), channel_id=1, source_target_pairs={{0,16},{1,17},{2,18},{3,19},{4,20},{5,21},{6,22},{7,23},{8,24},{9,... | collective-permute-start | bytes 589832 | tf_op jit(solution)/shard_map/ppermute | solution.py:423
  2.4 8.0 %collective-permute-start = (bf16[208,128]{1,0:T(8,128)(2,1)S(1)}, bf16[208,128]{1,0:T(8,128)(2,1)S(1)}, u32[]{:S(2)}, u32[]{:S(2)}) collective-permute-start(bf16[208,128]{1,0:T(8,128)(2,1)S(1)} %get-tuple-element.17), channel_id=1, source_target_pairs={{0,28},{1,29},{2,30},{3,31},{4,24},{5,25},{6,26},{7,27},{8,20},{9,... | collective-permute-start | bytes 159752 | tf_op jit(solution)/shard_map/ppermute | solution.py:414
  8.2 5.9 %collective-permute-start.1 = (bf16[208,128]{1,0:T(8,128)(2,1)S(1)}, bf16[208,128]{1,0:T(8,128)(2,1)S(1)}, u32[]{:S(2)}, u32[]{:S(2)}) collective-permute-start(bf16[208,128]{1,0:T(8,128)(2,1)S(1)} %get-tuple-element.18), channel_id=1, source_target_pairs={{0,24},{1,25},{2,26},{3,27},{4,28},{5,29},{6,30},{7,31},{8,16},{9,... | collective-permute-start | bytes 159752 | tf_op jit(solution)/shard_map/ppermute | solution.py:414
  8.2 5.9 %collective-permute-start.2 = (bf16[208,128]{1,0:T(8,128)(2,1)S(1)}, bf16[208,128]{1,0:T(8,128)(2,1)S(1)}, u32[]{:S(2)}, u32[]{:S(2)}) collective-permute-start(bf16[208,128]{1,0:T(8,128)(2,1)S(1)} %get-tuple-element.19), channel_id=1, source_target_pairs={{0,20},{1,21},{2,22},{3,23},{4,16},{5,17},{6,18},{7,19},{8,28},{9,... | collective-permute-start | bytes 159752 | tf_op jit(solution)/shard_map/ppermute | solution.py:414
  14.8 6.1 %collective-permute-start.4 = (bf16[192,128]{1,0:T(8,128)(2,1)S(1)}, bf16[192,128]{1,0:T(8,128)(2,1)S(1)}, u32[]{:S(2)}, u32[]{:S(2)}) collective-permute-start(bf16[192,128]{1,0:T(8,128)(2,1)S(1)} %get-tuple-element.22), channel_id=1, source_target_pairs={{0,1},{1,0},{2,3},{3,2},{4,5},{5,4},{6,7},{7,6},{8,9},{9,8},{10,11... | collective-permute-start | bytes 147464 | tf_op jit(solution)/shard_map/ppermute | solution.py:414
  17.4 5.0 %collective-permute-start.5 = (bf16[192,128]{1,0:T(8,128)(2,1)S(1)}, bf16[192,128]{1,0:T(8,128)(2,1)S(1)}, u32[]{:S(2)}, u32[]{:S(2)}) collective-permute-start(bf16[192,128]{1,0:T(8,128)(2,1)S(1)} %get-tuple-element.23), channel_id=1, source_target_pairs={{0,1},{1,0},{2,3},{3,2},{4,5},{5,4},{6,7},{7,6},{8,9},{9,8},{10,11... | collective-permute-start | bytes 147464 | tf_op jit(solution)/shard_map/ppermute | solution.py:414
  17.4 1.8 %copy-start.2 = (s32[4,2]{0,1:T(2,128)S(1)}, s32[4,2]{0,1:T(2,128)}, u32[]{:S(2)}) copy-start(s32[4,2]{0,1:T(2,128)} %param.9) | copy-start | bytes 100
  17.4 5.0 %collective-permute-start.6 = (bf16[192,128]{1,0:T(8,128)(2,1)S(1)}, bf16[192,128]{1,0:T(8,128)(2,1)S(1)}, u32[]{:S(2)}, u32[]{:S(2)}) collective-permute-start(bf16[192,128]{1,0:T(8,128)(2,1)S(1)} %get-tuple-element.24), channel_id=1, source_target_pairs={{0,1},{1,0},{2,3},{3,2},{4,5},{5,4},{6,7},{7,6},{8,9},{9,8},{10,11... | collective-permute-start | bytes 147464 | tf_op jit(solution)/shard_map/ppermute | solution.py:414

commit v16 on v14

--- a/solution.py
+++ b/solution.py
@@ -16,6 +16,14 @@
 
 STATE, LANE, BLOCK, AWAY, GAIN = 0, 1, 2, 3, 4
 ROWS = 16
+
+
+def turn(d, n, col):
+    return jnp.where(jnp.logical_and(col % 2 == 1, d > 0), n - d, d)
+
+
+def partner(partition, d):
+    return partition ^ turn(d, lax.axis_size("net"), lax.axis_index("cols"))
 
 
 def times_transposed(rows, block):
@@ -67,7 +75,7 @@
         marks_ref[pl.ds(row, 1)] = jnp.where(mask, 1.0, 0.0)
 
     for d in range(n):
-        q = me ^ d
+        q = partner(me, d)
         for i in range(blocks):
             put(d * blocks + i, lane < jnp.where(recv_ref[0, q] == i, live_ref[0, q], 0))
             put(sent + d * blocks + i, lane < jnp.where(send_ref[0, q] == i, width, 0))
@@ -87,7 +95,7 @@
     lane = lax.broadcasted_iota(jnp.int32, (1, width), 1)
     row = jnp.zeros((1, width), jnp.float32)
     for e in range(lax.axis_size("net")):
-        row = jnp.where(lane == e, send_ref[0, partition ^ e].astype(jnp.float32), row)
+        row = jnp.where(lane == e, send_ref[0, partner(partition, e)].astype(jnp.float32), row)
     return row
 
 
@@ -131,7 +139,7 @@
         node,
         node - block_of * width,
         block_of % blocks,
-        (block_of // blocks) ^ me,
+        turn((block_of // blocks) ^ me, n, lax.axis_index("cols")),
     ]
     steps = gain_ref.shape[0]
     fill = -(GAIN + steps) % 8
@@ -150,11 +158,11 @@
         shot = jnp.where(mine, shot, 0.0)
         live = recv = jnp.zeros_like(away)
         for d in range(n):
-            live = jnp.where(away == float(d), live_ref[0, me ^ d].astype(jnp.float32), live)
-            recv = jnp.where(away == float(d), recv_ref[0, me ^ d].astype(jnp.float32), recv)
+            live = jnp.where(away == float(d), live_ref[0, partner(me, d)].astype(jnp.float32), live)
+            recv = jnp.where(away == float(d), recv_ref[0, partner(me, d)].astype(jnp.float32), recv)
         sent = [jnp.where(away == float(d), shot, 0.0).astype(first_ref.dtype) for d in range(n)]
         loads[1].wait()
-        ifaces = jnp.concatenate([iface_ref[me ^ d] for d in range(n)], axis=1)
+        ifaces = jnp.concatenate([iface_ref[partner(me, d)] for d in range(n)], axis=1)
         coupled = times_transposed(jnp.concatenate(sent, axis=1), ifaces)
         coupled = jnp.where(lane < live, coupled, 0.0)
         loads[0].wait()
@@ -162,14 +170,14 @@
             own = own_sum(i, first_ref, jac_ref, near_by(first_ref, cols_ref), table, 1)
             state_ref[i] = (own + jnp.where(recv == float(i), coupled, 0.0)).astype(state_ref.dtype)
         for d in range(1, n):
-            outgoing[d - 1][pl.ds(0, cols)] = state_ref[send_ref[0, me ^ d]]
+            outgoing[d - 1][pl.ds(0, cols)] = state_ref[send_ref[0, partner(me, d)]]
 
     @pl.when(jnp.logical_not(here))
     def _():
         make_marks(marks_ref, blocks, jac_ref.shape[1], cols_ref, send_ref, recv_ref, live_ref)
 
     for d in range(1, n):
-        row = table_row(send_ref, me ^ d, width).astype(state_ref.dtype)
+        row = table_row(send_ref, partner(me, d), width).astype(state_ref.dtype)
         outgoing[d - 1][pl.ds(cols, ROWS)] = jnp.broadcast_to(row, (ROWS, width))
 
 
@@ -222,7 +230,7 @@
         else:
             marks = [marks_ref[pl.ds(sent + j, 1)].astype(state_ref.dtype) for j in range(blocks)]
             block = picked([state_ref[j] for j in range(blocks)], marks)
-        term = times_transposed(block, iface_ref[step, 0, me ^ d])
+        term = times_transposed(block, iface_ref[step, 0, partner(me, d)])
         if keep is not None:
             term *= keep[:, d : d + 1]
         sums = [total + term * marks_ref[pl.ds(d * blocks + i, 1)] for i, total in enumerate(sums)]
@@ -409,7 +417,8 @@
         for a in range(tm):
             for q in range(n):
                 for c in range(col_parts):
-                    to = (other[a] * n + (q ^ d)) * col_parts + c if a in other else (a * n + q) * col_parts + (c ^ 1)
+                    p = q ^ (n - d if c % 2 == 1 and d > 0 else d)
+                    to = (other[a] * n + p) * col_parts + c if a in other else (a * n + q) * col_parts + (c ^ 1)
                     pairs.append(((a * n + q) * col_parts + c, to))
         return lax.ppermute(block, ("tm", "net", "cols"), pairs)
 

time: 22.4 us -> 22.5 us (level)
  no operation moved by 1% of the time
where the time goes in v16:
time: 22.5 us; the launch traced here: 22.3 us
  starting transfers between devices  11.3 us (50%)
  waiting for transfers between devices  7.28 us (32%)
  Pallas kernels  3.73 us (17%)
    ppermute x7, starting transfers between devices, swap(): return lax.ppermute(block, ('tm', 'net', 'cols'), pairs)  11.3 us
    ppermute x7, waiting for transfers between devices, swap(): return lax.ppermute(block, ('tm', 'net', 'cols'), pairs)  7.28 us
    pallas_call x1, Pallas kernels, local(): pl.pallas_call(second_kernel, out_shape=[f32((cols, table_rows)), f32((ma...  1.13 us
    pallas_call x1, Pallas kernels, close(): pl.pallas_call(functools.partial(close_kernel, step, section, firsts, sen...  1.06 us
    pallas_call x1, Pallas kernels, own(): pl.pallas_call(functools.partial(own_kernel, step), out_shape=f32(whole.s...  0.89 us
    pallas_call x1, Pallas kernels, join(): pl.pallas_call(functools.partial(join_kernel, step, fix, section), out_sh...  0.65 us
  transfers between devices with their start and end apart: 7, of which 4 were waited for; matrix products, arithmetic and copies ran while one was open for 0% of the time, Pallas kernels for 4%

profile of v16, /device:TPU:4, one launch (start us, length us, event | category | flops | bytes accessed | tf_op | source)
XLA Modules:
  0.0 22.3 jit_solution(12758766084934519744)
XLA Ops:
  0.0 0.0 copy-start
  0.0 0.0 copy-start.1
  0.0 1.1 %shard_map.82 = (f32[192,8]{1,0:T(8,128)S(1)}, f32[72,128]{1,0:T(8,128)S(1)}, bf16[4,192,128]{2,1,0:T(8,128)(2,1)S(1)}, bf16[208,128]{1,0:T(8,128)(2,1)S(1)}, bf...) custom-call(bf16[2,4,3,128,128]{4,3,2,1,0:T(8,128)(2,1)} %refs_13_.1, bf16[2,1,4,128,128]{4,3,2,1,0:T(8,128)(2,1)} %refs_1_.5, ...), custom_call_target="tpu_custom_call" | custom-call | tf_op jit(solution)/shard_map/pallas_call | solution.py:344
  1.1 0.2 collective-permute-start.3
  1.3 5.0 %collective-permute-start = (bf16[208,128]{1,0:T(8,128)(2,1)S(1)}, bf16[208,128]{1,0:T(8,128)(2,1)S(1)}, u32[]{:S(2)}, u32[]{:S(2)}) collective-permute-start(bf16[208,128]{1,0:T(8,128)(2,1)S(1)} %get-tuple-element.17), channel_id=1, source_target_pairs={{0,28},{1,21},{2,30},{3,23},{4,24},{5,17},{6,26},{7,19},{8,20},{9,... | collective-permute-start | bytes 159752 | tf_op jit(solution)/shard_map/ppermute | solution.py:423
  6.3 0.4 %collective-permute-start.1 = (bf16[208,128]{1,0:T(8,128)(2,1)S(1)}, bf16[208,128]{1,0:T(8,128)(2,1)S(1)}, u32[]{:S(2)}, u32[]{:S(2)}) collective-permute-start(bf16[208,128]{1,0:T(8,128)(2,1)S(1)} %get-tuple-element.18), channel_id=1, source_target_pairs={{0,24},{1,25},{2,26},{3,27},{4,28},{5,29},{6,30},{7,31},{8,16},{9,... | collective-permute-start | bytes 159752 | tf_op jit(solution)/shard_map/ppermute | solution.py:423
  6.7 1.3 %collective-permute-start.2 = (bf16[208,128]{1,0:T(8,128)(2,1)S(1)}, bf16[208,128]{1,0:T(8,128)(2,1)S(1)}, u32[]{:S(2)}, u32[]{:S(2)}) collective-permute-start(bf16[208,128]{1,0:T(8,128)(2,1)S(1)} %get-tuple-element.19), channel_id=1, source_target_pairs={{0,20},{1,29},{2,22},{3,31},{4,16},{5,25},{6,18},{7,27},{8,28},{9,... | collective-permute-start | bytes 159752 | tf_op jit(solution)/shard_map/ppermute | solution.py:423
  8.0 1.0 %collective-permute-done.refs_4_.refs_12_ = bf16[208,128]{1,0:T(8,128)(2,1)S(1)} collective-permute-done((bf16[208,128]{1,0:T(8,128)(2,1)S(1)}, bf16[208,128]{1,0:T(8,128)(2,1)S(1)}, u32[]{:S(2)}, u32[]{:S(2)}) %collective-permute-start) | collective-permute-done | bytes 53280 | tf_op jit(solution)/shard_map/ppermute | solution.py:423
  8.9 3.4 %collective-permute-done.1.refs_5_.refs_11_ = bf16[208,128]{1,0:T(8,128)(2,1)S(1)} collective-permute-done((bf16[208,128]{1,0:T(8,128)(2,1)S(1)}, bf16[208,128]{1,0:T(8,128)(2,1)S(1)}, u32[]{:S(2)}, u32[]{:S(2)}) %collective-permute-start.1) | collective-permute-done | bytes 53280 | tf_op jit(solution)/shard_map/ppermute | solution.py:423
  12.3 0.0 collective-permute-done.2.refs_6_.refs_10_
  12.3 0.0 collective-permute-done.3.refs_7_
  12.3 0.0 copy-done
  12.3 0.0 copy-done.1
  12.3 0.6 %shard_map.83 = (bf16[4,192,128]{2,1,0:T(8,128)(2,1)S(1)}, bf16[192,128]{1,0:T(8,128)(2,1)S(1)}, bf16[192,128]{1,0:T(8,128)(2,1)S(1)}, bf16[192,128]{1,0:T(8,128)(2,1)S(1)}) custom-call(bf16[2,4,3,128,128]{4,3,2,1,0:T(8,128)(2,1)S(1)} %copy-done, bf16[2,1,4,128,128]{4,3,2,1,0:T(8,128)(2,1)S(1)} %copy-done.1, ...), custom_call_target="tpu_custom_call" | custom-call | tf_op jit(solution)/shard_map/pallas_call | solution.py:371
  13.0 2.7 %collective-permute-start.4 = (bf16[192,128]{1,0:T(8,128)(2,1)S(1)}, bf16[192,128]{1,0:T(8,128)(2,1)S(1)}, u32[]{:S(2)}, u32[]{:S(2)}) collective-permute-start(bf16[192,128]{1,0:T(8,128)(2,1)S(1)} %get-tuple-element.22), channel_id=1, source_target_pairs={{0,1},{1,0},{2,3},{3,2},{4,5},{5,4},{6,7},{7,6},{8,9},{9,8},{10,11... | collective-permute-start | bytes 147464 | tf_op jit(solution)/shard_map/ppermute | solution.py:423
  15.7 0.3 %collective-permute-start.5 = (bf16[192,128]{1,0:T(8,128)(2,1)S(1)}, bf16[192,128]{1,0:T(8,128)(2,1)S(1)}, u32[]{:S(2)}, u32[]{:S(2)}) collective-permute-start(bf16[192,128]{1,0:T(8,128)(2,1)S(1)} %get-tuple-element.23), channel_id=1, source_target_pairs={{0,1},{1,0},{2,3},{3,2},{4,5},{5,4},{6,7},{7,6},{8,9},{9,8},{10,11... | collective-permute-start | bytes 147464 | tf_op jit(solution)/shard_map/ppermute | solution.py:423
  16.0 0.0 copy-start.2
  16.0 1.4 %collective-permute-start.6 = (bf16[192,128]{1,0:T(8,128)(2,1)S(1)}, bf16[192,128]{1,0:T(8,128)(2,1)S(1)}, u32[]{:S(2)}, u32[]{:S(2)}) collective-permute-start(bf16[192,128]{1,0:T(8,128)(2,1)S(1)} %get-tuple-element.24), channel_id=1, source_target_pairs={{0,1},{1,0},{2,3},{3,2},{4,5},{5,4},{6,7},{7,6},{8,9},{9,8},{10,11... | collective-permute-start | bytes 147464 | tf_op jit(solution)/shard_map/ppermute | solution.py:423
  17.4 0.0 copy-done.2
  17.5 0.9 %shard_map.84.refs_0_ = f32[4,192,128]{2,1,0:T(8,128)S(1)} custom-call(bf16[4,192,128]{2,1,0:T(8,128)(2,1)S(1)} %get-tuple-element.21.state_ref.refs_7_.refs_8_, bf16[2,4,3,128,128]{4,3,2,1,0:T(8,128)(2,1)S(1)} %copy-done, s32[2,4]{1,0:T(2,128)S(1)} %bitcast.4, f32[192,8]{1,0:T(8,128)S(1)} %get-tuple-element.15.refs_2_.table_ref), custom_call_target="tpu_custom_call" | custom-call | tf_op jit(solution)/shard_map/pallas_call | solution.py:362
  18.3 1.2 %collective-permute-done.4.refs_4_ = bf16[192,128]{1,0:T(8,128)(2,1)S(1)} collective-permute-done((bf16[192,128]{1,0:T(8,128)(2,1)S(1)}, bf16[192,128]{1,0:T(8,128)(2,1)S(1)}, u32[]{:S(2)}, u32[]{:S(2)}) %collective-permute-start.4) | collective-permute-done | bytes 49184 | tf_op jit(solution)/shard_map/ppermute | solution.py:423
  19.6 1.7 %collective-permute-done.5.refs_5_ = bf16[192,128]{1,0:T(8,128)(2,1)S(1)} collective-permute-done((bf16[192,128]{1,0:T(8,128)(2,1)S(1)}, bf16[192,128]{1,0:T(8,128)(2,1)S(1)}, u32[]{:S(2)}, u32[]{:S(2)}) %collective-permute-start.5) | collective-permute-done | bytes 49184 | tf_op jit(solution)/shard_map/ppermute | solution.py:423
  21.3 0.0 collective-permute-done.6.refs_6_
  21.3 1.1 %shard_map.85 = bf16[2,192,512]{2,1,0:T(8,128)(2,1)} custom-call(f32[4,192,128]{2,1,0:T(8,128)S(1)} %shard_map.84.refs_0_, bf16[2,1,4,128,128]{4,3,2,1,0:T(8,128)(2,1)S(1)} %copy-done.1, f32[192,8]{1,0:T(8,128)S(1)} %get-tuple-element.15.refs_2_.table_ref, f32[72,128]{1,0:T(8,128)S(1)} %get-tuple-element.16.refs_3_, ...), custom_call_target="tpu_custom_call" | custom-call | tf_op jit(solution)/shard_map/pallas_call | solution.py:404
Async XLA Ops:
  0.0 12.3 %copy-start = (bf16[2,4,3,128,128]{4,3,2,1,0:T(8,128)(2,1)S(1)}, bf16[2,4,3,128,128]{4,3,2,1,0:T(8,128)(2,1)}, u32[]{:S(2)}) copy-start(bf16[2,4,3,128,128]{4,3,2,1,0:T(8,128)(2,1)} %refs_13_.1) | copy-start | bytes 2359300
  0.0 12.3 %copy-start.1 = (bf16[2,1,4,128,128]{4,3,2,1,0:T(8,128)(2,1)S(1)}, bf16[2,1,4,128,128]{4,3,2,1,0:T(8,128)(2,1)}, u32[]{:S(2)}) copy-start(bf16[2,1,4,128,128]{4,3,2,1,0:T(8,128)(2,1)} %refs_1_.5) | copy-start | bytes 786436
  1.1 11.2 %collective-permute-start.3 = (bf16[4,192,128]{2,1,0:T(8,128)(2,1)S(1)}, bf16[4,192,128]{2,1,0:T(8,128)(2,1)S(1)}, u32[]{:S(2)}, u32[]{:S(2)}) collective-permute-start(bf16[4,192,128]{2,1,0:T(8,128)(2,1)S(1)} %get-tuple-element.20.refs_9_), channel_id=1, source_target_pairs={{0,16},{1,17},{2,18},{3,19},{4,20},{5,21},{6,22},{7,23},{8,24},{9,... | collective-permute-start | bytes 589832 | tf_op jit(solution)/shard_map/ppermute | solution.py:423
  1.3 7.6 %collective-permute-start = (bf16[208,128]{1,0:T(8,128)(2,1)S(1)}, bf16[208,128]{1,0:T(8,128)(2,1)S(1)}, u32[]{:S(2)}, u32[]{:S(2)}) collective-permute-start(bf16[208,128]{1,0:T(8,128)(2,1)S(1)} %get-tuple-element.17), channel_id=1, source_target_pairs={{0,28},{1,21},{2,30},{3,23},{4,24},{5,17},{6,26},{7,19},{8,20},{9,... | collective-permute-start | bytes 159752 | tf_op jit(solution)/shard_map/ppermute | solution.py:423
  6.3 6.0 %collective-permute-start.1 = (bf16[208,128]{1,0:T(8,128)(2,1)S(1)}, bf16[208,128]{1,0:T(8,128)(2,1)S(1)}, u32[]{:S(2)}, u32[]{:S(2)}) collective-permute-start(bf16[208,128]{1,0:T(8,128)(2,1)S(1)} %get-tuple-element.18), channel_id=1, source_target_pairs={{0,24},{1,25},{2,26},{3,27},{4,28},{5,29},{6,30},{7,31},{8,16},{9,... | collective-permute-start | bytes 159752 | tf_op jit(solution)/shard_map/ppermute | solution.py:423
  6.7 5.6 %collective-permute-start.2 = (bf16[208,128]{1,0:T(8,128)(2,1)S(1)}, bf16[208,128]{1,0:T(8,128)(2,1)S(1)}, u32[]{:S(2)}, u32[]{:S(2)}) collective-permute-start(bf16[208,128]{1,0:T(8,128)(2,1)S(1)} %get-tuple-element.19), channel_id=1, source_target_pairs={{0,20},{1,29},{2,22},{3,31},{4,16},{5,25},{6,18},{7,27},{8,28},{9,... | collective-permute-start | bytes 159752 | tf_op jit(solution)/shard_map/ppermute | solution.py:423
  13.0 6.6 %collective-permute-start.4 = (bf16[192,128]{1,0:T(8,128)(2,1)S(1)}, bf16[192,128]{1,0:T(8,128)(2,1)S(1)}, u32[]{:S(2)}, u32[]{:S(2)}) collective-permute-start(bf16[192,128]{1,0:T(8,128)(2,1)S(1)} %get-tuple-element.22), channel_id=1, source_target_pairs={{0,1},{1,0},{2,3},{3,2},{4,5},{5,4},{6,7},{7,6},{8,9},{9,8},{10,11... | collective-permute-start | bytes 147464 | tf_op jit(solution)/shard_map/ppermute | solution.py:423
  15.7 5.6 %collective-permute-start.5 = (bf16[192,128]{1,0:T(8,128)(2,1)S(1)}, bf16[192,128]{1,0:T(8,128)(2,1)S(1)}, u32[]{:S(2)}, u32[]{:S(2)}) collective-permute-start(bf16[192,128]{1,0:T(8,128)(2,1)S(1)} %get-tuple-element.23), channel_id=1, source_target_pairs={{0,1},{1,0},{2,3},{3,2},{4,5},{5,4},{6,7},{7,6},{8,9},{9,8},{10,11... | collective-permute-start | bytes 147464 | tf_op jit(solution)/shard_map/ppermute | solution.py:423
  16.0 1.4 %copy-start.2 = (s32[4,2]{0,1:T(2,128)S(1)}, s32[4,2]{0,1:T(2,128)}, u32[]{:S(2)}) copy-start(s32[4,2]{0,1:T(2,128)} %param.9) | copy-start | bytes 100
  16.0 5.2 %collective-permute-start.6 = (bf16[192,128]{1,0:T(8,128)(2,1)S(1)}, bf16[192,128]{1,0:T(8,128)(2,1)S(1)}, u32[]{:S(2)}, u32[]{:S(2)}) collective-permute-start(bf16[192,128]{1,0:T(8,128)(2,1)S(1)} %get-tuple-element.24), channel_id=1, source_target_pairs={{0,1},{1,0},{2,3},{3,2},{4,5},{5,4},{6,7},{7,6},{8,9},{9,8},{10,11... | collective-permute-start | bytes 147464 | tf_op jit(solution)/shard_map/ppermute | solution.py:423

commit v17 on v14

--- a/solution.py
+++ b/solution.py
@@ -22,9 +22,13 @@
     return lax.dot_general(rows, block, (((1,), (1,)), ((), ())), preferred_element_type=jnp.float32)
 
 
-def injected(table, step, first_state, width):
+def hits(table, i, blocks, width):
+    first_state = (lax.axis_index("net") * blocks + i) * width
     lane = lax.broadcasted_iota(jnp.int32, (table.shape[0], width), 1)
-    hit = table[:, STATE : STATE + 1] == (lane + first_state).astype(jnp.float32)
+    return table[:, STATE : STATE + 1] == (lane + first_state).astype(jnp.float32)
+
+
+def injected(table, step, hit):
     return jnp.where(hit, table[:, GAIN + step : GAIN + step + 1], 0.0)
 
 
@@ -32,14 +36,15 @@
     return lambda i, k: state_ref[cols_ref[k, i]]
 
 
-def own_sum(i, state_ref, jac_ref, near, table, step):
+def own_sum(i, state_ref, jac_ref, near, table, step, hit=None):
     blocks, _, width = state_ref.shape
-    first = (lax.axis_index("net") * blocks + i) * width
+    if hit is None:
+        hit = hits(table, i, blocks, width)
     kinds = jac_ref.shape[1]
     rows = [state_ref[i]] + [near(i, k) for k in range(kinds - 1)]
     row_blocks = [jac_ref[i, k] for k in range(kinds)]
     total = times_transposed(jnp.concatenate(rows, axis=1), jnp.concatenate(row_blocks, axis=1))
-    return total + injected(table, step, first, width)
+    return total + injected(table, step, hit)
 
 
 def picked(blocks, marks):
@@ -108,22 +113,23 @@
     jac_ref, iface_ref, *loaded, first_ref, sems = refs
     cols_ref, send_ref, recv_ref, live_ref, node_ref, gain_ref = loaded
     blocks, cols, width = state_ref.shape
+    sources = [jac_hbm.at[1], iface_hbm.at[1, 0], *small]
     loads = [
         pltpu.make_async_copy(source, target, sems.at[i])
-        for i, (source, target) in enumerate(
-            zip([jac_hbm.at[1], iface_hbm.at[1, 0], *small], [jac_ref, iface_ref, *loaded])
-        )
+        for i, (source, target) in enumerate(zip(sources, [jac_ref, iface_ref, *loaded]))
     ]
     here = lax.axis_index("tm") == 0
+    for load in loads[6:]:
+        load.start()
 
     @pl.when(here)
     def _():
         for load in loads[:2]:
             load.start()
 
-    for load in loads[2:]:
+    for load in loads[2:6]:
         load.start()
-    for load in loads[2:]:
+    for load in loads[6:]:
         load.wait()
     node = node_ref[...]
     block_of = node // width
@@ -141,11 +147,14 @@
     @pl.when(here)
     def _():
         table = table_ref[...]
+        hit = [hits(table, i, blocks, width) for i in range(blocks)]
         for i in range(blocks):
-            first_ref[i] = injected(table, 0, (me * blocks + i) * width, width).astype(first_ref.dtype)
+            first_ref[i] = injected(table, 0, hit[i]).astype(first_ref.dtype)
         lane = lax.broadcasted_iota(jnp.int32, (cols, width), 1).astype(jnp.float32)
         shot = jnp.where(lane == table[:, LANE : LANE + 1], table[:, GAIN : GAIN + 1], 0.0)
         away, block = table[:, AWAY : AWAY + 1], table[:, BLOCK : BLOCK + 1]
+        for load in loads[2:6]:
+            load.wait()
         mine = jnp.logical_or(away != 0.0, block == send_ref[0, me].astype(jnp.float32))
         shot = jnp.where(mine, shot, 0.0)
         live = recv = jnp.zeros_like(away)
@@ -159,13 +168,15 @@
         coupled = jnp.where(lane < live, coupled, 0.0)
         loads[0].wait()
         for i in range(blocks):
-            own = own_sum(i, first_ref, jac_ref, near_by(first_ref, cols_ref), table, 1)
+            own = own_sum(i, first_ref, jac_ref, near_by(first_ref, cols_ref), table, 1, hit[i])
             state_ref[i] = (own + jnp.where(recv == float(i), coupled, 0.0)).astype(state_ref.dtype)
         for d in range(1, n):
             outgoing[d - 1][pl.ds(0, cols)] = state_ref[send_ref[0, me ^ d]]
 
     @pl.when(jnp.logical_not(here))
     def _():
+        for load in loads[2:6]:
+            load.wait()
         make_marks(marks_ref, blocks, jac_ref.shape[1], cols_ref, send_ref, recv_ref, live_ref)
 
     for d in range(1, n):
@@ -186,10 +197,26 @@
     return copies
 
 
-def own_kernel(step, state_ref, jac_ref, cols_ref, table_ref, z_ref):
+def own_kernel(step, state_ref, jac_ref, iface_ref, table_ref, marks_ref, z_ref):
     table = table_ref[...]
-    for i in range(state_ref.shape[0]):
-        z_ref[i] = own_sum(i, state_ref, jac_ref.at[step], near_by(state_ref, cols_ref), table, step)
+    n = lax.axis_size("net")
+    blocks = state_ref.shape[0]
+    kinds = jac_ref.shape[2]
+    sent, near, _, _ = marks_layout(n, blocks, kinds)
+    state = [state_ref[j] for j in range(blocks)]
+
+    def pick(row):
+        return picked(state, [marks_ref[pl.ds(row + j, 1)].astype(state_ref.dtype) for j in range(blocks)])
+
+    def near_block(i, k):
+        return pick(near + (i * (kinds - 1) + k) * blocks)
+
+    @pl.when(lax.axis_index("tm") > 0)
+    def _():
+        term = times_transposed(pick(sent), iface_ref[step, 0, lax.axis_index("net")])
+        for i in range(blocks):
+            own = own_sum(i, state_ref, jac_ref.at[step], near_block, table, step)
+            z_ref[i] = own + term * marks_ref[pl.ds(i, 1)]
 
 
 def first_states(opening, handed, jac_ref, iface_ref, ints, table_ref, made_ref, z_ref):
@@ -211,22 +238,17 @@
     return [made_ref.at[0], made_ref.at[1]]
 
 
-def joined(sums, step, iface_ref, marks_ref, state_ref, arrived, keep=None):
-    n = lax.axis_size("net")
+def joined(sums, step, iface_ref, marks_ref, arrived, keep=None):
     me = lax.axis_index("net")
-    blocks, cols, _ = state_ref.shape
-    sent = marks_layout(n, blocks, 1)[0]
-    for d in range(n):
-        if d:
-            block = arrived[d - 1][pl.ds(0, cols)]
-        else:
-            marks = [marks_ref[pl.ds(sent + j, 1)].astype(state_ref.dtype) for j in range(blocks)]
-            block = picked([state_ref[j] for j in range(blocks)], marks)
-        term = times_transposed(block, iface_ref[step, 0, me ^ d])
+    blocks, cols = len(sums), sums[0].shape[0]
+    if keep is not None:
+        sums = [total * keep[:, 0:1] for total in sums]
+    for d, block in enumerate(arrived, 1):
+        term = times_transposed(block[pl.ds(0, cols)], iface_ref[step, 0, me ^ d])
         if keep is not None:
             term *= keep[:, d : d + 1]
         sums = [total + term * marks_ref[pl.ds(d * blocks + i, 1)] for i, total in enumerate(sums)]
-    return [total.astype(state_ref.dtype) for total in sums]
+    return [total.astype(jnp.bfloat16) for total in sums]
 
 
 def give(made, marks_ref, state_ref, outgoing):
@@ -240,35 +262,19 @@
         outgoing[d - 1][...] = picked(made, marks)
 
 
-def join_kernel(step, fix, section, *refs):
-    n = lax.axis_size("net")
-    first_ref, iface_ref, table_ref, marks_ref, *refs = refs
-    arrived, state_in_ref, state_ref, outgoing = refs[: n - 1][::-1], refs[n - 1], refs[n], refs[n + 1 :]
-    blocks, cols, _ = state_in_ref.shape
+def join_kernel(step, fix, section, z_ref, iface_ref, table_ref, marks_ref, *refs):
+    n = lax.axis_size("net")
+    arrived, state_ref, outgoing = refs[: n - 1][::-1], refs[n - 1], refs[n:]
+    blocks, cols, _ = z_ref.shape
 
     @pl.when(lax.axis_index("tm") == section)
     def _():
         keep = None
         if fix:
-            kinds = first_ref.shape[2]
-            table = table_ref[...]
-            _, near, own_row, _ = marks_layout(n, blocks, kinds)
-            state = [state_in_ref[j] for j in range(blocks)]
-
-            def near_block(i, k):
-                rows = [near + (i * (kinds - 1) + k) * blocks + j for j in range(blocks)]
-                return picked(state, [marks_ref[pl.ds(row, 1)].astype(state_ref.dtype) for row in rows])
-
-            rows = [marks_ref[pl.ds(own_row, 1)]]
+            rows = [marks_ref[pl.ds(marks_layout(n, blocks, fix)[2], 1)]]
             rows += [block[cols : cols + 1].astype(jnp.float32) for block in arrived]
-            keep = kept(table, rows)
-            sums = [
-                own_sum(i, state_in_ref, first_ref.at[step], near_block, table, step) * keep[:, 0:1]
-                for i in range(blocks)
-            ]
-        else:
-            sums = [first_ref[i] for i in range(blocks)]
-        made = joined(sums, step, iface_ref, marks_ref, state_in_ref, arrived, keep)
+            keep = kept(table_ref[...], rows)
+        made = joined([z_ref[i] for i in range(blocks)], step, iface_ref, marks_ref, arrived, keep)
         give(made, marks_ref, state_ref, outgoing)
 
 
@@ -279,7 +285,7 @@
         *refs, made_ref, acc_ref, cols_ref, send_ref, recv_ref, live_ref, load_sems = refs
         ints = [cols_ref, send_ref, recv_ref, live_ref]
     z_ref, iface_ref, table_ref, marks_ref, *refs = refs
-    arrived, state_in_ref, refs = refs[: n - 1][::-1], refs[n - 1], refs[n:]
+    arrived, refs = refs[: n - 1][::-1], refs[n - 1 :]
     before, refs = refs[:before], refs[before:]
     if firsts:
         opening_ref, handed, jac_ref, sources, refs = refs[0], refs[1:n], refs[n], refs[n + 1 : n + 5], refs[n + 5 :]
@@ -291,7 +297,7 @@
     def _():
         copies = write_start(before, 0, out_ref, sems)
         sums = [z_ref[i] for i in range(z_ref.shape[0])]
-        made = joined(sums, step, iface_ref, marks_ref, state_in_ref, arrived)
+        made = joined(sums, step, iface_ref, marks_ref, arrived)
         give(made, marks_ref, state_ref, outgoing)
         copies += write_start([state_ref], len(before), out_ref, sems)
         for copy in copies:
@@ -354,23 +360,23 @@
         return pl.pallas_call(
             functools.partial(own_kernel, step),
             out_shape=f32(whole.shape),
-            in_specs=[VMEM, VMEM, SMEM, VMEM],
+            in_specs=[VMEM] * 5,
             out_specs=VMEM,
             compiler_params=LIMIT,
-        )(state, jac, near, table)
-
-    def join(first, step, fix, state, arrived, section):
+        )(state, jac, iface_jac, table, marks)
+
+    def join(z, step, fix, arrived, section):
         return pl.pallas_call(
-            functools.partial(join_kernel, step, fix, section),
+            functools.partial(join_kernel, step, kinds if fix else 0, section),
             out_shape=[whole] + [one] * (n - 1),
-            in_specs=[VMEM] * (n + 4),
+            in_specs=[VMEM] * (n + 3),
             out_specs=[VMEM] * n,
             compiler_params=LIMIT,
-        )(first, iface_jac, table, marks, *arrived[::-1], state)
-
-    def close(z, step, state, arrived, section, before, out, send):
+        )(z, iface_jac, table, marks, *arrived[::-1])
+
+    def close(z, step, arrived, section, before, out, send):
         firsts = out is None
-        arrays = [z, iface_jac, table, marks, *arrived[::-1], state, *before]
+        arrays = [z, iface_jac, table, marks, *arrived[::-1], *before]
         specs = [VMEM] * len(arrays)
         scratch = [DMA((steps, blocks))]
         aliases = {}
@@ -428,12 +434,12 @@
             fix = r == 1 and s == 0
             if s > 0:
                 arrived = exchange(outgoing, r, r)
-            first = jac if fix else own(state, s)
+            z = own(state, s)
             if s < steps - 1:
-                state, *outgoing = join(first, s, fix, state, arrived, r)
+                state, *outgoing = join(z, s, fix, arrived, r)
                 before.append(state)
             else:
-                out, *rest = close(first, s, state, arrived, r, before, out, r < tm - 1)
+                out, *rest = close(z, s, arrived, r, before, out, r < tm - 1)
                 state, *outgoing = rest or [None]
     return out
 

time: 22.4 us -> 22.3 us (level)
  waiting for transfers between devices: 7.13 us -> 7.38 us
  Pallas kernels: 3.73 us -> 3.49 us
    ppermute x7, waiting for transfers between devices: 7.13 us -> 7.38 us  [swap(): return lax.ppermute(block, ('tm', 'net', 'cols'), pairs)]
    pallas_call x1 -> x2, Pallas kernels: 0.88 us -> 0.9 us  [own(): pl.pallas_call(functools.partial(own_kernel, step), out_shape=f32(whole.s...]
where the time goes in v17:
time: 22.3 us; the launch traced here: 22.2 us
  starting transfers between devices  11.3 us (51%)
  waiting for transfers between devices  7.38 us (33%)
  Pallas kernels  3.49 us (16%)
    ppermute x7, starting transfers between devices, swap(): return lax.ppermute(block, ('tm', 'net', 'cols'), pairs)  11.3 us
    ppermute x7, waiting for transfers between devices, swap(): return lax.ppermute(block, ('tm', 'net', 'cols'), pairs)  7.38 us
    pallas_call x1, Pallas kernels, local(): pl.pallas_call(second_kernel, out_shape=[f32((cols, table_rows)), f32((ma...  1.11 us
    pallas_call x1, Pallas kernels, close(): pl.pallas_call(functools.partial(close_kernel, step, section, firsts, sen...  1.03 us
    pallas_call x2, Pallas kernels, own(): pl.pallas_call(functools.partial(own_kernel, step), out_shape=f32(whole.s...  0.9 us
  transfers between devices with their start and end apart: 7, of which 4 were waited for; matrix products, arithmetic and copies ran while one was open for 0% of the time, Pallas kernels for 4%

profile of v17, /device:TPU:4, one launch (start us, length us, event | category | flops | bytes accessed | tf_op | source)
XLA Modules:
  0.0 22.2 jit_solution(9357595333407102185)
XLA Ops:
  0.0 0.0 copy-start
  0.0 0.0 copy-start.1
  0.0 1.1 %shard_map.82 = (f32[192,8]{1,0:T(8,128)S(1)}, f32[72,128]{1,0:T(8,128)S(1)}, bf16[4,192,128]{2,1,0:T(8,128)(2,1)S(1)}, bf16[208,128]{1,0:T(8,128)(2,1)S(1)}, bf...) custom-call(bf16[2,4,3,128,128]{4,3,2,1,0:T(8,128)(2,1)} %refs_12_.1, bf16[2,1,4,128,128]{4,3,2,1,0:T(8,128)(2,1)} %refs_1_.3, ...), custom_call_target="tpu_custom_call" | custom-call | tf_op jit(solution)/shard_map/pallas_call | solution.py:342
  1.1 0.1 collective-permute-start
  1.2 5.0 %collective-permute-start.1 = (bf16[208,128]{1,0:T(8,128)(2,1)S(1)}, bf16[208,128]{1,0:T(8,128)(2,1)S(1)}, u32[]{:S(2)}, u32[]{:S(2)}) collective-permute-start(bf16[208,128]{1,0:T(8,128)(2,1)S(1)} %get-tuple-element.18), channel_id=1, source_target_pairs={{0,28},{1,29},{2,30},{3,31},{4,24},{5,25},{6,26},{7,27},{8,20},{9,... | collective-permute-start | bytes 159752 | tf_op jit(solution)/shard_map/ppermute | solution.py:420
  6.3 0.3 %collective-permute-start.2 = (bf16[208,128]{1,0:T(8,128)(2,1)S(1)}, bf16[208,128]{1,0:T(8,128)(2,1)S(1)}, u32[]{:S(2)}, u32[]{:S(2)}) collective-permute-start(bf16[208,128]{1,0:T(8,128)(2,1)S(1)} %get-tuple-element.19), channel_id=1, source_target_pairs={{0,24},{1,25},{2,26},{3,27},{4,28},{5,29},{6,30},{7,31},{8,16},{9,... | collective-permute-start | bytes 159752 | tf_op jit(solution)/shard_map/ppermute | solution.py:420
  6.6 1.3 %collective-permute-start.3 = (bf16[208,128]{1,0:T(8,128)(2,1)S(1)}, bf16[208,128]{1,0:T(8,128)(2,1)S(1)}, u32[]{:S(2)}, u32[]{:S(2)}) collective-permute-start(bf16[208,128]{1,0:T(8,128)(2,1)S(1)} %get-tuple-element.20), channel_id=1, source_target_pairs={{0,20},{1,21},{2,22},{3,23},{4,16},{5,17},{6,18},{7,19},{8,28},{9,... | collective-permute-start | bytes 159752 | tf_op jit(solution)/shard_map/ppermute | solution.py:420
  7.9 1.0 %collective-permute-done.state_ref = bf16[4,192,128]{2,1,0:T(8,128)(2,1)S(1)} collective-permute-done((bf16[4,192,128]{2,1,0:T(8,128)(2,1)S(1)}, bf16[4,192,128]{2,1,0:T(8,128)(2,1)S(1)}, u32[]{:S(2)}, u32[]{:S(2)}) %collective-permute-start) | collective-permute-done | bytes 196640 | tf_op jit(solution)/shard_map/ppermute | solution.py:420
  9.0 0.0 copy-done
  9.0 0.0 copy-done.1
  9.0 0.5 %shard_map.83.z_ref = f32[4,192,128]{2,1,0:T(8,128)S(1)} custom-call(bf16[4,192,128]{2,1,0:T(8,128)(2,1)S(1)} %collective-permute-done.state_ref, bf16[2,4,3,128,128]{4,3,2,1,0:T(8,128)(2,1)S(1)} %copy-done, bf16[2,1,4,128,128]{4,3,2,1,0:T(8,128)(2,1)S(1)} %copy-done.1, f32[192,8]{1,0:T(8,128)S(1)} %get-tuple-element.16.table_ref.refs_2_, ...), custom_call_target="tpu_custom_call" | custom-call | tf_op jit(solution)/shard_map/pallas_call | solution.py:360
  9.4 0.0 collective-permute-done.1.refs_0_.refs_11_
  9.4 2.8 %collective-permute-done.2.refs_1_.refs_10_ = bf16[208,128]{1,0:T(8,128)(2,1)S(1)} collective-permute-done((bf16[208,128]{1,0:T(8,128)(2,1)S(1)}, bf16[208,128]{1,0:T(8,128)(2,1)S(1)}, u32[]{:S(2)}, u32[]{:S(2)}) %collective-permute-start.2) | collective-permute-done | bytes 53280 | tf_op jit(solution)/shard_map/ppermute | solution.py:420
  12.2 0.0 collective-permute-done.3.refs_2_.refs_9_
  12.2 0.4 %shard_map.84 = (bf16[4,192,128]{2,1,0:T(8,128)(2,1)S(1)}, bf16[192,128]{1,0:T(8,128)(2,1)S(1)}, bf16[192,128]{1,0:T(8,128)(2,1)S(1)}, bf16[192,128]{1,0:T(8,128)(2,1)S(1)}) custom-call(f32[4,192,128]{2,1,0:T(8,128)S(1)} %shard_map.83.z_ref, bf16[2,1,4,128,128]{4,3,2,1,0:T(8,128)(2,1)S(1)} %copy-done.1, f32[192,8]{1,0:T(8,128)S(1)} %get-tuple-element.16.table_ref.refs_2_, ...), custom_call_target="tpu_custom_call" | custom-call | tf_op jit(solution)/shard_map/pallas_call | solution.py:369
  12.7 3.2 %collective-permute-start.4 = (bf16[192,128]{1,0:T(8,128)(2,1)S(1)}, bf16[192,128]{1,0:T(8,128)(2,1)S(1)}, u32[]{:S(2)}, u32[]{:S(2)}) collective-permute-start(bf16[192,128]{1,0:T(8,128)(2,1)S(1)} %get-tuple-element.22), channel_id=1, source_target_pairs={{0,1},{1,0},{2,3},{3,2},{4,5},{5,4},{6,7},{7,6},{8,9},{9,8},{10,11... | collective-permute-start | bytes 147464 | tf_op jit(solution)/shard_map/ppermute | solution.py:420
  15.9 0.0 collective-permute-start.5
  15.9 1.2 %collective-permute-start.6 = (bf16[192,128]{1,0:T(8,128)(2,1)S(1)}, bf16[192,128]{1,0:T(8,128)(2,1)S(1)}, u32[]{:S(2)}, u32[]{:S(2)}) collective-permute-start(bf16[192,128]{1,0:T(8,128)(2,1)S(1)} %get-tuple-element.24), channel_id=1, source_target_pairs={{0,1},{1,0},{2,3},{3,2},{4,5},{5,4},{6,7},{7,6},{8,9},{9,8},{10,11... | collective-permute-start | bytes 147464 | tf_op jit(solution)/shard_map/ppermute | solution.py:420
  17.1 0.4 %shard_map.85.refs_0_ = f32[4,192,128]{2,1,0:T(8,128)S(1)} custom-call(bf16[4,192,128]{2,1,0:T(8,128)(2,1)S(1)} %get-tuple-element.21.state_ref.refs_7_, bf16[2,4,3,128,128]{4,3,2,1,0:T(8,128)(2,1)S(1)} %copy-done, bf16[2,1,4,128,128]{4,3,2,1,0:T(8,128)(2,1)S(1)} %copy-done.1, f32[192,8]{1,0:T(8,128)S(1)} %get-tuple-element.16.table_ref.refs_2_, ...), custom_call_target="tpu_custom_call" | custom-call | tf_op jit(solution)/shard_map/pallas_call | solution.py:360
  17.6 1.2 %collective-permute-done.4.refs_4_ = bf16[192,128]{1,0:T(8,128)(2,1)S(1)} collective-permute-done((bf16[192,128]{1,0:T(8,128)(2,1)S(1)}, bf16[192,128]{1,0:T(8,128)(2,1)S(1)}, u32[]{:S(2)}, u32[]{:S(2)}) %collective-permute-start.4) | collective-permute-done | bytes 49184 | tf_op jit(solution)/shard_map/ppermute | solution.py:420
  18.8 2.3 %collective-permute-done.5.refs_5_ = bf16[192,128]{1,0:T(8,128)(2,1)S(1)} collective-permute-done((bf16[192,128]{1,0:T(8,128)(2,1)S(1)}, bf16[192,128]{1,0:T(8,128)(2,1)S(1)}, u32[]{:S(2)}, u32[]{:S(2)}) %collective-permute-start.5) | collective-permute-done | bytes 49184 | tf_op jit(solution)/shard_map/ppermute | solution.py:420
  21.2 0.0 collective-permute-done.6.refs_6_
  21.2 1.0 %shard_map.86 = bf16[2,192,512]{2,1,0:T(8,128)(2,1)} custom-call(f32[4,192,128]{2,1,0:T(8,128)S(1)} %shard_map.85.refs_0_, bf16[2,1,4,128,128]{4,3,2,1,0:T(8,128)(2,1)S(1)} %copy-done.1, f32[192,8]{1,0:T(8,128)S(1)} %get-tuple-element.16.table_ref.refs_2_, f32[72,128]{1,0:T(8,128)S(1)} %get-tuple-element.17.marks_ref.refs_3_, ...), custom_call_target="tpu_custom_call" | custom-call | tf_op jit(solution)/shard_map/pallas_call | solution.py:402
Async XLA Ops:
  0.0 9.0 %copy-start = (bf16[2,4,3,128,128]{4,3,2,1,0:T(8,128)(2,1)S(1)}, bf16[2,4,3,128,128]{4,3,2,1,0:T(8,128)(2,1)}, u32[]{:S(2)}) copy-start(bf16[2,4,3,128,128]{4,3,2,1,0:T(8,128)(2,1)} %refs_12_.1) | copy-start | bytes 2359300
  0.0 9.0 %copy-start.1 = (bf16[2,1,4,128,128]{4,3,2,1,0:T(8,128)(2,1)S(1)}, bf16[2,1,4,128,128]{4,3,2,1,0:T(8,128)(2,1)}, u32[]{:S(2)}) copy-start(bf16[2,1,4,128,128]{4,3,2,1,0:T(8,128)(2,1)} %refs_1_.3) | copy-start | bytes 786436
  1.1 7.8 %collective-permute-start = (bf16[4,192,128]{2,1,0:T(8,128)(2,1)S(1)}, bf16[4,192,128]{2,1,0:T(8,128)(2,1)S(1)}, u32[]{:S(2)}, u32[]{:S(2)}) collective-permute-start(bf16[4,192,128]{2,1,0:T(8,128)(2,1)S(1)} %get-tuple-element.15.refs_8_), channel_id=1, source_target_pairs={{0,16},{1,17},{2,18},{3,19},{4,20},{5,21},{6,22},{7,23},{8,24},{9,... | collective-permute-start | bytes 589832 | tf_op jit(solution)/shard_map/ppermute | solution.py:420
  1.2 8.2 %collective-permute-start.1 = (bf16[208,128]{1,0:T(8,128)(2,1)S(1)}, bf16[208,128]{1,0:T(8,128)(2,1)S(1)}, u32[]{:S(2)}, u32[]{:S(2)}) collective-permute-start(bf16[208,128]{1,0:T(8,128)(2,1)S(1)} %get-tuple-element.18), channel_id=1, source_target_pairs={{0,28},{1,29},{2,30},{3,31},{4,24},{5,25},{6,26},{7,27},{8,20},{9,... | collective-permute-start | bytes 159752 | tf_op jit(solution)/shard_map/ppermute | solution.py:420
  6.3 5.9 %collective-permute-start.2 = (bf16[208,128]{1,0:T(8,128)(2,1)S(1)}, bf16[208,128]{1,0:T(8,128)(2,1)S(1)}, u32[]{:S(2)}, u32[]{:S(2)}) collective-permute-start(bf16[208,128]{1,0:T(8,128)(2,1)S(1)} %get-tuple-element.19), channel_id=1, source_target_pairs={{0,24},{1,25},{2,26},{3,27},{4,28},{5,29},{6,30},{7,31},{8,16},{9,... | collective-permute-start | bytes 159752 | tf_op jit(solution)/shard_map/ppermute | solution.py:420
  6.6 5.6 %collective-permute-start.3 = (bf16[208,128]{1,0:T(8,128)(2,1)S(1)}, bf16[208,128]{1,0:T(8,128)(2,1)S(1)}, u32[]{:S(2)}, u32[]{:S(2)}) collective-permute-start(bf16[208,128]{1,0:T(8,128)(2,1)S(1)} %get-tuple-element.20), channel_id=1, source_target_pairs={{0,20},{1,21},{2,22},{3,23},{4,16},{5,17},{6,18},{7,19},{8,28},{9,... | collective-permute-start | bytes 159752 | tf_op jit(solution)/shard_map/ppermute | solution.py:420
  12.7 6.2 %collective-permute-start.4 = (bf16[192,128]{1,0:T(8,128)(2,1)S(1)}, bf16[192,128]{1,0:T(8,128)(2,1)S(1)}, u32[]{:S(2)}, u32[]{:S(2)}) collective-permute-start(bf16[192,128]{1,0:T(8,128)(2,1)S(1)} %get-tuple-element.22), channel_id=1, source_target_pairs={{0,1},{1,0},{2,3},{3,2},{4,5},{5,4},{6,7},{7,6},{8,9},{9,8},{10,11... | collective-permute-start | bytes 147464 | tf_op jit(solution)/shard_map/ppermute | solution.py:420
  15.9 5.3 %collective-permute-start.5 = (bf16[192,128]{1,0:T(8,128)(2,1)S(1)}, bf16[192,128]{1,0:T(8,128)(2,1)S(1)}, u32[]{:S(2)}, u32[]{:S(2)}) collective-permute-start(bf16[192,128]{1,0:T(8,128)(2,1)S(1)} %get-tuple-element.23), channel_id=1, source_target_pairs={{0,1},{1,0},{2,3},{3,2},{4,5},{5,4},{6,7},{7,6},{8,9},{9,8},{10,11... | collective-permute-start | bytes 147464 | tf_op jit(solution)/shard_map/ppermute | solution.py:420
  15.9 5.3 %collective-permute-start.6 = (bf16[192,128]{1,0:T(8,128)(2,1)S(1)}, bf16[192,128]{1,0:T(8,128)(2,1)S(1)}, u32[]{:S(2)}, u32[]{:S(2)}) collective-permute-start(bf16[192,128]{1,0:T(8,128)(2,1)S(1)} %get-tuple-element.24), channel_id=1, source_target_pairs={{0,1},{1,0},{2,3},{3,2},{4,5},{5,4},{6,7},{7,6},{8,9},{9,8},{10,11... | collective-permute-start | bytes 147464 | tf_op jit(solution)/shard_map/ppermute | solution.py:420

commit v18 on v17

--- a/solution.py
+++ b/solution.py
@@ -262,9 +262,18 @@
         outgoing[d - 1][...] = picked(made, marks)
 
 
+def exchange_order(n, handed):
+    return list(range(n - 1, 0, -1)) if handed else [*range(n // 2, n), *range(n // 2 - 1, 0, -1)]
+
+
+def by_distance(refs, handed):
+    order = exchange_order(len(refs) + 1, handed)
+    return [refs[order.index(d)] for d in range(1, len(refs) + 1)]
+
+
 def join_kernel(step, fix, section, z_ref, iface_ref, table_ref, marks_ref, *refs):
     n = lax.axis_size("net")
-    arrived, state_ref, outgoing = refs[: n - 1][::-1], refs[n - 1], refs[n:]
+    arrived, state_ref, outgoing = by_distance(refs[: n - 1], step == 0), refs[n - 1], refs[n:]
     blocks, cols, _ = z_ref.shape
 
     @pl.when(lax.axis_index("tm") == section)
@@ -285,7 +294,7 @@
         *refs, made_ref, acc_ref, cols_ref, send_ref, recv_ref, live_ref, load_sems = refs
         ints = [cols_ref, send_ref, recv_ref, live_ref]
     z_ref, iface_ref, table_ref, marks_ref, *refs = refs
-    arrived, refs = refs[: n - 1][::-1], refs[n - 1 :]
+    arrived, refs = by_distance(refs[: n - 1], False), refs[n - 1 :]
     before, refs = refs[:before], refs[before:]
     if firsts:
         opening_ref, handed, jac_ref, sources, refs = refs[0], refs[1:n], refs[n], refs[n + 1 : n + 5], refs[n + 5 :]
@@ -372,11 +381,11 @@
             in_specs=[VMEM] * (n + 3),
             out_specs=[VMEM] * n,
             compiler_params=LIMIT,
-        )(z, iface_jac, table, marks, *arrived[::-1])
+        )(z, iface_jac, table, marks, *[arrived[d - 1] for d in exchange_order(n, step == 0)])
 
     def close(z, step, arrived, section, before, out, send):
         firsts = out is None
-        arrays = [z, iface_jac, table, marks, *arrived[::-1], *before]
+        arrays = [z, iface_jac, table, marks, *[arrived[d - 1] for d in exchange_order(n, False)], *before]
         specs = [VMEM] * len(arrays)
         scratch = [DMA((steps, blocks))]
         aliases = {}

time: 22.3 us -> 22.7 us (1.018)
  waiting for transfers between devices: 7.38 us -> 8.41 us
  starting transfers between devices: 11.3 us -> 10.6 us
    ppermute x7, waiting for transfers between devices: 7.38 us -> 8.41 us  [swap(): return lax.ppermute(block, ('tm', 'net', 'cols'), pairs)]
    ppermute x7, starting transfers between devices: 11.3 us -> 10.6 us  [swap(): return lax.ppermute(block, ('tm', 'net', 'cols'), pairs)]
where the time goes in v18:
time: 22.7 us; the launch traced here: 22.6 us
  starting transfers between devices  10.6 us (47%)
  waiting for transfers between devices  8.41 us (37%)
  Pallas kernels  3.49 us (15%)
    ppermute x7, starting transfers between devices, swap(): return lax.ppermute(block, ('tm', 'net', 'cols'), pairs)  10.6 us
    ppermute x7, waiting for transfers between devices, swap(): return lax.ppermute(block, ('tm', 'net', 'cols'), pairs)  8.41 us
    pallas_call x1, Pallas kernels, local(): pl.pallas_call(second_kernel, out_shape=[f32((cols, table_rows)), f32((ma...  1.11 us
    pallas_call x1, Pallas kernels, close(): pl.pallas_call(functools.partial(close_kernel, step, section, firsts, sen...  1.03 us
    pallas_call x2, Pallas kernels, own(): pl.pallas_call(functools.partial(own_kernel, step), out_shape=f32(whole.s...  0.9 us
  transfers between devices with their start and end apart: 7, of which 4 were waited for; matrix products, arithmetic and copies ran while one was open for 0% of the time, Pallas kernels for 4%

profile of v18, /device:TPU:4, one launch (start us, length us, event | category | flops | bytes accessed | tf_op | source)
XLA Modules:
  0.0 22.6 jit_solution(16023546178989953071)
XLA Ops:
  0.0 0.0 copy-start
  0.0 0.0 copy-start.1
  0.0 1.1 %shard_map.82 = (f32[192,8]{1,0:T(8,128)S(1)}, f32[72,128]{1,0:T(8,128)S(1)}, bf16[4,192,128]{2,1,0:T(8,128)(2,1)S(1)}, bf16[208,128]{1,0:T(8,128)(2,1)S(1)}, bf...) custom-call(bf16[2,4,3,128,128]{4,3,2,1,0:T(8,128)(2,1)} %refs_12_.1, bf16[2,1,4,128,128]{4,3,2,1,0:T(8,128)(2,1)} %refs_1_.3, ...), custom_call_target="tpu_custom_call" | custom-call | tf_op jit(solution)/shard_map/pallas_call | solution.py:351
  1.1 0.1 collective-permute-start
  1.2 5.0 %collective-permute-start.1 = (bf16[208,128]{1,0:T(8,128)(2,1)S(1)}, bf16[208,128]{1,0:T(8,128)(2,1)S(1)}, u32[]{:S(2)}, u32[]{:S(2)}) collective-permute-start(bf16[208,128]{1,0:T(8,128)(2,1)S(1)} %get-tuple-element.18), channel_id=1, source_target_pairs={{0,28},{1,29},{2,30},{3,31},{4,24},{5,25},{6,26},{7,27},{8,20},{9,... | collective-permute-start | bytes 159752 | tf_op jit(solution)/shard_map/ppermute | solution.py:429
  6.3 0.3 %collective-permute-start.2 = (bf16[208,128]{1,0:T(8,128)(2,1)S(1)}, bf16[208,128]{1,0:T(8,128)(2,1)S(1)}, u32[]{:S(2)}, u32[]{:S(2)}) collective-permute-start(bf16[208,128]{1,0:T(8,128)(2,1)S(1)} %get-tuple-element.19), channel_id=1, source_target_pairs={{0,24},{1,25},{2,26},{3,27},{4,28},{5,29},{6,30},{7,31},{8,16},{9,... | collective-permute-start | bytes 159752 | tf_op jit(solution)/shard_map/ppermute | solution.py:429
  6.6 1.3 %collective-permute-start.3 = (bf16[208,128]{1,0:T(8,128)(2,1)S(1)}, bf16[208,128]{1,0:T(8,128)(2,1)S(1)}, u32[]{:S(2)}, u32[]{:S(2)}) collective-permute-start(bf16[208,128]{1,0:T(8,128)(2,1)S(1)} %get-tuple-element.20), channel_id=1, source_target_pairs={{0,20},{1,21},{2,22},{3,23},{4,16},{5,17},{6,18},{7,19},{8,28},{9,... | collective-permute-start | bytes 159752 | tf_op jit(solution)/shard_map/ppermute | solution.py:429
  7.9 1.0 %collective-permute-done.state_ref = bf16[4,192,128]{2,1,0:T(8,128)(2,1)S(1)} collective-permute-done((bf16[4,192,128]{2,1,0:T(8,128)(2,1)S(1)}, bf16[4,192,128]{2,1,0:T(8,128)(2,1)S(1)}, u32[]{:S(2)}, u32[]{:S(2)}) %collective-permute-start) | collective-permute-done | bytes 196640 | tf_op jit(solution)/shard_map/ppermute | solution.py:429
  9.0 0.0 copy-done
  9.0 0.0 copy-done.1
  9.0 0.5 %shard_map.83.z_ref = f32[4,192,128]{2,1,0:T(8,128)S(1)} custom-call(bf16[4,192,128]{2,1,0:T(8,128)(2,1)S(1)} %collective-permute-done.state_ref, bf16[2,4,3,128,128]{4,3,2,1,0:T(8,128)(2,1)S(1)} %copy-done, bf16[2,1,4,128,128]{4,3,2,1,0:T(8,128)(2,1)S(1)} %copy-done.1, f32[192,8]{1,0:T(8,128)S(1)} %get-tuple-element.16.table_ref.refs_2_, ...), custom_call_target="tpu_custom_call" | custom-call | tf_op jit(solution)/shard_map/pallas_call | solution.py:369
  9.4 0.0 collective-permute-done.1.refs_0_.refs_11_
  9.4 2.8 %collective-permute-done.2.refs_1_.refs_10_ = bf16[208,128]{1,0:T(8,128)(2,1)S(1)} collective-permute-done((bf16[208,128]{1,0:T(8,128)(2,1)S(1)}, bf16[208,128]{1,0:T(8,128)(2,1)S(1)}, u32[]{:S(2)}, u32[]{:S(2)}) %collective-permute-start.2) | collective-permute-done | bytes 53280 | tf_op jit(solution)/shard_map/ppermute | solution.py:429
  12.2 0.0 collective-permute-done.3.refs_2_.refs_9_
  12.2 0.4 %shard_map.84 = (bf16[4,192,128]{2,1,0:T(8,128)(2,1)S(1)}, bf16[192,128]{1,0:T(8,128)(2,1)S(1)}, bf16[192,128]{1,0:T(8,128)(2,1)S(1)}, bf16[192,128]{1,0:T(8,128)(2,1)S(1)}) custom-call(f32[4,192,128]{2,1,0:T(8,128)S(1)} %shard_map.83.z_ref, bf16[2,1,4,128,128]{4,3,2,1,0:T(8,128)(2,1)S(1)} %copy-done.1, f32[192,8]{1,0:T(8,128)S(1)} %get-tuple-element.16.table_ref.refs_2_, ...), custom_call_target="tpu_custom_call" | custom-call | tf_op jit(solution)/shard_map/pallas_call | solution.py:378
  12.7 3.0 %collective-permute-start.4 = (bf16[192,128]{1,0:T(8,128)(2,1)S(1)}, bf16[192,128]{1,0:T(8,128)(2,1)S(1)}, u32[]{:S(2)}, u32[]{:S(2)}) collective-permute-start(bf16[192,128]{1,0:T(8,128)(2,1)S(1)} %get-tuple-element.22), channel_id=1, source_target_pairs={{0,1},{1,0},{2,3},{3,2},{4,5},{5,4},{6,7},{7,6},{8,9},{9,8},{10,11... | collective-permute-start | bytes 147464 | tf_op jit(solution)/shard_map/ppermute | solution.py:429
  15.6 0.5 %collective-permute-start.5 = (bf16[192,128]{1,0:T(8,128)(2,1)S(1)}, bf16[192,128]{1,0:T(8,128)(2,1)S(1)}, u32[]{:S(2)}, u32[]{:S(2)}) collective-permute-start(bf16[192,128]{1,0:T(8,128)(2,1)S(1)} %get-tuple-element.23), channel_id=1, source_target_pairs={{0,1},{1,0},{2,3},{3,2},{4,5},{5,4},{6,7},{7,6},{8,9},{9,8},{10,11... | collective-permute-start | bytes 147464 | tf_op jit(solution)/shard_map/ppermute | solution.py:429
  16.1 0.4 %collective-permute-start.6 = (bf16[192,128]{1,0:T(8,128)(2,1)S(1)}, bf16[192,128]{1,0:T(8,128)(2,1)S(1)}, u32[]{:S(2)}, u32[]{:S(2)}) collective-permute-start(bf16[192,128]{1,0:T(8,128)(2,1)S(1)} %get-tuple-element.24), channel_id=1, source_target_pairs={{0,1},{1,0},{2,3},{3,2},{4,5},{5,4},{6,7},{7,6},{8,9},{9,8},{10,11... | collective-permute-start | bytes 147464 | tf_op jit(solution)/shard_map/ppermute | solution.py:429
  16.5 0.4 %shard_map.85.refs_0_ = f32[4,192,128]{2,1,0:T(8,128)S(1)} custom-call(bf16[4,192,128]{2,1,0:T(8,128)(2,1)S(1)} %get-tuple-element.21.state_ref.refs_7_, bf16[2,4,3,128,128]{4,3,2,1,0:T(8,128)(2,1)S(1)} %copy-done, bf16[2,1,4,128,128]{4,3,2,1,0:T(8,128)(2,1)S(1)} %copy-done.1, f32[192,8]{1,0:T(8,128)S(1)} %get-tuple-element.16.table_ref.refs_2_, ...), custom_call_target="tpu_custom_call" | custom-call | tf_op jit(solution)/shard_map/pallas_call | solution.py:369
  16.9 0.8 %collective-permute-done.4.refs_4_ = bf16[192,128]{1,0:T(8,128)(2,1)S(1)} collective-permute-done((bf16[192,128]{1,0:T(8,128)(2,1)S(1)}, bf16[192,128]{1,0:T(8,128)(2,1)S(1)}, u32[]{:S(2)}, u32[]{:S(2)}) %collective-permute-start.4) | collective-permute-done | bytes 49184 | tf_op jit(solution)/shard_map/ppermute | solution.py:429
  17.7 3.8 %collective-permute-done.5.refs_5_ = bf16[192,128]{1,0:T(8,128)(2,1)S(1)} collective-permute-done((bf16[192,128]{1,0:T(8,128)(2,1)S(1)}, bf16[192,128]{1,0:T(8,128)(2,1)S(1)}, u32[]{:S(2)}, u32[]{:S(2)}) %collective-permute-start.5) | collective-permute-done | bytes 49184 | tf_op jit(solution)/shard_map/ppermute | solution.py:429
  21.5 0.0 collective-permute-done.6.refs_6_
  21.5 1.0 %shard_map.86 = bf16[2,192,512]{2,1,0:T(8,128)(2,1)} custom-call(f32[4,192,128]{2,1,0:T(8,128)S(1)} %shard_map.85.refs_0_, bf16[2,1,4,128,128]{4,3,2,1,0:T(8,128)(2,1)S(1)} %copy-done.1, f32[192,8]{1,0:T(8,128)S(1)} %get-tuple-element.16.table_ref.refs_2_, f32[72,128]{1,0:T(8,128)S(1)} %get-tuple-element.17.marks_ref.refs_3_, ...), custom_call_target="tpu_custom_call" | custom-call | tf_op jit(solution)/shard_map/pallas_call | solution.py:411
Async XLA Ops:
  0.0 9.0 %copy-start = (bf16[2,4,3,128,128]{4,3,2,1,0:T(8,128)(2,1)S(1)}, bf16[2,4,3,128,128]{4,3,2,1,0:T(8,128)(2,1)}, u32[]{:S(2)}) copy-start(bf16[2,4,3,128,128]{4,3,2,1,0:T(8,128)(2,1)} %refs_12_.1) | copy-start | bytes 2359300
  0.0 9.0 %copy-start.1 = (bf16[2,1,4,128,128]{4,3,2,1,0:T(8,128)(2,1)S(1)}, bf16[2,1,4,128,128]{4,3,2,1,0:T(8,128)(2,1)}, u32[]{:S(2)}) copy-start(bf16[2,1,4,128,128]{4,3,2,1,0:T(8,128)(2,1)} %refs_1_.3) | copy-start | bytes 786436
  1.1 7.8 %collective-permute-start = (bf16[4,192,128]{2,1,0:T(8,128)(2,1)S(1)}, bf16[4,192,128]{2,1,0:T(8,128)(2,1)S(1)}, u32[]{:S(2)}, u32[]{:S(2)}) collective-permute-start(bf16[4,192,128]{2,1,0:T(8,128)(2,1)S(1)} %get-tuple-element.15.refs_8_), channel_id=1, source_target_pairs={{0,16},{1,17},{2,18},{3,19},{4,20},{5,21},{6,22},{7,23},{8,24},{9,... | collective-permute-start | bytes 589832 | tf_op jit(solution)/shard_map/ppermute | solution.py:429
  1.2 8.2 %collective-permute-start.1 = (bf16[208,128]{1,0:T(8,128)(2,1)S(1)}, bf16[208,128]{1,0:T(8,128)(2,1)S(1)}, u32[]{:S(2)}, u32[]{:S(2)}) collective-permute-start(bf16[208,128]{1,0:T(8,128)(2,1)S(1)} %get-tuple-element.18), channel_id=1, source_target_pairs={{0,28},{1,29},{2,30},{3,31},{4,24},{5,25},{6,26},{7,27},{8,20},{9,... | collective-permute-start | bytes 159752 | tf_op jit(solution)/shard_map/ppermute | solution.py:429
  6.3 6.0 %collective-permute-start.2 = (bf16[208,128]{1,0:T(8,128)(2,1)S(1)}, bf16[208,128]{1,0:T(8,128)(2,1)S(1)}, u32[]{:S(2)}, u32[]{:S(2)}) collective-permute-start(bf16[208,128]{1,0:T(8,128)(2,1)S(1)} %get-tuple-element.19), channel_id=1, source_target_pairs={{0,24},{1,25},{2,26},{3,27},{4,28},{5,29},{6,30},{7,31},{8,16},{9,... | collective-permute-start | bytes 159752 | tf_op jit(solution)/shard_map/ppermute | solution.py:429
  6.6 5.6 %collective-permute-start.3 = (bf16[208,128]{1,0:T(8,128)(2,1)S(1)}, bf16[208,128]{1,0:T(8,128)(2,1)S(1)}, u32[]{:S(2)}, u32[]{:S(2)}) collective-permute-start(bf16[208,128]{1,0:T(8,128)(2,1)S(1)} %get-tuple-element.20), channel_id=1, source_target_pairs={{0,20},{1,21},{2,22},{3,23},{4,16},{5,17},{6,18},{7,19},{8,28},{9,... | collective-permute-start | bytes 159752 | tf_op jit(solution)/shard_map/ppermute | solution.py:429
  12.7 5.1 %collective-permute-start.4 = (bf16[192,128]{1,0:T(8,128)(2,1)S(1)}, bf16[192,128]{1,0:T(8,128)(2,1)S(1)}, u32[]{:S(2)}, u32[]{:S(2)}) collective-permute-start(bf16[192,128]{1,0:T(8,128)(2,1)S(1)} %get-tuple-element.22), channel_id=1, source_target_pairs={{0,1},{1,0},{2,3},{3,2},{4,5},{5,4},{6,7},{7,6},{8,9},{9,8},{10,11... | collective-permute-start | bytes 147464 | tf_op jit(solution)/shard_map/ppermute | solution.py:429
  15.6 5.9 %collective-permute-start.5 = (bf16[192,128]{1,0:T(8,128)(2,1)S(1)}, bf16[192,128]{1,0:T(8,128)(2,1)S(1)}, u32[]{:S(2)}, u32[]{:S(2)}) collective-permute-start(bf16[192,128]{1,0:T(8,128)(2,1)S(1)} %get-tuple-element.23), channel_id=1, source_target_pairs={{0,1},{1,0},{2,3},{3,2},{4,5},{5,4},{6,7},{7,6},{8,9},{9,8},{10,11... | collective-permute-start | bytes 147464 | tf_op jit(solution)/shard_map/ppermute | solution.py:429
  16.1 5.4 %collective-permute-start.6 = (bf16[192,128]{1,0:T(8,128)(2,1)S(1)}, bf16[192,128]{1,0:T(8,128)(2,1)S(1)}, u32[]{:S(2)}, u32[]{:S(2)}) collective-permute-start(bf16[192,128]{1,0:T(8,128)(2,1)S(1)} %get-tuple-element.24), channel_id=1, source_target_pairs={{0,1},{1,0},{2,3},{3,2},{4,5},{5,4},{6,7},{7,6},{8,9},{9,8},{10,11... | collective-permute-start | bytes 147464 | tf_op jit(solution)/shard_map/ppermute | solution.py:429

commit v19 on v18

--- a/solution.py
+++ b/solution.py
@@ -263,7 +263,7 @@
 
 
 def exchange_order(n, handed):
-    return list(range(n - 1, 0, -1)) if handed else [*range(n // 2, n), *range(n // 2 - 1, 0, -1)]
+    return [*range(n // 2, n), *range(n // 2 - 1, 0, -1)] if handed else list(range(n - 1, 0, -1))
 
 
 def by_distance(refs, handed):

time: 22.7 us -> 22 us (0.969)
  waiting for transfers between devices: 8.41 us -> 7.21 us
  starting transfers between devices: 10.6 us -> 11.1 us
    ppermute x7, waiting for transfers between devices: 8.41 us -> 7.21 us  [swap(): return lax.ppermute(block, ('tm', 'net', 'cols'), pairs)]
    ppermute x7, starting transfers between devices: 10.6 us -> 11.1 us  [swap(): return lax.ppermute(block, ('tm', 'net', 'cols'), pairs)]
  transfers between devices with their start and end apart: 7 -> 7, of which waited for: 4 -> 5; matrix products, arithmetic and copies ran while one was open for 0% -> 0% of each run, Pallas kernels for 4% -> 4%
where the time goes in v19:
time: 22 us; the launch traced here: 21.8 us
  starting transfers between devices  11.1 us (50%)
  waiting for transfers between devices  7.21 us (33%)
  Pallas kernels  3.49 us (16%)
    ppermute x7, starting transfers between devices, swap(): return lax.ppermute(block, ('tm', 'net', 'cols'), pairs)  11.1 us
    ppermute x7, waiting for transfers between devices, swap(): return lax.ppermute(block, ('tm', 'net', 'cols'), pairs)  7.21 us
    pallas_call x1, Pallas kernels, local(): pl.pallas_call(second_kernel, out_shape=[f32((cols, table_rows)), f32((ma...  1.11 us
    pallas_call x1, Pallas kernels, close(): pl.pallas_call(functools.partial(close_kernel, step, section, firsts, sen...  1.03 us
    pallas_call x2, Pallas kernels, own(): pl.pallas_call(functools.partial(own_kernel, step), out_shape=f32(whole.s...  0.9 us
    pallas_call x1, Pallas kernels, join(): pl.pallas_call(functools.partial(join_kernel, step, kinds if fix else 0,...  0.45 us
  transfers between devices with their start and end apart: 7, of which 5 were waited for; matrix products, arithmetic and copies ran while one was open for 0% of the time, Pallas kernels for 4%

profile of v19, /device:TPU:4, one launch (start us, length us, event | category | flops | bytes accessed | tf_op | source)
XLA Modules:
  0.0 21.8 jit_solution(1441561610314626593)
XLA Ops:
  0.0 0.0 copy-start
  0.0 0.0 copy-start.1
  0.0 1.1 %shard_map.82 = (f32[192,8]{1,0:T(8,128)S(1)}, f32[72,128]{1,0:T(8,128)S(1)}, bf16[4,192,128]{2,1,0:T(8,128)(2,1)S(1)}, bf16[208,128]{1,0:T(8,128)(2,1)S(1)}, bf...) custom-call(bf16[2,4,3,128,128]{4,3,2,1,0:T(8,128)(2,1)} %refs_12_.1, bf16[2,1,4,128,128]{4,3,2,1,0:T(8,128)(2,1)} %refs_1_.3, ...), custom_call_target="tpu_custom_call" | custom-call | tf_op jit(solution)/shard_map/pallas_call | solution.py:351
  1.1 0.1 collective-permute-start
  1.2 4.0 %collective-permute-start.1 = (bf16[208,128]{1,0:T(8,128)(2,1)S(1)}, bf16[208,128]{1,0:T(8,128)(2,1)S(1)}, u32[]{:S(2)}, u32[]{:S(2)}) collective-permute-start(bf16[208,128]{1,0:T(8,128)(2,1)S(1)} %get-tuple-element.18), channel_id=1, source_target_pairs={{0,24},{1,25},{2,26},{3,27},{4,28},{5,29},{6,30},{7,31},{8,16},{9,... | collective-permute-start | bytes 159752 | tf_op jit(solution)/shard_map/ppermute | solution.py:429
  5.2 2.3 %collective-permute-start.2 = (bf16[208,128]{1,0:T(8,128)(2,1)S(1)}, bf16[208,128]{1,0:T(8,128)(2,1)S(1)}, u32[]{:S(2)}, u32[]{:S(2)}) collective-permute-start(bf16[208,128]{1,0:T(8,128)(2,1)S(1)} %get-tuple-element.19), channel_id=1, source_target_pairs={{0,28},{1,29},{2,30},{3,31},{4,24},{5,25},{6,26},{7,27},{8,20},{9,... | collective-permute-start | bytes 159752 | tf_op jit(solution)/shard_map/ppermute | solution.py:429
  7.5 0.2 %collective-permute-start.3 = (bf16[208,128]{1,0:T(8,128)(2,1)S(1)}, bf16[208,128]{1,0:T(8,128)(2,1)S(1)}, u32[]{:S(2)}, u32[]{:S(2)}) collective-permute-start(bf16[208,128]{1,0:T(8,128)(2,1)S(1)} %get-tuple-element.20), channel_id=1, source_target_pairs={{0,20},{1,21},{2,22},{3,23},{4,16},{5,17},{6,18},{7,19},{8,28},{9,... | collective-permute-start | bytes 159752 | tf_op jit(solution)/shard_map/ppermute | solution.py:429
  7.7 1.2 %collective-permute-done.state_ref = bf16[4,192,128]{2,1,0:T(8,128)(2,1)S(1)} collective-permute-done((bf16[4,192,128]{2,1,0:T(8,128)(2,1)S(1)}, bf16[4,192,128]{2,1,0:T(8,128)(2,1)S(1)}, u32[]{:S(2)}, u32[]{:S(2)}) %collective-permute-start) | collective-permute-done | bytes 196640 | tf_op jit(solution)/shard_map/ppermute | solution.py:429
  9.0 0.0 copy-done
  9.0 0.0 copy-done.1
  9.0 0.5 %shard_map.83.z_ref = f32[4,192,128]{2,1,0:T(8,128)S(1)} custom-call(bf16[4,192,128]{2,1,0:T(8,128)(2,1)S(1)} %collective-permute-done.state_ref, bf16[2,4,3,128,128]{4,3,2,1,0:T(8,128)(2,1)S(1)} %copy-done, bf16[2,1,4,128,128]{4,3,2,1,0:T(8,128)(2,1)S(1)} %copy-done.1, f32[192,8]{1,0:T(8,128)S(1)} %get-tuple-element.16.table_ref.refs_2_, ...), custom_call_target="tpu_custom_call" | custom-call | tf_op jit(solution)/shard_map/pallas_call | solution.py:369
  9.4 0.0 collective-permute-done.1.refs_0_.refs_10_
  9.4 2.8 %collective-permute-done.2.refs_1_.refs_11_ = bf16[208,128]{1,0:T(8,128)(2,1)S(1)} collective-permute-done((bf16[208,128]{1,0:T(8,128)(2,1)S(1)}, bf16[208,128]{1,0:T(8,128)(2,1)S(1)}, u32[]{:S(2)}, u32[]{:S(2)}) %collective-permute-start.2) | collective-permute-done | bytes 53280 | tf_op jit(solution)/shard_map/ppermute | solution.py:429
  12.3 0.5 %collective-permute-done.3.refs_2_.refs_9_ = bf16[208,128]{1,0:T(8,128)(2,1)S(1)} collective-permute-done((bf16[208,128]{1,0:T(8,128)(2,1)S(1)}, bf16[208,128]{1,0:T(8,128)(2,1)S(1)}, u32[]{:S(2)}, u32[]{:S(2)}) %collective-permute-start.3) | collective-permute-done | bytes 53280 | tf_op jit(solution)/shard_map/ppermute | solution.py:429
  12.8 0.4 %shard_map.84 = (bf16[4,192,128]{2,1,0:T(8,128)(2,1)S(1)}, bf16[192,128]{1,0:T(8,128)(2,1)S(1)}, bf16[192,128]{1,0:T(8,128)(2,1)S(1)}, bf16[192,128]{1,0:T(8,128)(2,1)S(1)}) custom-call(f32[4,192,128]{2,1,0:T(8,128)S(1)} %shard_map.83.z_ref, bf16[2,1,4,128,128]{4,3,2,1,0:T(8,128)(2,1)S(1)} %copy-done.1, f32[192,8]{1,0:T(8,128)S(1)} %get-tuple-element.16.table_ref.refs_2_, ...), custom_call_target="tpu_custom_call" | custom-call | tf_op jit(solution)/shard_map/pallas_call | solution.py:378
  13.3 2.2 %collective-permute-start.4 = (bf16[192,128]{1,0:T(8,128)(2,1)S(1)}, bf16[192,128]{1,0:T(8,128)(2,1)S(1)}, u32[]{:S(2)}, u32[]{:S(2)}) collective-permute-start(bf16[192,128]{1,0:T(8,128)(2,1)S(1)} %get-tuple-element.22), channel_id=1, source_target_pairs={{0,1},{1,0},{2,3},{3,2},{4,5},{5,4},{6,7},{7,6},{8,9},{9,8},{10,11... | collective-permute-start | bytes 147464 | tf_op jit(solution)/shard_map/ppermute | solution.py:429
  15.5 0.0 collective-permute-start.5
  15.5 2.2 %collective-permute-start.6 = (bf16[192,128]{1,0:T(8,128)(2,1)S(1)}, bf16[192,128]{1,0:T(8,128)(2,1)S(1)}, u32[]{:S(2)}, u32[]{:S(2)}) collective-permute-start(bf16[192,128]{1,0:T(8,128)(2,1)S(1)} %get-tuple-element.24), channel_id=1, source_target_pairs={{0,1},{1,0},{2,3},{3,2},{4,5},{5,4},{6,7},{7,6},{8,9},{9,8},{10,11... | collective-permute-start | bytes 147464 | tf_op jit(solution)/shard_map/ppermute | solution.py:429
  17.7 0.4 %shard_map.85.refs_0_ = f32[4,192,128]{2,1,0:T(8,128)S(1)} custom-call(bf16[4,192,128]{2,1,0:T(8,128)(2,1)S(1)} %get-tuple-element.21.state_ref.refs_7_, bf16[2,4,3,128,128]{4,3,2,1,0:T(8,128)(2,1)S(1)} %copy-done, bf16[2,1,4,128,128]{4,3,2,1,0:T(8,128)(2,1)S(1)} %copy-done.1, f32[192,8]{1,0:T(8,128)S(1)} %get-tuple-element.16.table_ref.refs_2_, ...), custom_call_target="tpu_custom_call" | custom-call | tf_op jit(solution)/shard_map/pallas_call | solution.py:369
  18.2 1.3 %collective-permute-done.4.refs_4_ = bf16[192,128]{1,0:T(8,128)(2,1)S(1)} collective-permute-done((bf16[192,128]{1,0:T(8,128)(2,1)S(1)}, bf16[192,128]{1,0:T(8,128)(2,1)S(1)}, u32[]{:S(2)}, u32[]{:S(2)}) %collective-permute-start.4) | collective-permute-done | bytes 49184 | tf_op jit(solution)/shard_map/ppermute | solution.py:429
  19.5 1.3 %collective-permute-done.5.refs_5_ = bf16[192,128]{1,0:T(8,128)(2,1)S(1)} collective-permute-done((bf16[192,128]{1,0:T(8,128)(2,1)S(1)}, bf16[192,128]{1,0:T(8,128)(2,1)S(1)}, u32[]{:S(2)}, u32[]{:S(2)}) %collective-permute-start.5) | collective-permute-done | bytes 49184 | tf_op jit(solution)/shard_map/ppermute | solution.py:429
  20.8 0.0 collective-permute-done.6.refs_6_
  20.8 1.0 %shard_map.86 = bf16[2,192,512]{2,1,0:T(8,128)(2,1)} custom-call(f32[4,192,128]{2,1,0:T(8,128)S(1)} %shard_map.85.refs_0_, bf16[2,1,4,128,128]{4,3,2,1,0:T(8,128)(2,1)S(1)} %copy-done.1, f32[192,8]{1,0:T(8,128)S(1)} %get-tuple-element.16.table_ref.refs_2_, f32[72,128]{1,0:T(8,128)S(1)} %get-tuple-element.17.marks_ref.refs_3_, ...), custom_call_target="tpu_custom_call" | custom-call | tf_op jit(solution)/shard_map/pallas_call | solution.py:411
Async XLA Ops:
  0.0 9.0 %copy-start = (bf16[2,4,3,128,128]{4,3,2,1,0:T(8,128)(2,1)S(1)}, bf16[2,4,3,128,128]{4,3,2,1,0:T(8,128)(2,1)}, u32[]{:S(2)}) copy-start(bf16[2,4,3,128,128]{4,3,2,1,0:T(8,128)(2,1)} %refs_12_.1) | copy-start | bytes 2359300
  0.0 9.0 %copy-start.1 = (bf16[2,1,4,128,128]{4,3,2,1,0:T(8,128)(2,1)S(1)}, bf16[2,1,4,128,128]{4,3,2,1,0:T(8,128)(2,1)}, u32[]{:S(2)}) copy-start(bf16[2,1,4,128,128]{4,3,2,1,0:T(8,128)(2,1)} %refs_1_.3) | copy-start | bytes 786436
  1.1 7.8 %collective-permute-start = (bf16[4,192,128]{2,1,0:T(8,128)(2,1)S(1)}, bf16[4,192,128]{2,1,0:T(8,128)(2,1)S(1)}, u32[]{:S(2)}, u32[]{:S(2)}) collective-permute-start(bf16[4,192,128]{2,1,0:T(8,128)(2,1)S(1)} %get-tuple-element.15.refs_8_), channel_id=1, source_target_pairs={{0,16},{1,17},{2,18},{3,19},{4,20},{5,21},{6,22},{7,23},{8,24},{9,... | collective-permute-start | bytes 589832 | tf_op jit(solution)/shard_map/ppermute | solution.py:429
  1.2 8.2 %collective-permute-start.1 = (bf16[208,128]{1,0:T(8,128)(2,1)S(1)}, bf16[208,128]{1,0:T(8,128)(2,1)S(1)}, u32[]{:S(2)}, u32[]{:S(2)}) collective-permute-start(bf16[208,128]{1,0:T(8,128)(2,1)S(1)} %get-tuple-element.18), channel_id=1, source_target_pairs={{0,24},{1,25},{2,26},{3,27},{4,28},{5,29},{6,30},{7,31},{8,16},{9,... | collective-permute-start | bytes 159752 | tf_op jit(solution)/shard_map/ppermute | solution.py:429
  5.2 7.0 %collective-permute-start.2 = (bf16[208,128]{1,0:T(8,128)(2,1)S(1)}, bf16[208,128]{1,0:T(8,128)(2,1)S(1)}, u32[]{:S(2)}, u32[]{:S(2)}) collective-permute-start(bf16[208,128]{1,0:T(8,128)(2,1)S(1)} %get-tuple-element.19), channel_id=1, source_target_pairs={{0,28},{1,29},{2,30},{3,31},{4,24},{5,25},{6,26},{7,27},{8,20},{9,... | collective-permute-start | bytes 159752 | tf_op jit(solution)/shard_map/ppermute | solution.py:429
  7.5 5.3 %collective-permute-start.3 = (bf16[208,128]{1,0:T(8,128)(2,1)S(1)}, bf16[208,128]{1,0:T(8,128)(2,1)S(1)}, u32[]{:S(2)}, u32[]{:S(2)}) collective-permute-start(bf16[208,128]{1,0:T(8,128)(2,1)S(1)} %get-tuple-element.20), channel_id=1, source_target_pairs={{0,20},{1,21},{2,22},{3,23},{4,16},{5,17},{6,18},{7,19},{8,28},{9,... | collective-permute-start | bytes 159752 | tf_op jit(solution)/shard_map/ppermute | solution.py:429
  13.3 6.2 %collective-permute-start.4 = (bf16[192,128]{1,0:T(8,128)(2,1)S(1)}, bf16[192,128]{1,0:T(8,128)(2,1)S(1)}, u32[]{:S(2)}, u32[]{:S(2)}) collective-permute-start(bf16[192,128]{1,0:T(8,128)(2,1)S(1)} %get-tuple-element.22), channel_id=1, source_target_pairs={{0,1},{1,0},{2,3},{3,2},{4,5},{5,4},{6,7},{7,6},{8,9},{9,8},{10,11... | collective-permute-start | bytes 147464 | tf_op jit(solution)/shard_map/ppermute | solution.py:429
  15.5 5.3 %collective-permute-start.5 = (bf16[192,128]{1,0:T(8,128)(2,1)S(1)}, bf16[192,128]{1,0:T(8,128)(2,1)S(1)}, u32[]{:S(2)}, u32[]{:S(2)}) collective-permute-start(bf16[192,128]{1,0:T(8,128)(2,1)S(1)} %get-tuple-element.23), channel_id=1, source_target_pairs={{0,1},{1,0},{2,3},{3,2},{4,5},{5,4},{6,7},{7,6},{8,9},{9,8},{10,11... | collective-permute-start | bytes 147464 | tf_op jit(solution)/shard_map/ppermute | solution.py:429
  15.5 5.3 %collective-permute-start.6 = (bf16[192,128]{1,0:T(8,128)(2,1)S(1)}, bf16[192,128]{1,0:T(8,128)(2,1)S(1)}, u32[]{:S(2)}, u32[]{:S(2)}) collective-permute-start(bf16[192,128]{1,0:T(8,128)(2,1)S(1)} %get-tuple-element.24), channel_id=1, source_target_pairs={{0,1},{1,0},{2,3},{3,2},{4,5},{5,4},{6,7},{7,6},{8,9},{9,8},{10,11... | collective-permute-start | bytes 147464 | tf_op jit(solution)/shard_map/ppermute | solution.py:429

commit v20 on v19

--- a/solution.py
+++ b/solution.py
@@ -15,6 +15,7 @@
 DMA = pltpu.SemaphoreType.DMA
 
 STATE, LANE, BLOCK, AWAY, GAIN = 0, 1, 2, 3, 4
+PANELS = 2
 ROWS = 16
 
 
@@ -109,10 +110,10 @@
     jac_hbm, iface_hbm, *small, table_ref, marks_ref, state_ref = refs[:11]
     n = lax.axis_size("net")
     me = lax.axis_index("net")
-    outgoing, refs = refs[11 : 10 + n], refs[10 + n :]
-    jac_ref, iface_ref, *loaded, first_ref, sems = refs
+    outgoing, (jac_ref, iface_ref, *loaded, first_ref, sems) = refs[11:-10], refs[-10:]
     cols_ref, send_ref, recv_ref, live_ref, node_ref, gain_ref = loaded
     blocks, cols, width = state_ref.shape
+    panel = cols // PANELS
     sources = [jac_hbm.at[1], iface_hbm.at[1, 0], *small]
     loads = [
         pltpu.make_async_copy(source, target, sems.at[i])
@@ -170,8 +171,10 @@
         for i in range(blocks):
             own = own_sum(i, first_ref, jac_ref, near_by(first_ref, cols_ref), table, 1, hit[i])
             state_ref[i] = (own + jnp.where(recv == float(i), coupled, 0.0)).astype(state_ref.dtype)
-        for d in range(1, n):
-            outgoing[d - 1][pl.ds(0, cols)] = state_ref[send_ref[0, me ^ d]]
+        for h in range(PANELS):
+            for d in range(1, n):
+                block = state_ref[send_ref[0, me ^ d], pl.ds(h * panel, panel)]
+                outgoing[h * (n - 1) + d - 1][pl.ds(0, panel)] = block
 
     @pl.when(jnp.logical_not(here))
     def _():
@@ -181,26 +184,25 @@
 
     for d in range(1, n):
         row = table_row(send_ref, me ^ d, width).astype(state_ref.dtype)
-        outgoing[d - 1][pl.ds(cols, ROWS)] = jnp.broadcast_to(row, (ROWS, width))
-
-
-def write_start(states, first, out_ref, sems):
+        outgoing[d - 1][pl.ds(panel, ROWS)] = jnp.broadcast_to(row, (ROWS, width))
+
+
+def write_start(states, first, out_ref, sems, row=0):
     copies = []
     for s, state_ref in enumerate(states, first):
-        width = state_ref.shape[2]
-        for i in range(state_ref.shape[0]):
-            copies.append(
-                pltpu.make_async_copy(state_ref.at[i], out_ref.at[s, :, pl.ds(i * width, width)], sems.at[s, i])
-            )
+        blocks, cols, width = state_ref.shape
+        for i in range(blocks):
+            target = out_ref.at[s, pl.ds(row, cols), pl.ds(i * width, width)]
+            copies.append(pltpu.make_async_copy(state_ref.at[i], target, sems.at[s, i]))
     for copy in copies:
         copy.start()
     return copies
 
 
-def own_kernel(step, state_ref, jac_ref, iface_ref, table_ref, marks_ref, z_ref):
-    table = table_ref[...]
-    n = lax.axis_size("net")
-    blocks = state_ref.shape[0]
+def own_kernel(step, row, state_ref, jac_ref, iface_ref, table_ref, marks_ref, z_ref):
+    n = lax.axis_size("net")
+    blocks, cols, _ = state_ref.shape
+    table = table_ref[pl.ds(row, cols)]
     kinds = jac_ref.shape[2]
     sent, near, _, _ = marks_layout(n, blocks, kinds)
     state = [state_ref[j] for j in range(blocks)]
@@ -231,7 +233,7 @@
         add_coupled(made_ref[0, 0], iface_ref[0, 0, q], live_ref[0, q], recv_ref[0, q], z_ref)
     made_ref[0] = z_ref[...].astype(made_ref.dtype)
     rows = [table_row(send_ref, lax.axis_index("net"), width)]
-    rows += [block[cols : cols + 1].astype(jnp.float32) for block in handed]
+    rows += [block[cols // PANELS : cols // PANELS + 1].astype(jnp.float32) for block in handed]
     keep = kept(table, rows)[:, 0:1]
     for i in range(blocks):
         made_ref[1, i] = jnp.where(keep > 0.0, opening[i], jnp.zeros_like(opening[i]))
@@ -271,23 +273,24 @@
     return [refs[order.index(d)] for d in range(1, len(refs) + 1)]
 
 
-def join_kernel(step, fix, section, z_ref, iface_ref, table_ref, marks_ref, *refs):
-    n = lax.axis_size("net")
-    arrived, state_ref, outgoing = by_distance(refs[: n - 1], step == 0), refs[n - 1], refs[n:]
-    blocks, cols, _ = z_ref.shape
+def join_kernel(step, fix, section, row, z_row, z_ref, iface_ref, table_ref, marks_ref, *refs):
+    n = lax.axis_size("net")
+    arrived, (state_ref, *outgoing) = by_distance(refs[: n - 1], step == 0), refs[-n:]
+    carriers = by_distance(refs[-n - (n - 1) : -n], step == 0)
+    blocks, cols, _ = state_ref.shape
 
     @pl.when(lax.axis_index("tm") == section)
     def _():
         keep = None
         if fix:
             rows = [marks_ref[pl.ds(marks_layout(n, blocks, fix)[2], 1)]]
-            rows += [block[cols : cols + 1].astype(jnp.float32) for block in arrived]
-            keep = kept(table_ref[...], rows)
-        made = joined([z_ref[i] for i in range(blocks)], step, iface_ref, marks_ref, arrived, keep)
-        give(made, marks_ref, state_ref, outgoing)
-
-
-def close_kernel(step, section, firsts, send, before, *refs):
+            rows += [block[cols : cols + 1].astype(jnp.float32) for block in carriers]
+            keep = kept(table_ref[pl.ds(row, cols)], rows)
+        sums = [z_ref[i, pl.ds(z_row, cols)] for i in range(blocks)]
+        give(joined(sums, step, iface_ref, marks_ref, arrived, keep), marks_ref, state_ref, outgoing)
+
+
+def close_kernel(step, section, row, firsts, send, before, *refs):
     n = lax.axis_size("net")
     *refs, sems = refs
     if firsts:
@@ -304,11 +307,11 @@
 
     @pl.when(lax.axis_index("tm") == section)
     def _():
-        copies = write_start(before, 0, out_ref, sems)
+        copies = write_start(before, 0, out_ref, sems, row)
         sums = [z_ref[i] for i in range(z_ref.shape[0])]
         made = joined(sums, step, iface_ref, marks_ref, arrived)
         give(made, marks_ref, state_ref, outgoing)
-        copies += write_start([state_ref], len(before), out_ref, sems)
+        copies += write_start([state_ref], len(before), out_ref, sems, row)
         for copy in copies:
             copy.wait()
 
@@ -339,7 +342,8 @@
     near = block_cols.T
     bf16 = functools.partial(jax.ShapeDtypeStruct, dtype=jnp.bfloat16)
     f32 = functools.partial(jax.ShapeDtypeStruct, dtype=jnp.float32)
-    whole, one = bf16((blocks, cols, width)), bf16((cols, width))
+    panel = cols // PANELS
+    whole, part, one = bf16((blocks, cols, width)), bf16((blocks, panel, width)), bf16((panel, width))
     table_rows = GAIN + steps + -(GAIN + steps) % 8
     written = bf16((steps, cols, blocks * width))
 
@@ -351,9 +355,10 @@
     table, marks, state, *outgoing = pl.pallas_call(
         second_kernel,
         out_shape=[f32((cols, table_rows)), f32((marks_rows, width)), whole]
-        + [bf16((cols + ROWS, width))] * (n - 1),
+        + [bf16((panel + ROWS, width))] * (n - 1)
+        + [one] * ((PANELS - 1) * (n - 1)),
         in_specs=[HBM] * len(pinned),
-        out_specs=[VMEM] * (n + 2),
+        out_specs=[VMEM] * (3 + PANELS * (n - 1)),
         scratch_shapes=[
             pltpu.VMEM((blocks, kinds, width, width), jnp.bfloat16),
             pltpu.VMEM((n, width, width), jnp.bfloat16),
@@ -365,27 +370,33 @@
         compiler_params=LIMIT,
     )(*pinned)
 
-    def own(state, step):
+    def own(state, step, row):
         return pl.pallas_call(
-            functools.partial(own_kernel, step),
-            out_shape=f32(whole.shape),
+            functools.partial(own_kernel, step, row),
+            out_shape=f32(state.shape),
             in_specs=[VMEM] * 5,
             out_specs=VMEM,
             compiler_params=LIMIT,
         )(state, jac, iface_jac, table, marks)
 
-    def join(z, step, fix, arrived, section):
+    def ordered(arrived, step):
+        return [arrived[d - 1] for d in exchange_order(n, step == 0)]
+
+    def join(z, z_row, step, fix, arrived, carriers, section, row):
+        arrays = [z, iface_jac, table, marks, *ordered(arrived, step)]
+        if carriers is not arrived:
+            arrays += ordered(carriers, step)
         return pl.pallas_call(
-            functools.partial(join_kernel, step, kinds if fix else 0, section),
-            out_shape=[whole] + [one] * (n - 1),
-            in_specs=[VMEM] * (n + 3),
+            functools.partial(join_kernel, step, kinds if fix else 0, section, row, z_row),
+            out_shape=[part] + [one] * (n - 1),
+            in_specs=[VMEM] * len(arrays),
             out_specs=[VMEM] * n,
             compiler_params=LIMIT,
-        )(z, iface_jac, table, marks, *[arrived[d - 1] for d in exchange_order(n, step == 0)])
-
-    def close(z, step, arrived, section, before, out, send):
+        )(*arrays)
+
+    def close(z, step, arrived, section, row, before, out, send):
         firsts = out is None
-        arrays = [z, iface_jac, table, marks, *[arrived[d - 1] for d in exchange_order(n, False)], *before]
+        arrays = [z, iface_jac, table, marks, *ordered(arrived, step), *before]
         specs = [VMEM] * len(arrays)
         scratch = [DMA((steps, blocks))]
         aliases = {}
@@ -404,12 +415,12 @@
             specs.append(ANY)
         shapes, out_specs = [written], [ANY]
         if send:
-            shapes += [whole] + [one] * (n - 1)
+            shapes += [part] + [one] * (n - 1)
             out_specs += [VMEM] * n
         else:
-            scratch.insert(0, pltpu.VMEM(whole.shape, jnp.bfloat16))
+            scratch.insert(0, pltpu.VMEM(part.shape, jnp.bfloat16))
         return pl.pallas_call(
-            functools.partial(close_kernel, step, section, firsts, send, len(before)),
+            functools.partial(close_kernel, step, section, row, firsts, send, len(before)),
             out_shape=shapes,
             in_specs=specs,
             out_specs=out_specs,
@@ -432,24 +443,30 @@
         return [swap(outgoing[d - 1], first, second, d) for d in range(1, n)]
 
     opening = state
+    sends = [outgoing[h * (n - 1) : (h + 1) * (n - 1)] for h in range(PANELS)]
+    states = [None] * PANELS
     out = None
     for r in range(1, tm):
-        arrived = exchange(outgoing, r - 1, r)
-        state = swap(state, r - 1, r, 0)
+        arrived = [exchange(blocks_out, r - 1, r) for blocks_out in sends]
         if r == 1:
-            handed = arrived
-        before = []
+            handed = arrived[0]
+            z = own(swap(state, 0, 1, 0), 0, 0)
+            sums = [(z, h * panel) for h in range(PANELS)]
+        else:
+            sums = [(own(swap(states[h], r - 1, r, 0), 0, h * panel), 0) for h in range(PANELS)]
+        before = [[] for _ in range(PANELS)]
         for s in range(steps):
-            fix = r == 1 and s == 0
             if s > 0:
-                arrived = exchange(outgoing, r, r)
-            z = own(state, s)
-            if s < steps - 1:
-                state, *outgoing = join(z, s, fix, arrived, r)
-                before.append(state)
-            else:
-                out, *rest = close(z, s, arrived, r, before, out, r < tm - 1)
-                state, *outgoing = rest or [None]
+                arrived = [exchange(blocks_out, r, r) for blocks_out in sends]
+                sums = [(own(states[h], s, h * panel), 0) for h in range(PANELS)]
+            for h in range(PANELS):
+                row = h * panel
+                if s < steps - 1:
+                    states[h], *sends[h] = join(*sums[h], s, r == 1 and s == 0, arrived[h], arrived[0] if s == 0 and r == 1 else arrived[h], r, row)
+                    before[h].append(states[h])
+                else:
+                    out, *rest = close(sums[h][0], s, arrived[h], r, row, before[h], out, r < tm - 1)
+                    states[h], *sends[h] = rest or [None]
     return out
 
 

time: 22 us -> 28.6 us (1.30)
  starting transfers between devices: 11.1 us -> 21.9 us
  waiting for transfers between devices: 7.21 us -> 1.59 us
  Pallas kernels: 3.49 us -> 4.77 us
    ppermute x7 -> x13, starting transfers between devices: 11.1 us -> 21.9 us  [swap(): return lax.ppermute(block, ('tm', 'net', 'cols'), pairs)]
    ppermute x7 -> x13, waiting for transfers between devices: 7.21 us -> 1.59 us  [swap(): return lax.ppermute(block, ('tm', 'net', 'cols'), pairs)]
    pallas_call x3 -> x5, Pallas kernels: 1.93 us -> 3.05 us  [the longest x2 1.89 us: close(): pl.pallas_call(functools.partial(close_kernel, step, section, row, firsts...]
    pallas_call x1 -> x2, Pallas kernels: 0.45 us -> 0.6 us  [join(): pl.pallas_call(functools.partial(join_kernel, step, kinds if fix else 0,...]
  transfers between devices with their start and end apart: 7 -> 13, of which waited for: 5 -> 2; matrix products, arithmetic and copies ran while one was open for 0% -> 0% of each run, Pallas kernels for 4% -> 10%
where the time goes in v20:
time: 28.6 us; the launch traced here: 28.4 us
  starting transfers between devices  21.9 us (77%)
  Pallas kernels  4.77 us (17%)
  waiting for transfers between devices  1.59 us (6%)
    ppermute x13, starting transfers between devices, swap(): return lax.ppermute(block, ('tm', 'net', 'cols'), pairs)  21.9 us
    pallas_call x2, Pallas kernels, close(): pl.pallas_call(functools.partial(close_kernel, step, section, row, firsts...  1.89 us
    ppermute x13, waiting for transfers between devices, swap(): return lax.ppermute(block, ('tm', 'net', 'cols'), pairs)  1.59 us
    pallas_call x3, Pallas kernels, own(): pl.pallas_call(functools.partial(own_kernel, step, row), out_shape=f32(st...  1.17 us
    pallas_call x1, Pallas kernels, local(): pl.pallas_call(second_kernel, out_shape=[f32((cols, table_rows)), f32((ma...  1.11 us
    pallas_call x2, Pallas kernels, join(): pl.pallas_call(functools.partial(join_kernel, step, kinds if fix else 0,...  0.6 us
  transfers between devices with their start and end apart: 13, of which 2 were waited for; matrix products, arithmetic and copies ran while one was open for 0% of the time, Pallas kernels for 10%

profile of v20, /device:TPU:4, one launch (start us, length us, event | category | flops | bytes accessed | tf_op | source)
XLA Modules:
  0.0 28.4 jit_solution(6390835332979986729)
XLA Ops:
  0.0 1.1 %shard_map.82 = (f32[192,8]{1,0:T(8,128)S(1)}, f32[72,128]{1,0:T(8,128)S(1)}, bf16[4,192,128]{2,1,0:T(8,128)(2,1)S(1)}, bf16[112,128]{1,0:T(8,128)(2,1)S(1)}, bf...) custom-call(bf16[2,4,3,128,128]{4,3,2,1,0:T(8,128)(2,1)} %refs_12_.1, ...), custom_call_target="tpu_custom_call" | custom-call | tf_op jit(solution)/shard_map/pallas_call | solution.py:355
  1.1 0.1 collective-permute-start
  1.2 4.0 %collective-permute-start.4 = (bf16[112,128]{1,0:T(8,128)(2,1)S(1)}, bf16[112,128]{1,0:T(8,128)(2,1)S(1)}, u32[]{:S(2)}, u32[]{:S(2)}) collective-permute-start(bf16[112,128]{1,0:T(8,128)(2,1)S(1)} %get-tuple-element.28), channel_id=1, source_target_pairs={{0,24},{1,25},{2,26},{3,27},{4,28},{5,29},{6,30},{7,31},{8,16},{9,... | collective-permute-start | bytes 86024 | tf_op jit(solution)/shard_map/ppermute | solution.py:440
  5.2 2.3 %collective-permute-start.5 = (bf16[112,128]{1,0:T(8,128)(2,1)S(1)}, bf16[112,128]{1,0:T(8,128)(2,1)S(1)}, u32[]{:S(2)}, u32[]{:S(2)}) collective-permute-start(bf16[112,128]{1,0:T(8,128)(2,1)S(1)} %get-tuple-element.29), channel_id=1, source_target_pairs={{0,28},{1,29},{2,30},{3,31},{4,24},{5,25},{6,26},{7,27},{8,20},{9,... | collective-permute-start | bytes 86024 | tf_op jit(solution)/shard_map/ppermute | solution.py:440
  7.5 0.2 collective-permute-start.6
  7.7 3.7 %collective-permute-start.1 = (bf16[96,128]{1,0:T(8,128)(2,1)S(1)}, bf16[96,128]{1,0:T(8,128)(2,1)S(1)}, u32[]{:S(2)}, u32[]{:S(2)}) collective-permute-start(bf16[96,128]{1,0:T(8,128)(2,1)S(1)} %get-tuple-element.25), channel_id=1, source_target_pairs={{0,24},{1,25},{2,26},{3,27},{4,28},{5,29},{6,30},{7,31},{8,16},{9,... | collective-permute-start | bytes 73736 | tf_op jit(solution)/shard_map/ppermute | solution.py:440
  11.4 0.0 collective-permute-done.4.refs_3_.refs_0_.refs_10_
  11.4 1.3 %collective-permute-start.2 = (bf16[96,128]{1,0:T(8,128)(2,1)S(1)}, bf16[96,128]{1,0:T(8,128)(2,1)S(1)}, u32[]{:S(2)}, u32[]{:S(2)}) collective-permute-start(bf16[96,128]{1,0:T(8,128)(2,1)S(1)} %get-tuple-element.26), channel_id=1, source_target_pairs={{0,28},{1,29},{2,30},{3,31},{4,24},{5,25},{6,26},{7,27},{8,20},{9,... | collective-permute-start | bytes 73736 | tf_op jit(solution)/shard_map/ppermute | solution.py:440
  12.8 0.0 collective-permute-done.state_ref
  12.8 0.0 collective-permute-start.3
  12.8 0.5 %shard_map.83.z_ref = f32[4,192,128]{2,1,0:T(8,128)S(1)} custom-call(bf16[4,192,128]{2,1,0:T(8,128)(2,1)S(1)} %collective-permute-done.state_ref, bf16[2,4,3,128,128]{4,3,2,1,0:T(8,128)(2,1)S(1)} %copy-done, bf16[2,1,4,128,128]{4,3,2,1,0:T(8,128)(2,1)S(1)} %copy-done.1, f32[192,8]{1,0:T(8,128)S(1)} %get-tuple-element.23.table_ref.refs_2_, ...), custom_call_target="tpu_custom_call" | custom-call | tf_op jit(solution)/shard_map/pallas_call | solution.py:374
  13.3 0.0 collective-permute-done.5.refs_4_.refs_1_.refs_11_
  13.3 0.3 %shard_map.86 = (bf16[4,96,128]{2,1,0:T(8,128)(2,1)S(1)}, bf16[96,128]{1,0:T(8,128)(2,1)S(1)}, bf16[96,128]{1,0:T(8,128)(2,1)S(1)}, bf16[96,128]{1,0:T(8,128)(2,1)S(1)}) custom-call(f32[4,192,128]{2,1,0:T(8,128)S(1)} %shard_map.83.z_ref, bf16[2,1,4,128,128]{4,3,2,1,0:T(8,128)(2,1)S(1)} %copy-done.1, f32[192,8]{1,0:T(8,128)S(1)} %get-tuple-element.23.table_ref.refs_2_, ...), custom_call_target="tpu_custom_call" | custom-call | tf_op jit(solution)/shard_map/pallas_call | solution.py:389
  13.6 3.2 %collective-permute-start.10 = (bf16[96,128]{1,0:T(8,128)(2,1)S(1)}, bf16[96,128]{1,0:T(8,128)(2,1)S(1)}, u32[]{:S(2)}, u32[]{:S(2)}) collective-permute-start(bf16[96,128]{1,0:T(8,128)(2,1)S(1)} %get-tuple-element.36), channel_id=1, source_target_pairs={{0,1},{1,0},{2,3},{3,2},{4,5},{5,4},{6,7},{7,6},{8,9},{9,8},{10,11... | collective-permute-start | bytes 73736 | tf_op jit(solution)/shard_map/ppermute | solution.py:440
  16.8 0.0 collective-permute-done.1.refs_0_
  16.8 1.1 %collective-permute-done.2.refs_1_ = bf16[96,128]{1,0:T(8,128)(2,1)S(1)} collective-permute-done((bf16[96,128]{1,0:T(8,128)(2,1)S(1)}, bf16[96,128]{1,0:T(8,128)(2,1)S(1)}, u32[]{:S(2)}, u32[]{:S(2)}) %collective-permute-start.2) | collective-permute-done | bytes 24608 | tf_op jit(solution)/shard_map/ppermute | solution.py:440
  18.0 0.0 collective-permute-done.3.refs_2_
  18.0 0.3 %shard_map.84 = (bf16[4,96,128]{2,1,0:T(8,128)(2,1)S(1)}, bf16[96,128]{1,0:T(8,128)(2,1)S(1)}, bf16[96,128]{1,0:T(8,128)(2,1)S(1)}, bf16[96,128]{1,0:T(8,128)(2,1)S(1)}) custom-call(f32[4,192,128]{2,1,0:T(8,128)S(1)} %shard_map.83.z_ref, bf16[2,1,4,128,128]{4,3,2,1,0:T(8,128)(2,1)S(1)} %copy-done.1, f32[192,8]{1,0:T(8,128)S(1)} %get-tuple-element.23.table_ref.refs_2_, ...), custom_call_target="tpu_custom_call" | custom-call | tf_op jit(solution)/shard_map/pallas_call | solution.py:389
  18.3 2.1 %collective-permute-start.7 = (bf16[96,128]{1,0:T(8,128)(2,1)S(1)}, bf16[96,128]{1,0:T(8,128)(2,1)S(1)}, u32[]{:S(2)}, u32[]{:S(2)}) collective-permute-start(bf16[96,128]{1,0:T(8,128)(2,1)S(1)} %get-tuple-element.32), channel_id=1, source_target_pairs={{0,1},{1,0},{2,3},{3,2},{4,5},{5,4},{6,7},{7,6},{8,9},{9,8},{10,11... | collective-permute-start | bytes 73736 | tf_op jit(solution)/shard_map/ppermute | solution.py:440
  20.4 2.4 %collective-permute-start.12 = (bf16[96,128]{1,0:T(8,128)(2,1)S(1)}, bf16[96,128]{1,0:T(8,128)(2,1)S(1)}, u32[]{:S(2)}, u32[]{:S(2)}) collective-permute-start(bf16[96,128]{1,0:T(8,128)(2,1)S(1)} %get-tuple-element.38), channel_id=1, source_target_pairs={{0,1},{1,0},{2,3},{3,2},{4,5},{5,4},{6,7},{7,6},{8,9},{9,8},{10,11... | collective-permute-start | bytes 73736 | tf_op jit(solution)/shard_map/ppermute | solution.py:440
  22.7 0.6 %collective-permute-start.8 = (bf16[96,128]{1,0:T(8,128)(2,1)S(1)}, bf16[96,128]{1,0:T(8,128)(2,1)S(1)}, u32[]{:S(2)}, u32[]{:S(2)}) collective-permute-start(bf16[96,128]{1,0:T(8,128)(2,1)S(1)} %get-tuple-element.33), channel_id=1, source_target_pairs={{0,1},{1,0},{2,3},{3,2},{4,5},{5,4},{6,7},{7,6},{8,9},{9,8},{10,11... | collective-permute-start | bytes 73736 | tf_op jit(solution)/shard_map/ppermute | solution.py:440
  23.3 0.0 collective-permute-done.10.refs_4_
  23.3 2.0 %collective-permute-start.9 = (bf16[96,128]{1,0:T(8,128)(2,1)S(1)}, bf16[96,128]{1,0:T(8,128)(2,1)S(1)}, u32[]{:S(2)}, u32[]{:S(2)}) collective-permute-start(bf16[96,128]{1,0:T(8,128)(2,1)S(1)} %get-tuple-element.34), channel_id=1, source_target_pairs={{0,1},{1,0},{2,3},{3,2},{4,5},{5,4},{6,7},{7,6},{8,9},{9,8},{10,11... | collective-permute-start | bytes 73736 | tf_op jit(solution)/shard_map/ppermute | solution.py:440
  25.3 0.3 %shard_map.85.refs_0_ = f32[4,96,128]{2,1,0:T(8,128)S(1)} custom-call(bf16[4,96,128]{2,1,0:T(8,128)(2,1)S(1)} %get-tuple-element.31.state_ref.refs_7_, bf16[2,4,3,128,128]{4,3,2,1,0:T(8,128)(2,1)S(1)} %copy-done, bf16[2,1,4,128,128]{4,3,2,1,0:T(8,128)(2,1)S(1)} %copy-done.1, f32[192,8]{1,0:T(8,128)S(1)} %get-tuple-element.23.table_ref.refs_2_, ...), custom_call_target="tpu_custom_call" | custom-call | tf_op jit(solution)/shard_map/pallas_call | solution.py:374
  25.7 0.4 %shard_map.87.refs_0_ = f32[4,96,128]{2,1,0:T(8,128)S(1)} custom-call(bf16[4,96,128]{2,1,0:T(8,128)(2,1)S(1)} %get-tuple-element.35.state_ref.refs_7_, bf16[2,4,3,128,128]{4,3,2,1,0:T(8,128)(2,1)S(1)} %copy-done, bf16[2,1,4,128,128]{4,3,2,1,0:T(8,128)(2,1)S(1)} %copy-done.1, f32[192,8]{1,0:T(8,128)S(1)} %get-tuple-element.23.table_ref.refs_2_, ...), custom_call_target="tpu_custom_call" | custom-call | tf_op jit(solution)/shard_map/pallas_call | solution.py:374
  26.0 0.0 collective-permute-done.11.refs_5_
  26.0 0.0 collective-permute-done.12.refs_6_
  26.1 1.0 %shard_map.88.refs_8_ = bf16[2,192,512]{2,1,0:T(8,128)(2,1)} custom-call(f32[4,96,128]{2,1,0:T(8,128)S(1)} %shard_map.87.refs_0_, bf16[2,1,4,128,128]{4,3,2,1,0:T(8,128)(2,1)S(1)} %copy-done.1, f32[192,8]{1,0:T(8,128)S(1)} %get-tuple-element.23.table_ref.refs_2_, f32[72,128]{1,0:T(8,128)S(1)} %get-tuple-element.24.marks_ref.refs_3_, ...), custom_call_target="tpu_custom_call" | custom-call | tf_op jit(solution)/shard_map/pallas_call | solution.py:422
  27.0 0.0 collective-permute-done.7.refs_4_
  27.0 0.4 %collective-permute-done.8.refs_5_ = bf16[96,128]{1,0:T(8,128)(2,1)S(1)} collective-permute-done((bf16[96,128]{1,0:T(8,128)(2,1)S(1)}, bf16[96,128]{1,0:T(8,128)(2,1)S(1)}, u32[]{:S(2)}, u32[]{:S(2)}) %collective-permute-start.8) | collective-permute-done | bytes 24608 | tf_op jit(solution)/shard_map/ppermute | solution.py:440
  27.5 0.0 collective-permute-done.9.refs_6_
  27.5 0.9 %shard_map.89 = bf16[2,192,512]{2,1,0:T(8,128)(2,1)} custom-call(f32[4,96,128]{2,1,0:T(8,128)S(1)} %shard_map.85.refs_0_, bf16[2,1,4,128,128]{4,3,2,1,0:T(8,128)(2,1)S(1)} %copy-done.1, f32[192,8]{1,0:T(8,128)S(1)} %get-tuple-element.23.table_ref.refs_2_, f32[72,128]{1,0:T(8,128)S(1)} %get-tuple-element.24.marks_ref.refs_3_, ...), custom_call_target="tpu_custom_call", output_to_operand_aliasing={{}: (8, {})} | custom-call | tf_op jit(solution)/shard_map/pallas_call | solution.py:422
  (6 shorter events, 0.0 us)
Async XLA Ops:
  0.0 12.8 %copy-start = (bf16[2,4,3,128,128]{4,3,2,1,0:T(8,128)(2,1)S(1)}, bf16[2,4,3,128,128]{4,3,2,1,0:T(8,128)(2,1)}, u32[]{:S(2)}) copy-start(bf16[2,4,3,128,128]{4,3,2,1,0:T(8,128)(2,1)} %refs_12_.1) | copy-start | bytes 2359300
  0.0 12.8 %copy-start.1 = (bf16[2,1,4,128,128]{4,3,2,1,0:T(8,128)(2,1)S(1)}, bf16[2,1,4,128,128]{4,3,2,1,0:T(8,128)(2,1)}, u32[]{:S(2)}) copy-start(bf16[2,1,4,128,128]{4,3,2,1,0:T(8,128)(2,1)} %refs_1_.5) | copy-start | bytes 786436
  1.1 11.7 %collective-permute-start = (bf16[4,192,128]{2,1,0:T(8,128)(2,1)S(1)}, bf16[4,192,128]{2,1,0:T(8,128)(2,1)S(1)}, u32[]{:S(2)}, u32[]{:S(2)}) collective-permute-start(bf16[4,192,128]{2,1,0:T(8,128)(2,1)S(1)} %get-tuple-element.22.refs_8_), channel_id=1, source_target_pairs={{0,16},{1,17},{2,18},{3,19},{4,20},{5,21},{6,22},{7,23},{8,24},{9,... | collective-permute-start | bytes 589832 | tf_op jit(solution)/shard_map/ppermute | solution.py:440
  1.2 10.2 %collective-permute-start.4 = (bf16[112,128]{1,0:T(8,128)(2,1)S(1)}, bf16[112,128]{1,0:T(8,128)(2,1)S(1)}, u32[]{:S(2)}, u32[]{:S(2)}) collective-permute-start(bf16[112,128]{1,0:T(8,128)(2,1)S(1)} %get-tuple-element.28), channel_id=1, source_target_pairs={{0,24},{1,25},{2,26},{3,27},{4,28},{5,29},{6,30},{7,31},{8,16},{9,... | collective-permute-start | bytes 86024 | tf_op jit(solution)/shard_map/ppermute | solution.py:440
  5.2 8.0 %collective-permute-start.5 = (bf16[112,128]{1,0:T(8,128)(2,1)S(1)}, bf16[112,128]{1,0:T(8,128)(2,1)S(1)}, u32[]{:S(2)}, u32[]{:S(2)}) collective-permute-start(bf16[112,128]{1,0:T(8,128)(2,1)S(1)} %get-tuple-element.29), channel_id=1, source_target_pairs={{0,28},{1,29},{2,30},{3,31},{4,24},{5,25},{6,26},{7,27},{8,20},{9,... | collective-permute-start | bytes 86024 | tf_op jit(solution)/shard_map/ppermute | solution.py:440
  7.5 5.8 %collective-permute-start.6 = (bf16[112,128]{1,0:T(8,128)(2,1)S(1)}, bf16[112,128]{1,0:T(8,128)(2,1)S(1)}, u32[]{:S(2)}, u32[]{:S(2)}) collective-permute-start(bf16[112,128]{1,0:T(8,128)(2,1)S(1)} %get-tuple-element.30), channel_id=1, source_target_pairs={{0,20},{1,21},{2,22},{3,23},{4,16},{5,17},{6,18},{7,19},{8,28},{9,... | collective-permute-start | bytes 86024 | tf_op jit(solution)/shard_map/ppermute | solution.py:440
  7.7 9.1 %collective-permute-start.1 = (bf16[96,128]{1,0:T(8,128)(2,1)S(1)}, bf16[96,128]{1,0:T(8,128)(2,1)S(1)}, u32[]{:S(2)}, u32[]{:S(2)}) collective-permute-start(bf16[96,128]{1,0:T(8,128)(2,1)S(1)} %get-tuple-element.25), channel_id=1, source_target_pairs={{0,24},{1,25},{2,26},{3,27},{4,28},{5,29},{6,30},{7,31},{8,16},{9,... | collective-permute-start | bytes 73736 | tf_op jit(solution)/shard_map/ppermute | solution.py:440
  11.4 6.5 %collective-permute-start.2 = (bf16[96,128]{1,0:T(8,128)(2,1)S(1)}, bf16[96,128]{1,0:T(8,128)(2,1)S(1)}, u32[]{:S(2)}, u32[]{:S(2)}) collective-permute-start(bf16[96,128]{1,0:T(8,128)(2,1)S(1)} %get-tuple-element.26), channel_id=1, source_target_pairs={{0,28},{1,29},{2,30},{3,31},{4,24},{5,25},{6,26},{7,27},{8,20},{9,... | collective-permute-start | bytes 73736 | tf_op jit(solution)/shard_map/ppermute | solution.py:440
  12.8 5.2 %collective-permute-start.3 = (bf16[96,128]{1,0:T(8,128)(2,1)S(1)}, bf16[96,128]{1,0:T(8,128)(2,1)S(1)}, u32[]{:S(2)}, u32[]{:S(2)}) collective-permute-start(bf16[96,128]{1,0:T(8,128)(2,1)S(1)} %get-tuple-element.27), channel_id=1, source_target_pairs={{0,20},{1,21},{2,22},{3,23},{4,16},{5,17},{6,18},{7,19},{8,28},{9,... | collective-permute-start | bytes 73736 | tf_op jit(solution)/shard_map/ppermute | solution.py:440
  13.6 9.7 %collective-permute-start.10 = (bf16[96,128]{1,0:T(8,128)(2,1)S(1)}, bf16[96,128]{1,0:T(8,128)(2,1)S(1)}, u32[]{:S(2)}, u32[]{:S(2)}) collective-permute-start(bf16[96,128]{1,0:T(8,128)(2,1)S(1)} %get-tuple-element.36), channel_id=1, source_target_pairs={{0,1},{1,0},{2,3},{3,2},{4,5},{5,4},{6,7},{7,6},{8,9},{9,8},{10,11... | collective-permute-start | bytes 73736 | tf_op jit(solution)/shard_map/ppermute | solution.py:440
  18.3 8.8 %collective-permute-start.7 = (bf16[96,128]{1,0:T(8,128)(2,1)S(1)}, bf16[96,128]{1,0:T(8,128)(2,1)S(1)}, u32[]{:S(2)}, u32[]{:S(2)}) collective-permute-start(bf16[96,128]{1,0:T(8,128)(2,1)S(1)} %get-tuple-element.32), channel_id=1, source_target_pairs={{0,1},{1,0},{2,3},{3,2},{4,5},{5,4},{6,7},{7,6},{8,9},{9,8},{10,11... | collective-permute-start | bytes 73736 | tf_op jit(solution)/shard_map/ppermute | solution.py:440
  20.4 5.7 %collective-permute-start.11 = (bf16[96,128]{1,0:T(8,128)(2,1)S(1)}, bf16[96,128]{1,0:T(8,128)(2,1)S(1)}, u32[]{:S(2)}, u32[]{:S(2)}) collective-permute-start(bf16[96,128]{1,0:T(8,128)(2,1)S(1)} %get-tuple-element.37), channel_id=1, source_target_pairs={{0,1},{1,0},{2,3},{3,2},{4,5},{5,4},{6,7},{7,6},{8,9},{9,8},{10,11... | collective-permute-start | bytes 73736 | tf_op jit(solution)/shard_map/ppermute | solution.py:440
  20.4 5.7 %collective-permute-start.12 = (bf16[96,128]{1,0:T(8,128)(2,1)S(1)}, bf16[96,128]{1,0:T(8,128)(2,1)S(1)}, u32[]{:S(2)}, u32[]{:S(2)}) collective-permute-start(bf16[96,128]{1,0:T(8,128)(2,1)S(1)} %get-tuple-element.38), channel_id=1, source_target_pairs={{0,1},{1,0},{2,3},{3,2},{4,5},{5,4},{6,7},{7,6},{8,9},{9,8},{10,11... | collective-permute-start | bytes 73736 | tf_op jit(solution)/shard_map/ppermute | solution.py:440
  22.7 4.7 %collective-permute-start.8 = (bf16[96,128]{1,0:T(8,128)(2,1)S(1)}, bf16[96,128]{1,0:T(8,128)(2,1)S(1)}, u32[]{:S(2)}, u32[]{:S(2)}) collective-permute-start(bf16[96,128]{1,0:T(8,128)(2,1)S(1)} %get-tuple-element.33), channel_id=1, source_target_pairs={{0,1},{1,0},{2,3},{3,2},{4,5},{5,4},{6,7},{7,6},{8,9},{9,8},{10,11... | collective-permute-start | bytes 73736 | tf_op jit(solution)/shard_map/ppermute | solution.py:440
  23.3 4.2 %collective-permute-start.9 = (bf16[96,128]{1,0:T(8,128)(2,1)S(1)}, bf16[96,128]{1,0:T(8,128)(2,1)S(1)}, u32[]{:S(2)}, u32[]{:S(2)}) collective-permute-start(bf16[96,128]{1,0:T(8,128)(2,1)S(1)} %get-tuple-element.34), channel_id=1, source_target_pairs={{0,1},{1,0},{2,3},{3,2},{4,5},{5,4},{6,7},{7,6},{8,9},{9,8},{10,11... | collective-permute-start | bytes 73736 | tf_op jit(solution)/shard_map/ppermute | solution.py:440

commit v21 on v19

--- a/solution.py
+++ b/solution.py
@@ -36,15 +36,16 @@
     return lambda i, k: state_ref[cols_ref[k, i]]
 
 
-def own_sum(i, state_ref, jac_ref, near, table, step, hit=None):
-    blocks, _, width = state_ref.shape
-    if hit is None:
-        hit = hits(table, i, blocks, width)
+def products(i, state_ref, jac_ref, near):
     kinds = jac_ref.shape[1]
     rows = [state_ref[i]] + [near(i, k) for k in range(kinds - 1)]
     row_blocks = [jac_ref[i, k] for k in range(kinds)]
-    total = times_transposed(jnp.concatenate(rows, axis=1), jnp.concatenate(row_blocks, axis=1))
-    return total + injected(table, step, hit)
+    return times_transposed(jnp.concatenate(rows, axis=1), jnp.concatenate(row_blocks, axis=1))
+
+
+def own_sum(i, state_ref, jac_ref, near, table, step):
+    blocks, _, width = state_ref.shape
+    return products(i, state_ref, jac_ref, near) + injected(table, step, hits(table, i, blocks, width))
 
 
 def picked(blocks, marks):
@@ -147,20 +148,28 @@
     @pl.when(here)
     def _():
         table = table_ref[...]
-        hit = [hits(table, i, blocks, width) for i in range(blocks)]
+
+        def spread(column):
+            return jnp.broadcast_to(column, (cols, width))
+
+        lane = lax.broadcasted_iota(jnp.int32, (cols, width), 1).astype(jnp.float32)
+        place = spread(table[:, STATE : STATE + 1] - (me * blocks * width).astype(jnp.float32)) - lane
+        gain = spread(table[:, GAIN : GAIN + 1])
+        later_gain = spread(table[:, GAIN + 1 : GAIN + 2])
+        hit = [place == float(i * width) for i in range(blocks)]
         for i in range(blocks):
-            first_ref[i] = injected(table, 0, hit[i]).astype(first_ref.dtype)
-        lane = lax.broadcasted_iota(jnp.int32, (cols, width), 1).astype(jnp.float32)
-        shot = jnp.where(lane == table[:, LANE : LANE + 1], table[:, GAIN : GAIN + 1], 0.0)
+            first_ref[i] = jnp.where(hit[i], gain, 0.0).astype(first_ref.dtype)
         away, block = table[:, AWAY : AWAY + 1], table[:, BLOCK : BLOCK + 1]
         for load in loads[2:6]:
             load.wait()
         mine = jnp.logical_or(away != 0.0, block == send_ref[0, me].astype(jnp.float32))
-        shot = jnp.where(mine, shot, 0.0)
+        shot_lane = spread(jnp.where(mine, table[:, LANE : LANE + 1], -1.0))
+        shot = jnp.where(lane == shot_lane, gain, 0.0)
         live = recv = jnp.zeros_like(away)
         for d in range(n):
             live = jnp.where(away == float(d), live_ref[0, me ^ d].astype(jnp.float32), live)
             recv = jnp.where(away == float(d), recv_ref[0, me ^ d].astype(jnp.float32), recv)
+        away, live, recv = spread(away), spread(live), spread(recv)
         sent = [jnp.where(away == float(d), shot, 0.0).astype(first_ref.dtype) for d in range(n)]
         loads[1].wait()
         ifaces = jnp.concatenate([iface_ref[me ^ d] for d in range(n)], axis=1)
@@ -168,7 +177,8 @@
         coupled = jnp.where(lane < live, coupled, 0.0)
         loads[0].wait()
         for i in range(blocks):
-            own = own_sum(i, first_ref, jac_ref, near_by(first_ref, cols_ref), table, 1, hit[i])
+            own = products(i, first_ref, jac_ref, near_by(first_ref, cols_ref))
+            own += jnp.where(hit[i], later_gain, 0.0)
             state_ref[i] = (own + jnp.where(recv == float(i), coupled, 0.0)).astype(state_ref.dtype)
         for d in range(1, n):
             outgoing[d - 1][pl.ds(0, cols)] = state_ref[send_ref[0, me ^ d]]
@@ -263,7 +273,7 @@
 
 
 def exchange_order(n, handed):
-    return [*range(n // 2, n), *range(n // 2 - 1, 0, -1)] if handed else list(range(n - 1, 0, -1))
+    return [*range(n // 2, n), *range(n // 2 - 1, 0, -1)] if handed else list(range(1, n))
 
 
 def by_distance(refs, handed):

time: 22 us -> 23.2 us (1.055)
  waiting for transfers between devices: 7.21 us -> 8.41 us
    ppermute x7, waiting for transfers between devices: 7.21 us -> 8.41 us  [swap(): return lax.ppermute(block, ('tm', 'net', 'cols'), pairs)]
where the time goes in v21:
time: 23.2 us; the launch traced here: 23 us
  starting transfers between devices  11.1 us (48%)
  waiting for transfers between devices  8.41 us (36%)
  Pallas kernels  3.49 us (15%)
    ppermute x7, starting transfers between devices, swap(): return lax.ppermute(block, ('tm', 'net', 'cols'), pairs)  11.1 us
    ppermute x7, waiting for transfers between devices, swap(): return lax.ppermute(block, ('tm', 'net', 'cols'), pairs)  8.41 us
    pallas_call x1, Pallas kernels, local(): pl.pallas_call(second_kernel, out_shape=[f32((cols, table_rows)), f32((ma...  1.11 us
    pallas_call x1, Pallas kernels, close(): pl.pallas_call(functools.partial(close_kernel, step, section, firsts, sen...  1.03 us
    pallas_call x2, Pallas kernels, own(): pl.pallas_call(functools.partial(own_kernel, step), out_shape=f32(whole.s...  0.9 us
  transfers between devices with their start and end apart: 7, of which 5 were waited for; matrix products, arithmetic and copies ran while one was open for 0% of the time, Pallas kernels for 4%

profile of v21, /device:TPU:4, one launch (start us, length us, event | category | flops | bytes accessed | tf_op | source)
XLA Modules:
  0.0 23.0 jit_solution(9616790086026092614)
XLA Ops:
  0.0 0.0 copy-start
  0.0 0.0 copy-start.1
  0.0 1.1 %shard_map.82 = (f32[192,8]{1,0:T(8,128)S(1)}, f32[72,128]{1,0:T(8,128)S(1)}, bf16[4,192,128]{2,1,0:T(8,128)(2,1)S(1)}, bf16[208,128]{1,0:T(8,128)(2,1)S(1)}, bf...) custom-call(bf16[2,4,3,128,128]{4,3,2,1,0:T(8,128)(2,1)} %refs_12_.1, bf16[2,1,4,128,128]{4,3,2,1,0:T(8,128)(2,1)} %refs_1_.3, ...), custom_call_target="tpu_custom_call" | custom-call | tf_op jit(solution)/shard_map/pallas_call | solution.py:361
  1.1 0.1 collective-permute-start
  1.2 4.0 %collective-permute-start.1 = (bf16[208,128]{1,0:T(8,128)(2,1)S(1)}, bf16[208,128]{1,0:T(8,128)(2,1)S(1)}, u32[]{:S(2)}, u32[]{:S(2)}) collective-permute-start(bf16[208,128]{1,0:T(8,128)(2,1)S(1)} %get-tuple-element.18), channel_id=1, source_target_pairs={{0,24},{1,25},{2,26},{3,27},{4,28},{5,29},{6,30},{7,31},{8,16},{9,... | collective-permute-start | bytes 159752 | tf_op jit(solution)/shard_map/ppermute | solution.py:439
  5.2 2.3 %collective-permute-start.2 = (bf16[208,128]{1,0:T(8,128)(2,1)S(1)}, bf16[208,128]{1,0:T(8,128)(2,1)S(1)}, u32[]{:S(2)}, u32[]{:S(2)}) collective-permute-start(bf16[208,128]{1,0:T(8,128)(2,1)S(1)} %get-tuple-element.19), channel_id=1, source_target_pairs={{0,28},{1,29},{2,30},{3,31},{4,24},{5,25},{6,26},{7,27},{8,20},{9,... | collective-permute-start | bytes 159752 | tf_op jit(solution)/shard_map/ppermute | solution.py:439
  7.5 0.2 collective-permute-start.3
  7.8 1.2 %collective-permute-done.state_ref = bf16[4,192,128]{2,1,0:T(8,128)(2,1)S(1)} collective-permute-done((bf16[4,192,128]{2,1,0:T(8,128)(2,1)S(1)}, bf16[4,192,128]{2,1,0:T(8,128)(2,1)S(1)}, u32[]{:S(2)}, u32[]{:S(2)}) %collective-permute-start) | collective-permute-done | bytes 196640 | tf_op jit(solution)/shard_map/ppermute | solution.py:439
  9.0 0.0 copy-done
  9.0 0.0 copy-done.1
  9.0 0.5 %shard_map.83.z_ref = f32[4,192,128]{2,1,0:T(8,128)S(1)} custom-call(bf16[4,192,128]{2,1,0:T(8,128)(2,1)S(1)} %collective-permute-done.state_ref, bf16[2,4,3,128,128]{4,3,2,1,0:T(8,128)(2,1)S(1)} %copy-done, bf16[2,1,4,128,128]{4,3,2,1,0:T(8,128)(2,1)S(1)} %copy-done.1, f32[192,8]{1,0:T(8,128)S(1)} %get-tuple-element.16.table_ref.refs_2_, ...), custom_call_target="tpu_custom_call" | custom-call | tf_op jit(solution)/shard_map/pallas_call | solution.py:379
  9.4 0.0 collective-permute-done.1.refs_0_.refs_10_
  9.5 2.9 %collective-permute-done.2.refs_1_.refs_11_ = bf16[208,128]{1,0:T(8,128)(2,1)S(1)} collective-permute-done((bf16[208,128]{1,0:T(8,128)(2,1)S(1)}, bf16[208,128]{1,0:T(8,128)(2,1)S(1)}, u32[]{:S(2)}, u32[]{:S(2)}) %collective-permute-start.2) | collective-permute-done | bytes 53280 | tf_op jit(solution)/shard_map/ppermute | solution.py:439
  12.4 0.5 %collective-permute-done.3.refs_2_.refs_9_ = bf16[208,128]{1,0:T(8,128)(2,1)S(1)} collective-permute-done((bf16[208,128]{1,0:T(8,128)(2,1)S(1)}, bf16[208,128]{1,0:T(8,128)(2,1)S(1)}, u32[]{:S(2)}, u32[]{:S(2)}) %collective-permute-start.3) | collective-permute-done | bytes 53280 | tf_op jit(solution)/shard_map/ppermute | solution.py:439
  12.8 0.4 %shard_map.84 = (bf16[4,192,128]{2,1,0:T(8,128)(2,1)S(1)}, bf16[192,128]{1,0:T(8,128)(2,1)S(1)}, bf16[192,128]{1,0:T(8,128)(2,1)S(1)}, bf16[192,128]{1,0:T(8,128)(2,1)S(1)}) custom-call(f32[4,192,128]{2,1,0:T(8,128)S(1)} %shard_map.83.z_ref, bf16[2,1,4,128,128]{4,3,2,1,0:T(8,128)(2,1)S(1)} %copy-done.1, f32[192,8]{1,0:T(8,128)S(1)} %get-tuple-element.16.table_ref.refs_2_, ...), custom_call_target="tpu_custom_call" | custom-call | tf_op jit(solution)/shard_map/pallas_call | solution.py:388
  13.3 0.6 %collective-permute-start.4 = (bf16[192,128]{1,0:T(8,128)(2,1)S(1)}, bf16[192,128]{1,0:T(8,128)(2,1)S(1)}, u32[]{:S(2)}, u32[]{:S(2)}) collective-permute-start(bf16[192,128]{1,0:T(8,128)(2,1)S(1)} %get-tuple-element.22), channel_id=1, source_target_pairs={{0,1},{1,0},{2,3},{3,2},{4,5},{5,4},{6,7},{7,6},{8,9},{9,8},{10,11... | collective-permute-start | bytes 147464 | tf_op jit(solution)/shard_map/ppermute | solution.py:439
  13.9 2.3 %collective-permute-start.5 = (bf16[192,128]{1,0:T(8,128)(2,1)S(1)}, bf16[192,128]{1,0:T(8,128)(2,1)S(1)}, u32[]{:S(2)}, u32[]{:S(2)}) collective-permute-start(bf16[192,128]{1,0:T(8,128)(2,1)S(1)} %get-tuple-element.23), channel_id=1, source_target_pairs={{0,1},{1,0},{2,3},{3,2},{4,5},{5,4},{6,7},{7,6},{8,9},{9,8},{10,11... | collective-permute-start | bytes 147464 | tf_op jit(solution)/shard_map/ppermute | solution.py:439
  16.1 1.6 %collective-permute-start.6 = (bf16[192,128]{1,0:T(8,128)(2,1)S(1)}, bf16[192,128]{1,0:T(8,128)(2,1)S(1)}, u32[]{:S(2)}, u32[]{:S(2)}) collective-permute-start(bf16[192,128]{1,0:T(8,128)(2,1)S(1)} %get-tuple-element.24), channel_id=1, source_target_pairs={{0,1},{1,0},{2,3},{3,2},{4,5},{5,4},{6,7},{7,6},{8,9},{9,8},{10,11... | collective-permute-start | bytes 147464 | tf_op jit(solution)/shard_map/ppermute | solution.py:439
  17.7 0.4 %shard_map.85.refs_0_ = f32[4,192,128]{2,1,0:T(8,128)S(1)} custom-call(bf16[4,192,128]{2,1,0:T(8,128)(2,1)S(1)} %get-tuple-element.21.state_ref.refs_7_, bf16[2,4,3,128,128]{4,3,2,1,0:T(8,128)(2,1)S(1)} %copy-done, bf16[2,1,4,128,128]{4,3,2,1,0:T(8,128)(2,1)S(1)} %copy-done.1, f32[192,8]{1,0:T(8,128)S(1)} %get-tuple-element.16.table_ref.refs_2_, ...), custom_call_target="tpu_custom_call" | custom-call | tf_op jit(solution)/shard_map/pallas_call | solution.py:379
  18.2 0.0 collective-permute-done.4.refs_4_
  18.2 0.6 %collective-permute-done.5.refs_5_ = bf16[192,128]{1,0:T(8,128)(2,1)S(1)} collective-permute-done((bf16[192,128]{1,0:T(8,128)(2,1)S(1)}, bf16[192,128]{1,0:T(8,128)(2,1)S(1)}, u32[]{:S(2)}, u32[]{:S(2)}) %collective-permute-start.5) | collective-permute-done | bytes 49184 | tf_op jit(solution)/shard_map/ppermute | solution.py:439
  18.9 3.2 %collective-permute-done.6.refs_6_ = bf16[192,128]{1,0:T(8,128)(2,1)S(1)} collective-permute-done((bf16[192,128]{1,0:T(8,128)(2,1)S(1)}, bf16[192,128]{1,0:T(8,128)(2,1)S(1)}, u32[]{:S(2)}, u32[]{:S(2)}) %collective-permute-start.6) | collective-permute-done | bytes 49184 | tf_op jit(solution)/shard_map/ppermute | solution.py:439
  22.0 1.0 %shard_map.86 = bf16[2,192,512]{2,1,0:T(8,128)(2,1)} custom-call(f32[4,192,128]{2,1,0:T(8,128)S(1)} %shard_map.85.refs_0_, bf16[2,1,4,128,128]{4,3,2,1,0:T(8,128)(2,1)S(1)} %copy-done.1, f32[192,8]{1,0:T(8,128)S(1)} %get-tuple-element.16.table_ref.refs_2_, f32[72,128]{1,0:T(8,128)S(1)} %get-tuple-element.17.marks_ref.refs_3_, ...), custom_call_target="tpu_custom_call" | custom-call | tf_op jit(solution)/shard_map/pallas_call | solution.py:421
Async XLA Ops:
  0.0 9.0 %copy-start = (bf16[2,4,3,128,128]{4,3,2,1,0:T(8,128)(2,1)S(1)}, bf16[2,4,3,128,128]{4,3,2,1,0:T(8,128)(2,1)}, u32[]{:S(2)}) copy-start(bf16[2,4,3,128,128]{4,3,2,1,0:T(8,128)(2,1)} %refs_12_.1) | copy-start | bytes 2359300
  0.0 9.0 %copy-start.1 = (bf16[2,1,4,128,128]{4,3,2,1,0:T(8,128)(2,1)S(1)}, bf16[2,1,4,128,128]{4,3,2,1,0:T(8,128)(2,1)}, u32[]{:S(2)}) copy-start(bf16[2,1,4,128,128]{4,3,2,1,0:T(8,128)(2,1)} %refs_1_.3) | copy-start | bytes 786436
  1.1 7.8 %collective-permute-start = (bf16[4,192,128]{2,1,0:T(8,128)(2,1)S(1)}, bf16[4,192,128]{2,1,0:T(8,128)(2,1)S(1)}, u32[]{:S(2)}, u32[]{:S(2)}) collective-permute-start(bf16[4,192,128]{2,1,0:T(8,128)(2,1)S(1)} %get-tuple-element.15.refs_8_), channel_id=1, source_target_pairs={{0,16},{1,17},{2,18},{3,19},{4,20},{5,21},{6,22},{7,23},{8,24},{9,... | collective-permute-start | bytes 589832 | tf_op jit(solution)/shard_map/ppermute | solution.py:439
  1.2 8.2 %collective-permute-start.1 = (bf16[208,128]{1,0:T(8,128)(2,1)S(1)}, bf16[208,128]{1,0:T(8,128)(2,1)S(1)}, u32[]{:S(2)}, u32[]{:S(2)}) collective-permute-start(bf16[208,128]{1,0:T(8,128)(2,1)S(1)} %get-tuple-element.18), channel_id=1, source_target_pairs={{0,24},{1,25},{2,26},{3,27},{4,28},{5,29},{6,30},{7,31},{8,16},{9,... | collective-permute-start | bytes 159752 | tf_op jit(solution)/shard_map/ppermute | solution.py:439
  5.2 7.1 %collective-permute-start.2 = (bf16[208,128]{1,0:T(8,128)(2,1)S(1)}, bf16[208,128]{1,0:T(8,128)(2,1)S(1)}, u32[]{:S(2)}, u32[]{:S(2)}) collective-permute-start(bf16[208,128]{1,0:T(8,128)(2,1)S(1)} %get-tuple-element.19), channel_id=1, source_target_pairs={{0,28},{1,29},{2,30},{3,31},{4,24},{5,25},{6,26},{7,27},{8,20},{9,... | collective-permute-start | bytes 159752 | tf_op jit(solution)/shard_map/ppermute | solution.py:439
  7.5 5.3 %collective-permute-start.3 = (bf16[208,128]{1,0:T(8,128)(2,1)S(1)}, bf16[208,128]{1,0:T(8,128)(2,1)S(1)}, u32[]{:S(2)}, u32[]{:S(2)}) collective-permute-start(bf16[208,128]{1,0:T(8,128)(2,1)S(1)} %get-tuple-element.20), channel_id=1, source_target_pairs={{0,20},{1,21},{2,22},{3,23},{4,16},{5,17},{6,18},{7,19},{8,28},{9,... | collective-permute-start | bytes 159752 | tf_op jit(solution)/shard_map/ppermute | solution.py:439
  13.3 4.9 %collective-permute-start.4 = (bf16[192,128]{1,0:T(8,128)(2,1)S(1)}, bf16[192,128]{1,0:T(8,128)(2,1)S(1)}, u32[]{:S(2)}, u32[]{:S(2)}) collective-permute-start(bf16[192,128]{1,0:T(8,128)(2,1)S(1)} %get-tuple-element.22), channel_id=1, source_target_pairs={{0,1},{1,0},{2,3},{3,2},{4,5},{5,4},{6,7},{7,6},{8,9},{9,8},{10,11... | collective-permute-start | bytes 147464 | tf_op jit(solution)/shard_map/ppermute | solution.py:439
  13.9 5.0 %collective-permute-start.5 = (bf16[192,128]{1,0:T(8,128)(2,1)S(1)}, bf16[192,128]{1,0:T(8,128)(2,1)S(1)}, u32[]{:S(2)}, u32[]{:S(2)}) collective-permute-start(bf16[192,128]{1,0:T(8,128)(2,1)S(1)} %get-tuple-element.23), channel_id=1, source_target_pairs={{0,1},{1,0},{2,3},{3,2},{4,5},{5,4},{6,7},{7,6},{8,9},{9,8},{10,11... | collective-permute-start | bytes 147464 | tf_op jit(solution)/shard_map/ppermute | solution.py:439
  16.1 5.9 %collective-permute-start.6 = (bf16[192,128]{1,0:T(8,128)(2,1)S(1)}, bf16[192,128]{1,0:T(8,128)(2,1)S(1)}, u32[]{:S(2)}, u32[]{:S(2)}) collective-permute-start(bf16[192,128]{1,0:T(8,128)(2,1)S(1)} %get-tuple-element.24), channel_id=1, source_target_pairs={{0,1},{1,0},{2,3},{3,2},{4,5},{5,4},{6,7},{7,6},{8,9},{9,8},{10,11... | collective-permute-start | bytes 147464 | tf_op jit(solution)/shard_map/ppermute | solution.py:439

commit v22 on v21

--- a/solution.py
+++ b/solution.py
@@ -273,7 +273,7 @@
 
 
 def exchange_order(n, handed):
-    return [*range(n // 2, n), *range(n // 2 - 1, 0, -1)] if handed else list(range(1, n))
+    return [*range(n // 2, n), *range(n // 2 - 1, 0, -1)] if handed else [1, *range(n - 1, 1, -1)]
 
 
 def by_distance(refs, handed):

time: 23.2 us -> 22.8 us (0.983)
  starting transfers between devices: 11.1 us -> 10.2 us
  waiting for transfers between devices: 8.41 us -> 8.94 us
    ppermute x7, starting transfers between devices: 11.1 us -> 10.2 us  [swap(): return lax.ppermute(block, ('tm', 'net', 'cols'), pairs)]
    ppermute x7, waiting for transfers between devices: 8.41 us -> 8.94 us  [swap(): return lax.ppermute(block, ('tm', 'net', 'cols'), pairs)]
  transfers between devices with their start and end apart: 7 -> 7, of which waited for: 5 -> 6; matrix products, arithmetic and copies ran while one was open for 0% -> 0% of each run, Pallas kernels for 4% -> 4%
where the time goes in v22:
time: 22.8 us; the launch traced here: 22.7 us
  starting transfers between devices  10.2 us (45%)
  waiting for transfers between devices  8.94 us (39%)
  Pallas kernels  3.49 us (15%)
    ppermute x7, starting transfers between devices, swap(): return lax.ppermute(block, ('tm', 'net', 'cols'), pairs)  10.2 us
    ppermute x7, waiting for transfers between devices, swap(): return lax.ppermute(block, ('tm', 'net', 'cols'), pairs)  8.94 us
    pallas_call x1, Pallas kernels, local(): pl.pallas_call(second_kernel, out_shape=[f32((cols, table_rows)), f32((ma...  1.11 us
    pallas_call x1, Pallas kernels, close(): pl.pallas_call(functools.partial(close_kernel, step, section, firsts, sen...  1.03 us
    pallas_call x2, Pallas kernels, own(): pl.pallas_call(functools.partial(own_kernel, step), out_shape=f32(whole.s...  0.91 us
  transfers between devices with their start and end apart: 7, of which 6 were waited for; matrix products, arithmetic and copies ran while one was open for 0% of the time, Pallas kernels for 4%

profile of v22, /device:TPU:4, one launch (start us, length us, event | category | flops | bytes accessed | tf_op | source)
XLA Modules:
  0.0 22.7 jit_solution(14254959502451284828)
XLA Ops:
  0.0 0.0 copy-start
  0.0 0.0 copy-start.1
  0.0 1.1 %shard_map.82 = (f32[192,8]{1,0:T(8,128)S(1)}, f32[72,128]{1,0:T(8,128)S(1)}, bf16[4,192,128]{2,1,0:T(8,128)(2,1)S(1)}, bf16[208,128]{1,0:T(8,128)(2,1)S(1)}, bf...) custom-call(bf16[2,4,3,128,128]{4,3,2,1,0:T(8,128)(2,1)} %refs_12_.1, bf16[2,1,4,128,128]{4,3,2,1,0:T(8,128)(2,1)} %refs_1_.3, ...), custom_call_target="tpu_custom_call" | custom-call | tf_op jit(solution)/shard_map/pallas_call | solution.py:361
  1.1 0.1 collective-permute-start
  1.2 4.0 %collective-permute-start.1 = (bf16[208,128]{1,0:T(8,128)(2,1)S(1)}, bf16[208,128]{1,0:T(8,128)(2,1)S(1)}, u32[]{:S(2)}, u32[]{:S(2)}) collective-permute-start(bf16[208,128]{1,0:T(8,128)(2,1)S(1)} %get-tuple-element.18), channel_id=1, source_target_pairs={{0,24},{1,25},{2,26},{3,27},{4,28},{5,29},{6,30},{7,31},{8,16},{9,... | collective-permute-start | bytes 159752 | tf_op jit(solution)/shard_map/ppermute | solution.py:439
  5.2 2.3 %collective-permute-start.2 = (bf16[208,128]{1,0:T(8,128)(2,1)S(1)}, bf16[208,128]{1,0:T(8,128)(2,1)S(1)}, u32[]{:S(2)}, u32[]{:S(2)}) collective-permute-start(bf16[208,128]{1,0:T(8,128)(2,1)S(1)} %get-tuple-element.19), channel_id=1, source_target_pairs={{0,28},{1,29},{2,30},{3,31},{4,24},{5,25},{6,26},{7,27},{8,20},{9,... | collective-permute-start | bytes 159752 | tf_op jit(solution)/shard_map/ppermute | solution.py:439
  7.5 0.2 %collective-permute-start.3 = (bf16[208,128]{1,0:T(8,128)(2,1)S(1)}, bf16[208,128]{1,0:T(8,128)(2,1)S(1)}, u32[]{:S(2)}, u32[]{:S(2)}) collective-permute-start(bf16[208,128]{1,0:T(8,128)(2,1)S(1)} %get-tuple-element.20), channel_id=1, source_target_pairs={{0,20},{1,21},{2,22},{3,23},{4,16},{5,17},{6,18},{7,19},{8,28},{9,... | collective-permute-start | bytes 159752 | tf_op jit(solution)/shard_map/ppermute | solution.py:439
  7.8 1.2 %collective-permute-done.state_ref = bf16[4,192,128]{2,1,0:T(8,128)(2,1)S(1)} collective-permute-done((bf16[4,192,128]{2,1,0:T(8,128)(2,1)S(1)}, bf16[4,192,128]{2,1,0:T(8,128)(2,1)S(1)}, u32[]{:S(2)}, u32[]{:S(2)}) %collective-permute-start) | collective-permute-done | bytes 196640 | tf_op jit(solution)/shard_map/ppermute | solution.py:439
  9.0 0.0 copy-done
  9.0 0.0 copy-done.1
  9.0 0.5 %shard_map.83.z_ref = f32[4,192,128]{2,1,0:T(8,128)S(1)} custom-call(bf16[4,192,128]{2,1,0:T(8,128)(2,1)S(1)} %collective-permute-done.state_ref, bf16[2,4,3,128,128]{4,3,2,1,0:T(8,128)(2,1)S(1)} %copy-done, bf16[2,1,4,128,128]{4,3,2,1,0:T(8,128)(2,1)S(1)} %copy-done.1, f32[192,8]{1,0:T(8,128)S(1)} %get-tuple-element.16.table_ref.refs_2_, ...), custom_call_target="tpu_custom_call" | custom-call | tf_op jit(solution)/shard_map/pallas_call | solution.py:379
  9.4 0.0 collective-permute-done.1.refs_0_.refs_10_
  9.5 2.9 %collective-permute-done.2.refs_1_.refs_11_ = bf16[208,128]{1,0:T(8,128)(2,1)S(1)} collective-permute-done((bf16[208,128]{1,0:T(8,128)(2,1)S(1)}, bf16[208,128]{1,0:T(8,128)(2,1)S(1)}, u32[]{:S(2)}, u32[]{:S(2)}) %collective-permute-start.2) | collective-permute-done | bytes 53280 | tf_op jit(solution)/shard_map/ppermute | solution.py:439
  12.4 0.5 %collective-permute-done.3.refs_2_.refs_9_ = bf16[208,128]{1,0:T(8,128)(2,1)S(1)} collective-permute-done((bf16[208,128]{1,0:T(8,128)(2,1)S(1)}, bf16[208,128]{1,0:T(8,128)(2,1)S(1)}, u32[]{:S(2)}, u32[]{:S(2)}) %collective-permute-start.3) | collective-permute-done | bytes 53280 | tf_op jit(solution)/shard_map/ppermute | solution.py:439
  12.8 0.4 %shard_map.84 = (bf16[4,192,128]{2,1,0:T(8,128)(2,1)S(1)}, bf16[192,128]{1,0:T(8,128)(2,1)S(1)}, bf16[192,128]{1,0:T(8,128)(2,1)S(1)}, bf16[192,128]{1,0:T(8,128)(2,1)S(1)}) custom-call(f32[4,192,128]{2,1,0:T(8,128)S(1)} %shard_map.83.z_ref, bf16[2,1,4,128,128]{4,3,2,1,0:T(8,128)(2,1)S(1)} %copy-done.1, f32[192,8]{1,0:T(8,128)S(1)} %get-tuple-element.16.table_ref.refs_2_, ...), custom_call_target="tpu_custom_call" | custom-call | tf_op jit(solution)/shard_map/pallas_call | solution.py:388
  13.3 0.6 %collective-permute-start.4 = (bf16[192,128]{1,0:T(8,128)(2,1)S(1)}, bf16[192,128]{1,0:T(8,128)(2,1)S(1)}, u32[]{:S(2)}, u32[]{:S(2)}) collective-permute-start(bf16[192,128]{1,0:T(8,128)(2,1)S(1)} %get-tuple-element.22), channel_id=1, source_target_pairs={{0,1},{1,0},{2,3},{3,2},{4,5},{5,4},{6,7},{7,6},{8,9},{9,8},{10,11... | collective-permute-start | bytes 147464 | tf_op jit(solution)/shard_map/ppermute | solution.py:439
  13.9 2.5 %collective-permute-start.5 = (bf16[192,128]{1,0:T(8,128)(2,1)S(1)}, bf16[192,128]{1,0:T(8,128)(2,1)S(1)}, u32[]{:S(2)}, u32[]{:S(2)}) collective-permute-start(bf16[192,128]{1,0:T(8,128)(2,1)S(1)} %get-tuple-element.23), channel_id=1, source_target_pairs={{0,1},{1,0},{2,3},{3,2},{4,5},{5,4},{6,7},{7,6},{8,9},{9,8},{10,11... | collective-permute-start | bytes 147464 | tf_op jit(solution)/shard_map/ppermute | solution.py:439
  16.3 0.5 %collective-permute-start.6 = (bf16[192,128]{1,0:T(8,128)(2,1)S(1)}, bf16[192,128]{1,0:T(8,128)(2,1)S(1)}, u32[]{:S(2)}, u32[]{:S(2)}) collective-permute-start(bf16[192,128]{1,0:T(8,128)(2,1)S(1)} %get-tuple-element.24), channel_id=1, source_target_pairs={{0,1},{1,0},{2,3},{3,2},{4,5},{5,4},{6,7},{7,6},{8,9},{9,8},{10,11... | collective-permute-start | bytes 147464 | tf_op jit(solution)/shard_map/ppermute | solution.py:439
  16.8 0.4 %shard_map.85.refs_0_ = f32[4,192,128]{2,1,0:T(8,128)S(1)} custom-call(bf16[4,192,128]{2,1,0:T(8,128)(2,1)S(1)} %get-tuple-element.21.state_ref.refs_7_, bf16[2,4,3,128,128]{4,3,2,1,0:T(8,128)(2,1)S(1)} %copy-done, bf16[2,1,4,128,128]{4,3,2,1,0:T(8,128)(2,1)S(1)} %copy-done.1, f32[192,8]{1,0:T(8,128)S(1)} %get-tuple-element.16.table_ref.refs_2_, ...), custom_call_target="tpu_custom_call" | custom-call | tf_op jit(solution)/shard_map/pallas_call | solution.py:379
  17.3 0.2 collective-permute-done.4.refs_4_
  17.5 2.2 %collective-permute-done.5.refs_5_ = bf16[192,128]{1,0:T(8,128)(2,1)S(1)} collective-permute-done((bf16[192,128]{1,0:T(8,128)(2,1)S(1)}, bf16[192,128]{1,0:T(8,128)(2,1)S(1)}, u32[]{:S(2)}, u32[]{:S(2)}) %collective-permute-start.5) | collective-permute-done | bytes 49184 | tf_op jit(solution)/shard_map/ppermute | solution.py:439
  19.8 1.9 %collective-permute-done.6.refs_6_ = bf16[192,128]{1,0:T(8,128)(2,1)S(1)} collective-permute-done((bf16[192,128]{1,0:T(8,128)(2,1)S(1)}, bf16[192,128]{1,0:T(8,128)(2,1)S(1)}, u32[]{:S(2)}, u32[]{:S(2)}) %collective-permute-start.6) | collective-permute-done | bytes 49184 | tf_op jit(solution)/shard_map/ppermute | solution.py:439
  21.6 1.0 %shard_map.86 = bf16[2,192,512]{2,1,0:T(8,128)(2,1)} custom-call(f32[4,192,128]{2,1,0:T(8,128)S(1)} %shard_map.85.refs_0_, bf16[2,1,4,128,128]{4,3,2,1,0:T(8,128)(2,1)S(1)} %copy-done.1, f32[192,8]{1,0:T(8,128)S(1)} %get-tuple-element.16.table_ref.refs_2_, f32[72,128]{1,0:T(8,128)S(1)} %get-tuple-element.17.marks_ref.refs_3_, ...), custom_call_target="tpu_custom_call" | custom-call | tf_op jit(solution)/shard_map/pallas_call | solution.py:421
Async XLA Ops:
  0.0 9.0 %copy-start = (bf16[2,4,3,128,128]{4,3,2,1,0:T(8,128)(2,1)S(1)}, bf16[2,4,3,128,128]{4,3,2,1,0:T(8,128)(2,1)}, u32[]{:S(2)}) copy-start(bf16[2,4,3,128,128]{4,3,2,1,0:T(8,128)(2,1)} %refs_12_.1) | copy-start | bytes 2359300
  0.0 9.0 %copy-start.1 = (bf16[2,1,4,128,128]{4,3,2,1,0:T(8,128)(2,1)S(1)}, bf16[2,1,4,128,128]{4,3,2,1,0:T(8,128)(2,1)}, u32[]{:S(2)}) copy-start(bf16[2,1,4,128,128]{4,3,2,1,0:T(8,128)(2,1)} %refs_1_.3) | copy-start | bytes 786436
  1.1 7.8 %collective-permute-start = (bf16[4,192,128]{2,1,0:T(8,128)(2,1)S(1)}, bf16[4,192,128]{2,1,0:T(8,128)(2,1)S(1)}, u32[]{:S(2)}, u32[]{:S(2)}) collective-permute-start(bf16[4,192,128]{2,1,0:T(8,128)(2,1)S(1)} %get-tuple-element.15.refs_8_), channel_id=1, source_target_pairs={{0,16},{1,17},{2,18},{3,19},{4,20},{5,21},{6,22},{7,23},{8,24},{9,... | collective-permute-start | bytes 589832 | tf_op jit(solution)/shard_map/ppermute | solution.py:439
  1.2 8.2 %collective-permute-start.1 = (bf16[208,128]{1,0:T(8,128)(2,1)S(1)}, bf16[208,128]{1,0:T(8,128)(2,1)S(1)}, u32[]{:S(2)}, u32[]{:S(2)}) collective-permute-start(bf16[208,128]{1,0:T(8,128)(2,1)S(1)} %get-tuple-element.18), channel_id=1, source_target_pairs={{0,24},{1,25},{2,26},{3,27},{4,28},{5,29},{6,30},{7,31},{8,16},{9,... | collective-permute-start | bytes 159752 | tf_op jit(solution)/shard_map/ppermute | solution.py:439
  5.2 7.1 %collective-permute-start.2 = (bf16[208,128]{1,0:T(8,128)(2,1)S(1)}, bf16[208,128]{1,0:T(8,128)(2,1)S(1)}, u32[]{:S(2)}, u32[]{:S(2)}) collective-permute-start(bf16[208,128]{1,0:T(8,128)(2,1)S(1)} %get-tuple-element.19), channel_id=1, source_target_pairs={{0,28},{1,29},{2,30},{3,31},{4,24},{5,25},{6,26},{7,27},{8,20},{9,... | collective-permute-start | bytes 159752 | tf_op jit(solution)/shard_map/ppermute | solution.py:439
  7.5 5.3 %collective-permute-start.3 = (bf16[208,128]{1,0:T(8,128)(2,1)S(1)}, bf16[208,128]{1,0:T(8,128)(2,1)S(1)}, u32[]{:S(2)}, u32[]{:S(2)}) collective-permute-start(bf16[208,128]{1,0:T(8,128)(2,1)S(1)} %get-tuple-element.20), channel_id=1, source_target_pairs={{0,20},{1,21},{2,22},{3,23},{4,16},{5,17},{6,18},{7,19},{8,28},{9,... | collective-permute-start | bytes 159752 | tf_op jit(solution)/shard_map/ppermute | solution.py:439
  13.3 4.2 %collective-permute-start.4 = (bf16[192,128]{1,0:T(8,128)(2,1)S(1)}, bf16[192,128]{1,0:T(8,128)(2,1)S(1)}, u32[]{:S(2)}, u32[]{:S(2)}) collective-permute-start(bf16[192,128]{1,0:T(8,128)(2,1)S(1)} %get-tuple-element.22), channel_id=1, source_target_pairs={{0,1},{1,0},{2,3},{3,2},{4,5},{5,4},{6,7},{7,6},{8,9},{9,8},{10,11... | collective-permute-start | bytes 147464 | tf_op jit(solution)/shard_map/ppermute | solution.py:439
  13.9 5.9 %collective-permute-start.5 = (bf16[192,128]{1,0:T(8,128)(2,1)S(1)}, bf16[192,128]{1,0:T(8,128)(2,1)S(1)}, u32[]{:S(2)}, u32[]{:S(2)}) collective-permute-start(bf16[192,128]{1,0:T(8,128)(2,1)S(1)} %get-tuple-element.23), channel_id=1, source_target_pairs={{0,1},{1,0},{2,3},{3,2},{4,5},{5,4},{6,7},{7,6},{8,9},{9,8},{10,11... | collective-permute-start | bytes 147464 | tf_op jit(solution)/shard_map/ppermute | solution.py:439
  16.3 5.3 %collective-permute-start.6 = (bf16[192,128]{1,0:T(8,128)(2,1)S(1)}, bf16[192,128]{1,0:T(8,128)(2,1)S(1)}, u32[]{:S(2)}, u32[]{:S(2)}) collective-permute-start(bf16[192,128]{1,0:T(8,128)(2,1)S(1)} %get-tuple-element.24), channel_id=1, source_target_pairs={{0,1},{1,0},{2,3},{3,2},{4,5},{5,4},{6,7},{7,6},{8,9},{9,8},{10,11... | collective-permute-start | bytes 147464 | tf_op jit(solution)/shard_map/ppermute | solution.py:439

commit v23 on v22

--- a/solution.py
+++ b/solution.py
@@ -273,7 +273,8 @@
 
 
 def exchange_order(n, handed):
-    return [*range(n // 2, n), *range(n // 2 - 1, 0, -1)] if handed else [1, *range(n - 1, 1, -1)]
+    near = [n // 2, *[d for d in range(1, n) if d != n // 2]]
+    return near if handed else list(range(n - 1, 0, -1))
 
 
 def by_distance(refs, handed):

time: 22.8 us -> 23.2 us (1.018)
  starting transfers between devices: 10.2 us -> 11.3 us
  waiting for transfers between devices: 8.94 us -> 8.15 us
    ppermute x7, starting transfers between devices: 10.2 us -> 11.3 us  [swap(): return lax.ppermute(block, ('tm', 'net', 'cols'), pairs)]
    ppermute x7, waiting for transfers between devices: 8.94 us -> 8.15 us  [swap(): return lax.ppermute(block, ('tm', 'net', 'cols'), pairs)]
  transfers between devices with their start and end apart: 7 -> 7, of which waited for: 6 -> 5; matrix products, arithmetic and copies ran while one was open for 0% -> 0% of each run, Pallas kernels for 4% -> 4%
where the time goes in v23:
time: 23.2 us; the launch traced here: 23 us
  starting transfers between devices  11.3 us (49%)
  waiting for transfers between devices  8.15 us (35%)
  Pallas kernels  3.49 us (15%)
    ppermute x7, starting transfers between devices, swap(): return lax.ppermute(block, ('tm', 'net', 'cols'), pairs)  11.3 us
    ppermute x7, waiting for transfers between devices, swap(): return lax.ppermute(block, ('tm', 'net', 'cols'), pairs)  8.15 us
    pallas_call x1, Pallas kernels, local(): pl.pallas_call(second_kernel, out_shape=[f32((cols, table_rows)), f32((ma...  1.11 us
    pallas_call x1, Pallas kernels, close(): pl.pallas_call(functools.partial(close_kernel, step, section, firsts, sen...  1.03 us
    pallas_call x2, Pallas kernels, own(): pl.pallas_call(functools.partial(own_kernel, step), out_shape=f32(whole.s...  0.91 us
  transfers between devices with their start and end apart: 7, of which 5 were waited for; matrix products, arithmetic and copies ran while one was open for 0% of the time, Pallas kernels for 4%

profile of v23, /device:TPU:4, one launch (start us, length us, event | category | flops | bytes accessed | tf_op | source)
XLA Modules:
  0.0 23.0 jit_solution(17232491027001083197)
XLA Ops:
  0.0 0.0 copy-start
  0.0 0.0 copy-start.1
  0.0 1.1 %shard_map.82 = (f32[192,8]{1,0:T(8,128)S(1)}, f32[72,128]{1,0:T(8,128)S(1)}, bf16[4,192,128]{2,1,0:T(8,128)(2,1)S(1)}, bf16[208,128]{1,0:T(8,128)(2,1)S(1)}, bf...) custom-call(bf16[2,4,3,128,128]{4,3,2,1,0:T(8,128)(2,1)} %refs_12_.1, bf16[2,1,4,128,128]{4,3,2,1,0:T(8,128)(2,1)} %refs_1_.3, ...), custom_call_target="tpu_custom_call" | custom-call | tf_op jit(solution)/shard_map/pallas_call | solution.py:362
  1.1 0.1 collective-permute-start
  1.2 4.0 %collective-permute-start.1 = (bf16[208,128]{1,0:T(8,128)(2,1)S(1)}, bf16[208,128]{1,0:T(8,128)(2,1)S(1)}, u32[]{:S(2)}, u32[]{:S(2)}) collective-permute-start(bf16[208,128]{1,0:T(8,128)(2,1)S(1)} %get-tuple-element.18), channel_id=1, source_target_pairs={{0,24},{1,25},{2,26},{3,27},{4,28},{5,29},{6,30},{7,31},{8,16},{9,... | collective-permute-start | bytes 159752 | tf_op jit(solution)/shard_map/ppermute | solution.py:440
  5.2 2.5 %collective-permute-start.2 = (bf16[208,128]{1,0:T(8,128)(2,1)S(1)}, bf16[208,128]{1,0:T(8,128)(2,1)S(1)}, u32[]{:S(2)}, u32[]{:S(2)}) collective-permute-start(bf16[208,128]{1,0:T(8,128)(2,1)S(1)} %get-tuple-element.19), channel_id=1, source_target_pairs={{0,20},{1,21},{2,22},{3,23},{4,16},{5,17},{6,18},{7,19},{8,28},{9,... | collective-permute-start | bytes 159752 | tf_op jit(solution)/shard_map/ppermute | solution.py:440
  7.8 0.2 collective-permute-start.3
  7.9 1.6 %collective-permute-done.state_ref = bf16[4,192,128]{2,1,0:T(8,128)(2,1)S(1)} collective-permute-done((bf16[4,192,128]{2,1,0:T(8,128)(2,1)S(1)}, bf16[4,192,128]{2,1,0:T(8,128)(2,1)S(1)}, u32[]{:S(2)}, u32[]{:S(2)}) %collective-permute-start) | collective-permute-done | bytes 196640 | tf_op jit(solution)/shard_map/ppermute | solution.py:440
  9.5 0.0 copy-done
  9.5 0.0 copy-done.1
  9.5 0.5 %shard_map.83.z_ref = f32[4,192,128]{2,1,0:T(8,128)S(1)} custom-call(bf16[4,192,128]{2,1,0:T(8,128)(2,1)S(1)} %collective-permute-done.state_ref, bf16[2,4,3,128,128]{4,3,2,1,0:T(8,128)(2,1)S(1)} %copy-done, bf16[2,1,4,128,128]{4,3,2,1,0:T(8,128)(2,1)S(1)} %copy-done.1, f32[192,8]{1,0:T(8,128)S(1)} %get-tuple-element.16.table_ref.refs_2_, ...), custom_call_target="tpu_custom_call" | custom-call | tf_op jit(solution)/shard_map/pallas_call | solution.py:380
  10.0 0.0 collective-permute-done.1.refs_0_.refs_10_
  10.0 0.3 %collective-permute-done.2.refs_1_.refs_9_ = bf16[208,128]{1,0:T(8,128)(2,1)S(1)} collective-permute-done((bf16[208,128]{1,0:T(8,128)(2,1)S(1)}, bf16[208,128]{1,0:T(8,128)(2,1)S(1)}, u32[]{:S(2)}, u32[]{:S(2)}) %collective-permute-start.2) | collective-permute-done | bytes 53280 | tf_op jit(solution)/shard_map/ppermute | solution.py:440
  10.3 4.3 %collective-permute-done.3.refs_2_.refs_11_ = bf16[208,128]{1,0:T(8,128)(2,1)S(1)} collective-permute-done((bf16[208,128]{1,0:T(8,128)(2,1)S(1)}, bf16[208,128]{1,0:T(8,128)(2,1)S(1)}, u32[]{:S(2)}, u32[]{:S(2)}) %collective-permute-start.3) | collective-permute-done | bytes 53280 | tf_op jit(solution)/shard_map/ppermute | solution.py:440
  14.6 0.4 %shard_map.84 = (bf16[4,192,128]{2,1,0:T(8,128)(2,1)S(1)}, bf16[192,128]{1,0:T(8,128)(2,1)S(1)}, bf16[192,128]{1,0:T(8,128)(2,1)S(1)}, bf16[192,128]{1,0:T(8,128)(2,1)S(1)}) custom-call(f32[4,192,128]{2,1,0:T(8,128)S(1)} %shard_map.83.z_ref, bf16[2,1,4,128,128]{4,3,2,1,0:T(8,128)(2,1)S(1)} %copy-done.1, f32[192,8]{1,0:T(8,128)S(1)} %get-tuple-element.16.table_ref.refs_2_, ...), custom_call_target="tpu_custom_call" | custom-call | tf_op jit(solution)/shard_map/pallas_call | solution.py:389
  15.0 0.8 %collective-permute-start.4 = (bf16[192,128]{1,0:T(8,128)(2,1)S(1)}, bf16[192,128]{1,0:T(8,128)(2,1)S(1)}, u32[]{:S(2)}, u32[]{:S(2)}) collective-permute-start(bf16[192,128]{1,0:T(8,128)(2,1)S(1)} %get-tuple-element.22), channel_id=1, source_target_pairs={{0,1},{1,0},{2,3},{3,2},{4,5},{5,4},{6,7},{7,6},{8,9},{9,8},{10,11... | collective-permute-start | bytes 147464 | tf_op jit(solution)/shard_map/ppermute | solution.py:440
  15.9 0.0 collective-permute-start.5
  15.9 3.6 %collective-permute-start.6 = (bf16[192,128]{1,0:T(8,128)(2,1)S(1)}, bf16[192,128]{1,0:T(8,128)(2,1)S(1)}, u32[]{:S(2)}, u32[]{:S(2)}) collective-permute-start(bf16[192,128]{1,0:T(8,128)(2,1)S(1)} %get-tuple-element.24), channel_id=1, source_target_pairs={{0,1},{1,0},{2,3},{3,2},{4,5},{5,4},{6,7},{7,6},{8,9},{9,8},{10,11... | collective-permute-start | bytes 147464 | tf_op jit(solution)/shard_map/ppermute | solution.py:440
  19.5 0.4 %shard_map.85.refs_0_ = f32[4,192,128]{2,1,0:T(8,128)S(1)} custom-call(bf16[4,192,128]{2,1,0:T(8,128)(2,1)S(1)} %get-tuple-element.21.state_ref.refs_7_, bf16[2,4,3,128,128]{4,3,2,1,0:T(8,128)(2,1)S(1)} %copy-done, bf16[2,1,4,128,128]{4,3,2,1,0:T(8,128)(2,1)S(1)} %copy-done.1, f32[192,8]{1,0:T(8,128)S(1)} %get-tuple-element.16.table_ref.refs_2_, ...), custom_call_target="tpu_custom_call" | custom-call | tf_op jit(solution)/shard_map/pallas_call | solution.py:380
  19.9 1.1 %collective-permute-done.4.refs_4_ = bf16[192,128]{1,0:T(8,128)(2,1)S(1)} collective-permute-done((bf16[192,128]{1,0:T(8,128)(2,1)S(1)}, bf16[192,128]{1,0:T(8,128)(2,1)S(1)}, u32[]{:S(2)}, u32[]{:S(2)}) %collective-permute-start.4) | collective-permute-done | bytes 49184 | tf_op jit(solution)/shard_map/ppermute | solution.py:440
  21.1 0.8 %collective-permute-done.5.refs_5_ = bf16[192,128]{1,0:T(8,128)(2,1)S(1)} collective-permute-done((bf16[192,128]{1,0:T(8,128)(2,1)S(1)}, bf16[192,128]{1,0:T(8,128)(2,1)S(1)}, u32[]{:S(2)}, u32[]{:S(2)}) %collective-permute-start.5) | collective-permute-done | bytes 49184 | tf_op jit(solution)/shard_map/ppermute | solution.py:440
  21.9 0.0 collective-permute-done.6.refs_6_
  21.9 1.0 %shard_map.86 = bf16[2,192,512]{2,1,0:T(8,128)(2,1)} custom-call(f32[4,192,128]{2,1,0:T(8,128)S(1)} %shard_map.85.refs_0_, bf16[2,1,4,128,128]{4,3,2,1,0:T(8,128)(2,1)S(1)} %copy-done.1, f32[192,8]{1,0:T(8,128)S(1)} %get-tuple-element.16.table_ref.refs_2_, f32[72,128]{1,0:T(8,128)S(1)} %get-tuple-element.17.marks_ref.refs_3_, ...), custom_call_target="tpu_custom_call" | custom-call | tf_op jit(solution)/shard_map/pallas_call | solution.py:422
Async XLA Ops:
  0.0 9.5 %copy-start = (bf16[2,4,3,128,128]{4,3,2,1,0:T(8,128)(2,1)S(1)}, bf16[2,4,3,128,128]{4,3,2,1,0:T(8,128)(2,1)}, u32[]{:S(2)}) copy-start(bf16[2,4,3,128,128]{4,3,2,1,0:T(8,128)(2,1)} %refs_12_.1) | copy-start | bytes 2359300
  0.0 9.5 %copy-start.1 = (bf16[2,1,4,128,128]{4,3,2,1,0:T(8,128)(2,1)S(1)}, bf16[2,1,4,128,128]{4,3,2,1,0:T(8,128)(2,1)}, u32[]{:S(2)}) copy-start(bf16[2,1,4,128,128]{4,3,2,1,0:T(8,128)(2,1)} %refs_1_.3) | copy-start | bytes 786436
  1.1 8.4 %collective-permute-start = (bf16[4,192,128]{2,1,0:T(8,128)(2,1)S(1)}, bf16[4,192,128]{2,1,0:T(8,128)(2,1)S(1)}, u32[]{:S(2)}, u32[]{:S(2)}) collective-permute-start(bf16[4,192,128]{2,1,0:T(8,128)(2,1)S(1)} %get-tuple-element.15.refs_8_), channel_id=1, source_target_pairs={{0,16},{1,17},{2,18},{3,19},{4,20},{5,21},{6,22},{7,23},{8,24},{9,... | collective-permute-start | bytes 589832 | tf_op jit(solution)/shard_map/ppermute | solution.py:440
  1.2 8.8 %collective-permute-start.1 = (bf16[208,128]{1,0:T(8,128)(2,1)S(1)}, bf16[208,128]{1,0:T(8,128)(2,1)S(1)}, u32[]{:S(2)}, u32[]{:S(2)}) collective-permute-start(bf16[208,128]{1,0:T(8,128)(2,1)S(1)} %get-tuple-element.18), channel_id=1, source_target_pairs={{0,24},{1,25},{2,26},{3,27},{4,28},{5,29},{6,30},{7,31},{8,16},{9,... | collective-permute-start | bytes 159752 | tf_op jit(solution)/shard_map/ppermute | solution.py:440
  5.2 5.0 %collective-permute-start.2 = (bf16[208,128]{1,0:T(8,128)(2,1)S(1)}, bf16[208,128]{1,0:T(8,128)(2,1)S(1)}, u32[]{:S(2)}, u32[]{:S(2)}) collective-permute-start(bf16[208,128]{1,0:T(8,128)(2,1)S(1)} %get-tuple-element.19), channel_id=1, source_target_pairs={{0,20},{1,21},{2,22},{3,23},{4,16},{5,17},{6,18},{7,19},{8,28},{9,... | collective-permute-start | bytes 159752 | tf_op jit(solution)/shard_map/ppermute | solution.py:440
  7.8 6.8 %collective-permute-start.3 = (bf16[208,128]{1,0:T(8,128)(2,1)S(1)}, bf16[208,128]{1,0:T(8,128)(2,1)S(1)}, u32[]{:S(2)}, u32[]{:S(2)}) collective-permute-start(bf16[208,128]{1,0:T(8,128)(2,1)S(1)} %get-tuple-element.20), channel_id=1, source_target_pairs={{0,28},{1,29},{2,30},{3,31},{4,24},{5,25},{6,26},{7,27},{8,20},{9,... | collective-permute-start | bytes 159752 | tf_op jit(solution)/shard_map/ppermute | solution.py:440
  15.0 6.1 %collective-permute-start.4 = (bf16[192,128]{1,0:T(8,128)(2,1)S(1)}, bf16[192,128]{1,0:T(8,128)(2,1)S(1)}, u32[]{:S(2)}, u32[]{:S(2)}) collective-permute-start(bf16[192,128]{1,0:T(8,128)(2,1)S(1)} %get-tuple-element.22), channel_id=1, source_target_pairs={{0,1},{1,0},{2,3},{3,2},{4,5},{5,4},{6,7},{7,6},{8,9},{9,8},{10,11... | collective-permute-start | bytes 147464 | tf_op jit(solution)/shard_map/ppermute | solution.py:440
  15.9 6.0 %collective-permute-start.5 = (bf16[192,128]{1,0:T(8,128)(2,1)S(1)}, bf16[192,128]{1,0:T(8,128)(2,1)S(1)}, u32[]{:S(2)}, u32[]{:S(2)}) collective-permute-start(bf16[192,128]{1,0:T(8,128)(2,1)S(1)} %get-tuple-element.23), channel_id=1, source_target_pairs={{0,1},{1,0},{2,3},{3,2},{4,5},{5,4},{6,7},{7,6},{8,9},{9,8},{10,11... | collective-permute-start | bytes 147464 | tf_op jit(solution)/shard_map/ppermute | solution.py:440
  15.9 6.0 %collective-permute-start.6 = (bf16[192,128]{1,0:T(8,128)(2,1)S(1)}, bf16[192,128]{1,0:T(8,128)(2,1)S(1)}, u32[]{:S(2)}, u32[]{:S(2)}) collective-permute-start(bf16[192,128]{1,0:T(8,128)(2,1)S(1)} %get-tuple-element.24), channel_id=1, source_target_pairs={{0,1},{1,0},{2,3},{3,2},{4,5},{5,4},{6,7},{7,6},{8,9},{9,8},{10,11... | collective-permute-start | bytes 147464 | tf_op jit(solution)/shard_map/ppermute | solution.py:440

commit v24 on v22

--- a/solution.py
+++ b/solution.py
@@ -273,7 +273,8 @@
 
 
 def exchange_order(n, handed):
-    return [*range(n // 2, n), *range(n // 2 - 1, 0, -1)] if handed else [1, *range(n - 1, 1, -1)]
+    handing = [*range(n // 2, n), *range(n // 2 - 1, 0, -1)]
+    return handing if handed else [n - 1, *range(1, n - 1)]
 
 
 def by_distance(refs, handed):

time: 22.8 us -> 22.2 us (0.974)
  the two profiles are of different devices: /device:TPU:4 before, /device:TPU:12 now
where the time goes in v24:
time: 22.2 us; the launch traced here: 22 us
  starting transfers between devices  10.8 us (49%)
  waiting for transfers between devices  7.69 us (35%)
  Pallas kernels  3.5 us (16%)
    ppermute x7, starting transfers between devices, swap(): return lax.ppermute(block, ('tm', 'net', 'cols'), pairs)  10.8 us
    ppermute x7, waiting for transfers between devices, swap(): return lax.ppermute(block, ('tm', 'net', 'cols'), pairs)  7.69 us
    pallas_call x1, Pallas kernels, local(): pl.pallas_call(second_kernel, out_shape=[f32((cols, table_rows)), f32((ma...  1.11 us
    pallas_call x1, Pallas kernels, close(): pl.pallas_call(functools.partial(close_kernel, step, section, firsts, sen...  1.03 us
    pallas_call x2, Pallas kernels, own(): pl.pallas_call(functools.partial(own_kernel, step), out_shape=f32(whole.s...  0.91 us
    pallas_call x1, Pallas kernels, join(): pl.pallas_call(functools.partial(join_kernel, step, kinds if fix else 0,...  0.46 us
  transfers between devices with their start and end apart: 7, of which 3 were waited for; matrix products, arithmetic and copies ran while one was open for 0% of the time, Pallas kernels for 4%

profile of v24, /device:TPU:12, one launch (start us, length us, event | category | flops | bytes accessed | tf_op | source)
XLA Modules:
  0.0 22.0 jit_solution(12114952489368817546)
XLA Ops:
  0.0 0.0 copy-start
  0.0 0.0 copy-start.1
  0.0 1.1 %shard_map.82 = (f32[192,8]{1,0:T(8,128)S(1)}, f32[72,128]{1,0:T(8,128)S(1)}, bf16[4,192,128]{2,1,0:T(8,128)(2,1)S(1)}, bf16[208,128]{1,0:T(8,128)(2,1)S(1)}, bf...) custom-call(bf16[2,4,3,128,128]{4,3,2,1,0:T(8,128)(2,1)} %refs_12_.1, bf16[2,1,4,128,128]{4,3,2,1,0:T(8,128)(2,1)} %refs_1_.3, ...), custom_call_target="tpu_custom_call" | custom-call | tf_op jit(solution)/shard_map/pallas_call | solution.py:362
  1.1 1.6 %collective-permute-start = (bf16[4,192,128]{2,1,0:T(8,128)(2,1)S(1)}, bf16[4,192,128]{2,1,0:T(8,128)(2,1)S(1)}, u32[]{:S(2)}, u32[]{:S(2)}) collective-permute-start(bf16[4,192,128]{2,1,0:T(8,128)(2,1)S(1)} %get-tuple-element.15.refs_8_), channel_id=1, source_target_pairs={{0,16},{1,17},{2,18},{3,19},{4,20},{5,21},{6,22},{7,23},{8,24},{9,... | collective-permute-start | bytes 589832 | tf_op jit(solution)/shard_map/ppermute | solution.py:440
  2.7 2.5 %collective-permute-start.1 = (bf16[208,128]{1,0:T(8,128)(2,1)S(1)}, bf16[208,128]{1,0:T(8,128)(2,1)S(1)}, u32[]{:S(2)}, u32[]{:S(2)}) collective-permute-start(bf16[208,128]{1,0:T(8,128)(2,1)S(1)} %get-tuple-element.18), channel_id=1, source_target_pairs={{0,24},{1,25},{2,26},{3,27},{4,28},{5,29},{6,30},{7,31},{8,16},{9,... | collective-permute-start | bytes 159752 | tf_op jit(solution)/shard_map/ppermute | solution.py:440
  5.2 0.0 collective-permute-start.2
  5.2 2.7 %collective-permute-start.3 = (bf16[208,128]{1,0:T(8,128)(2,1)S(1)}, bf16[208,128]{1,0:T(8,128)(2,1)S(1)}, u32[]{:S(2)}, u32[]{:S(2)}) collective-permute-start(bf16[208,128]{1,0:T(8,128)(2,1)S(1)} %get-tuple-element.20), channel_id=1, source_target_pairs={{0,20},{1,21},{2,22},{3,23},{4,16},{5,17},{6,18},{7,19},{8,28},{9,... | collective-permute-start | bytes 159752 | tf_op jit(solution)/shard_map/ppermute | solution.py:440
  7.9 3.3 %collective-permute-done.state_ref = bf16[4,192,128]{2,1,0:T(8,128)(2,1)S(1)} collective-permute-done((bf16[4,192,128]{2,1,0:T(8,128)(2,1)S(1)}, bf16[4,192,128]{2,1,0:T(8,128)(2,1)S(1)}, u32[]{:S(2)}, u32[]{:S(2)}) %collective-permute-start) | collective-permute-done | bytes 196640 | tf_op jit(solution)/shard_map/ppermute | solution.py:440
  11.3 0.0 copy-done
  11.3 0.0 copy-done.1
  11.3 0.5 %shard_map.83.z_ref = f32[4,192,128]{2,1,0:T(8,128)S(1)} custom-call(bf16[4,192,128]{2,1,0:T(8,128)(2,1)S(1)} %collective-permute-done.state_ref, bf16[2,4,3,128,128]{4,3,2,1,0:T(8,128)(2,1)S(1)} %copy-done, bf16[2,1,4,128,128]{4,3,2,1,0:T(8,128)(2,1)S(1)} %copy-done.1, f32[192,8]{1,0:T(8,128)S(1)} %get-tuple-element.16.table_ref.refs_2_, ...), custom_call_target="tpu_custom_call" | custom-call | tf_op jit(solution)/shard_map/pallas_call | solution.py:380
  11.7 0.0 collective-permute-done.1.refs_0_.refs_10_
  11.7 0.0 collective-permute-done.2.refs_1_.refs_11_
  11.7 0.0 collective-permute-done.3.refs_2_.refs_9_
  11.8 0.5 %shard_map.84 = (bf16[4,192,128]{2,1,0:T(8,128)(2,1)S(1)}, bf16[192,128]{1,0:T(8,128)(2,1)S(1)}, bf16[192,128]{1,0:T(8,128)(2,1)S(1)}, bf16[192,128]{1,0:T(8,128)(2,1)S(1)}) custom-call(f32[4,192,128]{2,1,0:T(8,128)S(1)} %shard_map.83.z_ref, bf16[2,1,4,128,128]{4,3,2,1,0:T(8,128)(2,1)S(1)} %copy-done.1, f32[192,8]{1,0:T(8,128)S(1)} %get-tuple-element.16.table_ref.refs_2_, ...), custom_call_target="tpu_custom_call" | custom-call | tf_op jit(solution)/shard_map/pallas_call | solution.py:389
  12.2 1.6 %collective-permute-start.4 = (bf16[192,128]{1,0:T(8,128)(2,1)S(1)}, bf16[192,128]{1,0:T(8,128)(2,1)S(1)}, u32[]{:S(2)}, u32[]{:S(2)}) collective-permute-start(bf16[192,128]{1,0:T(8,128)(2,1)S(1)} %get-tuple-element.22), channel_id=1, source_target_pairs={{0,1},{1,0},{2,3},{3,2},{4,5},{5,4},{6,7},{7,6},{8,9},{9,8},{10,11... | collective-permute-start | bytes 147464 | tf_op jit(solution)/shard_map/ppermute | solution.py:440
  13.9 2.1 %collective-permute-start.5 = (bf16[192,128]{1,0:T(8,128)(2,1)S(1)}, bf16[192,128]{1,0:T(8,128)(2,1)S(1)}, u32[]{:S(2)}, u32[]{:S(2)}) collective-permute-start(bf16[192,128]{1,0:T(8,128)(2,1)S(1)} %get-tuple-element.23), channel_id=1, source_target_pairs={{0,1},{1,0},{2,3},{3,2},{4,5},{5,4},{6,7},{7,6},{8,9},{9,8},{10,11... | collective-permute-start | bytes 147464 | tf_op jit(solution)/shard_map/ppermute | solution.py:440
  16.0 0.2 collective-permute-start.6
  16.2 0.4 %shard_map.85.refs_0_ = f32[4,192,128]{2,1,0:T(8,128)S(1)} custom-call(bf16[4,192,128]{2,1,0:T(8,128)(2,1)S(1)} %get-tuple-element.21.state_ref.refs_7_, bf16[2,4,3,128,128]{4,3,2,1,0:T(8,128)(2,1)S(1)} %copy-done, bf16[2,1,4,128,128]{4,3,2,1,0:T(8,128)(2,1)S(1)} %copy-done.1, f32[192,8]{1,0:T(8,128)S(1)} %get-tuple-element.16.table_ref.refs_2_, ...), custom_call_target="tpu_custom_call" | custom-call | tf_op jit(solution)/shard_map/pallas_call | solution.py:380
  16.6 0.0 collective-permute-done.4.refs_4_
  16.6 1.9 %collective-permute-done.5.refs_5_ = bf16[192,128]{1,0:T(8,128)(2,1)S(1)} collective-permute-done((bf16[192,128]{1,0:T(8,128)(2,1)S(1)}, bf16[192,128]{1,0:T(8,128)(2,1)S(1)}, u32[]{:S(2)}, u32[]{:S(2)}) %collective-permute-start.5) | collective-permute-done | bytes 49184 | tf_op jit(solution)/shard_map/ppermute | solution.py:440
  18.6 2.4 %collective-permute-done.6.refs_6_ = bf16[192,128]{1,0:T(8,128)(2,1)S(1)} collective-permute-done((bf16[192,128]{1,0:T(8,128)(2,1)S(1)}, bf16[192,128]{1,0:T(8,128)(2,1)S(1)}, u32[]{:S(2)}, u32[]{:S(2)}) %collective-permute-start.6) | collective-permute-done | bytes 49184 | tf_op jit(solution)/shard_map/ppermute | solution.py:440
  21.0 1.0 %shard_map.86 = bf16[2,192,512]{2,1,0:T(8,128)(2,1)} custom-call(f32[4,192,128]{2,1,0:T(8,128)S(1)} %shard_map.85.refs_0_, bf16[2,1,4,128,128]{4,3,2,1,0:T(8,128)(2,1)S(1)} %copy-done.1, f32[192,8]{1,0:T(8,128)S(1)} %get-tuple-element.16.table_ref.refs_2_, f32[72,128]{1,0:T(8,128)S(1)} %get-tuple-element.17.marks_ref.refs_3_, ...), custom_call_target="tpu_custom_call" | custom-call | tf_op jit(solution)/shard_map/pallas_call | solution.py:422
Async XLA Ops:
  0.0 11.3 %copy-start = (bf16[2,4,3,128,128]{4,3,2,1,0:T(8,128)(2,1)S(1)}, bf16[2,4,3,128,128]{4,3,2,1,0:T(8,128)(2,1)}, u32[]{:S(2)}) copy-start(bf16[2,4,3,128,128]{4,3,2,1,0:T(8,128)(2,1)} %refs_12_.1) | copy-start | bytes 2359300
  0.0 11.3 %copy-start.1 = (bf16[2,1,4,128,128]{4,3,2,1,0:T(8,128)(2,1)S(1)}, bf16[2,1,4,128,128]{4,3,2,1,0:T(8,128)(2,1)}, u32[]{:S(2)}) copy-start(bf16[2,1,4,128,128]{4,3,2,1,0:T(8,128)(2,1)} %refs_1_.3) | copy-start | bytes 786436
  1.1 10.1 %collective-permute-start = (bf16[4,192,128]{2,1,0:T(8,128)(2,1)S(1)}, bf16[4,192,128]{2,1,0:T(8,128)(2,1)S(1)}, u32[]{:S(2)}, u32[]{:S(2)}) collective-permute-start(bf16[4,192,128]{2,1,0:T(8,128)(2,1)S(1)} %get-tuple-element.15.refs_8_), channel_id=1, source_target_pairs={{0,16},{1,17},{2,18},{3,19},{4,20},{5,21},{6,22},{7,23},{8,24},{9,... | collective-permute-start | bytes 589832 | tf_op jit(solution)/shard_map/ppermute | solution.py:440
  2.7 9.0 %collective-permute-start.1 = (bf16[208,128]{1,0:T(8,128)(2,1)S(1)}, bf16[208,128]{1,0:T(8,128)(2,1)S(1)}, u32[]{:S(2)}, u32[]{:S(2)}) collective-permute-start(bf16[208,128]{1,0:T(8,128)(2,1)S(1)} %get-tuple-element.18), channel_id=1, source_target_pairs={{0,24},{1,25},{2,26},{3,27},{4,28},{5,29},{6,30},{7,31},{8,16},{9,... | collective-permute-start | bytes 159752 | tf_op jit(solution)/shard_map/ppermute | solution.py:440
  5.2 6.5 %collective-permute-start.2 = (bf16[208,128]{1,0:T(8,128)(2,1)S(1)}, bf16[208,128]{1,0:T(8,128)(2,1)S(1)}, u32[]{:S(2)}, u32[]{:S(2)}) collective-permute-start(bf16[208,128]{1,0:T(8,128)(2,1)S(1)} %get-tuple-element.19), channel_id=1, source_target_pairs={{0,28},{1,29},{2,30},{3,31},{4,24},{5,25},{6,26},{7,27},{8,20},{9,... | collective-permute-start | bytes 159752 | tf_op jit(solution)/shard_map/ppermute | solution.py:440
  5.2 6.5 %collective-permute-start.3 = (bf16[208,128]{1,0:T(8,128)(2,1)S(1)}, bf16[208,128]{1,0:T(8,128)(2,1)S(1)}, u32[]{:S(2)}, u32[]{:S(2)}) collective-permute-start(bf16[208,128]{1,0:T(8,128)(2,1)S(1)} %get-tuple-element.20), channel_id=1, source_target_pairs={{0,20},{1,21},{2,22},{3,23},{4,16},{5,17},{6,18},{7,19},{8,28},{9,... | collective-permute-start | bytes 159752 | tf_op jit(solution)/shard_map/ppermute | solution.py:440
  12.2 4.4 %collective-permute-start.4 = (bf16[192,128]{1,0:T(8,128)(2,1)S(1)}, bf16[192,128]{1,0:T(8,128)(2,1)S(1)}, u32[]{:S(2)}, u32[]{:S(2)}) collective-permute-start(bf16[192,128]{1,0:T(8,128)(2,1)S(1)} %get-tuple-element.22), channel_id=1, source_target_pairs={{0,1},{1,0},{2,3},{3,2},{4,5},{5,4},{6,7},{7,6},{8,9},{9,8},{10,11... | collective-permute-start | bytes 147464 | tf_op jit(solution)/shard_map/ppermute | solution.py:440
  13.9 4.7 %collective-permute-start.5 = (bf16[192,128]{1,0:T(8,128)(2,1)S(1)}, bf16[192,128]{1,0:T(8,128)(2,1)S(1)}, u32[]{:S(2)}, u32[]{:S(2)}) collective-permute-start(bf16[192,128]{1,0:T(8,128)(2,1)S(1)} %get-tuple-element.23), channel_id=1, source_target_pairs={{0,1},{1,0},{2,3},{3,2},{4,5},{5,4},{6,7},{7,6},{8,9},{9,8},{10,11... | collective-permute-start | bytes 147464 | tf_op jit(solution)/shard_map/ppermute | solution.py:440
  16.0 5.0 %collective-permute-start.6 = (bf16[192,128]{1,0:T(8,128)(2,1)S(1)}, bf16[192,128]{1,0:T(8,128)(2,1)S(1)}, u32[]{:S(2)}, u32[]{:S(2)}) collective-permute-start(bf16[192,128]{1,0:T(8,128)(2,1)S(1)} %get-tuple-element.24), channel_id=1, source_target_pairs={{0,1},{1,0},{2,3},{3,2},{4,5},{5,4},{6,7},{7,6},{8,9},{9,8},{10,11... | collective-permute-start | bytes 147464 | tf_op jit(solution)/shard_map/ppermute | solution.py:440

commit v25 on v19

--- a/solution.py
+++ b/solution.py
@@ -263,7 +263,7 @@
 
 
 def exchange_order(n, handed):
-    return [*range(n // 2, n), *range(n // 2 - 1, 0, -1)] if handed else list(range(n - 1, 0, -1))
+    return [n - 1, *range(1, n - 1)] if handed else list(range(n - 1, 0, -1))
 
 
 def by_distance(refs, handed):

time: 22 us -> 22.6 us (1.027)
  waiting for transfers between devices: 7.21 us -> 7.63 us
    ppermute x7, waiting for transfers between devices: 7.21 us -> 7.63 us  [swap(): return lax.ppermute(block, ('tm', 'net', 'cols'), pairs)]
  transfers between devices with their start and end apart: 7 -> 7, of which waited for: 5 -> 6; matrix products, arithmetic and copies ran while one was open for 0% -> 0% of each run, Pallas kernels for 4% -> 4%
where the time goes in v25:
time: 22.6 us; the launch traced here: 22.4 us
  starting transfers between devices  11.3 us (50%)
  waiting for transfers between devices  7.63 us (34%)
  Pallas kernels  3.49 us (15%)
    ppermute x7, starting transfers between devices, swap(): return lax.ppermute(block, ('tm', 'net', 'cols'), pairs)  11.3 us
    ppermute x7, waiting for transfers between devices, swap(): return lax.ppermute(block, ('tm', 'net', 'cols'), pairs)  7.63 us
    pallas_call x1, Pallas kernels, local(): pl.pallas_call(second_kernel, out_shape=[f32((cols, table_rows)), f32((ma...  1.11 us
    pallas_call x1, Pallas kernels, close(): pl.pallas_call(functools.partial(close_kernel, step, section, firsts, sen...  1.03 us
    pallas_call x2, Pallas kernels, own(): pl.pallas_call(functools.partial(own_kernel, step), out_shape=f32(whole.s...  0.9 us
  transfers between devices with their start and end apart: 7, of which 6 were waited for; matrix products, arithmetic and copies ran while one was open for 0% of the time, Pallas kernels for 4%

profile of v25, /device:TPU:4, one launch (start us, length us, event | category | flops | bytes accessed | tf_op | source)
XLA Modules:
  0.0 22.4 jit_solution(11763768136051790699)
XLA Ops:
  0.0 0.0 copy-start
  0.0 0.0 copy-start.1
  0.0 1.1 %shard_map.82 = (f32[192,8]{1,0:T(8,128)S(1)}, f32[72,128]{1,0:T(8,128)S(1)}, bf16[4,192,128]{2,1,0:T(8,128)(2,1)S(1)}, bf16[208,128]{1,0:T(8,128)(2,1)S(1)}, bf...) custom-call(bf16[2,4,3,128,128]{4,3,2,1,0:T(8,128)(2,1)} %refs_12_.1, bf16[2,1,4,128,128]{4,3,2,1,0:T(8,128)(2,1)} %refs_1_.3, ...), custom_call_target="tpu_custom_call" | custom-call | tf_op jit(solution)/shard_map/pallas_call | solution.py:351
  1.1 0.1 collective-permute-start
  1.2 5.0 %collective-permute-start.1 = (bf16[208,128]{1,0:T(8,128)(2,1)S(1)}, bf16[208,128]{1,0:T(8,128)(2,1)S(1)}, u32[]{:S(2)}, u32[]{:S(2)}) collective-permute-start(bf16[208,128]{1,0:T(8,128)(2,1)S(1)} %get-tuple-element.18), channel_id=1, source_target_pairs={{0,28},{1,29},{2,30},{3,31},{4,24},{5,25},{6,26},{7,27},{8,20},{9,... | collective-permute-start | bytes 159752 | tf_op jit(solution)/shard_map/ppermute | solution.py:429
  6.3 0.5 %collective-permute-start.2 = (bf16[208,128]{1,0:T(8,128)(2,1)S(1)}, bf16[208,128]{1,0:T(8,128)(2,1)S(1)}, u32[]{:S(2)}, u32[]{:S(2)}) collective-permute-start(bf16[208,128]{1,0:T(8,128)(2,1)S(1)} %get-tuple-element.19), channel_id=1, source_target_pairs={{0,20},{1,21},{2,22},{3,23},{4,16},{5,17},{6,18},{7,19},{8,28},{9,... | collective-permute-start | bytes 159752 | tf_op jit(solution)/shard_map/ppermute | solution.py:429
  6.7 1.2 %collective-permute-start.3 = (bf16[208,128]{1,0:T(8,128)(2,1)S(1)}, bf16[208,128]{1,0:T(8,128)(2,1)S(1)}, u32[]{:S(2)}, u32[]{:S(2)}) collective-permute-start(bf16[208,128]{1,0:T(8,128)(2,1)S(1)} %get-tuple-element.20), channel_id=1, source_target_pairs={{0,24},{1,25},{2,26},{3,27},{4,28},{5,29},{6,30},{7,31},{8,16},{9,... | collective-permute-start | bytes 159752 | tf_op jit(solution)/shard_map/ppermute | solution.py:429
  7.9 1.0 %collective-permute-done.state_ref = bf16[4,192,128]{2,1,0:T(8,128)(2,1)S(1)} collective-permute-done((bf16[4,192,128]{2,1,0:T(8,128)(2,1)S(1)}, bf16[4,192,128]{2,1,0:T(8,128)(2,1)S(1)}, u32[]{:S(2)}, u32[]{:S(2)}) %collective-permute-start) | collective-permute-done | bytes 196640 | tf_op jit(solution)/shard_map/ppermute | solution.py:429
  9.0 0.0 copy-done
  9.0 0.0 copy-done.1
  9.0 0.5 %shard_map.83.z_ref = f32[4,192,128]{2,1,0:T(8,128)S(1)} custom-call(bf16[4,192,128]{2,1,0:T(8,128)(2,1)S(1)} %collective-permute-done.state_ref, bf16[2,4,3,128,128]{4,3,2,1,0:T(8,128)(2,1)S(1)} %copy-done, bf16[2,1,4,128,128]{4,3,2,1,0:T(8,128)(2,1)S(1)} %copy-done.1, f32[192,8]{1,0:T(8,128)S(1)} %get-tuple-element.16.table_ref.refs_2_, ...), custom_call_target="tpu_custom_call" | custom-call | tf_op jit(solution)/shard_map/pallas_call | solution.py:369
  9.4 0.0 collective-permute-done.1.refs_0_.refs_11_
  9.4 1.8 %collective-permute-done.2.refs_1_.refs_9_ = bf16[208,128]{1,0:T(8,128)(2,1)S(1)} collective-permute-done((bf16[208,128]{1,0:T(8,128)(2,1)S(1)}, bf16[208,128]{1,0:T(8,128)(2,1)S(1)}, u32[]{:S(2)}, u32[]{:S(2)}) %collective-permute-start.2) | collective-permute-done | bytes 53280 | tf_op jit(solution)/shard_map/ppermute | solution.py:429
  11.3 1.9 %collective-permute-done.3.refs_2_.refs_10_ = bf16[208,128]{1,0:T(8,128)(2,1)S(1)} collective-permute-done((bf16[208,128]{1,0:T(8,128)(2,1)S(1)}, bf16[208,128]{1,0:T(8,128)(2,1)S(1)}, u32[]{:S(2)}, u32[]{:S(2)}) %collective-permute-start.3) | collective-permute-done | bytes 53280 | tf_op jit(solution)/shard_map/ppermute | solution.py:429
  13.2 0.4 %shard_map.84 = (bf16[4,192,128]{2,1,0:T(8,128)(2,1)S(1)}, bf16[192,128]{1,0:T(8,128)(2,1)S(1)}, bf16[192,128]{1,0:T(8,128)(2,1)S(1)}, bf16[192,128]{1,0:T(8,128)(2,1)S(1)}) custom-call(f32[4,192,128]{2,1,0:T(8,128)S(1)} %shard_map.83.z_ref, bf16[2,1,4,128,128]{4,3,2,1,0:T(8,128)(2,1)S(1)} %copy-done.1, f32[192,8]{1,0:T(8,128)S(1)} %get-tuple-element.16.table_ref.refs_2_, ...), custom_call_target="tpu_custom_call" | custom-call | tf_op jit(solution)/shard_map/pallas_call | solution.py:378
  13.6 2.3 %collective-permute-start.4 = (bf16[192,128]{1,0:T(8,128)(2,1)S(1)}, bf16[192,128]{1,0:T(8,128)(2,1)S(1)}, u32[]{:S(2)}, u32[]{:S(2)}) collective-permute-start(bf16[192,128]{1,0:T(8,128)(2,1)S(1)} %get-tuple-element.22), channel_id=1, source_target_pairs={{0,1},{1,0},{2,3},{3,2},{4,5},{5,4},{6,7},{7,6},{8,9},{9,8},{10,11... | collective-permute-start | bytes 147464 | tf_op jit(solution)/shard_map/ppermute | solution.py:429
  15.9 1.2 %collective-permute-start.5 = (bf16[192,128]{1,0:T(8,128)(2,1)S(1)}, bf16[192,128]{1,0:T(8,128)(2,1)S(1)}, u32[]{:S(2)}, u32[]{:S(2)}) collective-permute-start(bf16[192,128]{1,0:T(8,128)(2,1)S(1)} %get-tuple-element.23), channel_id=1, source_target_pairs={{0,1},{1,0},{2,3},{3,2},{4,5},{5,4},{6,7},{7,6},{8,9},{9,8},{10,11... | collective-permute-start | bytes 147464 | tf_op jit(solution)/shard_map/ppermute | solution.py:429
  17.1 1.0 %collective-permute-start.6 = (bf16[192,128]{1,0:T(8,128)(2,1)S(1)}, bf16[192,128]{1,0:T(8,128)(2,1)S(1)}, u32[]{:S(2)}, u32[]{:S(2)}) collective-permute-start(bf16[192,128]{1,0:T(8,128)(2,1)S(1)} %get-tuple-element.24), channel_id=1, source_target_pairs={{0,1},{1,0},{2,3},{3,2},{4,5},{5,4},{6,7},{7,6},{8,9},{9,8},{10,11... | collective-permute-start | bytes 147464 | tf_op jit(solution)/shard_map/ppermute | solution.py:429
  18.1 0.4 %shard_map.85.refs_0_ = f32[4,192,128]{2,1,0:T(8,128)S(1)} custom-call(bf16[4,192,128]{2,1,0:T(8,128)(2,1)S(1)} %get-tuple-element.21.state_ref.refs_7_, bf16[2,4,3,128,128]{4,3,2,1,0:T(8,128)(2,1)S(1)} %copy-done, bf16[2,1,4,128,128]{4,3,2,1,0:T(8,128)(2,1)S(1)} %copy-done.1, f32[192,8]{1,0:T(8,128)S(1)} %get-tuple-element.16.table_ref.refs_2_, ...), custom_call_target="tpu_custom_call" | custom-call | tf_op jit(solution)/shard_map/pallas_call | solution.py:369
  18.5 1.2 %collective-permute-done.4.refs_4_ = bf16[192,128]{1,0:T(8,128)(2,1)S(1)} collective-permute-done((bf16[192,128]{1,0:T(8,128)(2,1)S(1)}, bf16[192,128]{1,0:T(8,128)(2,1)S(1)}, u32[]{:S(2)}, u32[]{:S(2)}) %collective-permute-start.4) | collective-permute-done | bytes 49184 | tf_op jit(solution)/shard_map/ppermute | solution.py:429
  19.7 1.2 %collective-permute-done.5.refs_5_ = bf16[192,128]{1,0:T(8,128)(2,1)S(1)} collective-permute-done((bf16[192,128]{1,0:T(8,128)(2,1)S(1)}, bf16[192,128]{1,0:T(8,128)(2,1)S(1)}, u32[]{:S(2)}, u32[]{:S(2)}) %collective-permute-start.5) | collective-permute-done | bytes 49184 | tf_op jit(solution)/shard_map/ppermute | solution.py:429
  20.9 0.5 %collective-permute-done.6.refs_6_ = bf16[192,128]{1,0:T(8,128)(2,1)S(1)} collective-permute-done((bf16[192,128]{1,0:T(8,128)(2,1)S(1)}, bf16[192,128]{1,0:T(8,128)(2,1)S(1)}, u32[]{:S(2)}, u32[]{:S(2)}) %collective-permute-start.6) | collective-permute-done | bytes 49184 | tf_op jit(solution)/shard_map/ppermute | solution.py:429
  21.4 1.0 %shard_map.86 = bf16[2,192,512]{2,1,0:T(8,128)(2,1)} custom-call(f32[4,192,128]{2,1,0:T(8,128)S(1)} %shard_map.85.refs_0_, bf16[2,1,4,128,128]{4,3,2,1,0:T(8,128)(2,1)S(1)} %copy-done.1, f32[192,8]{1,0:T(8,128)S(1)} %get-tuple-element.16.table_ref.refs_2_, f32[72,128]{1,0:T(8,128)S(1)} %get-tuple-element.17.marks_ref.refs_3_, ...), custom_call_target="tpu_custom_call" | custom-call | tf_op jit(solution)/shard_map/pallas_call | solution.py:411
Async XLA Ops:
  0.0 9.0 %copy-start = (bf16[2,4,3,128,128]{4,3,2,1,0:T(8,128)(2,1)S(1)}, bf16[2,4,3,128,128]{4,3,2,1,0:T(8,128)(2,1)}, u32[]{:S(2)}) copy-start(bf16[2,4,3,128,128]{4,3,2,1,0:T(8,128)(2,1)} %refs_12_.1) | copy-start | bytes 2359300
  0.0 9.0 %copy-start.1 = (bf16[2,1,4,128,128]{4,3,2,1,0:T(8,128)(2,1)S(1)}, bf16[2,1,4,128,128]{4,3,2,1,0:T(8,128)(2,1)}, u32[]{:S(2)}) copy-start(bf16[2,1,4,128,128]{4,3,2,1,0:T(8,128)(2,1)} %refs_1_.3) | copy-start | bytes 786436
  1.1 7.8 %collective-permute-start = (bf16[4,192,128]{2,1,0:T(8,128)(2,1)S(1)}, bf16[4,192,128]{2,1,0:T(8,128)(2,1)S(1)}, u32[]{:S(2)}, u32[]{:S(2)}) collective-permute-start(bf16[4,192,128]{2,1,0:T(8,128)(2,1)S(1)} %get-tuple-element.15.refs_8_), channel_id=1, source_target_pairs={{0,16},{1,17},{2,18},{3,19},{4,20},{5,21},{6,22},{7,23},{8,24},{9,... | collective-permute-start | bytes 589832 | tf_op jit(solution)/shard_map/ppermute | solution.py:429
  1.2 8.2 %collective-permute-start.1 = (bf16[208,128]{1,0:T(8,128)(2,1)S(1)}, bf16[208,128]{1,0:T(8,128)(2,1)S(1)}, u32[]{:S(2)}, u32[]{:S(2)}) collective-permute-start(bf16[208,128]{1,0:T(8,128)(2,1)S(1)} %get-tuple-element.18), channel_id=1, source_target_pairs={{0,28},{1,29},{2,30},{3,31},{4,24},{5,25},{6,26},{7,27},{8,20},{9,... | collective-permute-start | bytes 159752 | tf_op jit(solution)/shard_map/ppermute | solution.py:429
  6.3 5.0 %collective-permute-start.2 = (bf16[208,128]{1,0:T(8,128)(2,1)S(1)}, bf16[208,128]{1,0:T(8,128)(2,1)S(1)}, u32[]{:S(2)}, u32[]{:S(2)}) collective-permute-start(bf16[208,128]{1,0:T(8,128)(2,1)S(1)} %get-tuple-element.19), channel_id=1, source_target_pairs={{0,20},{1,21},{2,22},{3,23},{4,16},{5,17},{6,18},{7,19},{8,28},{9,... | collective-permute-start | bytes 159752 | tf_op jit(solution)/shard_map/ppermute | solution.py:429
  6.7 6.4 %collective-permute-start.3 = (bf16[208,128]{1,0:T(8,128)(2,1)S(1)}, bf16[208,128]{1,0:T(8,128)(2,1)S(1)}, u32[]{:S(2)}, u32[]{:S(2)}) collective-permute-start(bf16[208,128]{1,0:T(8,128)(2,1)S(1)} %get-tuple-element.20), channel_id=1, source_target_pairs={{0,24},{1,25},{2,26},{3,27},{4,28},{5,29},{6,30},{7,31},{8,16},{9,... | collective-permute-start | bytes 159752 | tf_op jit(solution)/shard_map/ppermute | solution.py:429
  13.6 6.1 %collective-permute-start.4 = (bf16[192,128]{1,0:T(8,128)(2,1)S(1)}, bf16[192,128]{1,0:T(8,128)(2,1)S(1)}, u32[]{:S(2)}, u32[]{:S(2)}) collective-permute-start(bf16[192,128]{1,0:T(8,128)(2,1)S(1)} %get-tuple-element.22), channel_id=1, source_target_pairs={{0,1},{1,0},{2,3},{3,2},{4,5},{5,4},{6,7},{7,6},{8,9},{9,8},{10,11... | collective-permute-start | bytes 147464 | tf_op jit(solution)/shard_map/ppermute | solution.py:429
  15.9 5.0 %collective-permute-start.5 = (bf16[192,128]{1,0:T(8,128)(2,1)S(1)}, bf16[192,128]{1,0:T(8,128)(2,1)S(1)}, u32[]{:S(2)}, u32[]{:S(2)}) collective-permute-start(bf16[192,128]{1,0:T(8,128)(2,1)S(1)} %get-tuple-element.23), channel_id=1, source_target_pairs={{0,1},{1,0},{2,3},{3,2},{4,5},{5,4},{6,7},{7,6},{8,9},{9,8},{10,11... | collective-permute-start | bytes 147464 | tf_op jit(solution)/shard_map/ppermute | solution.py:429
  17.1 4.3 %collective-permute-start.6 = (bf16[192,128]{1,0:T(8,128)(2,1)S(1)}, bf16[192,128]{1,0:T(8,128)(2,1)S(1)}, u32[]{:S(2)}, u32[]{:S(2)}) collective-permute-start(bf16[192,128]{1,0:T(8,128)(2,1)S(1)} %get-tuple-element.24), channel_id=1, source_target_pairs={{0,1},{1,0},{2,3},{3,2},{4,5},{5,4},{6,7},{7,6},{8,9},{9,8},{10,11... | collective-permute-start | bytes 147464 | tf_op jit(solution)/shard_map/ppermute | solution.py:429

commit v26 on v19

--- a/solution.py
+++ b/solution.py
@@ -184,7 +184,7 @@
         outgoing[d - 1][pl.ds(cols, ROWS)] = jnp.broadcast_to(row, (ROWS, width))
 
 
-def write_start(states, first, out_ref, sems):
+def write_copies(states, first, out_ref, sems):
     copies = []
     for s, state_ref in enumerate(states, first):
         width = state_ref.shape[2]
@@ -192,9 +192,15 @@
             copies.append(
                 pltpu.make_async_copy(state_ref.at[i], out_ref.at[s, :, pl.ds(i * width, width)], sems.at[s, i])
             )
+    return copies
+
+
+def write(states, first, out_ref, sems):
+    copies = write_copies(states, first, out_ref, sems)
     for copy in copies:
         copy.start()
-    return copies
+    for copy in copies:
+        copy.wait()
 
 
 def own_kernel(step, state_ref, jac_ref, iface_ref, table_ref, marks_ref, z_ref):
@@ -287,29 +293,28 @@
         give(made, marks_ref, state_ref, outgoing)
 
 
-def close_kernel(step, section, firsts, send, before, *refs):
+def write_kernel(step, section, firsts, before, state_ref, jac_ref, iface_ref, table_ref, marks_ref, *refs):
     n = lax.axis_size("net")
     *refs, sems = refs
+    before, refs = refs[:before], refs[before:]
     if firsts:
         *refs, made_ref, acc_ref, cols_ref, send_ref, recv_ref, live_ref, load_sems = refs
         ints = [cols_ref, send_ref, recv_ref, live_ref]
-    z_ref, iface_ref, table_ref, marks_ref, *refs = refs
-    arrived, refs = by_distance(refs[: n - 1], False), refs[n - 1 :]
-    before, refs = refs[:before], refs[before:]
-    if firsts:
-        opening_ref, handed, jac_ref, sources, refs = refs[0], refs[1:n], refs[n], refs[n + 1 : n + 5], refs[n + 5 :]
+        opening_ref, handed, sources, (z_ref, out_ref) = refs[0], refs[1:n], refs[n : n + 4], refs[n + 4 :]
     else:
-        refs = refs[1:]
-    out_ref, state_ref, *outgoing = refs
-
-    @pl.when(lax.axis_index("tm") == section)
-    def _():
-        copies = write_start(before, 0, out_ref, sems)
-        sums = [z_ref[i] for i in range(z_ref.shape[0])]
-        made = joined(sums, step, iface_ref, marks_ref, arrived)
-        give(made, marks_ref, state_ref, outgoing)
-        copies += write_start([state_ref], len(before), out_ref, sems)
-        for copy in copies:
+        _, z_ref, out_ref = refs
+    here = lax.axis_index("tm") == section
+
+    @pl.when(here)
+    def _():
+        for copy in write_copies(before, 0, out_ref, sems):
+            copy.start()
+
+    own_kernel(step, state_ref, jac_ref, iface_ref, table_ref, marks_ref, z_ref)
+
+    @pl.when(here)
+    def _():
+        for copy in write_copies(before, 0, out_ref, sems):
             copy.wait()
 
     if firsts:
@@ -325,8 +330,18 @@
             for load in loads:
                 load.wait()
             made = first_states(opening_ref, handed, jac_ref, iface_ref, ints, table_ref, made_ref, acc_ref)
-            for copy in write_start(made, 0, out_ref, sems):
-                copy.wait()
+            write(made, 0, out_ref, sems)
+
+
+def close_kernel(step, section, place, z_ref, iface_ref, marks_ref, *refs):
+    n = lax.axis_size("net")
+    arrived, (_, out_ref, state_ref, *outgoing, sems) = by_distance(refs[: n - 1], False), refs[n - 1 :]
+
+    @pl.when(lax.axis_index("tm") == section)
+    def _():
+        sums = [z_ref[i] for i in range(z_ref.shape[0])]
+        give(joined(sums, step, iface_ref, marks_ref, arrived), marks_ref, state_ref, outgoing)
+        write([state_ref], place, out_ref, sems)
 
 
 def local(jac, block_cols, iface_jac, iface_send, iface_recv, iface_live, ctrl_node, ctrl_gain):
@@ -383,15 +398,15 @@
             compiler_params=LIMIT,
         )(z, iface_jac, table, marks, *[arrived[d - 1] for d in exchange_order(n, step == 0)])
 
-    def close(z, step, arrived, section, before, out, send):
+    def own_and_write(state, step, section, before, out):
         firsts = out is None
-        arrays = [z, iface_jac, table, marks, *[arrived[d - 1] for d in exchange_order(n, False)], *before]
+        arrays = [state, jac, iface_jac, table, marks, *before]
         specs = [VMEM] * len(arrays)
         scratch = [DMA((steps, blocks))]
         aliases = {}
         if firsts:
-            arrays += [opening, *handed, jac, *pinned[2:6]]
-            specs += [VMEM] * (n + 1) + [HBM] * 4
+            arrays += [opening, *handed, *pinned[2:6]]
+            specs += [VMEM] * n + [HBM] * 4
             scratch = [
                 pltpu.VMEM((2, *whole.shape), jnp.bfloat16),
                 pltpu.VMEM(whole.shape, jnp.float32),
@@ -399,24 +414,30 @@
                 DMA((4,)),
             ] + scratch
         else:
-            aliases = {len(arrays): 0}
+            aliases = {len(arrays): 1}
             arrays.append(out)
             specs.append(ANY)
-        shapes, out_specs = [written], [ANY]
-        if send:
-            shapes += [whole] + [one] * (n - 1)
-            out_specs += [VMEM] * n
-        else:
-            scratch.insert(0, pltpu.VMEM(whole.shape, jnp.bfloat16))
         return pl.pallas_call(
-            functools.partial(close_kernel, step, section, firsts, send, len(before)),
-            out_shape=shapes,
+            functools.partial(write_kernel, step, section, firsts, len(before)),
+            out_shape=[f32(whole.shape), written],
             in_specs=specs,
-            out_specs=out_specs,
+            out_specs=[VMEM, ANY],
             input_output_aliases=aliases,
             scratch_shapes=scratch,
             compiler_params=LIMIT,
         )(*arrays)
+
+    def close(z, step, arrived, section, out, send):
+        ordered = [arrived[d - 1] for d in exchange_order(n, False)]
+        return pl.pallas_call(
+            functools.partial(close_kernel, step, section, steps - 1),
+            out_shape=[written] + ([whole] + [one] * (n - 1) if send else []),
+            in_specs=[VMEM] * (n + 2) + [ANY],
+            out_specs=[ANY] + [VMEM] * (n if send else 0),
+            input_output_aliases={n + 2: 0},
+            scratch_shapes=([] if send else [pltpu.VMEM(whole.shape, jnp.bfloat16)]) + [DMA((steps, blocks))],
+            compiler_params=LIMIT,
+        )(z, iface_jac, marks, *ordered, out)
 
     def swap(block, first, second, d):
         other = {first: second, second: first}
@@ -443,12 +464,12 @@
             fix = r == 1 and s == 0
             if s > 0:
                 arrived = exchange(outgoing, r, r)
-            z = own(state, s)
             if s < steps - 1:
-                state, *outgoing = join(z, s, fix, arrived, r)
+                state, *outgoing = join(own(state, s), s, fix, arrived, r)
                 before.append(state)
             else:
-                out, *rest = close(z, s, arrived, r, before, out, r < tm - 1)
+                z, out = own_and_write(state, s, r, before, out)
+                out, *rest = close(z, s, arrived, r, out, r < tm - 1)
                 state, *outgoing = rest or [None]
     return out
 

time: 22 us -> 21.9 us (level)
  waiting for transfers between devices: 7.21 us -> 6.87 us
  Pallas kernels: 3.49 us -> 3.79 us
    pallas_call x1 -> x2, Pallas kernels: 1.03 us -> 1.78 us  [the longest x1 0.99 us: close(): pl.pallas_call(functools.partial(close_kernel, step, section, steps - 1),...]
    pallas_call x2 -> x1, Pallas kernels: 0.9 us -> 0.46 us  [own(): pl.pallas_call(functools.partial(own_kernel, step), out_shape=f32(whole.s...]
    ppermute x7, waiting for transfers between devices: 7.21 us -> 6.87 us  [swap(): return lax.ppermute(block, ('tm', 'net', 'cols'), pairs)]
  transfers between devices with their start and end apart: 7 -> 7, of which waited for: 5 -> 5; matrix products, arithmetic and copies ran while one was open for 0% -> 0% of each run, Pallas kernels for 4% -> 6%
where the time goes in v26:
time: 21.9 us; the launch traced here: 21.8 us
  starting transfers between devices  11.1 us (51%)
  waiting for transfers between devices  6.87 us (31%)
  Pallas kernels  3.79 us (17%)
    ppermute x7, starting transfers between devices, swap(): return lax.ppermute(block, ('tm', 'net', 'cols'), pairs)  11.1 us
    ppermute x7, waiting for transfers between devices, swap(): return lax.ppermute(block, ('tm', 'net', 'cols'), pairs)  6.87 us
    pallas_call x1, Pallas kernels, local(): pl.pallas_call(second_kernel, out_shape=[f32((cols, table_rows)), f32((ma...  1.11 us
    pallas_call x1, Pallas kernels, close(): pl.pallas_call(functools.partial(close_kernel, step, section, steps - 1),...  0.99 us
    pallas_call x1, Pallas kernels, own_and_write(): pl.pallas_call(functools.partial(write_kernel, step, section, firsts, len...  0.79 us
    pallas_call x1, Pallas kernels, own(): pl.pallas_call(functools.partial(own_kernel, step), out_shape=f32(whole.s...  0.46 us
    pallas_call x1, Pallas kernels, join(): pl.pallas_call(functools.partial(join_kernel, step, kinds if fix else 0,...  0.45 us
  transfers between devices with their start and end apart: 7, of which 5 were waited for; matrix products, arithmetic and copies ran while one was open for 0% of the time, Pallas kernels for 6%

profile of v26, /device:TPU:4, one launch (start us, length us, event | category | flops | bytes accessed | tf_op | source)
XLA Modules:
  0.0 21.8 jit_solution(14574124437372199610)
XLA Ops:
  0.0 0.0 copy-start
  0.0 0.0 copy-start.1
  0.0 1.1 %shard_map.82 = (f32[192,8]{1,0:T(8,128)S(1)}, f32[72,128]{1,0:T(8,128)S(1)}, bf16[4,192,128]{2,1,0:T(8,128)(2,1)S(1)}, bf16[208,128]{1,0:T(8,128)(2,1)S(1)}, bf...) custom-call(bf16[2,4,3,128,128]{4,3,2,1,0:T(8,128)(2,1)} %jac_ref.3, bf16[2,1,4,128,128]{4,3,2,1,0:T(8,128)(2,1)} %iface_ref.7, ...), custom_call_target="tpu_custom_call" | custom-call | tf_op jit(solution)/shard_map/pallas_call | solution.py:366
  1.1 0.1 collective-permute-start
  1.2 4.0 %collective-permute-start.1 = (bf16[208,128]{1,0:T(8,128)(2,1)S(1)}, bf16[208,128]{1,0:T(8,128)(2,1)S(1)}, u32[]{:S(2)}, u32[]{:S(2)}) collective-permute-start(bf16[208,128]{1,0:T(8,128)(2,1)S(1)} %get-tuple-element.20), channel_id=1, source_target_pairs={{0,24},{1,25},{2,26},{3,27},{4,28},{5,29},{6,30},{7,31},{8,16},{9,... | collective-permute-start | bytes 159752 | tf_op jit(solution)/shard_map/ppermute | solution.py:450
  5.2 2.3 %collective-permute-start.2 = (bf16[208,128]{1,0:T(8,128)(2,1)S(1)}, bf16[208,128]{1,0:T(8,128)(2,1)S(1)}, u32[]{:S(2)}, u32[]{:S(2)}) collective-permute-start(bf16[208,128]{1,0:T(8,128)(2,1)S(1)} %get-tuple-element.21), channel_id=1, source_target_pairs={{0,28},{1,29},{2,30},{3,31},{4,24},{5,25},{6,26},{7,27},{8,20},{9,... | collective-permute-start | bytes 159752 | tf_op jit(solution)/shard_map/ppermute | solution.py:450
  7.5 0.2 %collective-permute-start.3 = (bf16[208,128]{1,0:T(8,128)(2,1)S(1)}, bf16[208,128]{1,0:T(8,128)(2,1)S(1)}, u32[]{:S(2)}, u32[]{:S(2)}) collective-permute-start(bf16[208,128]{1,0:T(8,128)(2,1)S(1)} %get-tuple-element.22), channel_id=1, source_target_pairs={{0,20},{1,21},{2,22},{3,23},{4,16},{5,17},{6,18},{7,19},{8,28},{9,... | collective-permute-start | bytes 159752 | tf_op jit(solution)/shard_map/ppermute | solution.py:450
  7.7 1.2 %collective-permute-done.state_ref = bf16[4,192,128]{2,1,0:T(8,128)(2,1)S(1)} collective-permute-done((bf16[4,192,128]{2,1,0:T(8,128)(2,1)S(1)}, bf16[4,192,128]{2,1,0:T(8,128)(2,1)S(1)}, u32[]{:S(2)}, u32[]{:S(2)}) %collective-permute-start) | collective-permute-done | bytes 196640 | tf_op jit(solution)/shard_map/ppermute | solution.py:450
  9.0 0.0 copy-done
  9.0 0.0 copy-done.1
  9.0 0.5 %shard_map.83.z_ref = f32[4,192,128]{2,1,0:T(8,128)S(1)} custom-call(bf16[4,192,128]{2,1,0:T(8,128)(2,1)S(1)} %collective-permute-done.state_ref, bf16[2,4,3,128,128]{4,3,2,1,0:T(8,128)(2,1)S(1)} %copy-done, bf16[2,1,4,128,128]{4,3,2,1,0:T(8,128)(2,1)S(1)} %copy-done.1, f32[192,8]{1,0:T(8,128)S(1)} %get-tuple-element.18.table_ref, ...), custom_call_target="tpu_custom_call" | custom-call | tf_op jit(solution)/shard_map/pallas_call | solution.py:384
  9.4 0.0 collective-permute-done.1.refs_0_.refs_3_
  9.4 2.8 %collective-permute-done.2.refs_1_.refs_4_ = bf16[208,128]{1,0:T(8,128)(2,1)S(1)} collective-permute-done((bf16[208,128]{1,0:T(8,128)(2,1)S(1)}, bf16[208,128]{1,0:T(8,128)(2,1)S(1)}, u32[]{:S(2)}, u32[]{:S(2)}) %collective-permute-start.2) | collective-permute-done | bytes 53280 | tf_op jit(solution)/shard_map/ppermute | solution.py:450
  12.3 0.5 %collective-permute-done.3.refs_2_ = bf16[208,128]{1,0:T(8,128)(2,1)S(1)} collective-permute-done((bf16[208,128]{1,0:T(8,128)(2,1)S(1)}, bf16[208,128]{1,0:T(8,128)(2,1)S(1)}, u32[]{:S(2)}, u32[]{:S(2)}) %collective-permute-start.3) | collective-permute-done | bytes 53280 | tf_op jit(solution)/shard_map/ppermute | solution.py:450
  12.8 0.4 %shard_map.84 = (bf16[4,192,128]{2,1,0:T(8,128)(2,1)S(1)}, bf16[192,128]{1,0:T(8,128)(2,1)S(1)}, bf16[192,128]{1,0:T(8,128)(2,1)S(1)}, bf16[192,128]{1,0:T(8,128)(2,1)S(1)}) custom-call(f32[4,192,128]{2,1,0:T(8,128)S(1)} %shard_map.83.z_ref, bf16[2,1,4,128,128]{4,3,2,1,0:T(8,128)(2,1)S(1)} %copy-done.1, f32[192,8]{1,0:T(8,128)S(1)} %get-tuple-element.18.table_ref, ...), custom_call_target="tpu_custom_call" | custom-call | tf_op jit(solution)/shard_map/pallas_call | solution.py:393
  13.3 2.2 %collective-permute-start.4 = (bf16[192,128]{1,0:T(8,128)(2,1)S(1)}, bf16[192,128]{1,0:T(8,128)(2,1)S(1)}, u32[]{:S(2)}, u32[]{:S(2)}) collective-permute-start(bf16[192,128]{1,0:T(8,128)(2,1)S(1)} %get-tuple-element.25), channel_id=1, source_target_pairs={{0,1},{1,0},{2,3},{3,2},{4,5},{5,4},{6,7},{7,6},{8,9},{9,8},{10,11... | collective-permute-start | bytes 147464 | tf_op jit(solution)/shard_map/ppermute | solution.py:450
  15.5 0.0 collective-permute-start.5
  15.5 2.2 %collective-permute-start.6 = (bf16[192,128]{1,0:T(8,128)(2,1)S(1)}, bf16[192,128]{1,0:T(8,128)(2,1)S(1)}, u32[]{:S(2)}, u32[]{:S(2)}) collective-permute-start(bf16[192,128]{1,0:T(8,128)(2,1)S(1)} %get-tuple-element.27), channel_id=1, source_target_pairs={{0,1},{1,0},{2,3},{3,2},{4,5},{5,4},{6,7},{7,6},{8,9},{9,8},{10,11... | collective-permute-start | bytes 147464 | tf_op jit(solution)/shard_map/ppermute | solution.py:450
  17.7 0.8 %shard_map.85 = (f32[4,192,128]{2,1,0:T(8,128)S(1)}, bf16[2,192,512]{2,1,0:T(8,128)(2,1)}) custom-call(bf16[4,192,128]{2,1,0:T(8,128)(2,1)S(1)} %get-tuple-element.23.state_ref.refs_0_, bf16[2,4,3,128,128]{4,3,2,1,0:T(8,128)(2,1)S(1)} %copy-done, bf16[2,1,4,128,128]{4,3,2,1,0:T(8,128)(2,1)S(1)} %copy-done.1, f32[192,8]{1,0:T(8,128)S(1)} %get-tuple-element.18.table_ref, ...), custom_call_target="tpu_custom_call" | custom-call | tf_op jit(solution)/shard_map/pallas_call | solution.py:420
  18.5 0.9 %collective-permute-done.4.refs_0_ = bf16[192,128]{1,0:T(8,128)(2,1)S(1)} collective-permute-done((bf16[192,128]{1,0:T(8,128)(2,1)S(1)}, bf16[192,128]{1,0:T(8,128)(2,1)S(1)}, u32[]{:S(2)}, u32[]{:S(2)}) %collective-permute-start.4) | collective-permute-done | bytes 49184 | tf_op jit(solution)/shard_map/ppermute | solution.py:450
  19.5 1.3 %collective-permute-done.5.refs_1_ = bf16[192,128]{1,0:T(8,128)(2,1)S(1)} collective-permute-done((bf16[192,128]{1,0:T(8,128)(2,1)S(1)}, bf16[192,128]{1,0:T(8,128)(2,1)S(1)}, u32[]{:S(2)}, u32[]{:S(2)}) %collective-permute-start.5) | collective-permute-done | bytes 49184 | tf_op jit(solution)/shard_map/ppermute | solution.py:450
  20.8 0.0 collective-permute-done.6.refs_2_
  20.8 1.0 %shard_map.86 = bf16[2,192,512]{2,1,0:T(8,128)(2,1)} custom-call(f32[4,192,128]{2,1,0:T(8,128)S(1)} %get-tuple-element.24.z_ref, bf16[2,1,4,128,128]{4,3,2,1,0:T(8,128)(2,1)S(1)} %copy-done.1, f32[72,128]{1,0:T(8,128)S(1)} %get-tuple-element.19.marks_ref, bf16[192,128]{1,0:T(8,128)(2,1)S(1)} %collective-permute-done.4.refs_0_, ...), custom_call_target="tpu_custom_call", output_to_operand_aliasing={{}: (6, {})} | custom-call | tf_op jit(solution)/shard_map/pallas_call | solution.py:432
Async XLA Ops:
  0.0 9.0 %copy-start = (bf16[2,4,3,128,128]{4,3,2,1,0:T(8,128)(2,1)S(1)}, bf16[2,4,3,128,128]{4,3,2,1,0:T(8,128)(2,1)}, u32[]{:S(2)}) copy-start(bf16[2,4,3,128,128]{4,3,2,1,0:T(8,128)(2,1)} %jac_ref.3) | copy-start | bytes 2359300
  0.0 9.0 %copy-start.1 = (bf16[2,1,4,128,128]{4,3,2,1,0:T(8,128)(2,1)S(1)}, bf16[2,1,4,128,128]{4,3,2,1,0:T(8,128)(2,1)}, u32[]{:S(2)}) copy-start(bf16[2,1,4,128,128]{4,3,2,1,0:T(8,128)(2,1)} %iface_ref.7) | copy-start | bytes 786436
  1.1 7.8 %collective-permute-start = (bf16[4,192,128]{2,1,0:T(8,128)(2,1)S(1)}, bf16[4,192,128]{2,1,0:T(8,128)(2,1)S(1)}, u32[]{:S(2)}, u32[]{:S(2)}) collective-permute-start(bf16[4,192,128]{2,1,0:T(8,128)(2,1)S(1)} %get-tuple-element.17.refs_1_), channel_id=1, source_target_pairs={{0,16},{1,17},{2,18},{3,19},{4,20},{5,21},{6,22},{7,23},{8,24},{9,... | collective-permute-start | bytes 589832 | tf_op jit(solution)/shard_map/ppermute | solution.py:450
  1.2 8.2 %collective-permute-start.1 = (bf16[208,128]{1,0:T(8,128)(2,1)S(1)}, bf16[208,128]{1,0:T(8,128)(2,1)S(1)}, u32[]{:S(2)}, u32[]{:S(2)}) collective-permute-start(bf16[208,128]{1,0:T(8,128)(2,1)S(1)} %get-tuple-element.20), channel_id=1, source_target_pairs={{0,24},{1,25},{2,26},{3,27},{4,28},{5,29},{6,30},{7,31},{8,16},{9,... | collective-permute-start | bytes 159752 | tf_op jit(solution)/shard_map/ppermute | solution.py:450
  5.2 7.0 %collective-permute-start.2 = (bf16[208,128]{1,0:T(8,128)(2,1)S(1)}, bf16[208,128]{1,0:T(8,128)(2,1)S(1)}, u32[]{:S(2)}, u32[]{:S(2)}) collective-permute-start(bf16[208,128]{1,0:T(8,128)(2,1)S(1)} %get-tuple-element.21), channel_id=1, source_target_pairs={{0,28},{1,29},{2,30},{3,31},{4,24},{5,25},{6,26},{7,27},{8,20},{9,... | collective-permute-start | bytes 159752 | tf_op jit(solution)/shard_map/ppermute | solution.py:450
  7.5 5.3 %collective-permute-start.3 = (bf16[208,128]{1,0:T(8,128)(2,1)S(1)}, bf16[208,128]{1,0:T(8,128)(2,1)S(1)}, u32[]{:S(2)}, u32[]{:S(2)}) collective-permute-start(bf16[208,128]{1,0:T(8,128)(2,1)S(1)} %get-tuple-element.22), channel_id=1, source_target_pairs={{0,20},{1,21},{2,22},{3,23},{4,16},{5,17},{6,18},{7,19},{8,28},{9,... | collective-permute-start | bytes 159752 | tf_op jit(solution)/shard_map/ppermute | solution.py:450
  13.3 6.2 %collective-permute-start.4 = (bf16[192,128]{1,0:T(8,128)(2,1)S(1)}, bf16[192,128]{1,0:T(8,128)(2,1)S(1)}, u32[]{:S(2)}, u32[]{:S(2)}) collective-permute-start(bf16[192,128]{1,0:T(8,128)(2,1)S(1)} %get-tuple-element.25), channel_id=1, source_target_pairs={{0,1},{1,0},{2,3},{3,2},{4,5},{5,4},{6,7},{7,6},{8,9},{9,8},{10,11... | collective-permute-start | bytes 147464 | tf_op jit(solution)/shard_map/ppermute | solution.py:450
  15.5 5.3 %collective-permute-start.5 = (bf16[192,128]{1,0:T(8,128)(2,1)S(1)}, bf16[192,128]{1,0:T(8,128)(2,1)S(1)}, u32[]{:S(2)}, u32[]{:S(2)}) collective-permute-start(bf16[192,128]{1,0:T(8,128)(2,1)S(1)} %get-tuple-element.26), channel_id=1, source_target_pairs={{0,1},{1,0},{2,3},{3,2},{4,5},{5,4},{6,7},{7,6},{8,9},{9,8},{10,11... | collective-permute-start | bytes 147464 | tf_op jit(solution)/shard_map/ppermute | solution.py:450
  15.5 5.3 %collective-permute-start.6 = (bf16[192,128]{1,0:T(8,128)(2,1)S(1)}, bf16[192,128]{1,0:T(8,128)(2,1)S(1)}, u32[]{:S(2)}, u32[]{:S(2)}) collective-permute-start(bf16[192,128]{1,0:T(8,128)(2,1)S(1)} %get-tuple-element.27), channel_id=1, source_target_pairs={{0,1},{1,0},{2,3},{3,2},{4,5},{5,4},{6,7},{7,6},{8,9},{9,8},{10,11... | collective-permute-start | bytes 147464 | tf_op jit(solution)/shard_map/ppermute | solution.py:450

commit v27 on v26

--- a/solution.py
+++ b/solution.py
@@ -261,7 +261,7 @@
     blocks = len(made)
     n = lax.axis_size("net")
     sent = marks_layout(n, blocks, 1)[0]
-    for i in range(blocks):
+    for i in range(blocks) if state_ref is not None else ():
         state_ref[i] = made[i]
     for d in range(1, n) if outgoing else ():
         marks = [marks_ref[pl.ds(sent + d * blocks + j, 1)].astype(made[j].dtype) for j in range(blocks)]
@@ -339,9 +339,22 @@
 
     @pl.when(lax.axis_index("tm") == section)
     def _():
-        sums = [z_ref[i] for i in range(z_ref.shape[0])]
-        give(joined(sums, step, iface_ref, marks_ref, arrived), marks_ref, state_ref, outgoing)
-        write([state_ref], place, out_ref, sems)
+        me = lax.axis_index("net")
+        blocks = z_ref.shape[0]
+        terms = [times_transposed(block[...], iface_ref[step, 0, me ^ d]) for d, block in enumerate(arrived, 1)]
+        copies = write_copies([state_ref], place, out_ref, sems)
+        made = []
+        for i in range(blocks):
+            total = z_ref[i]
+            for d, term in enumerate(terms, 1):
+                total += term * marks_ref[pl.ds(d * blocks + i, 1)]
+            made.append(total.astype(state_ref.dtype))
+            state_ref[i] = made[i]
+            copies[i].start()
+        if outgoing:
+            give(made, marks_ref, None, outgoing)
+        for copy in copies:
+            copy.wait()
 
 
 def local(jac, block_cols, iface_jac, iface_send, iface_recv, iface_live, ctrl_node, ctrl_gain):

time: 21.9 us -> 21.9 us (level)
  no operation moved by 1% of the time
where the time goes in v27:
time: 21.9 us; the launch traced here: 21.8 us
  starting transfers between devices  11.1 us (51%)
  waiting for transfers between devices  6.87 us (31%)
  Pallas kernels  3.79 us (17%)
    ppermute x7, starting transfers between devices, swap(): return lax.ppermute(block, ('tm', 'net', 'cols'), pairs)  11.1 us
    ppermute x7, waiting for transfers between devices, swap(): return lax.ppermute(block, ('tm', 'net', 'cols'), pairs)  6.87 us
    pallas_call x1, Pallas kernels, local(): pl.pallas_call(second_kernel, out_shape=[f32((cols, table_rows)), f32((ma...  1.11 us
    pallas_call x1, Pallas kernels, close(): pl.pallas_call(functools.partial(close_kernel, step, section, steps - 1),...  0.99 us
    pallas_call x1, Pallas kernels, own_and_write(): pl.pallas_call(functools.partial(write_kernel, step, section, firsts, len...  0.79 us
    pallas_call x1, Pallas kernels, own(): pl.pallas_call(functools.partial(own_kernel, step), out_shape=f32(whole.s...  0.46 us
    pallas_call x1, Pallas kernels, join(): pl.pallas_call(functools.partial(join_kernel, step, kinds if fix else 0,...  0.45 us
  transfers between devices with their start and end apart: 7, of which 5 were waited for; matrix products, arithmetic and copies ran while one was open for 0% of the time, Pallas kernels for 6%

profile of v27, /device:TPU:4, one launch (start us, length us, event | category | flops | bytes accessed | tf_op | source)
XLA Modules:
  0.0 21.8 jit_solution(476365462722906899)
XLA Ops:
  0.0 0.0 copy-start
  0.0 0.0 copy-start.1
  0.0 1.1 %shard_map.82 = (f32[192,8]{1,0:T(8,128)S(1)}, f32[72,128]{1,0:T(8,128)S(1)}, bf16[4,192,128]{2,1,0:T(8,128)(2,1)S(1)}, bf16[208,128]{1,0:T(8,128)(2,1)S(1)}, bf...) custom-call(bf16[2,4,3,128,128]{4,3,2,1,0:T(8,128)(2,1)} %jac_ref.3, bf16[2,1,4,128,128]{4,3,2,1,0:T(8,128)(2,1)} %iface_ref.7, ...), custom_call_target="tpu_custom_call" | custom-call | tf_op jit(solution)/shard_map/pallas_call | solution.py:379
  1.1 0.1 collective-permute-start
  1.2 4.0 %collective-permute-start.1 = (bf16[208,128]{1,0:T(8,128)(2,1)S(1)}, bf16[208,128]{1,0:T(8,128)(2,1)S(1)}, u32[]{:S(2)}, u32[]{:S(2)}) collective-permute-start(bf16[208,128]{1,0:T(8,128)(2,1)S(1)} %get-tuple-element.20), channel_id=1, source_target_pairs={{0,24},{1,25},{2,26},{3,27},{4,28},{5,29},{6,30},{7,31},{8,16},{9,... | collective-permute-start | bytes 159752 | tf_op jit(solution)/shard_map/ppermute | solution.py:463
  5.2 2.3 %collective-permute-start.2 = (bf16[208,128]{1,0:T(8,128)(2,1)S(1)}, bf16[208,128]{1,0:T(8,128)(2,1)S(1)}, u32[]{:S(2)}, u32[]{:S(2)}) collective-permute-start(bf16[208,128]{1,0:T(8,128)(2,1)S(1)} %get-tuple-element.21), channel_id=1, source_target_pairs={{0,28},{1,29},{2,30},{3,31},{4,24},{5,25},{6,26},{7,27},{8,20},{9,... | collective-permute-start | bytes 159752 | tf_op jit(solution)/shard_map/ppermute | solution.py:463
  7.5 0.2 %collective-permute-start.3 = (bf16[208,128]{1,0:T(8,128)(2,1)S(1)}, bf16[208,128]{1,0:T(8,128)(2,1)S(1)}, u32[]{:S(2)}, u32[]{:S(2)}) collective-permute-start(bf16[208,128]{1,0:T(8,128)(2,1)S(1)} %get-tuple-element.22), channel_id=1, source_target_pairs={{0,20},{1,21},{2,22},{3,23},{4,16},{5,17},{6,18},{7,19},{8,28},{9,... | collective-permute-start | bytes 159752 | tf_op jit(solution)/shard_map/ppermute | solution.py:463
  7.7 1.2 %collective-permute-done.state_ref = bf16[4,192,128]{2,1,0:T(8,128)(2,1)S(1)} collective-permute-done((bf16[4,192,128]{2,1,0:T(8,128)(2,1)S(1)}, bf16[4,192,128]{2,1,0:T(8,128)(2,1)S(1)}, u32[]{:S(2)}, u32[]{:S(2)}) %collective-permute-start) | collective-permute-done | bytes 196640 | tf_op jit(solution)/shard_map/ppermute | solution.py:463
  9.0 0.0 copy-done
  9.0 0.0 copy-done.1
  9.0 0.5 %shard_map.83.z_ref = f32[4,192,128]{2,1,0:T(8,128)S(1)} custom-call(bf16[4,192,128]{2,1,0:T(8,128)(2,1)S(1)} %collective-permute-done.state_ref, bf16[2,4,3,128,128]{4,3,2,1,0:T(8,128)(2,1)S(1)} %copy-done, bf16[2,1,4,128,128]{4,3,2,1,0:T(8,128)(2,1)S(1)} %copy-done.1, f32[192,8]{1,0:T(8,128)S(1)} %get-tuple-element.18.table_ref, ...), custom_call_target="tpu_custom_call" | custom-call | tf_op jit(solution)/shard_map/pallas_call | solution.py:397
  9.4 0.0 collective-permute-done.1.refs_0_.refs_3_
  9.4 2.8 %collective-permute-done.2.refs_1_.refs_4_ = bf16[208,128]{1,0:T(8,128)(2,1)S(1)} collective-permute-done((bf16[208,128]{1,0:T(8,128)(2,1)S(1)}, bf16[208,128]{1,0:T(8,128)(2,1)S(1)}, u32[]{:S(2)}, u32[]{:S(2)}) %collective-permute-start.2) | collective-permute-done | bytes 53280 | tf_op jit(solution)/shard_map/ppermute | solution.py:463
  12.3 0.5 %collective-permute-done.3.refs_2_ = bf16[208,128]{1,0:T(8,128)(2,1)S(1)} collective-permute-done((bf16[208,128]{1,0:T(8,128)(2,1)S(1)}, bf16[208,128]{1,0:T(8,128)(2,1)S(1)}, u32[]{:S(2)}, u32[]{:S(2)}) %collective-permute-start.3) | collective-permute-done | bytes 53280 | tf_op jit(solution)/shard_map/ppermute | solution.py:463
  12.8 0.4 %shard_map.84 = (bf16[4,192,128]{2,1,0:T(8,128)(2,1)S(1)}, bf16[192,128]{1,0:T(8,128)(2,1)S(1)}, bf16[192,128]{1,0:T(8,128)(2,1)S(1)}, bf16[192,128]{1,0:T(8,128)(2,1)S(1)}) custom-call(f32[4,192,128]{2,1,0:T(8,128)S(1)} %shard_map.83.z_ref, bf16[2,1,4,128,128]{4,3,2,1,0:T(8,128)(2,1)S(1)} %copy-done.1, f32[192,8]{1,0:T(8,128)S(1)} %get-tuple-element.18.table_ref, ...), custom_call_target="tpu_custom_call" | custom-call | tf_op jit(solution)/shard_map/pallas_call | solution.py:406
  13.3 2.2 %collective-permute-start.4 = (bf16[192,128]{1,0:T(8,128)(2,1)S(1)}, bf16[192,128]{1,0:T(8,128)(2,1)S(1)}, u32[]{:S(2)}, u32[]{:S(2)}) collective-permute-start(bf16[192,128]{1,0:T(8,128)(2,1)S(1)} %get-tuple-element.25), channel_id=1, source_target_pairs={{0,1},{1,0},{2,3},{3,2},{4,5},{5,4},{6,7},{7,6},{8,9},{9,8},{10,11... | collective-permute-start | bytes 147464 | tf_op jit(solution)/shard_map/ppermute | solution.py:463
  15.5 0.0 collective-permute-start.5
  15.5 2.2 %collective-permute-start.6 = (bf16[192,128]{1,0:T(8,128)(2,1)S(1)}, bf16[192,128]{1,0:T(8,128)(2,1)S(1)}, u32[]{:S(2)}, u32[]{:S(2)}) collective-permute-start(bf16[192,128]{1,0:T(8,128)(2,1)S(1)} %get-tuple-element.27), channel_id=1, source_target_pairs={{0,1},{1,0},{2,3},{3,2},{4,5},{5,4},{6,7},{7,6},{8,9},{9,8},{10,11... | collective-permute-start | bytes 147464 | tf_op jit(solution)/shard_map/ppermute | solution.py:463
  17.7 0.8 %shard_map.85 = (f32[4,192,128]{2,1,0:T(8,128)S(1)}, bf16[2,192,512]{2,1,0:T(8,128)(2,1)}) custom-call(bf16[4,192,128]{2,1,0:T(8,128)(2,1)S(1)} %get-tuple-element.23.state_ref.refs_0_, bf16[2,4,3,128,128]{4,3,2,1,0:T(8,128)(2,1)S(1)} %copy-done, bf16[2,1,4,128,128]{4,3,2,1,0:T(8,128)(2,1)S(1)} %copy-done.1, f32[192,8]{1,0:T(8,128)S(1)} %get-tuple-element.18.table_ref, ...), custom_call_target="tpu_custom_call" | custom-call | tf_op jit(solution)/shard_map/pallas_call | solution.py:433
  18.5 0.9 %collective-permute-done.4.refs_0_ = bf16[192,128]{1,0:T(8,128)(2,1)S(1)} collective-permute-done((bf16[192,128]{1,0:T(8,128)(2,1)S(1)}, bf16[192,128]{1,0:T(8,128)(2,1)S(1)}, u32[]{:S(2)}, u32[]{:S(2)}) %collective-permute-start.4) | collective-permute-done | bytes 49184 | tf_op jit(solution)/shard_map/ppermute | solution.py:463
  19.5 1.3 %collective-permute-done.5.refs_1_ = bf16[192,128]{1,0:T(8,128)(2,1)S(1)} collective-permute-done((bf16[192,128]{1,0:T(8,128)(2,1)S(1)}, bf16[192,128]{1,0:T(8,128)(2,1)S(1)}, u32[]{:S(2)}, u32[]{:S(2)}) %collective-permute-start.5) | collective-permute-done | bytes 49184 | tf_op jit(solution)/shard_map/ppermute | solution.py:463
  20.8 0.0 collective-permute-done.6.refs_2_
  20.8 1.0 %shard_map.86 = bf16[2,192,512]{2,1,0:T(8,128)(2,1)} custom-call(f32[4,192,128]{2,1,0:T(8,128)S(1)} %get-tuple-element.24.z_ref, bf16[2,1,4,128,128]{4,3,2,1,0:T(8,128)(2,1)S(1)} %copy-done.1, f32[72,128]{1,0:T(8,128)S(1)} %get-tuple-element.19.marks_ref, bf16[192,128]{1,0:T(8,128)(2,1)S(1)} %collective-permute-done.4.refs_0_, ...), custom_call_target="tpu_custom_call", output_to_operand_aliasing={{}: (6, {})} | custom-call | tf_op jit(solution)/shard_map/pallas_call | solution.py:445
Async XLA Ops:
  0.0 9.0 %copy-start = (bf16[2,4,3,128,128]{4,3,2,1,0:T(8,128)(2,1)S(1)}, bf16[2,4,3,128,128]{4,3,2,1,0:T(8,128)(2,1)}, u32[]{:S(2)}) copy-start(bf16[2,4,3,128,128]{4,3,2,1,0:T(8,128)(2,1)} %jac_ref.3) | copy-start | bytes 2359300
  0.0 9.0 %copy-start.1 = (bf16[2,1,4,128,128]{4,3,2,1,0:T(8,128)(2,1)S(1)}, bf16[2,1,4,128,128]{4,3,2,1,0:T(8,128)(2,1)}, u32[]{:S(2)}) copy-start(bf16[2,1,4,128,128]{4,3,2,1,0:T(8,128)(2,1)} %iface_ref.7) | copy-start | bytes 786436
  1.1 7.8 %collective-permute-start = (bf16[4,192,128]{2,1,0:T(8,128)(2,1)S(1)}, bf16[4,192,128]{2,1,0:T(8,128)(2,1)S(1)}, u32[]{:S(2)}, u32[]{:S(2)}) collective-permute-start(bf16[4,192,128]{2,1,0:T(8,128)(2,1)S(1)} %get-tuple-element.17.refs_1_), channel_id=1, source_target_pairs={{0,16},{1,17},{2,18},{3,19},{4,20},{5,21},{6,22},{7,23},{8,24},{9,... | collective-permute-start | bytes 589832 | tf_op jit(solution)/shard_map/ppermute | solution.py:463
  1.2 8.2 %collective-permute-start.1 = (bf16[208,128]{1,0:T(8,128)(2,1)S(1)}, bf16[208,128]{1,0:T(8,128)(2,1)S(1)}, u32[]{:S(2)}, u32[]{:S(2)}) collective-permute-start(bf16[208,128]{1,0:T(8,128)(2,1)S(1)} %get-tuple-element.20), channel_id=1, source_target_pairs={{0,24},{1,25},{2,26},{3,27},{4,28},{5,29},{6,30},{7,31},{8,16},{9,... | collective-permute-start | bytes 159752 | tf_op jit(solution)/shard_map/ppermute | solution.py:463
  5.2 7.0 %collective-permute-start.2 = (bf16[208,128]{1,0:T(8,128)(2,1)S(1)}, bf16[208,128]{1,0:T(8,128)(2,1)S(1)}, u32[]{:S(2)}, u32[]{:S(2)}) collective-permute-start(bf16[208,128]{1,0:T(8,128)(2,1)S(1)} %get-tuple-element.21), channel_id=1, source_target_pairs={{0,28},{1,29},{2,30},{3,31},{4,24},{5,25},{6,26},{7,27},{8,20},{9,... | collective-permute-start | bytes 159752 | tf_op jit(solution)/shard_map/ppermute | solution.py:463
  7.5 5.3 %collective-permute-start.3 = (bf16[208,128]{1,0:T(8,128)(2,1)S(1)}, bf16[208,128]{1,0:T(8,128)(2,1)S(1)}, u32[]{:S(2)}, u32[]{:S(2)}) collective-permute-start(bf16[208,128]{1,0:T(8,128)(2,1)S(1)} %get-tuple-element.22), channel_id=1, source_target_pairs={{0,20},{1,21},{2,22},{3,23},{4,16},{5,17},{6,18},{7,19},{8,28},{9,... | collective-permute-start | bytes 159752 | tf_op jit(solution)/shard_map/ppermute | solution.py:463
  13.3 6.2 %collective-permute-start.4 = (bf16[192,128]{1,0:T(8,128)(2,1)S(1)}, bf16[192,128]{1,0:T(8,128)(2,1)S(1)}, u32[]{:S(2)}, u32[]{:S(2)}) collective-permute-start(bf16[192,128]{1,0:T(8,128)(2,1)S(1)} %get-tuple-element.25), channel_id=1, source_target_pairs={{0,1},{1,0},{2,3},{3,2},{4,5},{5,4},{6,7},{7,6},{8,9},{9,8},{10,11... | collective-permute-start | bytes 147464 | tf_op jit(solution)/shard_map/ppermute | solution.py:463
  15.5 5.3 %collective-permute-start.5 = (bf16[192,128]{1,0:T(8,128)(2,1)S(1)}, bf16[192,128]{1,0:T(8,128)(2,1)S(1)}, u32[]{:S(2)}, u32[]{:S(2)}) collective-permute-start(bf16[192,128]{1,0:T(8,128)(2,1)S(1)} %get-tuple-element.26), channel_id=1, source_target_pairs={{0,1},{1,0},{2,3},{3,2},{4,5},{5,4},{6,7},{7,6},{8,9},{9,8},{10,11... | collective-permute-start | bytes 147464 | tf_op jit(solution)/shard_map/ppermute | solution.py:463
  15.5 5.3 %collective-permute-start.6 = (bf16[192,128]{1,0:T(8,128)(2,1)S(1)}, bf16[192,128]{1,0:T(8,128)(2,1)S(1)}, u32[]{:S(2)}, u32[]{:S(2)}) collective-permute-start(bf16[192,128]{1,0:T(8,128)(2,1)S(1)} %get-tuple-element.27), channel_id=1, source_target_pairs={{0,1},{1,0},{2,3},{3,2},{4,5},{5,4},{6,7},{7,6},{8,9},{9,8},{10,11... | collective-permute-start | bytes 147464 | tf_op jit(solution)/shard_map/ppermute | solution.py:463

commit v28 on v26

--- a/solution.py
+++ b/solution.py
@@ -269,7 +269,7 @@
 
 
 def exchange_order(n, handed):
-    return [*range(n // 2, n), *range(n // 2 - 1, 0, -1)] if handed else list(range(n - 1, 0, -1))
+    return [*range(n // 2, n), *range(n // 2 - 1, 0, -1)]
 
 
 def by_distance(refs, handed):

time: 21.9 us -> 22 us (level)
  waiting for transfers between devices: 6.87 us -> 7.83 us
  starting transfers between devices: 11.1 us -> 10.2 us
    ppermute x7, waiting for transfers between devices: 6.87 us -> 7.83 us  [swap(): return lax.ppermute(block, ('tm', 'net', 'cols'), pairs)]
    ppermute x7, starting transfers between devices: 11.1 us -> 10.2 us  [swap(): return lax.ppermute(block, ('tm', 'net', 'cols'), pairs)]
where the time goes in v28:
time: 22 us; the launch traced here: 21.8 us
  starting transfers between devices  10.2 us (46%)
  waiting for transfers between devices  7.83 us (36%)
  Pallas kernels  3.8 us (17%)
    ppermute x7, starting transfers between devices, swap(): return lax.ppermute(block, ('tm', 'net', 'cols'), pairs)  10.2 us
    ppermute x7, waiting for transfers between devices, swap(): return lax.ppermute(block, ('tm', 'net', 'cols'), pairs)  7.83 us
    pallas_call x1, Pallas kernels, local(): pl.pallas_call(second_kernel, out_shape=[f32((cols, table_rows)), f32((ma...  1.11 us
    pallas_call x1, Pallas kernels, close(): pl.pallas_call(functools.partial(close_kernel, step, section, steps - 1),...  1 us
    pallas_call x1, Pallas kernels, own_and_write(): pl.pallas_call(functools.partial(write_kernel, step, section, firsts, len...  0.79 us
    pallas_call x1, Pallas kernels, own(): pl.pallas_call(functools.partial(own_kernel, step), out_shape=f32(whole.s...  0.46 us
    pallas_call x1, Pallas kernels, join(): pl.pallas_call(functools.partial(join_kernel, step, kinds if fix else 0,...  0.45 us
  transfers between devices with their start and end apart: 7, of which 5 were waited for; matrix products, arithmetic and copies ran while one was open for 0% of the time, Pallas kernels for 6%

profile of v28, /device:TPU:4, one launch (start us, length us, event | category | flops | bytes accessed | tf_op | source)
XLA Modules:
  0.0 21.8 jit_solution(9524030437898094755)
XLA Ops:
  0.0 0.0 copy-start
  0.0 0.0 copy-start.1
  0.0 1.1 %shard_map.82 = (f32[192,8]{1,0:T(8,128)S(1)}, f32[72,128]{1,0:T(8,128)S(1)}, bf16[4,192,128]{2,1,0:T(8,128)(2,1)S(1)}, bf16[208,128]{1,0:T(8,128)(2,1)S(1)}, bf...) custom-call(bf16[2,4,3,128,128]{4,3,2,1,0:T(8,128)(2,1)} %jac_ref.3, bf16[2,1,4,128,128]{4,3,2,1,0:T(8,128)(2,1)} %iface_ref.7, ...), custom_call_target="tpu_custom_call" | custom-call | tf_op jit(solution)/shard_map/pallas_call | solution.py:366
  1.1 0.1 collective-permute-start
  1.2 4.0 %collective-permute-start.1 = (bf16[208,128]{1,0:T(8,128)(2,1)S(1)}, bf16[208,128]{1,0:T(8,128)(2,1)S(1)}, u32[]{:S(2)}, u32[]{:S(2)}) collective-permute-start(bf16[208,128]{1,0:T(8,128)(2,1)S(1)} %get-tuple-element.20), channel_id=1, source_target_pairs={{0,24},{1,25},{2,26},{3,27},{4,28},{5,29},{6,30},{7,31},{8,16},{9,... | collective-permute-start | bytes 159752 | tf_op jit(solution)/shard_map/ppermute | solution.py:450
  5.2 2.3 %collective-permute-start.2 = (bf16[208,128]{1,0:T(8,128)(2,1)S(1)}, bf16[208,128]{1,0:T(8,128)(2,1)S(1)}, u32[]{:S(2)}, u32[]{:S(2)}) collective-permute-start(bf16[208,128]{1,0:T(8,128)(2,1)S(1)} %get-tuple-element.21), channel_id=1, source_target_pairs={{0,28},{1,29},{2,30},{3,31},{4,24},{5,25},{6,26},{7,27},{8,20},{9,... | collective-permute-start | bytes 159752 | tf_op jit(solution)/shard_map/ppermute | solution.py:450
  7.5 0.2 %collective-permute-start.3 = (bf16[208,128]{1,0:T(8,128)(2,1)S(1)}, bf16[208,128]{1,0:T(8,128)(2,1)S(1)}, u32[]{:S(2)}, u32[]{:S(2)}) collective-permute-start(bf16[208,128]{1,0:T(8,128)(2,1)S(1)} %get-tuple-element.22), channel_id=1, source_target_pairs={{0,20},{1,21},{2,22},{3,23},{4,16},{5,17},{6,18},{7,19},{8,28},{9,... | collective-permute-start | bytes 159752 | tf_op jit(solution)/shard_map/ppermute | solution.py:450
  7.7 1.2 %collective-permute-done.state_ref = bf16[4,192,128]{2,1,0:T(8,128)(2,1)S(1)} collective-permute-done((bf16[4,192,128]{2,1,0:T(8,128)(2,1)S(1)}, bf16[4,192,128]{2,1,0:T(8,128)(2,1)S(1)}, u32[]{:S(2)}, u32[]{:S(2)}) %collective-permute-start) | collective-permute-done | bytes 196640 | tf_op jit(solution)/shard_map/ppermute | solution.py:450
  9.0 0.0 copy-done
  9.0 0.0 copy-done.1
  9.0 0.5 %shard_map.83.z_ref = f32[4,192,128]{2,1,0:T(8,128)S(1)} custom-call(bf16[4,192,128]{2,1,0:T(8,128)(2,1)S(1)} %collective-permute-done.state_ref, bf16[2,4,3,128,128]{4,3,2,1,0:T(8,128)(2,1)S(1)} %copy-done, bf16[2,1,4,128,128]{4,3,2,1,0:T(8,128)(2,1)S(1)} %copy-done.1, f32[192,8]{1,0:T(8,128)S(1)} %get-tuple-element.18.table_ref, ...), custom_call_target="tpu_custom_call" | custom-call | tf_op jit(solution)/shard_map/pallas_call | solution.py:384
  9.4 0.0 collective-permute-done.1.refs_0_.refs_3_
  9.4 2.8 %collective-permute-done.2.refs_1_.refs_4_ = bf16[208,128]{1,0:T(8,128)(2,1)S(1)} collective-permute-done((bf16[208,128]{1,0:T(8,128)(2,1)S(1)}, bf16[208,128]{1,0:T(8,128)(2,1)S(1)}, u32[]{:S(2)}, u32[]{:S(2)}) %collective-permute-start.2) | collective-permute-done | bytes 53280 | tf_op jit(solution)/shard_map/ppermute | solution.py:450
  12.3 0.5 %collective-permute-done.3.refs_2_ = bf16[208,128]{1,0:T(8,128)(2,1)S(1)} collective-permute-done((bf16[208,128]{1,0:T(8,128)(2,1)S(1)}, bf16[208,128]{1,0:T(8,128)(2,1)S(1)}, u32[]{:S(2)}, u32[]{:S(2)}) %collective-permute-start.3) | collective-permute-done | bytes 53280 | tf_op jit(solution)/shard_map/ppermute | solution.py:450
  12.8 0.4 %shard_map.84 = (bf16[4,192,128]{2,1,0:T(8,128)(2,1)S(1)}, bf16[192,128]{1,0:T(8,128)(2,1)S(1)}, bf16[192,128]{1,0:T(8,128)(2,1)S(1)}, bf16[192,128]{1,0:T(8,128)(2,1)S(1)}) custom-call(f32[4,192,128]{2,1,0:T(8,128)S(1)} %shard_map.83.z_ref, bf16[2,1,4,128,128]{4,3,2,1,0:T(8,128)(2,1)S(1)} %copy-done.1, f32[192,8]{1,0:T(8,128)S(1)} %get-tuple-element.18.table_ref, ...), custom_call_target="tpu_custom_call" | custom-call | tf_op jit(solution)/shard_map/pallas_call | solution.py:393
  13.3 1.6 %collective-permute-start.4 = (bf16[192,128]{1,0:T(8,128)(2,1)S(1)}, bf16[192,128]{1,0:T(8,128)(2,1)S(1)}, u32[]{:S(2)}, u32[]{:S(2)}) collective-permute-start(bf16[192,128]{1,0:T(8,128)(2,1)S(1)} %get-tuple-element.25), channel_id=1, source_target_pairs={{0,1},{1,0},{2,3},{3,2},{4,5},{5,4},{6,7},{7,6},{8,9},{9,8},{10,11... | collective-permute-start | bytes 147464 | tf_op jit(solution)/shard_map/ppermute | solution.py:450
  14.8 1.4 %collective-permute-start.5 = (bf16[192,128]{1,0:T(8,128)(2,1)S(1)}, bf16[192,128]{1,0:T(8,128)(2,1)S(1)}, u32[]{:S(2)}, u32[]{:S(2)}) collective-permute-start(bf16[192,128]{1,0:T(8,128)(2,1)S(1)} %get-tuple-element.26), channel_id=1, source_target_pairs={{0,1},{1,0},{2,3},{3,2},{4,5},{5,4},{6,7},{7,6},{8,9},{9,8},{10,11... | collective-permute-start | bytes 147464 | tf_op jit(solution)/shard_map/ppermute | solution.py:450
  16.2 0.6 %collective-permute-start.6 = (bf16[192,128]{1,0:T(8,128)(2,1)S(1)}, bf16[192,128]{1,0:T(8,128)(2,1)S(1)}, u32[]{:S(2)}, u32[]{:S(2)}) collective-permute-start(bf16[192,128]{1,0:T(8,128)(2,1)S(1)} %get-tuple-element.27), channel_id=1, source_target_pairs={{0,1},{1,0},{2,3},{3,2},{4,5},{5,4},{6,7},{7,6},{8,9},{9,8},{10,11... | collective-permute-start | bytes 147464 | tf_op jit(solution)/shard_map/ppermute | solution.py:450
  16.8 0.8 %shard_map.85 = (f32[4,192,128]{2,1,0:T(8,128)S(1)}, bf16[2,192,512]{2,1,0:T(8,128)(2,1)}) custom-call(bf16[4,192,128]{2,1,0:T(8,128)(2,1)S(1)} %get-tuple-element.23.state_ref.refs_0_, bf16[2,4,3,128,128]{4,3,2,1,0:T(8,128)(2,1)S(1)} %copy-done, bf16[2,1,4,128,128]{4,3,2,1,0:T(8,128)(2,1)S(1)} %copy-done.1, f32[192,8]{1,0:T(8,128)S(1)} %get-tuple-element.18.table_ref, ...), custom_call_target="tpu_custom_call" | custom-call | tf_op jit(solution)/shard_map/pallas_call | solution.py:420
  17.6 1.7 %collective-permute-done.4.refs_0_ = bf16[192,128]{1,0:T(8,128)(2,1)S(1)} collective-permute-done((bf16[192,128]{1,0:T(8,128)(2,1)S(1)}, bf16[192,128]{1,0:T(8,128)(2,1)S(1)}, u32[]{:S(2)}, u32[]{:S(2)}) %collective-permute-start.4) | collective-permute-done | bytes 49184 | tf_op jit(solution)/shard_map/ppermute | solution.py:450
  19.3 1.5 %collective-permute-done.5.refs_1_ = bf16[192,128]{1,0:T(8,128)(2,1)S(1)} collective-permute-done((bf16[192,128]{1,0:T(8,128)(2,1)S(1)}, bf16[192,128]{1,0:T(8,128)(2,1)S(1)}, u32[]{:S(2)}, u32[]{:S(2)}) %collective-permute-start.5) | collective-permute-done | bytes 49184 | tf_op jit(solution)/shard_map/ppermute | solution.py:450
  20.8 0.0 collective-permute-done.6.refs_2_
  20.8 1.0 %shard_map.86 = bf16[2,192,512]{2,1,0:T(8,128)(2,1)} custom-call(f32[4,192,128]{2,1,0:T(8,128)S(1)} %get-tuple-element.24.z_ref, bf16[2,1,4,128,128]{4,3,2,1,0:T(8,128)(2,1)S(1)} %copy-done.1, f32[72,128]{1,0:T(8,128)S(1)} %get-tuple-element.19.marks_ref, bf16[192,128]{1,0:T(8,128)(2,1)S(1)} %collective-permute-done.4.refs_0_, ...), custom_call_target="tpu_custom_call", output_to_operand_aliasing={{}: (6, {})} | custom-call | tf_op jit(solution)/shard_map/pallas_call | solution.py:432
Async XLA Ops:
  0.0 9.0 %copy-start = (bf16[2,4,3,128,128]{4,3,2,1,0:T(8,128)(2,1)S(1)}, bf16[2,4,3,128,128]{4,3,2,1,0:T(8,128)(2,1)}, u32[]{:S(2)}) copy-start(bf16[2,4,3,128,128]{4,3,2,1,0:T(8,128)(2,1)} %jac_ref.3) | copy-start | bytes 2359300
  0.0 9.0 %copy-start.1 = (bf16[2,1,4,128,128]{4,3,2,1,0:T(8,128)(2,1)S(1)}, bf16[2,1,4,128,128]{4,3,2,1,0:T(8,128)(2,1)}, u32[]{:S(2)}) copy-start(bf16[2,1,4,128,128]{4,3,2,1,0:T(8,128)(2,1)} %iface_ref.7) | copy-start | bytes 786436
  1.1 7.8 %collective-permute-start = (bf16[4,192,128]{2,1,0:T(8,128)(2,1)S(1)}, bf16[4,192,128]{2,1,0:T(8,128)(2,1)S(1)}, u32[]{:S(2)}, u32[]{:S(2)}) collective-permute-start(bf16[4,192,128]{2,1,0:T(8,128)(2,1)S(1)} %get-tuple-element.17.refs_1_), channel_id=1, source_target_pairs={{0,16},{1,17},{2,18},{3,19},{4,20},{5,21},{6,22},{7,23},{8,24},{9,... | collective-permute-start | bytes 589832 | tf_op jit(solution)/shard_map/ppermute | solution.py:450
  1.2 8.2 %collective-permute-start.1 = (bf16[208,128]{1,0:T(8,128)(2,1)S(1)}, bf16[208,128]{1,0:T(8,128)(2,1)S(1)}, u32[]{:S(2)}, u32[]{:S(2)}) collective-permute-start(bf16[208,128]{1,0:T(8,128)(2,1)S(1)} %get-tuple-element.20), channel_id=1, source_target_pairs={{0,24},{1,25},{2,26},{3,27},{4,28},{5,29},{6,30},{7,31},{8,16},{9,... | collective-permute-start | bytes 159752 | tf_op jit(solution)/shard_map/ppermute | solution.py:450
  5.2 7.0 %collective-permute-start.2 = (bf16[208,128]{1,0:T(8,128)(2,1)S(1)}, bf16[208,128]{1,0:T(8,128)(2,1)S(1)}, u32[]{:S(2)}, u32[]{:S(2)}) collective-permute-start(bf16[208,128]{1,0:T(8,128)(2,1)S(1)} %get-tuple-element.21), channel_id=1, source_target_pairs={{0,28},{1,29},{2,30},{3,31},{4,24},{5,25},{6,26},{7,27},{8,20},{9,... | collective-permute-start | bytes 159752 | tf_op jit(solution)/shard_map/ppermute | solution.py:450
  7.5 5.3 %collective-permute-start.3 = (bf16[208,128]{1,0:T(8,128)(2,1)S(1)}, bf16[208,128]{1,0:T(8,128)(2,1)S(1)}, u32[]{:S(2)}, u32[]{:S(2)}) collective-permute-start(bf16[208,128]{1,0:T(8,128)(2,1)S(1)} %get-tuple-element.22), channel_id=1, source_target_pairs={{0,20},{1,21},{2,22},{3,23},{4,16},{5,17},{6,18},{7,19},{8,28},{9,... | collective-permute-start | bytes 159752 | tf_op jit(solution)/shard_map/ppermute | solution.py:450
  13.3 6.1 %collective-permute-start.4 = (bf16[192,128]{1,0:T(8,128)(2,1)S(1)}, bf16[192,128]{1,0:T(8,128)(2,1)S(1)}, u32[]{:S(2)}, u32[]{:S(2)}) collective-permute-start(bf16[192,128]{1,0:T(8,128)(2,1)S(1)} %get-tuple-element.25), channel_id=1, source_target_pairs={{0,1},{1,0},{2,3},{3,2},{4,5},{5,4},{6,7},{7,6},{8,9},{9,8},{10,11... | collective-permute-start | bytes 147464 | tf_op jit(solution)/shard_map/ppermute | solution.py:450
  14.8 6.0 %collective-permute-start.5 = (bf16[192,128]{1,0:T(8,128)(2,1)S(1)}, bf16[192,128]{1,0:T(8,128)(2,1)S(1)}, u32[]{:S(2)}, u32[]{:S(2)}) collective-permute-start(bf16[192,128]{1,0:T(8,128)(2,1)S(1)} %get-tuple-element.26), channel_id=1, source_target_pairs={{0,1},{1,0},{2,3},{3,2},{4,5},{5,4},{6,7},{7,6},{8,9},{9,8},{10,11... | collective-permute-start | bytes 147464 | tf_op jit(solution)/shard_map/ppermute | solution.py:450
  16.2 4.6 %collective-permute-start.6 = (bf16[192,128]{1,0:T(8,128)(2,1)S(1)}, bf16[192,128]{1,0:T(8,128)(2,1)S(1)}, u32[]{:S(2)}, u32[]{:S(2)}) collective-permute-start(bf16[192,128]{1,0:T(8,128)(2,1)S(1)} %get-tuple-element.27), channel_id=1, source_target_pairs={{0,1},{1,0},{2,3},{3,2},{4,5},{5,4},{6,7},{7,6},{8,9},{9,8},{10,11... | collective-permute-start | bytes 147464 | tf_op jit(solution)/shard_map/ppermute | solution.py:450

commit v29 on v28

--- a/solution.py
+++ b/solution.py
@@ -269,7 +269,7 @@
 
 
 def exchange_order(n, handed):
-    return [*range(n // 2, n), *range(n // 2 - 1, 0, -1)]
+    return [1, *range(n - 1, 1, -1)] if handed else list(range(n - 1, 0, -1))
 
 
 def by_distance(refs, handed):

time: 22 us -> 22.9 us (1.041)
  starting transfers between devices: 10.2 us -> 11.1 us
    ppermute x7, starting transfers between devices: 10.2 us -> 11.1 us  [swap(): return lax.ppermute(block, ('tm', 'net', 'cols'), pairs)]
  transfers between devices with their start and end apart: 7 -> 7, of which waited for: 5 -> 5; matrix products, arithmetic and copies ran while one was open for 0% -> 0% of each run, Pallas kernels for 6% -> 5%
where the time goes in v29:
time: 22.9 us; the launch traced here: 22.7 us
  starting transfers between devices  11.1 us (48%)
  waiting for transfers between devices  7.79 us (34%)
  Pallas kernels  3.8 us (17%)
    ppermute x7, starting transfers between devices, swap(): return lax.ppermute(block, ('tm', 'net', 'cols'), pairs)  11.1 us
    ppermute x7, waiting for transfers between devices, swap(): return lax.ppermute(block, ('tm', 'net', 'cols'), pairs)  7.79 us
    pallas_call x1, Pallas kernels, local(): pl.pallas_call(second_kernel, out_shape=[f32((cols, table_rows)), f32((ma...  1.11 us
    pallas_call x1, Pallas kernels, close(): pl.pallas_call(functools.partial(close_kernel, step, section, steps - 1),...  1 us
    pallas_call x1, Pallas kernels, own_and_write(): pl.pallas_call(functools.partial(write_kernel, step, section, firsts, len...  0.79 us
  transfers between devices with their start and end apart: 7, of which 5 were waited for; matrix products, arithmetic and copies ran while one was open for 0% of the time, Pallas kernels for 5%

profile of v29, /device:TPU:4, one launch (start us, length us, event | category | flops | bytes accessed | tf_op | source)
XLA Modules:
  0.0 22.7 jit_solution(4507807478433241421)
XLA Ops:
  0.0 0.0 copy-start
  0.0 0.0 copy-start.1
  0.0 1.1 %shard_map.82 = (f32[192,8]{1,0:T(8,128)S(1)}, f32[72,128]{1,0:T(8,128)S(1)}, bf16[4,192,128]{2,1,0:T(8,128)(2,1)S(1)}, bf16[208,128]{1,0:T(8,128)(2,1)S(1)}, bf...) custom-call(bf16[2,4,3,128,128]{4,3,2,1,0:T(8,128)(2,1)} %jac_ref.3, bf16[2,1,4,128,128]{4,3,2,1,0:T(8,128)(2,1)} %iface_ref.7, ...), custom_call_target="tpu_custom_call" | custom-call | tf_op jit(solution)/shard_map/pallas_call | solution.py:366
  1.1 0.1 collective-permute-start
  1.2 3.0 %collective-permute-start.1 = (bf16[208,128]{1,0:T(8,128)(2,1)S(1)}, bf16[208,128]{1,0:T(8,128)(2,1)S(1)}, u32[]{:S(2)}, u32[]{:S(2)}) collective-permute-start(bf16[208,128]{1,0:T(8,128)(2,1)S(1)} %get-tuple-element.20), channel_id=1, source_target_pairs={{0,20},{1,21},{2,22},{3,23},{4,16},{5,17},{6,18},{7,19},{8,28},{9,... | collective-permute-start | bytes 159752 | tf_op jit(solution)/shard_map/ppermute | solution.py:450
  4.2 3.4 %collective-permute-start.2 = (bf16[208,128]{1,0:T(8,128)(2,1)S(1)}, bf16[208,128]{1,0:T(8,128)(2,1)S(1)}, u32[]{:S(2)}, u32[]{:S(2)}) collective-permute-start(bf16[208,128]{1,0:T(8,128)(2,1)S(1)} %get-tuple-element.21), channel_id=1, source_target_pairs={{0,28},{1,29},{2,30},{3,31},{4,24},{5,25},{6,26},{7,27},{8,20},{9,... | collective-permute-start | bytes 159752 | tf_op jit(solution)/shard_map/ppermute | solution.py:450
  7.6 0.1 collective-permute-start.3
  7.7 1.7 %collective-permute-done.state_ref = bf16[4,192,128]{2,1,0:T(8,128)(2,1)S(1)} collective-permute-done((bf16[4,192,128]{2,1,0:T(8,128)(2,1)S(1)}, bf16[4,192,128]{2,1,0:T(8,128)(2,1)S(1)}, u32[]{:S(2)}, u32[]{:S(2)}) %collective-permute-start) | collective-permute-done | bytes 196640 | tf_op jit(solution)/shard_map/ppermute | solution.py:450
  9.4 0.0 copy-done
  9.4 0.0 copy-done.1
  9.4 0.5 %shard_map.83.z_ref = f32[4,192,128]{2,1,0:T(8,128)S(1)} custom-call(bf16[4,192,128]{2,1,0:T(8,128)(2,1)S(1)} %collective-permute-done.state_ref, bf16[2,4,3,128,128]{4,3,2,1,0:T(8,128)(2,1)S(1)} %copy-done, bf16[2,1,4,128,128]{4,3,2,1,0:T(8,128)(2,1)S(1)} %copy-done.1, f32[192,8]{1,0:T(8,128)S(1)} %get-tuple-element.18.table_ref, ...), custom_call_target="tpu_custom_call" | custom-call | tf_op jit(solution)/shard_map/pallas_call | solution.py:384
  9.9 0.0 collective-permute-done.1.refs_0_.refs_2_
  9.9 1.2 %collective-permute-done.2.refs_1_.refs_4_ = bf16[208,128]{1,0:T(8,128)(2,1)S(1)} collective-permute-done((bf16[208,128]{1,0:T(8,128)(2,1)S(1)}, bf16[208,128]{1,0:T(8,128)(2,1)S(1)}, u32[]{:S(2)}, u32[]{:S(2)}) %collective-permute-start.2) | collective-permute-done | bytes 53280 | tf_op jit(solution)/shard_map/ppermute | solution.py:450
  11.1 3.0 %collective-permute-done.3.refs_2_.refs_3_ = bf16[208,128]{1,0:T(8,128)(2,1)S(1)} collective-permute-done((bf16[208,128]{1,0:T(8,128)(2,1)S(1)}, bf16[208,128]{1,0:T(8,128)(2,1)S(1)}, u32[]{:S(2)}, u32[]{:S(2)}) %collective-permute-start.3) | collective-permute-done | bytes 53280 | tf_op jit(solution)/shard_map/ppermute | solution.py:450
  14.1 0.4 %shard_map.84 = (bf16[4,192,128]{2,1,0:T(8,128)(2,1)S(1)}, bf16[192,128]{1,0:T(8,128)(2,1)S(1)}, bf16[192,128]{1,0:T(8,128)(2,1)S(1)}, bf16[192,128]{1,0:T(8,128)(2,1)S(1)}) custom-call(f32[4,192,128]{2,1,0:T(8,128)S(1)} %shard_map.83.z_ref, bf16[2,1,4,128,128]{4,3,2,1,0:T(8,128)(2,1)S(1)} %copy-done.1, f32[192,8]{1,0:T(8,128)S(1)} %get-tuple-element.18.table_ref, ...), custom_call_target="tpu_custom_call" | custom-call | tf_op jit(solution)/shard_map/pallas_call | solution.py:393
  14.6 1.2 %collective-permute-start.4 = (bf16[192,128]{1,0:T(8,128)(2,1)S(1)}, bf16[192,128]{1,0:T(8,128)(2,1)S(1)}, u32[]{:S(2)}, u32[]{:S(2)}) collective-permute-start(bf16[192,128]{1,0:T(8,128)(2,1)S(1)} %get-tuple-element.25), channel_id=1, source_target_pairs={{0,1},{1,0},{2,3},{3,2},{4,5},{5,4},{6,7},{7,6},{8,9},{9,8},{10,11... | collective-permute-start | bytes 147464 | tf_op jit(solution)/shard_map/ppermute | solution.py:450
  15.8 0.5 %collective-permute-start.5 = (bf16[192,128]{1,0:T(8,128)(2,1)S(1)}, bf16[192,128]{1,0:T(8,128)(2,1)S(1)}, u32[]{:S(2)}, u32[]{:S(2)}) collective-permute-start(bf16[192,128]{1,0:T(8,128)(2,1)S(1)} %get-tuple-element.26), channel_id=1, source_target_pairs={{0,1},{1,0},{2,3},{3,2},{4,5},{5,4},{6,7},{7,6},{8,9},{9,8},{10,11... | collective-permute-start | bytes 147464 | tf_op jit(solution)/shard_map/ppermute | solution.py:450
  16.3 2.7 %collective-permute-start.6 = (bf16[192,128]{1,0:T(8,128)(2,1)S(1)}, bf16[192,128]{1,0:T(8,128)(2,1)S(1)}, u32[]{:S(2)}, u32[]{:S(2)}) collective-permute-start(bf16[192,128]{1,0:T(8,128)(2,1)S(1)} %get-tuple-element.27), channel_id=1, source_target_pairs={{0,1},{1,0},{2,3},{3,2},{4,5},{5,4},{6,7},{7,6},{8,9},{9,8},{10,11... | collective-permute-start | bytes 147464 | tf_op jit(solution)/shard_map/ppermute | solution.py:450
  19.0 0.8 %shard_map.85 = (f32[4,192,128]{2,1,0:T(8,128)S(1)}, bf16[2,192,512]{2,1,0:T(8,128)(2,1)}) custom-call(bf16[4,192,128]{2,1,0:T(8,128)(2,1)S(1)} %get-tuple-element.23.state_ref.refs_0_, bf16[2,4,3,128,128]{4,3,2,1,0:T(8,128)(2,1)S(1)} %copy-done, bf16[2,1,4,128,128]{4,3,2,1,0:T(8,128)(2,1)S(1)} %copy-done.1, f32[192,8]{1,0:T(8,128)S(1)} %get-tuple-element.18.table_ref, ...), custom_call_target="tpu_custom_call" | custom-call | tf_op jit(solution)/shard_map/pallas_call | solution.py:420
  19.8 1.1 %collective-permute-done.4.refs_0_ = bf16[192,128]{1,0:T(8,128)(2,1)S(1)} collective-permute-done((bf16[192,128]{1,0:T(8,128)(2,1)S(1)}, bf16[192,128]{1,0:T(8,128)(2,1)S(1)}, u32[]{:S(2)}, u32[]{:S(2)}) %collective-permute-start.4) | collective-permute-done | bytes 49184 | tf_op jit(solution)/shard_map/ppermute | solution.py:450
  20.9 0.8 %collective-permute-done.5.refs_1_ = bf16[192,128]{1,0:T(8,128)(2,1)S(1)} collective-permute-done((bf16[192,128]{1,0:T(8,128)(2,1)S(1)}, bf16[192,128]{1,0:T(8,128)(2,1)S(1)}, u32[]{:S(2)}, u32[]{:S(2)}) %collective-permute-start.5) | collective-permute-done | bytes 49184 | tf_op jit(solution)/shard_map/ppermute | solution.py:450
  21.7 0.0 collective-permute-done.6.refs_2_
  21.7 1.0 %shard_map.86 = bf16[2,192,512]{2,1,0:T(8,128)(2,1)} custom-call(f32[4,192,128]{2,1,0:T(8,128)S(1)} %get-tuple-element.24.z_ref, bf16[2,1,4,128,128]{4,3,2,1,0:T(8,128)(2,1)S(1)} %copy-done.1, f32[72,128]{1,0:T(8,128)S(1)} %get-tuple-element.19.marks_ref, bf16[192,128]{1,0:T(8,128)(2,1)S(1)} %collective-permute-done.4.refs_0_, ...), custom_call_target="tpu_custom_call", output_to_operand_aliasing={{}: (6, {})} | custom-call | tf_op jit(solution)/shard_map/pallas_call | solution.py:432
Async XLA Ops:
  0.0 9.4 %copy-start = (bf16[2,4,3,128,128]{4,3,2,1,0:T(8,128)(2,1)S(1)}, bf16[2,4,3,128,128]{4,3,2,1,0:T(8,128)(2,1)}, u32[]{:S(2)}) copy-start(bf16[2,4,3,128,128]{4,3,2,1,0:T(8,128)(2,1)} %jac_ref.3) | copy-start | bytes 2359300
  0.0 9.4 %copy-start.1 = (bf16[2,1,4,128,128]{4,3,2,1,0:T(8,128)(2,1)S(1)}, bf16[2,1,4,128,128]{4,3,2,1,0:T(8,128)(2,1)}, u32[]{:S(2)}) copy-start(bf16[2,1,4,128,128]{4,3,2,1,0:T(8,128)(2,1)} %iface_ref.7) | copy-start | bytes 786436
  1.1 8.3 %collective-permute-start = (bf16[4,192,128]{2,1,0:T(8,128)(2,1)S(1)}, bf16[4,192,128]{2,1,0:T(8,128)(2,1)S(1)}, u32[]{:S(2)}, u32[]{:S(2)}) collective-permute-start(bf16[4,192,128]{2,1,0:T(8,128)(2,1)S(1)} %get-tuple-element.17.refs_1_), channel_id=1, source_target_pairs={{0,16},{1,17},{2,18},{3,19},{4,20},{5,21},{6,22},{7,23},{8,24},{9,... | collective-permute-start | bytes 589832 | tf_op jit(solution)/shard_map/ppermute | solution.py:450
  1.2 8.7 %collective-permute-start.1 = (bf16[208,128]{1,0:T(8,128)(2,1)S(1)}, bf16[208,128]{1,0:T(8,128)(2,1)S(1)}, u32[]{:S(2)}, u32[]{:S(2)}) collective-permute-start(bf16[208,128]{1,0:T(8,128)(2,1)S(1)} %get-tuple-element.20), channel_id=1, source_target_pairs={{0,20},{1,21},{2,22},{3,23},{4,16},{5,17},{6,18},{7,19},{8,28},{9,... | collective-permute-start | bytes 159752 | tf_op jit(solution)/shard_map/ppermute | solution.py:450
  4.2 6.8 %collective-permute-start.2 = (bf16[208,128]{1,0:T(8,128)(2,1)S(1)}, bf16[208,128]{1,0:T(8,128)(2,1)S(1)}, u32[]{:S(2)}, u32[]{:S(2)}) collective-permute-start(bf16[208,128]{1,0:T(8,128)(2,1)S(1)} %get-tuple-element.21), channel_id=1, source_target_pairs={{0,28},{1,29},{2,30},{3,31},{4,24},{5,25},{6,26},{7,27},{8,20},{9,... | collective-permute-start | bytes 159752 | tf_op jit(solution)/shard_map/ppermute | solution.py:450
  7.6 6.5 %collective-permute-start.3 = (bf16[208,128]{1,0:T(8,128)(2,1)S(1)}, bf16[208,128]{1,0:T(8,128)(2,1)S(1)}, u32[]{:S(2)}, u32[]{:S(2)}) collective-permute-start(bf16[208,128]{1,0:T(8,128)(2,1)S(1)} %get-tuple-element.22), channel_id=1, source_target_pairs={{0,24},{1,25},{2,26},{3,27},{4,28},{5,29},{6,30},{7,31},{8,16},{9,... | collective-permute-start | bytes 159752 | tf_op jit(solution)/shard_map/ppermute | solution.py:450
  14.6 6.4 %collective-permute-start.4 = (bf16[192,128]{1,0:T(8,128)(2,1)S(1)}, bf16[192,128]{1,0:T(8,128)(2,1)S(1)}, u32[]{:S(2)}, u32[]{:S(2)}) collective-permute-start(bf16[192,128]{1,0:T(8,128)(2,1)S(1)} %get-tuple-element.25), channel_id=1, source_target_pairs={{0,1},{1,0},{2,3},{3,2},{4,5},{5,4},{6,7},{7,6},{8,9},{9,8},{10,11... | collective-permute-start | bytes 147464 | tf_op jit(solution)/shard_map/ppermute | solution.py:450
  15.8 5.9 %collective-permute-start.5 = (bf16[192,128]{1,0:T(8,128)(2,1)S(1)}, bf16[192,128]{1,0:T(8,128)(2,1)S(1)}, u32[]{:S(2)}, u32[]{:S(2)}) collective-permute-start(bf16[192,128]{1,0:T(8,128)(2,1)S(1)} %get-tuple-element.26), channel_id=1, source_target_pairs={{0,1},{1,0},{2,3},{3,2},{4,5},{5,4},{6,7},{7,6},{8,9},{9,8},{10,11... | collective-permute-start | bytes 147464 | tf_op jit(solution)/shard_map/ppermute | solution.py:450
  16.3 5.4 %collective-permute-start.6 = (bf16[192,128]{1,0:T(8,128)(2,1)S(1)}, bf16[192,128]{1,0:T(8,128)(2,1)S(1)}, u32[]{:S(2)}, u32[]{:S(2)}) collective-permute-start(bf16[192,128]{1,0:T(8,128)(2,1)S(1)} %get-tuple-element.27), channel_id=1, source_target_pairs={{0,1},{1,0},{2,3},{3,2},{4,5},{5,4},{6,7},{7,6},{8,9},{9,8},{10,11... | collective-permute-start | bytes 147464 | tf_op jit(solution)/shard_map/ppermute | solution.py:450

commit v30 on v26

--- a/solution.py
+++ b/solution.py
@@ -36,15 +36,16 @@
     return lambda i, k: state_ref[cols_ref[k, i]]
 
 
-def own_sum(i, state_ref, jac_ref, near, table, step, hit=None):
-    blocks, _, width = state_ref.shape
-    if hit is None:
-        hit = hits(table, i, blocks, width)
+def products(i, state_ref, jac_ref, near):
     kinds = jac_ref.shape[1]
     rows = [state_ref[i]] + [near(i, k) for k in range(kinds - 1)]
     row_blocks = [jac_ref[i, k] for k in range(kinds)]
-    total = times_transposed(jnp.concatenate(rows, axis=1), jnp.concatenate(row_blocks, axis=1))
-    return total + injected(table, step, hit)
+    return times_transposed(jnp.concatenate(rows, axis=1), jnp.concatenate(row_blocks, axis=1))
+
+
+def own_sum(i, state_ref, jac_ref, near, table, step):
+    blocks, _, width = state_ref.shape
+    return products(i, state_ref, jac_ref, near) + injected(table, step, hits(table, i, blocks, width))
 
 
 def picked(blocks, marks):
@@ -147,20 +148,28 @@
     @pl.when(here)
     def _():
         table = table_ref[...]
-        hit = [hits(table, i, blocks, width) for i in range(blocks)]
+
+        def spread(column):
+            return jnp.broadcast_to(column, (cols, width))
+
+        lane = lax.broadcasted_iota(jnp.int32, (cols, width), 1).astype(jnp.float32)
+        place = spread(table[:, STATE : STATE + 1] - (me * blocks * width).astype(jnp.float32)) - lane
+        gain = spread(table[:, GAIN : GAIN + 1])
+        later_gain = spread(table[:, GAIN + 1 : GAIN + 2])
+        hit = [place == float(i * width) for i in range(blocks)]
         for i in range(blocks):
-            first_ref[i] = injected(table, 0, hit[i]).astype(first_ref.dtype)
-        lane = lax.broadcasted_iota(jnp.int32, (cols, width), 1).astype(jnp.float32)
-        shot = jnp.where(lane == table[:, LANE : LANE + 1], table[:, GAIN : GAIN + 1], 0.0)
+            first_ref[i] = jnp.where(hit[i], gain, 0.0).astype(first_ref.dtype)
         away, block = table[:, AWAY : AWAY + 1], table[:, BLOCK : BLOCK + 1]
         for load in loads[2:6]:
             load.wait()
         mine = jnp.logical_or(away != 0.0, block == send_ref[0, me].astype(jnp.float32))
-        shot = jnp.where(mine, shot, 0.0)
+        shot_lane = spread(jnp.where(mine, table[:, LANE : LANE + 1], -1.0))
+        shot = jnp.where(lane == shot_lane, gain, 0.0)
         live = recv = jnp.zeros_like(away)
         for d in range(n):
             live = jnp.where(away == float(d), live_ref[0, me ^ d].astype(jnp.float32), live)
             recv = jnp.where(away == float(d), recv_ref[0, me ^ d].astype(jnp.float32), recv)
+        away, live, recv = spread(away), spread(live), spread(recv)
         sent = [jnp.where(away == float(d), shot, 0.0).astype(first_ref.dtype) for d in range(n)]
         loads[1].wait()
         ifaces = jnp.concatenate([iface_ref[me ^ d] for d in range(n)], axis=1)
@@ -168,7 +177,8 @@
         coupled = jnp.where(lane < live, coupled, 0.0)
         loads[0].wait()
         for i in range(blocks):
-            own = own_sum(i, first_ref, jac_ref, near_by(first_ref, cols_ref), table, 1, hit[i])
+            own = products(i, first_ref, jac_ref, near_by(first_ref, cols_ref))
+            own += jnp.where(hit[i], later_gain, 0.0)
             state_ref[i] = (own + jnp.where(recv == float(i), coupled, 0.0)).astype(state_ref.dtype)
         for d in range(1, n):
             outgoing[d - 1][pl.ds(0, cols)] = state_ref[send_ref[0, me ^ d]]

time: 21.9 us -> 22 us (level)
  no operation moved by 1% of the time
where the time goes in v30:
time: 22 us; the launch traced here: 21.8 us
  starting transfers between devices  11.1 us (50%)
  waiting for transfers between devices  6.88 us (31%)
  Pallas kernels  3.79 us (17%)
    ppermute x7, starting transfers between devices, swap(): return lax.ppermute(block, ('tm', 'net', 'cols'), pairs)  11.1 us
    ppermute x7, waiting for transfers between devices, swap(): return lax.ppermute(block, ('tm', 'net', 'cols'), pairs)  6.88 us
    pallas_call x1, Pallas kernels, local(): pl.pallas_call(second_kernel, out_shape=[f32((cols, table_rows)), f32((ma...  1.11 us
    pallas_call x1, Pallas kernels, close(): pl.pallas_call(functools.partial(close_kernel, step, section, steps - 1),...  1 us
    pallas_call x1, Pallas kernels, own_and_write(): pl.pallas_call(functools.partial(write_kernel, step, section, firsts, len...  0.79 us
    pallas_call x1, Pallas kernels, own(): pl.pallas_call(functools.partial(own_kernel, step), out_shape=f32(whole.s...  0.45 us
    pallas_call x1, Pallas kernels, join(): pl.pallas_call(functools.partial(join_kernel, step, kinds if fix else 0,...  0.44 us
  transfers between devices with their start and end apart: 7, of which 5 were waited for; matrix products, arithmetic and copies ran while one was open for 0% of the time, Pallas kernels for 6%

profile of v30, /device:TPU:4, one launch (start us, length us, event | category | flops | bytes accessed | tf_op | source)
XLA Modules:
  0.0 21.8 jit_solution(6629025210354340088)
XLA Ops:
  0.0 0.0 copy-start
  0.0 0.0 copy-start.1
  0.0 1.1 %shard_map.82 = (f32[192,8]{1,0:T(8,128)S(1)}, f32[72,128]{1,0:T(8,128)S(1)}, bf16[4,192,128]{2,1,0:T(8,128)(2,1)S(1)}, bf16[208,128]{1,0:T(8,128)(2,1)S(1)}, bf...) custom-call(bf16[2,4,3,128,128]{4,3,2,1,0:T(8,128)(2,1)} %jac_ref.3, bf16[2,1,4,128,128]{4,3,2,1,0:T(8,128)(2,1)} %iface_ref.7, ...), custom_call_target="tpu_custom_call" | custom-call | tf_op jit(solution)/shard_map/pallas_call | solution.py:376
  1.1 0.1 collective-permute-start
  1.2 4.0 %collective-permute-start.1 = (bf16[208,128]{1,0:T(8,128)(2,1)S(1)}, bf16[208,128]{1,0:T(8,128)(2,1)S(1)}, u32[]{:S(2)}, u32[]{:S(2)}) collective-permute-start(bf16[208,128]{1,0:T(8,128)(2,1)S(1)} %get-tuple-element.20), channel_id=1, source_target_pairs={{0,24},{1,25},{2,26},{3,27},{4,28},{5,29},{6,30},{7,31},{8,16},{9,... | collective-permute-start | bytes 159752 | tf_op jit(solution)/shard_map/ppermute | solution.py:460
  5.2 2.3 %collective-permute-start.2 = (bf16[208,128]{1,0:T(8,128)(2,1)S(1)}, bf16[208,128]{1,0:T(8,128)(2,1)S(1)}, u32[]{:S(2)}, u32[]{:S(2)}) collective-permute-start(bf16[208,128]{1,0:T(8,128)(2,1)S(1)} %get-tuple-element.21), channel_id=1, source_target_pairs={{0,28},{1,29},{2,30},{3,31},{4,24},{5,25},{6,26},{7,27},{8,20},{9,... | collective-permute-start | bytes 159752 | tf_op jit(solution)/shard_map/ppermute | solution.py:460
  7.5 0.2 %collective-permute-start.3 = (bf16[208,128]{1,0:T(8,128)(2,1)S(1)}, bf16[208,128]{1,0:T(8,128)(2,1)S(1)}, u32[]{:S(2)}, u32[]{:S(2)}) collective-permute-start(bf16[208,128]{1,0:T(8,128)(2,1)S(1)} %get-tuple-element.22), channel_id=1, source_target_pairs={{0,20},{1,21},{2,22},{3,23},{4,16},{5,17},{6,18},{7,19},{8,28},{9,... | collective-permute-start | bytes 159752 | tf_op jit(solution)/shard_map/ppermute | solution.py:460
  7.8 1.2 %collective-permute-done.state_ref = bf16[4,192,128]{2,1,0:T(8,128)(2,1)S(1)} collective-permute-done((bf16[4,192,128]{2,1,0:T(8,128)(2,1)S(1)}, bf16[4,192,128]{2,1,0:T(8,128)(2,1)S(1)}, u32[]{:S(2)}, u32[]{:S(2)}) %collective-permute-start) | collective-permute-done | bytes 196640 | tf_op jit(solution)/shard_map/ppermute | solution.py:460
  9.0 0.0 copy-done
  9.0 0.0 copy-done.1
  9.0 0.5 %shard_map.83.z_ref = f32[4,192,128]{2,1,0:T(8,128)S(1)} custom-call(bf16[4,192,128]{2,1,0:T(8,128)(2,1)S(1)} %collective-permute-done.state_ref, bf16[2,4,3,128,128]{4,3,2,1,0:T(8,128)(2,1)S(1)} %copy-done, bf16[2,1,4,128,128]{4,3,2,1,0:T(8,128)(2,1)S(1)} %copy-done.1, f32[192,8]{1,0:T(8,128)S(1)} %get-tuple-element.18.table_ref, ...), custom_call_target="tpu_custom_call" | custom-call | tf_op jit(solution)/shard_map/pallas_call | solution.py:394
  9.4 0.0 collective-permute-done.1.refs_0_.refs_3_
  9.4 2.9 %collective-permute-done.2.refs_1_.refs_4_ = bf16[208,128]{1,0:T(8,128)(2,1)S(1)} collective-permute-done((bf16[208,128]{1,0:T(8,128)(2,1)S(1)}, bf16[208,128]{1,0:T(8,128)(2,1)S(1)}, u32[]{:S(2)}, u32[]{:S(2)}) %collective-permute-start.2) | collective-permute-done | bytes 53280 | tf_op jit(solution)/shard_map/ppermute | solution.py:460
  12.4 0.5 %collective-permute-done.3.refs_2_ = bf16[208,128]{1,0:T(8,128)(2,1)S(1)} collective-permute-done((bf16[208,128]{1,0:T(8,128)(2,1)S(1)}, bf16[208,128]{1,0:T(8,128)(2,1)S(1)}, u32[]{:S(2)}, u32[]{:S(2)}) %collective-permute-start.3) | collective-permute-done | bytes 53280 | tf_op jit(solution)/shard_map/ppermute | solution.py:460
  12.8 0.4 %shard_map.84 = (bf16[4,192,128]{2,1,0:T(8,128)(2,1)S(1)}, bf16[192,128]{1,0:T(8,128)(2,1)S(1)}, bf16[192,128]{1,0:T(8,128)(2,1)S(1)}, bf16[192,128]{1,0:T(8,128)(2,1)S(1)}) custom-call(f32[4,192,128]{2,1,0:T(8,128)S(1)} %shard_map.83.z_ref, bf16[2,1,4,128,128]{4,3,2,1,0:T(8,128)(2,1)S(1)} %copy-done.1, f32[192,8]{1,0:T(8,128)S(1)} %get-tuple-element.18.table_ref, ...), custom_call_target="tpu_custom_call" | custom-call | tf_op jit(solution)/shard_map/pallas_call | solution.py:403
  13.3 2.3 %collective-permute-start.4 = (bf16[192,128]{1,0:T(8,128)(2,1)S(1)}, bf16[192,128]{1,0:T(8,128)(2,1)S(1)}, u32[]{:S(2)}, u32[]{:S(2)}) collective-permute-start(bf16[192,128]{1,0:T(8,128)(2,1)S(1)} %get-tuple-element.25), channel_id=1, source_target_pairs={{0,1},{1,0},{2,3},{3,2},{4,5},{5,4},{6,7},{7,6},{8,9},{9,8},{10,11... | collective-permute-start | bytes 147464 | tf_op jit(solution)/shard_map/ppermute | solution.py:460
  15.6 0.0 collective-permute-start.5
  15.6 2.2 %collective-permute-start.6 = (bf16[192,128]{1,0:T(8,128)(2,1)S(1)}, bf16[192,128]{1,0:T(8,128)(2,1)S(1)}, u32[]{:S(2)}, u32[]{:S(2)}) collective-permute-start(bf16[192,128]{1,0:T(8,128)(2,1)S(1)} %get-tuple-element.27), channel_id=1, source_target_pairs={{0,1},{1,0},{2,3},{3,2},{4,5},{5,4},{6,7},{7,6},{8,9},{9,8},{10,11... | collective-permute-start | bytes 147464 | tf_op jit(solution)/shard_map/ppermute | solution.py:460
  17.7 0.8 %shard_map.85 = (f32[4,192,128]{2,1,0:T(8,128)S(1)}, bf16[2,192,512]{2,1,0:T(8,128)(2,1)}) custom-call(bf16[4,192,128]{2,1,0:T(8,128)(2,1)S(1)} %get-tuple-element.23.state_ref.refs_0_, bf16[2,4,3,128,128]{4,3,2,1,0:T(8,128)(2,1)S(1)} %copy-done, bf16[2,1,4,128,128]{4,3,2,1,0:T(8,128)(2,1)S(1)} %copy-done.1, f32[192,8]{1,0:T(8,128)S(1)} %get-tuple-element.18.table_ref, ...), custom_call_target="tpu_custom_call" | custom-call | tf_op jit(solution)/shard_map/pallas_call | solution.py:430
  18.5 1.0 %collective-permute-done.4.refs_0_ = bf16[192,128]{1,0:T(8,128)(2,1)S(1)} collective-permute-done((bf16[192,128]{1,0:T(8,128)(2,1)S(1)}, bf16[192,128]{1,0:T(8,128)(2,1)S(1)}, u32[]{:S(2)}, u32[]{:S(2)}) %collective-permute-start.4) | collective-permute-done | bytes 49184 | tf_op jit(solution)/shard_map/ppermute | solution.py:460
  19.5 1.3 %collective-permute-done.5.refs_1_ = bf16[192,128]{1,0:T(8,128)(2,1)S(1)} collective-permute-done((bf16[192,128]{1,0:T(8,128)(2,1)S(1)}, bf16[192,128]{1,0:T(8,128)(2,1)S(1)}, u32[]{:S(2)}, u32[]{:S(2)}) %collective-permute-start.5) | collective-permute-done | bytes 49184 | tf_op jit(solution)/shard_map/ppermute | solution.py:460
  20.8 0.0 collective-permute-done.6.refs_2_
  20.8 1.0 %shard_map.86 = bf16[2,192,512]{2,1,0:T(8,128)(2,1)} custom-call(f32[4,192,128]{2,1,0:T(8,128)S(1)} %get-tuple-element.24.z_ref, bf16[2,1,4,128,128]{4,3,2,1,0:T(8,128)(2,1)S(1)} %copy-done.1, f32[72,128]{1,0:T(8,128)S(1)} %get-tuple-element.19.marks_ref, bf16[192,128]{1,0:T(8,128)(2,1)S(1)} %collective-permute-done.4.refs_0_, ...), custom_call_target="tpu_custom_call", output_to_operand_aliasing={{}: (6, {})} | custom-call | tf_op jit(solution)/shard_map/pallas_call | solution.py:442
Async XLA Ops:
  0.0 9.0 %copy-start = (bf16[2,4,3,128,128]{4,3,2,1,0:T(8,128)(2,1)S(1)}, bf16[2,4,3,128,128]{4,3,2,1,0:T(8,128)(2,1)}, u32[]{:S(2)}) copy-start(bf16[2,4,3,128,128]{4,3,2,1,0:T(8,128)(2,1)} %jac_ref.3) | copy-start | bytes 2359300
  0.0 9.0 %copy-start.1 = (bf16[2,1,4,128,128]{4,3,2,1,0:T(8,128)(2,1)S(1)}, bf16[2,1,4,128,128]{4,3,2,1,0:T(8,128)(2,1)}, u32[]{:S(2)}) copy-start(bf16[2,1,4,128,128]{4,3,2,1,0:T(8,128)(2,1)} %iface_ref.7) | copy-start | bytes 786436
  1.1 7.8 %collective-permute-start = (bf16[4,192,128]{2,1,0:T(8,128)(2,1)S(1)}, bf16[4,192,128]{2,1,0:T(8,128)(2,1)S(1)}, u32[]{:S(2)}, u32[]{:S(2)}) collective-permute-start(bf16[4,192,128]{2,1,0:T(8,128)(2,1)S(1)} %get-tuple-element.17.refs_1_), channel_id=1, source_target_pairs={{0,16},{1,17},{2,18},{3,19},{4,20},{5,21},{6,22},{7,23},{8,24},{9,... | collective-permute-start | bytes 589832 | tf_op jit(solution)/shard_map/ppermute | solution.py:460
  1.2 8.2 %collective-permute-start.1 = (bf16[208,128]{1,0:T(8,128)(2,1)S(1)}, bf16[208,128]{1,0:T(8,128)(2,1)S(1)}, u32[]{:S(2)}, u32[]{:S(2)}) collective-permute-start(bf16[208,128]{1,0:T(8,128)(2,1)S(1)} %get-tuple-element.20), channel_id=1, source_target_pairs={{0,24},{1,25},{2,26},{3,27},{4,28},{5,29},{6,30},{7,31},{8,16},{9,... | collective-permute-start | bytes 159752 | tf_op jit(solution)/shard_map/ppermute | solution.py:460
  5.2 7.1 %collective-permute-start.2 = (bf16[208,128]{1,0:T(8,128)(2,1)S(1)}, bf16[208,128]{1,0:T(8,128)(2,1)S(1)}, u32[]{:S(2)}, u32[]{:S(2)}) collective-permute-start(bf16[208,128]{1,0:T(8,128)(2,1)S(1)} %get-tuple-element.21), channel_id=1, source_target_pairs={{0,28},{1,29},{2,30},{3,31},{4,24},{5,25},{6,26},{7,27},{8,20},{9,... | collective-permute-start | bytes 159752 | tf_op jit(solution)/shard_map/ppermute | solution.py:460
  7.5 5.3 %collective-permute-start.3 = (bf16[208,128]{1,0:T(8,128)(2,1)S(1)}, bf16[208,128]{1,0:T(8,128)(2,1)S(1)}, u32[]{:S(2)}, u32[]{:S(2)}) collective-permute-start(bf16[208,128]{1,0:T(8,128)(2,1)S(1)} %get-tuple-element.22), channel_id=1, source_target_pairs={{0,20},{1,21},{2,22},{3,23},{4,16},{5,17},{6,18},{7,19},{8,28},{9,... | collective-permute-start | bytes 159752 | tf_op jit(solution)/shard_map/ppermute | solution.py:460
  13.3 6.2 %collective-permute-start.4 = (bf16[192,128]{1,0:T(8,128)(2,1)S(1)}, bf16[192,128]{1,0:T(8,128)(2,1)S(1)}, u32[]{:S(2)}, u32[]{:S(2)}) collective-permute-start(bf16[192,128]{1,0:T(8,128)(2,1)S(1)} %get-tuple-element.25), channel_id=1, source_target_pairs={{0,1},{1,0},{2,3},{3,2},{4,5},{5,4},{6,7},{7,6},{8,9},{9,8},{10,11... | collective-permute-start | bytes 147464 | tf_op jit(solution)/shard_map/ppermute | solution.py:460
  15.6 5.3 %collective-permute-start.5 = (bf16[192,128]{1,0:T(8,128)(2,1)S(1)}, bf16[192,128]{1,0:T(8,128)(2,1)S(1)}, u32[]{:S(2)}, u32[]{:S(2)}) collective-permute-start(bf16[192,128]{1,0:T(8,128)(2,1)S(1)} %get-tuple-element.26), channel_id=1, source_target_pairs={{0,1},{1,0},{2,3},{3,2},{4,5},{5,4},{6,7},{7,6},{8,9},{9,8},{10,11... | collective-permute-start | bytes 147464 | tf_op jit(solution)/shard_map/ppermute | solution.py:460
  15.6 5.3 %collective-permute-start.6 = (bf16[192,128]{1,0:T(8,128)(2,1)S(1)}, bf16[192,128]{1,0:T(8,128)(2,1)S(1)}, u32[]{:S(2)}, u32[]{:S(2)}) collective-permute-start(bf16[192,128]{1,0:T(8,128)(2,1)S(1)} %get-tuple-element.27), channel_id=1, source_target_pairs={{0,1},{1,0},{2,3},{3,2},{4,5},{5,4},{6,7},{7,6},{8,9},{9,8},{10,11... | collective-permute-start | bytes 147464 | tf_op jit(solution)/shard_map/ppermute | solution.py:460
